TPU v7x, 32 devices: a whole 2x2x4 slice. The times are simulated.
32 devices in a mesh: dp: 16 (over z, y, core), tensor: 2 (over x).
Axes of the slice: x: 2, y: 2, z: 4, core: 2. Of those that a mesh axis runs over, the one named last changes fastest.
Arguments:
- mixer_x: bfloat16 [2048, 8192], P(('dp', 'tensor')), may hold values from -6 to 6
- gate_z: bfloat16 [2048, 8192], P(('dp', 'tensor')), may hold values from -6 to 6
- b_matrix: bfloat16 [2048, 1024], P(('dp', 'tensor')), may hold values from -6 to 6
- c_matrix: bfloat16 [2048, 1024], P(('dp', 'tensor')), may hold values from -6 to 6
- raw_steps: bfloat16 [2048, 128], P(('dp', 'tensor')), may hold values from -3 to 11
- decay_log: float32 [128], P('tensor'), may hold values from -1 to 3
- skip_gain: float32 [128], P('tensor'), may hold values from 0.5 to 1.5
- step_bias: float32 [128], P('tensor'), may hold values from -14 to -3
- norm_gain: float32 [8192], P('tensor'), may hold values from 0.5 to 1.5
- out_grad: bfloat16 [2048, 8192], P(('dp', 'tensor')), may hold values from -12 to 12
Outputs:
- grad_mixer_x: bfloat16 [2048, 8192], P(('dp', 'tensor'))
- grad_gate_z: bfloat16 [2048, 8192], P(('dp', 'tensor'))
- grad_b_matrix: bfloat16 [2048, 1024], P(('dp', 'tensor'))
- grad_c_matrix: bfloat16 [2048, 1024], P(('dp', 'tensor'))
- grad_raw_steps: bfloat16 [2048, 128], P(('dp', 'tensor'))
- grad_decay_log: float32 [128], P('tensor')
- grad_skip_gain: float32 [128], P('tensor')
- grad_step_bias: float32 [128], P('tensor')
- grad_norm_gain: float32 [8192], P('tensor')
All inputs are finite; a program needn't handle non-finite values.
Results may differ from a plain program's by a relative error of at most 0.013.
Values may be sent and summed in bfloat16 or wider, within the bound.
No kernel may reach another device: no remote copies, remote signals or barrier semaphores. Data moves between devices by JAX's collectives and lax.ppermute only.
A program may use at most 128 MiB of HBM per device.

v0:
```python
import jax
import jax.numpy as jnp
from jax import lax
from jax.sharding import PartitionSpec as P

MIXER_HEADS = 128
HEAD_DIM = 64
STATE = 128
GROUPS = 8


precise = lax.Precision.HIGHEST
epsilon = 1e-05


def prefix(array, axis, combine, identity, reverse):
    count, here = (lax.axis_size(axis), lax.axis_index(axis))
    everything = jax.tree.map(lambda part: lax.all_gather(part, axis), array)
    start = jax.tree.map(
        lambda part, zero: jnp.broadcast_to(jnp.asarray(zero, part.dtype), part.shape),
        array,
        identity,
    )

    def step(k, before):
        at = count - 1 - k if reverse else k
        reached = at > here if reverse else at < here
        new = combine(before, jax.tree.map(lambda part: part[at], everything))
        return jax.tree.map(lambda a, b: jnp.where(reached, a, b), new, before)

    return lax.fori_loop(0, count, step, start)


def decay_rates(raw_steps, decay_log, step_bias):
    stepsize = jax.nn.softplus(raw_steps.astype(jnp.float32) + step_bias)
    cumulative = jnp.cumsum(-jnp.exp(decay_log) * stepsize, axis=0)
    return (stepsize, cumulative)


def block_state(mixer_x, b_matrix, raw_steps, decay_log, step_bias):
    stepsize, cumulative = decay_rates(raw_steps, decay_log, step_bias)
    totals = cumulative[-1]
    weights = jnp.exp(totals[None] - cumulative) * stepsize
    scaled = mixer_x.astype(jnp.float32) * weights[..., None]
    states = jnp.einsum("lgkp,lgn->gkpn", scaled, b_matrix.astype(jnp.float32), precision=precise)
    return (states, totals)


def block_output(
    mixer_x,
    gate_z,
    b_matrix,
    c_matrix,
    raw_steps,
    decay_log,
    skip_gain,
    step_bias,
    norm_gain,
    inbound,
):
    stepsize, cumulative = decay_rates(raw_steps, decay_log, step_bias)
    value_rows = mixer_x.astype(jnp.float32)
    sources = b_matrix.astype(jnp.float32)
    readers = c_matrix.astype(jnp.float32)
    scores = jnp.einsum("tgn,sgn->gts", readers, sources, precision=precise)
    length = value_rows.shape[0]
    causal = lax.broadcasted_iota(jnp.int32, (length, length), 0) >= lax.broadcasted_iota(
        jnp.int32, (length, length), 1
    )
    by_head = jnp.transpose(cumulative, (1, 2, 0))
    spread = by_head[..., :, None] - by_head[..., None, :]
    decays = jnp.exp(jnp.where(causal, spread, -jnp.inf))
    weights = scores[:, None] * decays * jnp.transpose(stepsize, (1, 2, 0))[:, :, None, :]
    within = jnp.einsum("gkts,sgkp->tgkp", weights, value_rows, precision=precise)
    carried = (
        jnp.einsum("tgn,gkpn->tgkp", readers, inbound, precision=precise)
        * jnp.exp(cumulative)[..., None]
    )
    mixed = within + carried + skip_gain[None, :, :, None] * value_rows
    gated = mixed * jax.nn.silu(gate_z.astype(jnp.float32))
    power = jnp.mean(gated * gated, axis=(2, 3), keepdims=True)
    return gated * lax.rsqrt(power + epsilon) * norm_gain[None]


def link(earlier, later):
    return (earlier[0] + later[0], jnp.exp(later[0])[..., None, None] * earlier[1] + later[1])


def reduce_weights(terms):
    return lax.psum((terms[0], terms[1], terms[2], terms[3]), "dp")


def send_back(grads):
    return (
        lax.all_to_all(grads[0], "tensor", split_axis=0, concat_axis=1, tiled=True),
        lax.all_to_all(grads[1], "tensor", split_axis=0, concat_axis=1, tiled=True),
        lax.all_to_all(grads[2], "tensor", split_axis=0, concat_axis=1, tiled=True),
        lax.all_to_all(grads[3], "tensor", split_axis=0, concat_axis=1, tiled=True),
        lax.all_to_all(grads[4], "tensor", split_axis=0, concat_axis=1, tiled=True),
    )


def on_device(
    mixer_x,
    gate_z,
    b_matrix,
    c_matrix,
    raw_steps,
    decay_log,
    skip_gain,
    step_bias,
    norm_gain,
    out_grad,
):
    per_group = MIXER_HEADS // GROUPS
    decay_local = decay_log.reshape(-1, per_group)
    skip_local = skip_gain.reshape(-1, per_group)
    bias_local = step_bias.reshape(-1, per_group)
    gain_local = norm_gain.reshape(-1, per_group, HEAD_DIM)

    def head_view(array):
        return array.reshape(array.shape[0], -1, per_group, HEAD_DIM)

    def group_view(array):
        return array.reshape(array.shape[0], -1, STATE)

    def steps_view(array):
        return array.reshape(array.shape[0], -1, per_group)

    local_x, local_z, local_b, local_c, local_steps, local_grad = (
        lax.all_to_all(mixer_x, "tensor", split_axis=1, concat_axis=0, tiled=True),
        lax.all_to_all(gate_z, "tensor", split_axis=1, concat_axis=0, tiled=True),
        lax.all_to_all(b_matrix, "tensor", split_axis=1, concat_axis=0, tiled=True),
        lax.all_to_all(c_matrix, "tensor", split_axis=1, concat_axis=0, tiled=True),
        lax.all_to_all(raw_steps, "tensor", split_axis=1, concat_axis=0, tiled=True),
        lax.all_to_all(out_grad, "tensor", split_axis=1, concat_axis=0, tiled=True),
    )
    (states, totals), pull_state = jax.vjp(
        block_state,
        head_view(local_x),
        group_view(local_b),
        steps_view(local_steps),
        decay_local,
        bias_local,
    )
    empty = (jnp.zeros_like(totals), jnp.zeros_like(states))
    inbound = prefix((totals, states), "dp", link, empty, False)[1]
    totals, inbound, pull_state = (totals, inbound, pull_state)
    normed, pull_out = jax.vjp(
        block_output,
        head_view(local_x),
        head_view(local_z),
        group_view(local_b),
        group_view(local_c),
        steps_view(local_steps),
        decay_local,
        skip_local,
        bias_local,
        gain_local,
        inbound,
    )
    out_parts = pull_out(head_view(local_grad).astype(jnp.float32))
    empty = (jnp.zeros_like(totals), jnp.zeros_like(inbound))
    returned = prefix((totals, out_parts[9]), "dp", link, empty, True)[1]
    total_grad = jnp.sum(returned * jnp.exp(totals)[..., None, None] * inbound, axis=(2, 3))
    state_parts = pull_state((returned, total_grad))
    rows = local_x.shape[0]
    grad_values = (out_parts[0] + state_parts[0]).reshape(rows, -1)
    grad_gates = out_parts[1].reshape(rows, -1)
    grad_sources = (out_parts[2] + state_parts[1]).reshape(rows, -1)
    grad_readers = out_parts[3].reshape(rows, -1)
    grad_steps = (out_parts[4] + state_parts[2]).reshape(rows, -1)
    weight_terms = (
        (out_parts[5] + state_parts[3]).reshape(-1),
        out_parts[6].reshape(-1),
        (out_parts[7] + state_parts[4]).reshape(-1),
        out_parts[8].reshape(-1),
    )
    input_terms = (grad_values, grad_gates, grad_sources, grad_readers, grad_steps)
    returned_rows = send_back(input_terms)
    summed = reduce_weights(weight_terms)
    return (
        returned_rows[0],
        returned_rows[1],
        returned_rows[2],
        returned_rows[3],
        returned_rows[4],
        summed[0],
        summed[1],
        summed[2],
        summed[3],
    )


def solution(mesh):
    placed = (
        P(("dp", "tensor"), None),
        P(("dp", "tensor"), None),
        P(("dp", "tensor"), None),
        P(("dp", "tensor"), None),
        P(("dp", "tensor"), None),
        P("tensor"),
        P("tensor"),
        P("tensor"),
        P("tensor"),
        P(("dp", "tensor"), None),
    )
    return jax.shard_map(
        on_device,
        mesh=mesh,
        in_specs=placed,
        out_specs=(
            P(("dp", "tensor"), None),
            P(("dp", "tensor"), None),
            P(("dp", "tensor"), None),
            P(("dp", "tensor"), None),
            P(("dp", "tensor"), None),
            P("tensor"),
            P("tensor"),
            P("tensor"),
            P("tensor"),
        ),
        check_vma=False,
    )
```

profile of v0, /device:TPU:0, one launch (start us, length us, event | category | flops | bytes accessed | tf_op | source)
XLA Modules:
  0.0 650.1 jit_solution(13830544580956996412)
XLA Ops:
  8.8 4.2 all-to-all-start.3
  21.2 4.1 all-to-all-done.2
  31.1 10.7 %all-to-all-done.4 = bf16[64,2,4096]{2,0,1:T(8,128)(2,1)S(1)} async-done(((bf16[64,2,4096]{2,0,1:T(8,128)(2,1)}), bf16[64,2,4096]{2,0,1:T(8,128)(2,1)S(1)}, u32[]{:S(2)}, u32[]{:S(2)}) %all-to-all-start.4) | async-done | bytes 1048608 | tf_op jit(solution)/shard_map/all_to_all | solution.py:131
  58.1 4.4 all-to-all-start.5
  72.7 23.9 %all_gather.16 = f32[16,4,16]{2,1,0:T(4,128)} all-gather(f32[1,4,16]{2,1,0:T(4,128)S(1)} %get-tuple-element.327), channel_id=1, replica_groups=mesh['dp'=16,'tensor'=2] {'dp'}, dimensions={0}, use_global_device_ids=true | all-gather | bytes 4352 | tf_op jit(solution)/shard_map/all_gather | solution.py:18
  99.9 4.4 all-to-all-start
  107.2 4.8 reshape.221
  112.1 4.9 copy.177
  121.9 4.7 reshape.219
  126.6 4.9 copy.157
  131.5 87.0 %all-gather.5.cloned.1.call-done = f32[64,16,64,128]{3,2,1,0:T(8,128)} async-done(((f32[4,16,64,128]{3,2,1,0:T(8,128)}), f32[64,16,64,128]{3,2,1,0:T(8,128)}) %all-gather.5.cloned.1.call-update) | async-done | bytes 33554448 | tf_op jit(solution)/shard_map/all_gather | solution.py:18
  218.5 44.5 %while.30 = (s32[]{:T(128)}, f32[4,16,64,128]{3,2,1,0:T(8,128)S(1)}, s32[]{:T(128)}, f32[16,4,16]{2,1,0:T(4,128)}, f32[16,4,16,64,128]{4,3,2,1,0:T(8,128)}, /*index=5*/s32[]{:T(128)}, s32[]{:T(128)}) while((s32[]{:T(128)}, f32[4,16,64,128]{3,2,1,0:T(8,128)S(1)}, s32[]{:T(128)}, f32[16,4,16]{2,1,0:T(4,128)}, ...), condition=%wide.region_2.4_spmd.clone, body=%wide.region_1.3_spmd.clone.sunk | while | flops 2097156 | bytes 6292329 | solution.py:31
  265.3 4.7 multiply_reduce_fusion.5
  279.3 8.4 %fusion.11 = (f32[4,16,128]{2,1,0:T(8,128)}, f32[4,16,128]{2,1,0:T(8,128)}, f32[4,16,128]{2,1,0:T(8,128)}, f32[4,128,128]{2,1,0:T(8,128)}) fusion(f32[4,16,128]{2,1,0:T(8,128)} %copy.167, f32[4,16,128]{2,1,0:T(8,128)} %copy.165, f32[4,128,128]{2,1,0:T(8,128)} %fusion.89, pred[128,128]{1,0:T(8,128)(4,1)} %iota_compare_fusion, ...), kind=kOutput, calls=%fused_computation.23 | convolution fusion | flops 818847744 | bytes 3850240 | tf_op jit(solution)/shard_map/transpose(jvp(gkts,sgkp->tgkp))/dot_general | solution.py:74
  289.3 5.2 fusion.55
  301.1 5.0 reshape.233
  306.1 5.4 copy.219
  311.6 135.5 %all-gather.7.cloned.1.call-done = f32[64,16,64,128]{3,2,1,0:T(8,128)} async-done(((f32[4,16,64,128]{3,2,1,0:T(8,128)}), f32[64,16,64,128]{3,2,1,0:T(8,128)}) %all-gather.7.cloned.1.call-update) | async-done | bytes 33554448 | tf_op jit(solution)/shard_map/all_gather | solution.py:18
  447.1 72.2 %while.31 = (s32[]{:T(128)}, f32[4,16,64,128]{3,2,1,0:T(8,128)}, s32[]{:T(128)}, f32[16,4,16]{2,1,0:T(4,128)}, f32[16,4,16,64,128]{4,3,2,1,0:T(8,128)}, /*index=5*/s32[]{:T(128)}, s32[]{:T(128)}, s32[]{:T(128)}, s32[]{:T(128)}) while((s32[]{:T(128)}, f32[4,16,64,128]{3,2,1,0:T(8,128)}, s32[]{:T(128)}, f32[16,4,16]{2,1,0:T(4,128)}, ...), condition=%wide.region_6.8_spmd.clone, body=%wide.region_5.7_spmd.clone.sunk | while | flops 2097160 | bytes 6292391 | solution.py:31
  519.2 6.6 %fusion.17 = (f32[4,16]{1,0:T(4,128)}, f32[128,4,16]{0,2,1:T(8,128)}, f32[128,4,16]{0,2,1:T(8,128)}, f32[4,16,64,128]{3,2,1,0:T(8,128)}) fusion(f32[128,4,16,64]{0,3,2,1:T(8,128)} %copy-done.2, bf16[128,4,16,64]{0,3,2,1:T(8,128)(2,1)S(1)} %copy.169, f32[4,16,64,128]{3,2,1,0:T(8,128)} %copy-done.5, f32[4,16,64,128]{3,2,1,0:T(8,128)} %get-tuple-element.239, ...), kind=kOutput, calls=%fused_computation.29 | convolution fusion | flops 808959936 | bytes 9634048 | tf_op jit(solution)/shard_map/transpose(jvp(lgkp,lgn->gkpn))/dot_general | solution.py:45
  531.7 4.7 all-to-all-start.7
  545.7 4.9 fusion.64
  561.3 7.3 %fusion.50 = bf16[128,4,16,64]{0,3,2,1:T(8,128)(2,1)S(1)} fusion(f32[4,16,128]{2,1,0:T(8,128)} %copy.167, f32[4,16,128]{2,1,0:T(8,128)} %copy.165, f32[4,128,128]{2,1,0:T(8,128)} %fusion.89, pred[128,128]{1,0:T(8,128)(4,1)} %iota_compare_fusion, f32[128,4,16,64]{0,3,2,1:T(8,128)} %copy-done.2, f32[4,16,64,128]{3,2,1,0:T(8,128)} %get-tuple-element.330, ...), kind=kOutput, calls=%fused_computation.67 | convolution fusion | flops 812646400 | bytes 5619968 | tf_op jit(solution)/shard_map/transpose(jvp(gkts,sgkp->tgkp))/dot_general | solution.py:74
  581.2 59.4 %all-reduce.1 = (f32[64]{0:T(128)}, f32[64]{0:T(128)}, f32[64]{0:T(128)}, f32[4096]{0:T(1024)}) all-reduce(f32[64]{0:T(128)S(1)} %exponential_multiply_fusion, f32[64]{0:T(128)S(1)} %reshape.217, f32[64]{0:T(128)S(1)} %add.153, f32[4096]{0:T(1024)S(1)} %reshape.218), channel_id=1, replica_groups=mesh['dp'=16,'tensor'=2] {'dp'}, use_global_device_ids=true, to_apply=%region_19.21 | all-reduce | flops 4288 | bytes 34304 | tf_op jit(solution)/shard_map/psum | solution.py:90
  (230 shorter events, 229.7 us)
Async XLA Ops:
  7.2 9.6 %copy-start.21 = (bf16[64,1024]{1,0:T(8,128)(2,1)S(1)}, bf16[64,1024]{1,0:T(8,128)(2,1)}, u32[]{:S(2)}) copy-start(bf16[64,1024]{1,0:T(8,128)(2,1)} %param.17) | copy-start | bytes 393220
  8.8 8.6 %all-to-all-start.3 = ((bf16[2,2,2048]{2,1,0:T(2,128)(2,1)}), bf16[2,2,2048]{2,1,0:T(2,128)(2,1)S(1)}, u32[]{:S(2)}, u32[]{:S(2)}) async-start(bf16[2,2,2048]{2,1,0:T(2,128)(2,1)} %reshape.235), calls=%async_computation.3 | async-start | bytes 32768 | tf_op jit(solution)/shard_map/all_to_all | solution.py:135
  17.4 7.8 %all-to-all-start.2 = ((bf16[64,2,512]{2,0,1:T(8,128)(2,1)}), bf16[64,2,512]{2,0,1:T(8,128)(2,1)S(1)}, u32[]{:S(2)}, u32[]{:S(2)}) async-start(bf16[64,2,512]{2,0,1:T(8,128)(2,1)} %bitcast.157), calls=%async_computation.2 | async-start | bytes 262144 | tf_op jit(solution)/shard_map/all_to_all | solution.py:133
  21.2 9.9 %copy-start.6 = (f32[128,4,16]{2,1,0:T(4,128)}, f32[128,4,16]{2,1,0:T(4,128)S(1)}, u32[]{:S(2)}) copy-start(f32[128,4,16]{2,1,0:T(4,128)S(1)} %reshape.231) | copy-start | bytes 98308
  25.3 16.5 %all-to-all-start.4 = ((bf16[64,2,4096]{2,0,1:T(8,128)(2,1)}), bf16[64,2,4096]{2,0,1:T(8,128)(2,1)S(1)}, u32[]{:S(2)}, u32[]{:S(2)}) async-start(bf16[64,2,4096]{2,0,1:T(8,128)(2,1)} %bitcast.155), calls=%async_computation.4 | async-start | bytes 2097152 | tf_op jit(solution)/shard_map/all_to_all | solution.py:131
  28.9 189.7 %all-gather.5.cloned.1.call-start = ((), (), s32[]{:S(2)}) async-start(), calls=%async_computation.11 | async-start | bytes 35651584 | tf_op jit(solution)/shard_map/all_gather | solution.py:18
  50.3 7.8 %all-to-all-start.1 = ((bf16[64,2,512]{2,0,1:T(8,128)(2,1)}), bf16[64,2,512]{2,0,1:T(8,128)(2,1)S(1)}, u32[]{:S(2)}, u32[]{:S(2)}) async-start(bf16[64,2,512]{2,0,1:T(8,128)(2,1)} %bitcast.158), calls=%async_computation.1 | async-start | bytes 262144 | tf_op jit(solution)/shard_map/all_to_all | solution.py:134
  58.1 41.8 %all-to-all-start.5 = ((bf16[64,2,4096]{2,0,1:T(8,128)(2,1)}), bf16[64,2,4096]{2,0,1:T(8,128)(2,1)}, u32[]{:S(2)}, u32[]{:S(2)}) async-start(bf16[64,2,4096]{2,0,1:T(8,128)(2,1)} %bitcast.154), calls=%async_computation.5 | async-start | bytes 2097152 | tf_op jit(solution)/shard_map/all_to_all | solution.py:132
  99.9 19.1 %all-to-all-start = ((bf16[64,2,4096]{2,0,1:T(8,128)(2,1)}), bf16[64,2,4096]{2,0,1:T(8,128)(2,1)}, u32[]{:S(2)}, u32[]{:S(2)}) async-start(bf16[64,2,4096]{2,0,1:T(8,128)(2,1)} %bitcast.170), calls=%async_computation | async-start | bytes 2097152 | tf_op jit(solution)/shard_map/all_to_all | solution.py:136
  104.4 342.7 %all-gather.7.cloned.1.call-start = ((), (), s32[]{:S(2)}) async-start(), calls=%async_computation.12 | async-start | bytes 35651584 | tf_op jit(solution)/shard_map/all_gather | solution.py:18
  297.1 234.6 %all-to-all-start.9 = ((bf16[2,64,512]{2,1,0:T(8,128)(2,1)}), bf16[2,64,512]{2,1,0:T(8,128)(2,1)}, u32[]{:S(2)}, u32[]{:S(2)}) async-start(bf16[2,64,512]{2,1,0:T(8,128)(2,1)} %all_to_all.163), calls=%async_computation.9 | async-start | bytes 262144 | tf_op jit(solution)/shard_map/all_to_all | solution.py:98
  531.7 14.0 %copy-start.1 = (f32[4,16,64,128]{3,2,1,0:T(8,128)S(1)}, f32[4,16,64,128]{3,2,1,0:T(8,128)}, u32[]{:S(2)}) copy-start(f32[4,16,64,128]{3,2,1,0:T(8,128)} %get-tuple-element.239) | copy-start | bytes 6291460
  531.7 19.1 %all-to-all-start.7 = ((bf16[2,64,4096]{2,1,0:T(8,128)(2,1)}), bf16[2,64,4096]{2,1,0:T(8,128)(2,1)}, u32[]{:S(2)}, u32[]{:S(2)}) async-start(bf16[2,64,4096]{2,1,0:T(8,128)(2,1)} %copy.219), calls=%async_computation.7 | async-start | bytes 2097152 | tf_op jit(solution)/shard_map/all_to_all | solution.py:96
  540.4 13.7 %copy-start.8 = (bf16[128,4,128]{2,1,0:T(4,128)(2,1)S(1)}, bf16[128,4,128]{2,1,0:T(4,128)(2,1)}, u32[]{:S(2)}) copy-start(bf16[128,4,128]{2,1,0:T(4,128)(2,1)} %reshape.214) | copy-start | bytes 393220
  540.4 13.7 %copy-start.11 = (f32[4,128,128]{2,1,0:T(8,128)S(1)}, f32[4,128,128]{2,1,0:T(8,128)}, u32[]{:S(2)}) copy-start(f32[4,128,128]{2,1,0:T(8,128)} %get-tuple-element.282) | copy-start | bytes 786436
  550.8 7.1 %all-to-all-start.10 = ((bf16[2,2,2048]{2,1,0:T(2,128)(2,1)}), bf16[2,2,2048]{2,1,0:T(2,128)(2,1)S(1)}, u32[]{:S(2)}, u32[]{:S(2)}) async-start(bf16[2,2,2048]{2,1,0:T(2,128)(2,1)} %reshape.237), calls=%async_computation.10 | async-start | bytes 32768 | tf_op jit(solution)/shard_map/all_to_all | solution.py:99
  557.9 15.4 %all-to-all-start.8 = ((bf16[2,64,512]{2,1,0:T(8,128)(2,1)}), bf16[2,64,512]{2,1,0:T(8,128)(2,1)S(1)}, u32[]{:S(2)}, u32[]{:S(2)}) async-start(bf16[2,64,512]{2,1,0:T(8,128)(2,1)} %all_to_all.159), calls=%async_computation.8 | async-start | bytes 262144 | tf_op jit(solution)/shard_map/all_to_all | solution.py:97
  573.3 7.6 %copy-start.30 = (f32[4,16]{1,0:T(4,128)S(1)}, f32[4,16]{1,0:T(4,128)}, u32[]{:S(2)}) copy-start(f32[4,16]{1,0:T(4,128)} %get-tuple-element.320) | copy-start | bytes 772
  573.3 7.6 %copy-start.31 = (f32[4,16]{1,0:T(4,128)S(1)}, f32[4,16]{1,0:T(4,128)}, u32[]{:S(2)}) copy-start(f32[4,16]{1,0:T(4,128)} %get-tuple-element.322) | copy-start | bytes 772
  573.3 7.7 %copy-start.28 = (f32[4,16]{1,0:T(4,128)S(1)}, f32[4,16]{1,0:T(4,128)}, u32[]{:S(2)}) copy-start(f32[4,16]{1,0:T(4,128)} %get-tuple-element.286) | copy-start | bytes 772
  573.3 7.7 %copy-start.29 = (f32[4,16]{1,0:T(4,128)S(1)}, f32[4,16]{1,0:T(4,128)}, u32[]{:S(2)}) copy-start(f32[4,16]{1,0:T(4,128)} %get-tuple-element.287) | copy-start | bytes 772
  573.3 7.8 %copy-start.32 = (f32[4,16]{1,0:T(4,128)S(1)}, f32[4,16]{1,0:T(4,128)}, u32[]{:S(2)}) copy-start(f32[4,16]{1,0:T(4,128)} %get-tuple-element.283) | copy-start | bytes 772
  573.3 7.8 %copy-start.34 = (f32[64]{0:T(128)S(1)}, f32[64]{0:T(128)}, u32[]{:S(2)}) copy-start(f32[64]{0:T(128)} %param.20) | copy-start | bytes 772
  573.3 68.7 %all-to-all-start.6 = ((bf16[2,64,4096]{2,1,0:T(8,128)(2,1)}), bf16[2,64,4096]{2,1,0:T(8,128)(2,1)S(1)}, u32[]{:S(2)}, u32[]{:S(2)}) async-start(bf16[2,64,4096]{2,1,0:T(8,128)(2,1)} %copy.218), calls=%async_computation.6 | async-start | bytes 2097152 | tf_op jit(solution)/shard_map/all_to_all | solution.py:95
  (24 other events, 87.7 us)
Sparse Core Ops, SparseCore 0:
  49.7 168.7 all-gather.4
  278.8 168.2 all-gather.6
where the time goes:
time: 659 us; the launch traced here: 650 us
  waiting for transfers between devices  245 us (37%)
  other arithmetic  118 us (18%)
  local copies, waits for them, and re-layouts  98.3 us (15%)
  blocking collectives  83.3 us (13%)
  matrix products  48.3 us (7%)
  starting transfers between devices  42.4 us (6%)
  between operations  14.9 us (2%)
    all_gather x2, waiting for transfers between devices, prefix(): everything = jax.tree.map(lambda part: lax.all_gather(part, axis), array)  222 us
    select_n x32, other arithmetic, step(): return jax.tree.map(lambda a, b: jnp.where(reached, a, b), new, before)  94.6 us
    psum x1, blocking collectives, reduce_weights(): return lax.psum((terms[0], terms[1], terms[2], terms[3]), 'dp')  59.4 us
    all_gather x1, blocking collectives, prefix(): everything = jax.tree.map(lambda part: lax.all_gather(part, axis), array)  23.9 us
    exp x32, local copies, waits for them, and re-layouts, link(): jnp.exp(later[0])[..., None, None] * earlier[1] + later[1]  21.6 us
    dot_general x3, matrix products, block_output(): jnp.einsum('gkts,sgkp->tgkp', weights, value_rows, precision=precise)  20.4 us
    dot_general x3, matrix products, block_state(): jnp.einsum('lgkp,lgn->gkpn', scaled, b_matrix.astype(jnp.float32), precis...  14.8 us
  transfers between devices with their start and end apart: 13, of which 8 were waited for; matrix products, arithmetic and copies ran while one was open for 30% of the time, Pallas kernels for 0%

commit v1 on v0

v1 whole, which is shorter than its diff:
```python
import jax
import jax.numpy as jnp
from jax import lax
from jax.experimental import pallas as pl
from jax.experimental.pallas import tpu as pltpu
from jax.sharding import Mesh
from jax.sharding import PartitionSpec as P

MIXER_HEADS = 128
HEAD_DIM = 64
STATE = 128
GROUPS = 8
HEADS = MIXER_HEADS // GROUPS
WIDTH = HEADS * HEAD_DIM
PAIRS = HEADS // 2
CHUNK = 128
LANES = 128
epsilon = 1e-05
f32 = jnp.float32
bf16 = jnp.bfloat16

DT, CUM, WEIGHT, SHIFTED, ECUM, RATE, SIG = range(7)
X, B, C, STEPS = 0, WIDTH, WIDTH + STATE, WIDTH + 2 * STATE
FIRST = WIDTH + 2 * STATE + LANES
CLAMP = 80.0


def mm(a, b):
    return jnp.dot(a, b, preferred_element_type=f32)


def mm_nt(a, b):
    return lax.dot_general(a, b, (((1,), (1,)), ((), ())), preferred_element_type=f32)


def mm_tn(a, b):
    return lax.dot_general(a, b, (((0,), (0,)), ((), ())), preferred_element_type=f32)


def mm_exact(a, b):
    return jnp.dot(a, b, precision=lax.Precision.HIGHEST, preferred_element_type=f32)


def low_half(rows):
    return lax.broadcasted_iota(jnp.int32, (rows, LANES), 1) < HEAD_DIM


def spread_pair(values, kind, j):
    rows = values.shape[0]
    at = kind * HEADS + 2 * j
    return jnp.where(
        low_half(rows),
        jnp.broadcast_to(values[:, at : at + 1], (rows, LANES)),
        jnp.broadcast_to(values[:, at + 1 : at + 2], (rows, LANES)),
    )


def spread_row(row):
    rows = jnp.broadcast_to(row, (8, LANES))
    return jnp.concatenate([spread_pair(rows, 0, j) for j in range(PAIRS)], axis=1)


def head_matrix():
    channel = lax.broadcasted_iota(jnp.int32, (WIDTH, LANES), 0) // HEAD_DIM
    lane = lax.broadcasted_iota(jnp.int32, (WIDTH, LANES), 1) % HEADS
    return jnp.where(channel == lane, 1.0, 0.0).astype(bf16)


def head_sum(values, ones):
    high = values.astype(bf16)
    low = (values - high.astype(f32)).astype(bf16)
    return mm(high, ones) + mm(low, ones)


def split_pair(block):
    low = low_half(block.shape[0])
    zero = jnp.zeros_like(block)
    return jnp.concatenate(
        [jnp.where(low, block, zero), jnp.where(low, zero, block)], axis=0
    )


def blocks_of(sub_count, tensor_count):
    return [t * sub_count + s for s in range(sub_count) for t in range(tensor_count)]


def pack_first(owners, x_ref, b_ref, c_ref, steps_ref, out_ref):
    for j, g in enumerate(owners):
        out_ref[j, :, X : X + WIDTH] = x_ref[:, g * WIDTH : (g + 1) * WIDTH]
        out_ref[j, :, B : B + STATE] = b_ref[:, g * STATE : (g + 1) * STATE]
        out_ref[j, :, C : C + STATE] = c_ref[:, g * STATE : (g + 1) * STATE]
        out_ref[j, :, STEPS : STEPS + LANES] = steps_ref[...]


def pack_second(owners, z_ref, grad_ref, out_ref):
    for j, g in enumerate(owners):
        out_ref[j, :, :WIDTH] = z_ref[:, g * WIDTH : (g + 1) * WIDTH]
        out_ref[j, :, WIDTH:] = grad_ref[:, g * WIDTH : (g + 1) * WIDTH]


def unpack_gates(owners, in_ref, out_ref):
    for j, g in enumerate(owners):
        out_ref[:, g * WIDTH : (g + 1) * WIDTH] = in_ref[j]


def unpack_last(owners, in_ref, x_ref, b_ref, c_ref, steps_ref):
    steps = None
    for j, g in enumerate(owners):
        x_ref[:, g * WIDTH : (g + 1) * WIDTH] = in_ref[j, :, X : X + WIDTH]
        b_ref[:, g * STATE : (g + 1) * STATE] = in_ref[j, :, B : B + STATE]
        c_ref[:, g * STATE : (g + 1) * STATE] = in_ref[j, :, C : C + STATE]
        part = in_ref[j, :, STEPS : STEPS + LANES].astype(f32)
        steps = part if steps is None else steps + part
    steps_ref[...] = steps.astype(bf16)


def state_kernel(
    first_ref, pick_ref, heads_ref, sm_ref, smt_ref, own_ref, dec_ref, state_ref, whole_ref,
    carry, total,
):
    c = pl.program_id(0)

    @pl.when(c == 0)
    def _():
        carry[...] = jnp.zeros_like(carry)
        total[...] = jnp.zeros_like(total)

    raw = mm(first_ref[:, STEPS : STEPS + LANES], pick_ref[...]) + heads_ref[1:2, :]
    small = jnp.exp(-jnp.abs(raw))
    series = small * (1.0 - small * (0.5 - small * (1.0 / 3 - small * (0.25 - small * 0.2))))
    soft = jnp.maximum(raw, 0.0) + jnp.where(small < 0.015625, series, jnp.log(1.0 + small))
    sig = jnp.where(raw >= 0.0, 1.0, small) / (1.0 + small)
    rate = -jnp.exp(heads_ref[0:1, :]) * soft
    t = lax.broadcasted_iota(jnp.int32, (CHUNK, CHUNK), 0)
    s = lax.broadcasted_iota(jnp.int32, (CHUNK, CHUNK), 1)
    cum = mm_exact(jnp.where(t >= s, 1.0, 0.0), rate)
    after = mm_exact(jnp.where(t < s, 1.0, 0.0), rate)
    kind = lax.broadcasted_iota(jnp.int32, (CHUNK, LANES), 1) // HEADS
    sm = jnp.where(kind == DT, soft, jnp.zeros_like(soft))
    sm = jnp.where(kind == CUM, cum, sm)
    sm = jnp.where(kind == WEIGHT, soft * jnp.exp(after), sm)
    sm = jnp.where(kind == SHIFTED, cum - jnp.log(soft), sm)
    sm = jnp.where(kind == ECUM, jnp.exp(cum), sm)
    sm = jnp.where(kind == RATE, rate, sm)
    sm = jnp.where(kind == SIG, sig, sm)
    sm_ref[...] = sm
    smt_ref[...] = sm.T

    last = cum[CHUNK - 1 : CHUNK, :]
    total[...] += jnp.broadcast_to(last, total.shape)
    dec = spread_row(jnp.exp(last))
    dec_ref[0] = dec
    sources_t = first_ref[:, B : B + STATE].T
    for j in range(PAIRS):
        at = slice(j * LANES, (j + 1) * LANES)
        scaled = first_ref[:, at].astype(f32) * spread_pair(sm, WEIGHT, j)
        hi = scaled.astype(bf16)
        own = mm(sources_t, hi) + mm(sources_t, (scaled - hi.astype(f32)).astype(bf16))
        own_ref[0, :, at] = own
        new = dec[0:1, at] * carry[:, at] + own
        carry[:, at] = new
        state_ref[:, at] = new.astype(bf16)
    whole_ref[...] = spread_row(jnp.exp(total[0:1, :]))


def within_kernel(first_ref, sm_ref, smt_ref, out_ref):
    t = lax.broadcasted_iota(jnp.int32, (CHUNK, CHUNK), 0)
    s = lax.broadcasted_iota(jnp.int32, (CHUNK, CHUNK), 1)
    scores = mm_nt(first_ref[:, C : C + STATE], first_ref[:, B : B + STATE])
    scores = jnp.where(t >= s, scores, 0.0)
    for j in range(PAIRS):
        weights = []
        for h in (2 * j, 2 * j + 1):
            here = sm_ref[:, CUM * HEADS + h : CUM * HEADS + h + 1]
            there = smt_ref[SHIFTED * HEADS + h : SHIFTED * HEADS + h + 1, :]
            weights.append((scores * jnp.exp(jnp.minimum(here - there, CLAMP))).astype(bf16))
        at = slice(j * LANES, (j + 1) * LANES)
        out_ref[:, at] = mm(jnp.concatenate(weights, axis=1), split_pair(first_ref[:, at]))


def output_kernel(
    first_ref, second_ref, within_ref, sm_ref, inbound_ref, own_ref, dec_ref, gain_ref, skip_ref,
    gate_ref, mixed_ref, e_ref, back_ref, slab_ref, readers_ref, end_ref, param_ref,
    carry, pre, back_sum, gain_sum, skip_sum, ys, gated_s, high_s, low_s, scaled_s, wide_s,
):
    c = pl.program_id(0)

    @pl.when(c == 0)
    def _():
        carry[...] = inbound_ref[...].astype(f32)
        pre[...] = jnp.ones_like(pre)
        back_sum[...] = jnp.zeros_like(back_sum)
        gain_sum[...] = jnp.zeros_like(gain_sum)
        skip_sum[...] = jnp.zeros_like(skip_sum)

    sm = sm_ref[...]
    readers = first_ref[:, C : C + STATE]
    state = carry[...].astype(bf16)
    carried = mm(readers, state) + mm(readers, (carry[...]-state.astype(f32)).astype(bf16))
    power = jnp.zeros((CHUNK, LANES), f32)
    cross = jnp.zeros((CHUNK, LANES), f32)
    for j in range(PAIRS):
        at = slice(j * LANES, (j + 1) * LANES)
        values = first_ref[:, at].astype(f32)
        gates = second_ref[:, at].astype(f32)
        y = within_ref[:, at] + spread_pair(sm, ECUM, j) * carried[:, at]
        ys[:, at] = y
        mixed = y + skip_ref[0:1, at] * values
        gated = mixed * (gates / (1.0 + jnp.exp(-gates)))
        gated_s[:, at] = gated
        grad = second_ref[:, WIDTH + j * LANES : WIDTH + (j + 1) * LANES].astype(f32)
        power = power + gated * gated
        cross = cross + grad * gain_ref[0:1, at] * gated
    inverse = lax.rsqrt(jnp.sum(power, axis=1, keepdims=True) * (1.0 / WIDTH) + epsilon)
    pull = inverse * inverse * inverse * (jnp.sum(cross, axis=1, keepdims=True) * (1.0 / WIDTH))
    for j in range(PAIRS):
        at = slice(j * LANES, (j + 1) * LANES)
        values = first_ref[:, at].astype(f32)
        gates = second_ref[:, at].astype(f32)
        grad = second_ref[:, WIDTH + j * LANES : WIDTH + (j + 1) * LANES].astype(f32)
        y = ys[:, at]
        gated = gated_s[:, at]
        mixed = y + skip_ref[0:1, at] * values
        sig = 1.0 / (1.0 + jnp.exp(-gates))
        scaled = inverse * grad
        gain_sum[0:1, at] += jnp.sum(scaled * gated, axis=0, keepdims=True)
        d_gated = scaled * gain_ref[0:1, at] - pull * gated
        silu = gates * sig
        d_mixed = d_gated * silu
        gate_ref[:, at] = (d_gated * mixed * (sig + silu * (1.0 - sig))).astype(bf16)
        skip_sum[0:1, at] += jnp.sum(values * d_mixed, axis=0, keepdims=True)
        rounded = d_mixed.astype(bf16)
        mixed_ref[:, at] = rounded
        rounded = rounded.astype(f32)
        product = rounded * y
        high = product.astype(bf16)
        high_s[:, at] = high
        low_s[:, at] = (product - high.astype(f32)).astype(bf16)
        wide_s[:, at] = d_mixed * spread_pair(sm, ECUM, j)
    ones = head_matrix()
    e_ref[...] = mm(high_s[...], ones) + mm(low_s[...], ones)
    outgoing = wide_s[...].astype(bf16)
    lowg = (wide_s[...] - outgoing.astype(f32)).astype(bf16)
    readers_ref[...] = mm_nt(outgoing, state)
    back = mm(readers.T, outgoing) + mm(readers.T, lowg)
    back_ref[0] = back
    back_sum[...] += pre[0:1, :] * back
    slab_ref[...] = back_sum[...].astype(bf16)
    dec = dec_ref[0, 0:1, :]
    pre[...] = pre[...] * dec
    new = dec * carry[...] + own_ref[0]
    carry[...] = new
    end_ref[0] = new

    @pl.when(c == pl.num_programs(0) - 1)
    def _():
        for j in range(PAIRS):
            param_ref[j : j + 1, :] = gain_sum[0:1, j * LANES : (j + 1) * LANES]
        skips = head_sum(jnp.broadcast_to(skip_sum[0:1, :], (8, WIDTH)), ones)
        param_ref[PAIRS:, :] = skips


def local_kernel(
    first_ref, grad_ref, sm_ref, smt_ref, readers_ref, values_out, sources_out, readers_out
):
    s = lax.broadcasted_iota(jnp.int32, (CHUNK, CHUNK), 0)
    t = lax.broadcasted_iota(jnp.int32, (CHUNK, CHUNK), 1)
    causal = t >= s
    sources = first_ref[:, B : B + STATE]
    readers = first_ref[:, C : C + STATE]
    scores = jnp.where(causal, mm_nt(sources, readers), 0.0)
    total = jnp.zeros((CHUNK, CHUNK), f32)
    for j in range(PAIRS):
        at = slice(j * LANES, (j + 1) * LANES)
        grads = split_pair(grad_ref[:, at])
        weight_grads = mm_nt(first_ref[:, at], grads)
        weights = []
        for k, h in enumerate((2 * j, 2 * j + 1)):
            there = sm_ref[:, SHIFTED * HEADS + h : SHIFTED * HEADS + h + 1]
            here = smt_ref[CUM * HEADS + h : CUM * HEADS + h + 1, :]
            decay = jnp.exp(jnp.minimum(here - there, CLAMP))
            weights.append((scores * decay).astype(bf16))
            total = total + weight_grads[:, k * CHUNK : (k + 1) * CHUNK] * decay
        values_out[:, at] = mm(jnp.concatenate(weights, axis=1), grads)
    total = jnp.where(causal, total, 0.0).astype(bf16)
    sources_out[...] = mm(total, readers)
    readers_out[...] = (mm_tn(total, sources) + readers_ref[...]).astype(bf16)


def last_kernel(
    first_ref, within_ref, sources_ref, readers_ref, grad_ref, e_ref, sm_ref, outer_ref,
    back_ref, end_ref, dec_ref, skip_ref, heads_ref, place_ref,
    out_ref, param_ref,
    carry, high_s, low_s, scaled_s, flux_s,
):
    c = pl.program_id(0)

    @pl.when(c == 0)
    def _():
        carry[...] = outer_ref[...].astype(f32)
        param_ref[...] = jnp.zeros_like(param_ref)

    sm = sm_ref[...]
    state = carry[...]
    rounded = state.astype(bf16)
    arriving = mm(first_ref[:, B : B + STATE], rounded) + mm(first_ref[:, B : B + STATE], (state - rounded.astype(f32)).astype(bf16))
    for j in range(PAIRS):
        at = slice(j * LANES, (j + 1) * LANES)
        values = first_ref[:, at].astype(f32)
        weight = spread_pair(sm, WEIGHT, j)
        grad = within_ref[:, at] + weight * arriving[:, at]
        out_ref[:, at] = (grad + skip_ref[0:1, at] * grad_ref[:, at].astype(f32)).astype(bf16)
        product = values * grad
        high = product.astype(bf16)
        high_s[:, at] = high
        low_s[:, at] = (product - high.astype(f32)).astype(bf16)
        scaled_s[:, at] = (values * weight).astype(bf16)
        flux_s[:, at] = jnp.broadcast_to(
            jnp.sum(end_ref[0, :, at].astype(f32) * state[:, at], axis=0, keepdims=True), (8, LANES)
        )
    ones = head_matrix()
    g = mm(high_s[...], ones) + mm(low_s[...], ones)
    constant = head_sum(flux_s[...], ones)[0:1, :]
    sources = sources_ref[...] + mm_nt(scaled_s[...], rounded)
    out_ref[:, B : B + STATE] = sources.astype(bf16)
    out_ref[:, C : C + STATE] = readers_ref[...]
    s = lax.broadcasted_iota(jnp.int32, (CHUNK, CHUNK), 0)
    t = lax.broadcasted_iota(jnp.int32, (CHUNK, CHUNK), 1)
    flux = constant + mm_exact(jnp.where(t >= s, 1.0, 0.0), e_ref[...] - g)
    own_heads = lax.broadcasted_iota(jnp.int32, (CHUNK, LANES), 1) < HEADS
    steps = g / jnp.where(own_heads, sm, 1.0) - jnp.exp(heads_ref[0:1, :]) * flux
    steps = steps * pltpu.roll(sm, LANES - SIG * HEADS, 1)
    steps = jnp.where(own_heads, steps, 0.0)
    out_ref[:, STEPS : STEPS + LANES] = mm(steps.astype(bf16), place_ref[...]).astype(bf16)
    logs = jnp.where(own_heads, flux * pltpu.roll(sm, LANES - RATE * HEADS, 1), 0.0)
    param_ref[0:1, :] += jnp.sum(logs, axis=0, keepdims=True)
    param_ref[1:2, :] += jnp.sum(steps, axis=0, keepdims=True)
    carry[...] = dec_ref[0, 0:1, :] * state + back_ref[0]


def call(kernel, out_shape, flops, moved, grid=None, in_specs=None, out_specs=None, scratch=()):
    extra = {}
    if grid is not None:
        extra = dict(grid=grid, in_specs=in_specs, out_specs=out_specs)
    return pl.pallas_call(
        kernel,
        out_shape=out_shape,
        scratch_shapes=list(scratch),
        compiler_params=pltpu.CompilerParams(vmem_limit_bytes=40 * 1024 * 1024),
        cost_estimate=pl.CostEstimate(flops=flops, bytes_accessed=moved, transcendentals=0),
        **extra,
    )


def shifted(array, count, by):
    pairs = [(i, i + by) for i in range(count) if 0 <= i + by < count]
    return lax.ppermute(array, "slab", pairs)


def carry_over(state, decay, first_decay, count, sign):
    window, window_decay, step = state, decay, 1
    result = result_decay = None
    while step < count:
        arrived = shifted(window, count, sign * step)
        more = 2 * step < count
        if result is None:
            result, result_decay = arrived, first_decay
            if more:
                window = (state.astype(f32) + decay[0:1] * arrived.astype(f32)).astype(bf16)
                window_decay = decay * first_decay
        else:
            if more:
                arrived_decay = shifted(window_decay, count, sign * step)
                window = (window.astype(f32) + window_decay[0:1] * arrived.astype(f32)).astype(bf16)
                window_decay = window_decay * arrived_decay
            result = result.astype(f32) + result_decay[0:1] * arrived.astype(f32)
            if more:
                result_decay = result_decay * arrived_decay
        step *= 2
    return jnp.zeros_like(state) if result is None else result


def on_device(
    slab_count, sub_count, tensor_count,
    mixer_x, gate_z, b_matrix, c_matrix, raw_steps, decay_log, skip_gain, step_bias, norm_gain, out_grad,
):
    rows = mixer_x.shape[0]
    peers = sub_count * tensor_count
    tokens = rows * peers
    chunks = tokens // CHUNK
    owners = blocks_of(sub_count, tensor_count)
    sub = lax.axis_index("sub")
    group = lax.axis_index("tensor") * sub_count + sub

    def struct(shape, kind=f32):
        return jax.ShapeDtypeStruct(shape, kind)

    def exchange(array):
        return lax.all_to_all(array, ("sub", "tensor"), split_axis=0, concat_axis=0, tiled=True)

    own_logs = lax.dynamic_slice(decay_log, (sub * HEADS,), (HEADS,))
    own_bias = lax.dynamic_slice(step_bias, (sub * HEADS,), (HEADS,))
    own_skip = lax.dynamic_slice(skip_gain, (sub * HEADS,), (HEADS,))
    own_gain = lax.dynamic_slice(norm_gain, (sub * WIDTH,), (WIDTH,)).reshape(1, WIDTH)
    repeats = LANES // HEADS
    heads = jnp.stack([jnp.tile(own_logs, repeats), jnp.tile(own_bias, repeats)])
    skip_row = jnp.repeat(own_skip, HEAD_DIM).reshape(1, WIDTH)
    from_head = lax.broadcasted_iota(jnp.int32, (LANES, LANES), 0)
    to_lane = lax.broadcasted_iota(jnp.int32, (LANES, LANES), 1)
    pick = (from_head == group * HEADS + to_lane % HEADS).astype(bf16)
    place = ((to_lane == group * HEADS + from_head) & (from_head < HEADS)).astype(bf16)

    def packed(kernel, width, *arrays):
        size = peers * rows * width * 2
        out = struct((peers, rows, width), bf16)
        return call(lambda *refs: kernel(owners, *refs), out, 0, 2 * size)(*arrays)

    first = exchange(packed(pack_first, FIRST, mixer_x, b_matrix, c_matrix, raw_steps))
    first = first.reshape(tokens, FIRST)
    second = exchange(packed(pack_second, 2 * WIDTH, gate_z, out_grad))
    second = second.reshape(tokens, 2 * WIDTH)

    def row_block(width):
        return pl.BlockSpec((CHUNK, width), lambda c: (c, 0))

    def whole(*shape):
        return pl.BlockSpec(shape, lambda c: (0,) * len(shape))

    lane_block = pl.BlockSpec((LANES, CHUNK), lambda c: (0, c))
    state_block = pl.BlockSpec((1, STATE, WIDTH), lambda c: (c, 0, 0))
    dec_block = pl.BlockSpec((1, 8, WIDTH), lambda c: (c, 0, 0))
    grid = (chunks,)
    unit = 2 * tokens * CHUNK * WIDTH

    sm, smt, own, dec, state, decay = call(
        state_kernel,
        (
            struct((tokens, LANES)), struct((LANES, tokens)), struct((chunks, STATE, WIDTH)),
            struct((chunks, 8, WIDTH)), struct((STATE, WIDTH), bf16), struct((8, WIDTH)),
        ),
        unit, tokens * WIDTH * 8, grid,
        [row_block(FIRST), whole(LANES, LANES), whole(2, LANES)],
        (
            row_block(LANES), lane_block, state_block,
            dec_block, whole(STATE, WIDTH), whole(8, WIDTH),
        ),
        [pltpu.VMEM((STATE, WIDTH), f32), pltpu.VMEM((8, LANES), f32)],
    )(first, pick, heads)

    before = shifted(decay, slab_count, 1) if slab_count > 1 else None
    after = shifted(decay, slab_count, -1) if slab_count > 1 else None
    inbound = carry_over(state, decay, before, slab_count, 1)

    within = call(
        within_kernel,
        struct((tokens, WIDTH)),
        4 * unit, tokens * WIDTH * 8, grid,
        [row_block(FIRST), row_block(LANES), lane_block],
        row_block(WIDTH),
    )(first, sm, smt)

    d_gates, d_mixed, e, back, slab_back, readers_part, ends, params = call(
        output_kernel,
        (
            struct((tokens, WIDTH), bf16), struct((tokens, WIDTH), bf16), struct((tokens, LANES)),
            struct((chunks, STATE, WIDTH)), struct((STATE, WIDTH), bf16), struct((tokens, STATE)),
            struct((chunks, STATE, WIDTH)), struct((PAIRS + 8, LANES)),
        ),
        4 * unit, tokens * WIDTH * 20, grid,
        [
            row_block(FIRST), row_block(2 * WIDTH), row_block(WIDTH), row_block(LANES),
            whole(STATE, WIDTH), state_block, dec_block, whole(1, WIDTH), whole(1, WIDTH),
        ],
        (
            row_block(WIDTH), row_block(WIDTH), row_block(LANES),
            state_block, whole(STATE, WIDTH), row_block(STATE),
            state_block, whole(PAIRS + 8, LANES),
        ),
        [
            pltpu.VMEM((STATE, WIDTH), f32), pltpu.VMEM((8, WIDTH), f32),
            pltpu.VMEM((STATE, WIDTH), f32), pltpu.VMEM((8, WIDTH), f32),
            pltpu.VMEM((8, WIDTH), f32), pltpu.VMEM((CHUNK, WIDTH), f32),
            pltpu.VMEM((CHUNK, WIDTH), f32), pltpu.VMEM((CHUNK, WIDTH), bf16),
            pltpu.VMEM((CHUNK, WIDTH), bf16), pltpu.VMEM((CHUNK, WIDTH), bf16), pltpu.VMEM((CHUNK, WIDTH), f32),
        ],
    )(first, second, within, sm, inbound, own, dec, own_gain, skip_row)

    gates_back = exchange(d_gates.reshape(peers, rows, WIDTH))

    def gathered(array):
        copies = slab_count * sub_count
        sent = jnp.broadcast_to(array[None], (copies,) + array.shape)
        got = lax.all_to_all(sent, ("slab", "sub"), split_axis=0, concat_axis=0, tiled=True)
        return jnp.sum(got.reshape((slab_count, sub_count) + array.shape), axis=0)

    outer = carry_over(slab_back, decay, after, slab_count, -1)

    d_values, d_sources, d_readers = call(
        local_kernel,
        (
            struct((tokens, WIDTH)), struct((tokens, STATE)), struct((tokens, STATE), bf16),
        ),
        8 * unit, tokens * WIDTH * 8, grid,
        [row_block(FIRST), row_block(WIDTH), row_block(LANES), lane_block, row_block(STATE)],
        (row_block(WIDTH), row_block(STATE), row_block(STATE)),
    )(first, d_mixed, sm, smt, readers_part)

    def down(spec):
        def index(c):
            return tuple(spec.index_map(chunks - 1 - c))

        return pl.BlockSpec(spec.block_shape, index)

    rows_down = lambda width: down(row_block(width))
    last, last_params = call(
        last_kernel,
        (struct((tokens, FIRST), bf16), struct((8, LANES))),
        2 * unit, tokens * WIDTH * 16, grid,
        [
            rows_down(FIRST), rows_down(WIDTH), rows_down(STATE), rows_down(STATE),
            rows_down(WIDTH), rows_down(LANES), rows_down(LANES), whole(STATE, WIDTH),
            down(state_block), down(state_block), down(dec_block), whole(1, WIDTH),
            whole(2, LANES), whole(LANES, LANES),
        ],
        (rows_down(FIRST), whole(8, LANES)),
        [
            pltpu.VMEM((STATE, WIDTH), f32), pltpu.VMEM((CHUNK, WIDTH), bf16),
            pltpu.VMEM((CHUNK, WIDTH), bf16), pltpu.VMEM((CHUNK, WIDTH), bf16),
            pltpu.VMEM((8, WIDTH), f32),
        ],
    )(
        first, d_values, d_sources, d_readers, d_mixed, e, sm, outer, back, ends, dec,
        skip_row, heads, place,
    )

    last_back = exchange(last.reshape(peers, rows, FIRST))
    grad_gates = call(
        lambda *refs: unpack_gates(owners, *refs),
        struct((rows, GROUPS * WIDTH), bf16), 0, 4 * rows * GROUPS * WIDTH,
    )(gates_back)
    grad_x, grad_b, grad_c, grad_steps = call(
        lambda *refs: unpack_last(owners, *refs),
        (
            struct((rows, GROUPS * WIDTH), bf16), struct((rows, GROUPS * STATE), bf16),
            struct((rows, GROUPS * STATE), bf16), struct((rows, MIXER_HEADS), bf16),
        ),
        0, 4 * rows * GROUPS * FIRST,
    )(last_back)
    early = gathered(params)
    late = gathered(last_params)
    return (
        grad_x,
        grad_gates,
        grad_b,
        grad_c,
        grad_steps,
        late[:, 0, :HEADS].reshape(-1),
        early[:, PAIRS, :HEADS].reshape(-1),
        late[:, 1, :HEADS].reshape(-1),
        early[:, :PAIRS].reshape(-1),
    )


def solution(mesh):
    tensor_count = mesh.shape["tensor"]
    sub_count = GROUPS // tensor_count
    slab_count = mesh.shape["dp"] // sub_count
    devices = mesh.devices.reshape(slab_count, sub_count, tensor_count)
    split_mesh = Mesh(devices, ("slab", "sub", "tensor"))
    rows = P(("slab", "sub", "tensor"), None)
    param = P("tensor")

    def local(*arrays):
        return on_device(slab_count, sub_count, tensor_count, *arrays)

    return jax.shard_map(
        local,
        mesh=split_mesh,
        in_specs=(rows,) * 5 + (param,) * 4 + (rows,),
        out_specs=(rows,) * 5 + (param,) * 4,
        check_vma=False,
    )
```

time: 659 us -> 179 us (0.27); the launches traced: 650 us -> 178 us
  waiting for transfers between devices: 245 us -> 45.9 us
  other arithmetic: 118 us -> 4.49 us
  local copies, waits for them, and re-layouts: 98.3 us -> 33.1 us
  blocking collectives: 83.3 us -> 29.5 us
  matrix products: 48.3 us -> 0 us
  Pallas kernels: 0 us -> 26.7 us
  between operations: 14.9 us -> 1.06 us
    all_gather x2 -> x0, waiting for transfers between devices: 222 us -> none  [prefix(): everything = jax.tree.map(lambda part: lax.all_gather(part, axis), array)]
    select_n x32 -> x0, other arithmetic: 94.6 us -> none  [step(): return jax.tree.map(lambda a, b: jnp.where(reached, a, b), new, before)]
    psum x1 -> x0, blocking collectives: 59.4 us -> none  [reduce_weights(): return lax.psum((terms[0], terms[1], terms[2], terms[3]), 'dp')]
    dot_general x12 -> x0, matrix products: 48.3 us -> none  [the longest x3 20.4 us: block_output(): jnp.einsum('gkts,sgkp->tgkp', weights, value_rows, precision=precise)]
    all_to_all x18 -> x0, local copies, waits for them, and re-layouts: 33.8 us -> none  [the longest x3 12.8 us: send_back(): lax.all_to_all(grads[1], 'tensor', split_axis=0, concat_axis=1, tiled=True)]
    all_to_all x0 -> x2, blocking collectives: none -> 29.5 us  [the longest x1 17.4 us: exchange(): lax.all_to_all(array, ('sub', 'tensor'), split_axis=0, concat_axis=0, til...]
    pallas_call x0 -> x9, Pallas kernels: none -> 26.7 us  [the longest x1 8.49 us: on_device(): call(output_kernel, (struct((tokens, WIDTH), bf16), struct((tokens, WIDTH...]
    all_gather x1 -> x0, blocking collectives: 23.9 us -> none  [prefix(): everything = jax.tree.map(lambda part: lax.all_gather(part, axis), array)]
  transfers between devices with their start and end apart: 13 -> 10, of which waited for: 8 -> 5; matrix products, arithmetic and copies ran while one was open for 30% -> 6% of each run, Pallas kernels for 0% -> 9%
where the time goes in v1:
time: 179 us; the launch traced here: 178 us
  waiting for transfers between devices  45.9 us (26%)
  starting transfers between devices  37.4 us (21%)
  local copies, waits for them, and re-layouts  33.1 us (18%)
  blocking collectives  29.5 us (16%)
  Pallas kernels  26.7 us (15%)
  other arithmetic  4.49 us (3%)
    all_to_all x3, waiting for transfers between devices, exchange(): lax.all_to_all(array, ('sub', 'tensor'), split_axis=0, concat_axis=0, til...  32.3 us
    unnamed x88, local copies, waits for them, and re-layouts  26.8 us
    all_to_all x1, blocking collectives, exchange(): lax.all_to_all(array, ('sub', 'tensor'), split_axis=0, concat_axis=0, til...  17.4 us
    ppermute x6, starting transfers between devices, shifted(): return lax.ppermute(array, 'slab', pairs)  17.1 us
    ppermute x6, waiting for transfers between devices, shifted(): return lax.ppermute(array, 'slab', pairs)  13.6 us
    all_to_all x3, starting transfers between devices, exchange(): lax.all_to_all(array, ('sub', 'tensor'), split_axis=0, concat_axis=0, til...  12.6 us
    all_to_all x1, blocking collectives, gathered(): lax.all_to_all(sent, ('slab', 'sub'), split_axis=0, concat_axis=0, tiled=...  12.1 us
    pallas_call x1, Pallas kernels, on_device(): call(output_kernel, (struct((tokens, WIDTH), bf16), struct((tokens, WIDTH...  8.49 us
  transfers between devices with their start and end apart: 10, of which 5 were waited for; matrix products, arithmetic and copies ran while one was open for 6% of the time, Pallas kernels for 9%

profile of v1, /device:TPU:0, one launch (start us, length us, event | category | flops | bytes accessed | tf_op | source)
XLA Modules:
  0.0 178.0 jit_solution(4910930848032542147)
XLA Ops:
  5.7 5.3 %all-to-all-start = ((bf16[8,64,1408]{2,1,0:T(8,128)(2,1)}), bf16[8,64,1408]{2,1,0:T(8,128)(2,1)S(1)}, u32[]{:S(2)}, u32[]{:S(2)}) async-start(bf16[8,64,1408]{2,1,0:T(8,128)(2,1)} %shard_map.169), calls=%async_computation | async-start | bytes 2883584 | tf_op jit(solution)/shard_map/all_to_all | solution.py:399
  11.1 1.3 copy-done.2
  12.5 17.6 %all-to-all-done = bf16[8,64,1408]{2,1,0:T(8,128)(2,1)S(1)} async-done(((bf16[8,64,1408]{2,1,0:T(8,128)(2,1)}), bf16[8,64,1408]{2,1,0:T(8,128)(2,1)S(1)}, u32[]{:S(2)}, u32[]{:S(2)}) %all-to-all-start) | async-done | bytes 1441824 | tf_op jit(solution)/shard_map/all_to_all | solution.py:399
  30.1 3.6 %all-to-all-start.1 = ((bf16[8,64,2048]{2,1,0:T(8,128)(2,1)}), bf16[8,64,2048]{2,1,0:T(8,128)(2,1)S(1)}, u32[]{:S(2)}, u32[]{:S(2)}) async-start(bf16[8,64,2048]{2,1,0:T(8,128)(2,1)} %copy-done.2), calls=%async_computation.1 | async-start | bytes 4194304 | tf_op jit(solution)/shard_map/all_to_all | solution.py:399
  34.1 4.6 %shard_map.171 = (f32[512,128]{1,0:T(8,128)S(1)}, f32[128,512]{1,0:T(8,128)S(1)}, f32[4,128,1024]{2,1,0:T(8,128)S(1)}, f32[4,8,1024]{2,1,0:T(8,128)S(1)}, bf16[1...) custom-call(bf16[512,1408]{1,0:T(8,128)(2,1)S(1)} %bitcast.12, bf16[128,128]{1,0:T(8,128)(2,1)S(1)} %fusion.4.pick_ref, ...), custom_call_target="tpu_custom_call" | custom-call | flops 134217728 | bytes 4194304 | tf_op jit(solution)/shard_map/pallas_call | solution.py:435
  42.2 3.5 %collective-permute-start = (bf16[128,1024]{1,0:T(8,128)(2,1)S(1)}, bf16[128,1024]{1,0:T(8,128)(2,1)S(1)}, u32[]{:S(2)}, u32[]{:S(2)}) collective-permute-start(bf16[128,1024]{1,0:T(8,128)(2,1)S(1)} %get-tuple-element.34), channel_id=1, source_target_pairs={{0,8},{8,16},{16,24},{1,9},{9,17},{17,25},{2,10},{10,18},{18,26},{... | collective-permute-start | bytes 786440 | tf_op jit(solution)/shard_map/ppermute | solution.py:357
  45.7 6.0 %collective-permute-done = bf16[128,1024]{1,0:T(8,128)(2,1)S(1)} collective-permute-done((bf16[128,1024]{1,0:T(8,128)(2,1)S(1)}, bf16[128,1024]{1,0:T(8,128)(2,1)S(1)}, u32[]{:S(2)}, u32[]{:S(2)}) %collective-permute-start) | collective-permute-done | bytes 262176 | tf_op jit(solution)/shard_map/ppermute | solution.py:357
  52.5 6.1 %collective-permute-start.2 = (bf16[128,1024]{1,0:T(8,128)(2,1)}, bf16[128,1024]{1,0:T(8,128)(2,1)}, u32[]{:S(2)}, u32[]{:S(2)}) collective-permute-start(bf16[128,1024]{1,0:T(8,128)(2,1)} %fusion.1), channel_id=1, source_target_pairs={{0,16},{8,24},{1,17},{9,25},{2,18},{10,26},{3,19},{11,27},{4,20},{... | collective-permute-start | bytes 786440 | tf_op jit(solution)/shard_map/ppermute | solution.py:357
  61.5 3.5 %collective-permute-start.1 = (f32[8,1024]{1,0:T(8,128)}, f32[8,1024]{1,0:T(8,128)S(1)}, u32[]{:S(2)}, u32[]{:S(2)}) collective-permute-start(f32[8,1024]{1,0:T(8,128)} %copy-done.35), channel_id=1, source_target_pairs={{0,8},{8,16},{16,24},{1,9},{9,17},{17,25},{2,10},{10,18},{18,26},{... | collective-permute-start | bytes 98312 | tf_op jit(solution)/shard_map/ppermute | solution.py:357
  66.9 2.3 %shard_map.172.within_ref = f32[512,1024]{1,0:T(8,128)S(1)} custom-call(bf16[512,1408]{1,0:T(8,128)(2,1)S(1)} %bitcast.13, f32[512,128]{1,0:T(8,128)S(1)} %copy-done.4, f32[128,512]{1,0:T(8,128)S(1)} %copy-done.27), custom_call_target="tpu_custom_call" | custom-call | flops 536870912 | bytes 4194304 | tf_op jit(solution)/shard_map/pallas_call | solution.py:454
  69.2 1.3 copy-done
  70.6 1.8 %convert_add_fusion.1.inbound_ref = f32[128,1024]{1,0:T(8,128)} fusion(bf16[128,1024]{1,0:T(8,128)(2,1)S(1)} %copy-done.40, bf16[128,1024]{1,0:T(8,128)(2,1)} %collective-permute-done.2, f32[1024]{0:T(1024)S(1)} %bitcast.25), kind=kLoop, calls=%fused_computation.2 | loop fusion | flops 524288 | bytes 1052672 | tf_op jit(solution)/shard_map/add | solution.py:376
  72.4 1.6 copy-done.1
  76.9 8.5 %shard_map.173 = (bf16[512,1024]{1,0:T(8,128)(2,1)S(1)}, bf16[512,1024]{1,0:T(8,128)(2,1)S(1)}, f32[512,128]{1,0:T(8,128)S(1)}, f32[4,128,1024]{2,1,0:T(8,128)S(...) custom-call(bf16[512,1408]{1,0:T(8,128)(2,1)S(1)} %bitcast.14, ...), custom_call_target="tpu_custom_call" | custom-call | flops 536870912 | bytes 10485760 | tf_op jit(solution)/shard_map/pallas_call | solution.py:462
  85.4 1.3 copy-done.9
  93.4 6.8 %collective-permute-done.3 = bf16[128,1024]{1,0:T(8,128)(2,1)S(1)} collective-permute-done((bf16[128,1024]{1,0:T(8,128)(2,1)S(1)}, bf16[128,1024]{1,0:T(8,128)(2,1)S(1)}, u32[]{:S(2)}, u32[]{:S(2)}) %collective-permute-start.3) | collective-permute-done | bytes 262176 | tf_op jit(solution)/shard_map/ppermute | solution.py:357
  100.3 1.4 collective-permute-start.5
  103.1 7.7 %all-to-all-start.5 = ((f32[16,16,128]{2,1,0:T(8,128)}), f32[16,16,128]{2,1,0:T(8,128)}, u32[]{:S(2)}, u32[]{:S(2)}) async-start(f32[16,16,128]{2,1,0:T(8,128)} %broadcast_in_dim.8), calls=%async_computation.5 | async-start | bytes 262144 | tf_op jit(solution)/shard_map/all_to_all | solution.py:493
  114.9 2.6 %shard_map.174 = (f32[512,1024]{1,0:T(8,128)S(1)}, f32[512,128]{1,0:T(8,128)S(1)}, bf16[512,128]{1,0:T(8,128)(2,1)S(1)}) custom-call(bf16[512,1408]{1,0:T(8,128)(2,1)S(1)} %bitcast.15, bf16[512,1024]{1,0:T(8,128)(2,1)S(1)} %copy-done.16, f32[512,128]{1,0:T(8,128)S(1)} %copy-done.6, f32[128,512]{1,0:T(8,128)S(1)} %copy-done.28, f32[512,128]{1,0:T(8,128)S(1)} %copy-done.38), custom_call_target="tpu_custom_call" | custom-call | flops 1073741824 | bytes 4194304 | tf_op jit(solution)/shard_map/pallas_call | solution.py:498
  118.4 5.0 %shard_map.175 = (bf16[512,1408]{1,0:T(8,128)(2,1)S(1)}, f32[8,128]{1,0:T(8,128)S(1)}) custom-call(bf16[512,1408]{1,0:T(8,128)(2,1)S(1)} %bitcast.16, f32[512,1024]{1,0:T(8,128)S(1)} %get-tuple-element.40.within_ref, f32[512,128]{1,0:T(8,128)S(1)} %get-tuple-element.41.sources_ref, bf16[512,128]{1,0:T(8,128)(2,1)S(1)} %get-tuple-element.42.readers_ref, ...), custom_call_target="tpu_custom_call" | custom-call | flops 268435456 | bytes 8388608 | tf_op jit(solution)/shard_map/pallas_call | solution.py:515
  124.6 12.1 %all_to_all.30 = f32[16,8,128]{2,1,0:T(8,128)} all-to-all(f32[16,8,128]{2,1,0:T(8,128)S(1)} %broadcast_in_dim.7), channel_id=1, replica_groups=mesh['slab'=4,'sub'=4,'tensor'=2] {'slab','sub'}, dimensions={0} | all-to-all | bytes 131072 | tf_op jit(solution)/shard_map/all_to_all | solution.py:493
  136.6 17.4 %all_to_all.31.refs_0_ = bf16[8,64,1024]{2,1,0:T(8,128)(2,1)S(1)} all-to-all(bf16[8,64,1024]{2,1,0:T(8,128)(2,1)S(1)} %bitcast.19), channel_id=1, replica_groups=mesh['slab'=4,'sub'=4,'tensor'=2] {'sub','tensor'}, dimensions={0} | all-to-all | bytes 2097152 | tf_op jit(solution)/shard_map/all_to_all | solution.py:399
  154.0 3.7 %all-to-all-start.2 = ((bf16[8,64,1408]{2,1,0:T(8,128)(2,1)}), bf16[8,64,1408]{2,1,0:T(8,128)(2,1)S(1)}, u32[]{:S(2)}, u32[]{:S(2)}) async-start(bf16[8,64,1408]{2,1,0:T(8,128)(2,1)} %bitcast.18), calls=%async_computation.2 | async-start | bytes 2883584 | tf_op jit(solution)/shard_map/all_to_all | solution.py:399
  162.2 14.7 %all-to-all-done.2.refs_0_ = bf16[8,64,1408]{2,1,0:T(8,128)(2,1)S(1)} async-done(((bf16[8,64,1408]{2,1,0:T(8,128)(2,1)}), bf16[8,64,1408]{2,1,0:T(8,128)(2,1)S(1)}, u32[]{:S(2)}, u32[]{:S(2)}) %all-to-all-start.2) | async-done | bytes 1441824 | tf_op jit(solution)/shard_map/all_to_all | solution.py:399
  (129 shorter events, 37.0 us)
Async XLA Ops:
  5.6 5.3 %copy-start.21 = (bf16[64,8192]{1,0:T(8,128)(2,1)S(1)}, bf16[64,8192]{1,0:T(8,128)(2,1)}, u32[]{:S(2)}) copy-start(bf16[64,8192]{1,0:T(8,128)(2,1)} %refs_0_.3) | copy-start | bytes 3145732
  5.6 5.3 %copy-start.22 = (bf16[64,8192]{1,0:T(8,128)(2,1)S(1)}, bf16[64,8192]{1,0:T(8,128)(2,1)}, u32[]{:S(2)}) copy-start(bf16[64,8192]{1,0:T(8,128)(2,1)} %refs_1_.3) | copy-start | bytes 3145732
  5.7 24.4 %all-to-all-start = ((bf16[8,64,1408]{2,1,0:T(8,128)(2,1)}), bf16[8,64,1408]{2,1,0:T(8,128)(2,1)S(1)}, u32[]{:S(2)}, u32[]{:S(2)}) async-start(bf16[8,64,1408]{2,1,0:T(8,128)(2,1)} %shard_map.169), calls=%async_computation | async-start | bytes 2883584 | tf_op jit(solution)/shard_map/all_to_all | solution.py:399
  12.5 21.3 %copy-start.42 = (f32[64]{0:T(128)S(1)}, f32[64]{0:T(128)}, u32[]{:S(2)}) copy-start(f32[64]{0:T(128)} %param.15) | copy-start | bytes 772
  12.5 21.4 %copy-start.43 = (f32[64]{0:T(128)S(1)}, f32[64]{0:T(128)}, u32[]{:S(2)}) copy-start(f32[64]{0:T(128)} %param.17) | copy-start | bytes 772
  30.1 42.3 %all-to-all-start.1 = ((bf16[8,64,2048]{2,1,0:T(8,128)(2,1)}), bf16[8,64,2048]{2,1,0:T(8,128)(2,1)S(1)}, u32[]{:S(2)}, u32[]{:S(2)}) async-start(bf16[8,64,2048]{2,1,0:T(8,128)(2,1)} %copy-done.2), calls=%async_computation.1 | async-start | bytes 4194304 | tf_op jit(solution)/shard_map/all_to_all | solution.py:399
  42.2 17.2 %copy-start.35 = (f32[8,1024]{1,0:T(8,128)}, f32[8,1024]{1,0:T(8,128)S(1)}, u32[]{:S(2)}) copy-start(f32[8,1024]{1,0:T(8,128)S(1)} %get-tuple-element.35) | copy-start | bytes 98308
  42.2 9.6 %collective-permute-start = (bf16[128,1024]{1,0:T(8,128)(2,1)S(1)}, bf16[128,1024]{1,0:T(8,128)(2,1)S(1)}, u32[]{:S(2)}, u32[]{:S(2)}) collective-permute-start(bf16[128,1024]{1,0:T(8,128)(2,1)S(1)} %get-tuple-element.34), channel_id=1, source_target_pairs={{0,8},{8,16},{16,24},{1,9},{9,17},{17,25},{2,10},{10,18},{18,26},{... | collective-permute-start | bytes 786440 | tf_op jit(solution)/shard_map/ppermute | solution.py:357
  51.7 7.6 %copy-start.39 = (bf16[128,1024]{1,0:T(8,128)(2,1)}, bf16[128,1024]{1,0:T(8,128)(2,1)S(1)}, u32[]{:S(2)}) copy-start(bf16[128,1024]{1,0:T(8,128)(2,1)S(1)} %collective-permute-done) | copy-start | bytes 786436
  52.5 18.0 %collective-permute-start.2 = (bf16[128,1024]{1,0:T(8,128)(2,1)}, bf16[128,1024]{1,0:T(8,128)(2,1)}, u32[]{:S(2)}, u32[]{:S(2)}) collective-permute-start(bf16[128,1024]{1,0:T(8,128)(2,1)} %fusion.1), channel_id=1, source_target_pairs={{0,16},{8,24},{1,17},{9,25},{2,18},{10,26},{3,19},{11,27},{4,20},{... | collective-permute-start | bytes 786440 | tf_op jit(solution)/shard_map/ppermute | solution.py:357
  61.5 9.1 %collective-permute-start.1 = (f32[8,1024]{1,0:T(8,128)}, f32[8,1024]{1,0:T(8,128)S(1)}, u32[]{:S(2)}, u32[]{:S(2)}) collective-permute-start(f32[8,1024]{1,0:T(8,128)} %copy-done.35), channel_id=1, source_target_pairs={{0,8},{8,16},{16,24},{1,9},{9,17},{17,25},{2,10},{10,18},{18,26},{... | collective-permute-start | bytes 98312 | tf_op jit(solution)/shard_map/ppermute | solution.py:357
  66.9 3.7 %copy-start.40 = (bf16[128,1024]{1,0:T(8,128)(2,1)S(1)}, bf16[128,1024]{1,0:T(8,128)(2,1)}, u32[]{:S(2)}) copy-start(bf16[128,1024]{1,0:T(8,128)(2,1)} %copy-done.39) | copy-start | bytes 786436
  76.9 15.1 %copy-start.36 = (f32[8,1024]{1,0:T(8,128)S(1)}, f32[8,1024]{1,0:T(8,128)}, u32[]{:S(2)}) copy-start(f32[8,1024]{1,0:T(8,128)} %copy-done.35) | copy-start | bytes 98308
  90.8 11.7 %copy-start.37 = (f32[512,128]{1,0:T(8,128)}, f32[512,128]{1,0:T(8,128)S(1)}, u32[]{:S(2)}) copy-start(f32[512,128]{1,0:T(8,128)S(1)} %get-tuple-element.39.readers_ref) | copy-start | bytes 786436
  90.8 9.4 %collective-permute-start.3 = (bf16[128,1024]{1,0:T(8,128)(2,1)S(1)}, bf16[128,1024]{1,0:T(8,128)(2,1)S(1)}, u32[]{:S(2)}, u32[]{:S(2)}) collective-permute-start(bf16[128,1024]{1,0:T(8,128)(2,1)S(1)} %get-tuple-element.44), channel_id=1, source_target_pairs={{8,0},{16,8},{24,16},{9,1},{17,9},{25,17},{10,2},{18,10},{26,18},{... | collective-permute-start | bytes 786440 | tf_op jit(solution)/shard_map/ppermute | solution.py:357
  92.1 10.4 %collective-permute-start.4 = (f32[8,1024]{1,0:T(8,128)S(1)}, f32[8,1024]{1,0:T(8,128)S(1)}, u32[]{:S(2)}, u32[]{:S(2)}) collective-permute-start(f32[8,1024]{1,0:T(8,128)S(1)} %copy-done.36), channel_id=1, source_target_pairs={{8,0},{16,8},{24,16},{9,1},{17,9},{25,17},{10,2},{18,10},{26,18},{... | collective-permute-start | bytes 98312 | tf_op jit(solution)/shard_map/ppermute | solution.py:357
  100.2 18.1 %copy-start.17 = (bf16[512,1024]{1,0:T(8,128)(2,1)S(1)}, bf16[512,1024]{1,0:T(8,128)(2,1)}, u32[]{:S(2)}) copy-start(bf16[512,1024]{1,0:T(8,128)(2,1)} %copy-done.15) | copy-start | bytes 3145732
  100.3 18.0 %collective-permute-start.5 = (bf16[128,1024]{1,0:T(8,128)(2,1)S(1)}, bf16[128,1024]{1,0:T(8,128)(2,1)S(1)}, u32[]{:S(2)}, u32[]{:S(2)}) collective-permute-start(bf16[128,1024]{1,0:T(8,128)(2,1)S(1)} %fusion.3), channel_id=1, source_target_pairs={{16,0},{24,8},{17,1},{25,9},{18,2},{26,10},{19,3},{27,11},{20,4},{... | collective-permute-start | bytes 786440 | tf_op jit(solution)/shard_map/ppermute | solution.py:357
  103.1 21.4 %all-to-all-start.5 = ((f32[16,16,128]{2,1,0:T(8,128)}), f32[16,16,128]{2,1,0:T(8,128)}, u32[]{:S(2)}, u32[]{:S(2)}) async-start(f32[16,16,128]{2,1,0:T(8,128)} %broadcast_in_dim.8), calls=%async_computation.5 | async-start | bytes 262144 | tf_op jit(solution)/shard_map/all_to_all | solution.py:493
  114.9 3.5 %copy-start.30 = (f32[512,128]{1,0:T(8,128)S(1)}, f32[512,128]{1,0:T(8,128)}, u32[]{:S(2)}) copy-start(f32[512,128]{1,0:T(8,128)} %copy-done.29) | copy-start | bytes 786436
  114.9 3.5 %copy-start.31 = (bf16[128,128]{1,0:T(8,128)(2,1)S(1)}, bf16[128,128]{1,0:T(8,128)(2,1)}, u32[]{:S(2)}) copy-start(bf16[128,128]{1,0:T(8,128)(2,1)} %fusion.6.place_ref) | copy-start | bytes 98308
  118.4 18.2 %copy-start.20 = (bf16[512,1024]{1,0:T(8,128)(2,1)S(1)}, bf16[512,1024]{1,0:T(8,128)(2,1)}, u32[]{:S(2)}) copy-start(bf16[512,1024]{1,0:T(8,128)(2,1)} %copy-done.19) | copy-start | bytes 3145732
  154.0 5.9 %copy-start.41 = (f32[16,8,128]{2,1,0:T(8,128)S(1)}, f32[16,8,128]{2,1,0:T(8,128)}, u32[]{:S(2)}) copy-start(f32[16,8,128]{2,1,0:T(8,128)} %all_to_all.30) | copy-start | bytes 196612
  154.0 22.8 %all-to-all-start.2 = ((bf16[8,64,1408]{2,1,0:T(8,128)(2,1)}), bf16[8,64,1408]{2,1,0:T(8,128)(2,1)S(1)}, u32[]{:S(2)}, u32[]{:S(2)}) async-start(bf16[8,64,1408]{2,1,0:T(8,128)(2,1)} %bitcast.18), calls=%async_computation.2 | async-start | bytes 2883584 | tf_op jit(solution)/shard_map/all_to_all | solution.py:399
  (30 other events, 40.8 us)

commit v2 on v1

v2 whole, which is shorter than its diff:
```python
import jax
import jax.numpy as jnp
from jax import lax
from jax.experimental import pallas as pl
from jax.experimental.pallas import tpu as pltpu
from jax.sharding import Mesh
from jax.sharding import PartitionSpec as P

MIXER_HEADS = 128
HEAD_DIM = 64
STATE = 128
GROUPS = 8
CHANNELS = MIXER_HEADS * HEAD_DIM
HEADS = 8
WIDTH = HEADS * HEAD_DIM
GROUP_WIDTH = 2 * WIDTH
OWNERS = MIXER_HEADS // HEADS
LANES = 128
PAIRS = WIDTH // LANES
CHUNK = 128
STEP_ROWS = 16
epsilon = 1e-05
f32 = jnp.float32
bf16 = jnp.bfloat16

DT, CUM, WEIGHT, SHIFTED, ECUM, RATE, SIG = range(7)
KINDS = 8
CLAMP = 80.0


def mm(a, b):
    return jnp.dot(a, b, preferred_element_type=f32)


def mm_nt(a, b):
    return lax.dot_general(a, b, (((1,), (1,)), ((), ())), preferred_element_type=f32)


def mm_tn(a, b):
    return lax.dot_general(a, b, (((0,), (0,)), ((), ())), preferred_element_type=f32)


def mm_exact(a, b):
    return jnp.dot(a, b, precision=lax.Precision.HIGHEST, preferred_element_type=f32)


def two_terms(values):
    high = values.astype(bf16)
    return high, (values - high.astype(f32)).astype(bf16)


def mm_two(a, high, low):
    both = mm(a, jnp.concatenate([high, low], axis=1))
    width = high.shape[1]
    return both[:, :width] + both[:, width:]


def low_half(rows):
    return lax.broadcasted_iota(jnp.int32, (rows, LANES), 1) < HEAD_DIM


def spread_pair(values, kind, j):
    rows = values.shape[0]
    at = kind * HEADS + 2 * j
    return jnp.where(
        low_half(rows),
        jnp.broadcast_to(values[:, at : at + 1], (rows, LANES)),
        jnp.broadcast_to(values[:, at + 1 : at + 2], (rows, LANES)),
    )


def head_rows():
    row = lax.broadcasted_iota(jnp.int32, (16, WIDTH), 0)
    channel = lax.broadcasted_iota(jnp.int32, (16, WIDTH), 1) // HEAD_DIM
    return jnp.where(row == channel, 1.0, 0.0).astype(bf16)


def split_pair(block):
    low = low_half(block.shape[0])
    zero = jnp.zeros_like(block)
    return jnp.concatenate(
        [jnp.where(low, block, zero), jnp.where(low, zero, block)], axis=0
    )


def lanes(j):
    return slice(j * LANES, (j + 1) * LANES)


class Message:
    def __init__(self, rows):
        self.rows = rows
        self.per_chunk = CHUNK // rows

    def place(self, chunk, k):
        r = self.rows
        return (slice(chunk * self.per_chunk, (chunk + 1) * self.per_chunk), slice(k * r, (k + 1) * r))

    def get(self, ref, chunk, k):
        a, b = self.place(chunk, k)
        return ref[a, b, :].reshape(CHUNK, LANES)

    def put(self, ref, chunk, k, value):
        a, b = self.place(chunk, k)
        ref[a, b, :] = value.reshape(self.per_chunk, self.rows, LANES)


X, B = 0, PAIRS
FIRST = PAIRS + 1
Z, GRAD, C = 0, PAIRS, 2 * PAIRS
SECOND = 2 * PAIRS + 1
LAST_X, LAST_B, LAST_C = 0, PAIRS, PAIRS + 1
LAST = PAIRS + 2


def pack_first(owners, x_ref, b_ref, steps_ref, out_ref):
    r = x_ref.shape[0]
    steps = steps_ref[...].astype(f32)
    padded = jnp.concatenate([steps, jnp.zeros((LANES - r, LANES), f32)], axis=0)
    by_head = padded.T
    zero = jnp.zeros((STEP_ROWS - HEADS, LANES), f32)
    for peer, own in enumerate(owners):
        for j in range(PAIRS):
            out_ref[peer, j * r : (j + 1) * r, :] = x_ref[:, lanes(own * PAIRS + j)]
        out_ref[peer, B * r : (B + 1) * r, :] = b_ref[:, lanes(own // 2)]
        mine = jnp.concatenate([by_head[own * HEADS : (own + 1) * HEADS, :], zero], axis=0)
        out_ref[peer, FIRST * r :, :] = mine.astype(bf16)


def pack_second(owners, z_ref, grad_ref, c_ref, out_ref):
    r = z_ref.shape[0]
    for peer, own in enumerate(owners):
        for j in range(PAIRS):
            out_ref[peer, (Z + j) * r : (Z + j + 1) * r, :] = z_ref[:, lanes(own * PAIRS + j)]
            out_ref[peer, (GRAD + j) * r : (GRAD + j + 1) * r, :] = grad_ref[:, lanes(own * PAIRS + j)]
        out_ref[peer, C * r : (C + 1) * r, :] = c_ref[:, lanes(own // 2)]


def unpack_gates(owners, in_ref, out_ref):
    r = out_ref.shape[0]
    for peer, own in enumerate(owners):
        for j in range(PAIRS):
            out_ref[:, lanes(own * PAIRS + j)] = in_ref[peer, j * r : (j + 1) * r, :]


def unpack_last(owners, in_ref, x_ref, b_ref, c_ref, steps_ref):
    r = x_ref.shape[0]
    peer_of = {own: peer for peer, own in enumerate(owners)}
    for peer, own in enumerate(owners):
        for j in range(PAIRS):
            x_ref[:, lanes(own * PAIRS + j)] = in_ref[peer, j * r : (j + 1) * r, :]
    for g in range(GROUPS):
        for block, ref in ((LAST_B, b_ref), (LAST_C, c_ref)):
            at = slice(block * r, (block + 1) * r)
            halves = [in_ref[peer_of[2 * g + k], at, :].astype(f32) for k in range(2)]
            ref[:, lanes(g)] = (halves[0] + halves[1]).astype(bf16)
    by_head = jnp.concatenate(
        [in_ref[peer_of[own], LAST * r :, :].astype(f32)[:HEADS] for own in range(OWNERS)], axis=0
    )
    steps_ref[...] = by_head.T[:r, :].astype(bf16)


def state_kernel(
    message, per_step,
    first_ref, heads_ref, sm_ref, smt_ref, own_ref, dec_ref, state_ref, whole_ref,
    carry,
):
    @pl.when(pl.program_id(0) == 0)
    def _():
        carry[...] = jnp.zeros_like(carry)
        whole_ref[...] = jnp.ones_like(whole_ref)

    r = message.rows
    before = lax.broadcasted_iota(jnp.int32, (CHUNK, CHUNK), 0)
    after = lax.broadcasted_iota(jnp.int32, (CHUNK, CHUNK), 1)
    up_to = jnp.where(before <= after, 1.0, 0.0)
    beyond = jnp.where(before > after, 1.0, 0.0)
    for i in range(per_step):
        raw = None
        for p in range(message.per_chunk):
            part = first_ref[i * message.per_chunk + p, FIRST * r :, :].astype(f32)[:HEADS]
            part = part if p == 0 else pltpu.roll(part, p * r, 1)
            raw = part if raw is None else raw + part
        raw = raw + heads_ref[HEADS:, :]
        small = jnp.exp(-jnp.abs(raw))
        series = small * (
            1.0 - small * (0.5 - small * (1.0 / 3 - small * (0.25 - small * 0.2)))
        )
        soft = jnp.maximum(raw, 0.0) + jnp.where(small < 0.015625, series, jnp.log(1.0 + small))
        sig = jnp.where(raw >= 0.0, 1.0, small) / (1.0 + small)
        rate = -jnp.exp(heads_ref[:HEADS, :]) * soft
        cum = mm_exact(rate, up_to)
        rest = mm_exact(rate, beyond)
        rows = jnp.concatenate(
            [
                soft, cum, soft * jnp.exp(rest), cum - jnp.log(soft), jnp.exp(cum), rate, sig,
                jnp.zeros_like(soft),
            ],
            axis=0,
        )
        smt_ref[:, lanes(i)] = rows
        sm = jnp.concatenate([rows, jnp.zeros_like(rows)], axis=0).T
        sm_ref[i * CHUNK : (i + 1) * CHUNK, :] = sm
        last = jnp.broadcast_to(sm[CHUNK - 1 : CHUNK, :], (8, LANES))
        sources_t = message.get(first_ref, i, B).T
        for j in range(PAIRS):
            dec = spread_pair(last, ECUM, j)
            dec_ref[i, :, lanes(j)] = dec
            whole_ref[:, lanes(j)] = whole_ref[:, lanes(j)] * dec
            scaled = message.get(first_ref, i, X + j).astype(f32) * spread_pair(sm, WEIGHT, j)
            own = mm_two(sources_t, *two_terms(scaled))
            own_ref[i, :, lanes(j)] = own
            carry[:, lanes(j)] = dec[0:1] * carry[:, lanes(j)] + own
    state_ref[...] = carry[...].astype(bf16)


def within_kernel(message, per_step, first_ref, second_ref, sm_ref, smt_ref, out_ref):
    t = lax.broadcasted_iota(jnp.int32, (CHUNK, CHUNK), 0)
    s = lax.broadcasted_iota(jnp.int32, (CHUNK, CHUNK), 1)
    for i in range(per_step):
        rows = slice(i * CHUNK, (i + 1) * CHUNK)
        scores = mm_nt(message.get(second_ref, i, C), message.get(first_ref, i, B))
        scores = jnp.where(t >= s, scores, 0.0)
        for j in range(PAIRS):
            weights = []
            for h in (2 * j, 2 * j + 1):
                here = sm_ref[rows, CUM * HEADS + h : CUM * HEADS + h + 1]
                there = smt_ref[SHIFTED * HEADS + h : SHIFTED * HEADS + h + 1, lanes(i)]
                weights.append(
                    (scores * jnp.exp(jnp.minimum(here - there, CLAMP))).astype(bf16)
                )
            values = split_pair(message.get(first_ref, i, X + j))
            out_ref[rows, lanes(j)] = mm(jnp.concatenate(weights, axis=1), values)


def mix_kernel(
    message, per_step,
    first_ref, second_ref, within_ref, sm_ref, inbound_ref, own_ref, dec_ref, gain_ref, skip_ref,
    y_ref, start_ref, sums_ref,
    carry,
):
    @pl.when(pl.program_id(0) == 0)
    def _():
        carry[...] = inbound_ref[...].astype(f32)

    for i in range(per_step):
        rows = slice(i * CHUNK, (i + 1) * CHUNK)
        sm = sm_ref[rows, :]
        readers = message.get(second_ref, i, C)
        power = jnp.zeros((CHUNK, LANES), f32)
        cross = jnp.zeros((CHUNK, LANES), f32)
        for j in range(PAIRS):
            state = carry[:, lanes(j)]
            start_ref[i, :, lanes(j)] = state
            carried = mm_two(readers, *two_terms(state))
            carry[:, lanes(j)] = dec_ref[i, 0:1, lanes(j)] * state + own_ref[i, :, lanes(j)]
            y = within_ref[rows, lanes(j)] + spread_pair(sm, ECUM, j) * carried
            y_ref[rows, lanes(j)] = y
            values = message.get(first_ref, i, X + j).astype(f32)
            gates = message.get(second_ref, i, Z + j).astype(f32)
            grad = message.get(second_ref, i, GRAD + j).astype(f32)
            gated = (y + skip_ref[0:1, lanes(j)] * values) * (gates / (1.0 + jnp.exp(-gates)))
            power = power + gated * gated
            cross = cross + grad * gain_ref[0:1, lanes(j)] * gated
        sums_ref[i, 0:1, :] = jnp.sum(power.T, axis=0, keepdims=True)
        sums_ref[i, 1:2, :] = jnp.sum(cross.T, axis=0, keepdims=True)
        sums_ref[i, 2:, :] = jnp.zeros((6, LANES), f32)


def norm_kernel(
    message, per_step,
    first_ref, second_ref, y_ref, sm_ref, start_ref, dec_ref, sums_ref, other_ref, gain_ref, skip_ref,
    gate_ref, mixed_ref, e_ref, back_ref, slab_ref, readers_ref, param_ref,
    pre, back_sum, gain_sum, skip_sum, high_s, low_s, scaled_s,
):
    c = pl.program_id(0)

    @pl.when(c == 0)
    def _():
        pre[...] = jnp.ones_like(pre)
        back_sum[...] = jnp.zeros_like(back_sum)
        gain_sum[...] = jnp.zeros_like(gain_sum)
        skip_sum[...] = jnp.zeros_like(skip_sum)

    ones = head_rows()
    for i in range(per_step):
        rows = slice(i * CHUNK, (i + 1) * CHUNK)
        sm = sm_ref[rows, :]
        readers = message.get(second_ref, i, C)
        readers_t = readers.T
        sums = (sums_ref[i] + other_ref[i]) * (1.0 / GROUP_WIDTH)
        inverse_row = lax.rsqrt(sums[0:1] + epsilon)
        pull_row = inverse_row * inverse_row * inverse_row * sums[1:2]
        inverse = jnp.broadcast_to(inverse_row, (CHUNK, LANES)).T
        pull = jnp.broadcast_to(pull_row, (CHUNK, LANES)).T
        for j in range(PAIRS):
            at = lanes(j)
            values = message.get(first_ref, i, X + j).astype(f32)
            gates = message.get(second_ref, i, Z + j).astype(f32)
            grad = message.get(second_ref, i, GRAD + j).astype(f32)
            y = y_ref[rows, at]
            mixed = y + skip_ref[0:1, at] * values
            sig = 1.0 / (1.0 + jnp.exp(-gates))
            silu = gates * sig
            gated = mixed * silu
            scaled = inverse * grad
            gain_sum[0:1, at] += jnp.sum(scaled * gated, axis=0, keepdims=True)
            d_gated = scaled * gain_ref[0:1, at] - pull * gated
            d_mixed = d_gated * silu
            d_gate = d_gated * mixed * (sig + silu * (1.0 - sig))
            message.put(gate_ref, i, j, d_gate.astype(bf16))
            skip_sum[0:1, at] += jnp.sum(values * d_mixed, axis=0, keepdims=True)
            rounded = d_mixed.astype(bf16)
            mixed_ref[rows, at] = rounded
            high_s[:, at], low_s[:, at] = two_terms(rounded.astype(f32) * y)
            high, low = two_terms(d_mixed * spread_pair(sm, ECUM, j))
            scaled_s[:, at] = high
            back = mm_two(readers_t, high, low)
            back_ref[i, :, at] = back
            back_sum[:, at] += pre[0:1, at] * back
            pre[:, at] = pre[:, at] * dec_ref[i, :, at]
        e_ref[:, lanes(i)] = (mm_nt(ones, high_s[...]) + mm_nt(ones, low_s[...]))[:HEADS]
        readers_ref[rows, :] = mm_nt(scaled_s[...], start_ref[i].astype(bf16))
    slab_ref[...] = back_sum[...].astype(bf16)

    @pl.when(c == pl.num_programs(0) - 1)
    def _():
        for j in range(PAIRS):
            param_ref[j : j + 1, :] = gain_sum[0:1, lanes(j)]
        high, low = two_terms(jnp.broadcast_to(skip_sum[0:1, :], (LANES, WIDTH)))
        skips = (mm_nt(high, ones) + mm_nt(low, ones))[0:1]
        param_ref[PAIRS : PAIRS + 1, :] = jnp.concatenate(
            [skips, jnp.zeros((1, LANES - 16), f32)], axis=1
        )
        param_ref[PAIRS + 1 :, :] = jnp.zeros((8 - PAIRS - 1, LANES), f32)


def local_kernel(
    message, per_step,
    first_ref, second_ref, grad_ref, sm_ref, smt_ref, readers_ref,
    values_out, sources_out, readers_out,
):
    s = lax.broadcasted_iota(jnp.int32, (CHUNK, CHUNK), 0)
    t = lax.broadcasted_iota(jnp.int32, (CHUNK, CHUNK), 1)
    causal = t >= s
    for i in range(per_step):
        rows = slice(i * CHUNK, (i + 1) * CHUNK)
        sources = message.get(first_ref, i, B)
        readers = message.get(second_ref, i, C)
        scores = jnp.where(causal, mm_nt(sources, readers), 0.0)
        total = jnp.zeros((CHUNK, CHUNK), f32)
        for j in range(PAIRS):
            grads = split_pair(grad_ref[rows, lanes(j)])
            weight_grads = mm_nt(message.get(first_ref, i, X + j), grads)
            weights = []
            for k, h in enumerate((2 * j, 2 * j + 1)):
                there = sm_ref[rows, SHIFTED * HEADS + h : SHIFTED * HEADS + h + 1]
                here = smt_ref[CUM * HEADS + h : CUM * HEADS + h + 1, lanes(i)]
                decay = jnp.exp(jnp.minimum(here - there, CLAMP))
                weights.append((scores * decay).astype(bf16))
                total = total + weight_grads[:, lanes(k)] * decay
            values_out[rows, lanes(j)] = mm(jnp.concatenate(weights, axis=1), grads)
        total = jnp.where(causal, total, 0.0).astype(bf16)
        sources_out[rows, :] = mm(total, readers)
        readers_out[rows, :] = (mm_tn(total, sources) + readers_ref[rows, :]).astype(bf16)


def last_kernel(
    message, per_step,
    first_ref, within_ref, sources_ref, readers_ref, grad_ref, e_ref, sm_ref, smt_ref, outer_ref,
    back_ref, start_ref, dec_ref, skip_ref, heads_ref, early_ref,
    out_ref, param_ref,
    carry, sums, high_s, low_s, scaled_s, state_s, flux_s,
):
    c = pl.program_id(0)

    @pl.when(c == 0)
    def _():
        carry[...] = outer_ref[...].astype(f32)
        sums[...] = jnp.zeros_like(sums)

    r = message.rows
    ones = head_rows()
    before = lax.broadcasted_iota(jnp.int32, (CHUNK, CHUNK), 0)
    after = lax.broadcasted_iota(jnp.int32, (CHUNK, CHUNK), 1)
    earlier = jnp.where(before < after, 1.0, 0.0)
    decay_rate = jnp.exp(heads_ref[:HEADS, :])
    for i in reversed(range(per_step)):
        rows = slice(i * CHUNK, (i + 1) * CHUNK)
        sm = sm_ref[rows, :]
        sources = message.get(first_ref, i, B)
        for j in range(PAIRS):
            at = lanes(j)
            state = carry[:, at]
            high, low = two_terms(state)
            state_s[:, at] = high
            values = message.get(first_ref, i, X + j).astype(f32)
            weight = spread_pair(sm, WEIGHT, j)
            grad = within_ref[rows, at] + weight * mm_two(sources, high, low)
            skipped = skip_ref[0:1, at] * grad_ref[rows, at].astype(f32)
            message.put(out_ref, i, LAST_X + j, (grad + skipped).astype(bf16))
            high_s[:, at], low_s[:, at] = two_terms(values * grad)
            scaled_s[:, at] = (values * weight).astype(bf16)
            new = dec_ref[i, 0:1, at] * state + back_ref[i, :, at]
            carry[:, at] = new
            flux_s[:, at] = jnp.broadcast_to(
                jnp.sum(start_ref[i, :, at] * new, axis=0, keepdims=True), (16, LANES)
            )
        d_sources = sources_ref[rows, :] + mm_nt(scaled_s[...], state_s[...])
        message.put(out_ref, i, LAST_B, d_sources.astype(bf16))
        message.put(out_ref, i, LAST_C, readers_ref[rows, :])
        g = (mm_nt(ones, high_s[...]) + mm_nt(ones, low_s[...]))[:HEADS]
        high, low = two_terms(flux_s[...])
        constant = (mm_nt(ones, high) + mm_nt(ones, low))[:HEADS, 0:1]
        flux = constant + mm_exact(g - e_ref[:, lanes(i)], earlier)
        soft = smt_ref[DT * HEADS : (DT + 1) * HEADS, lanes(i)]
        rate = smt_ref[RATE * HEADS : (RATE + 1) * HEADS, lanes(i)]
        sig = smt_ref[SIG * HEADS : (SIG + 1) * HEADS, lanes(i)]
        steps = (g / soft - decay_rate * flux) * sig
        sums[:HEADS, :] += flux * rate
        sums[HEADS:, :] += steps
        steps = jnp.concatenate([steps, jnp.zeros_like(steps)], axis=0)
        for p in range(message.per_chunk):
            part = steps if p == 0 else pltpu.roll(steps, LANES - p * r, 1)
            out_ref[i * message.per_chunk + p, LAST * r :, :] = part.astype(bf16)

    @pl.when(c == pl.num_programs(0) - 1)
    def _():
        param_ref[...] = early_ref[...]
        for k in range(2):
            column = jnp.sum(sums[k * HEADS : (k + 1) * HEADS, :], axis=1, keepdims=True)
            block = jnp.broadcast_to(column, (HEADS, LANES))
            block = jnp.concatenate([block, jnp.zeros((LANES - HEADS, LANES), f32)], axis=0)
            param_ref[PAIRS + 1 + k : PAIRS + 2 + k, :] = block.T[0:1, :]


def call(kernel, out_shape, flops, moved, grid=None, in_specs=None, out_specs=None, scratch=()):
    extra = {}
    if grid is not None:
        extra = dict(grid=grid, in_specs=in_specs, out_specs=out_specs)
    return pl.pallas_call(
        kernel,
        out_shape=out_shape,
        scratch_shapes=list(scratch),
        compiler_params=pltpu.CompilerParams(vmem_limit_bytes=60 * 1024 * 1024),
        cost_estimate=pl.CostEstimate(flops=flops, bytes_accessed=moved, transcendentals=0),
        **extra,
    )


def shifted(array, count, by):
    pairs = [(i, i + by) for i in range(count) if 0 <= i + by < count]
    return lax.ppermute(array, "slab", pairs)


def carry_over(state, decay, first_decay, count, sign):
    window, window_decay, step = state, decay, 1
    result = result_decay = None
    while step < count:
        arrived = shifted(window, count, sign * step)
        more = 2 * step < count
        if result is None:
            result = arrived
            if more:
                result_decay = first_decay
                window = (state.astype(f32) + decay[0:1] * arrived.astype(f32)).astype(bf16)
                window_decay = decay * first_decay
        else:
            if more:
                arrived_decay = shifted(window_decay, count, sign * step)
                window = (window.astype(f32) + window_decay[0:1] * arrived.astype(f32)).astype(bf16)
                window_decay = window_decay * arrived_decay
            result = result.astype(f32) + result_decay[0:1] * arrived.astype(f32)
            if more:
                result_decay = result_decay * arrived_decay
        step *= 2
    return jnp.zeros_like(state) if result is None else result


def sum_over(array, axis, count):
    step = 1
    while step < count:
        array = array + lax.ppermute(array, axis, [(i, i ^ step) for i in range(count)])
        step *= 2
    return array


def on_device(
    slab_count, sub_count, tensor_count,
    mixer_x, gate_z, b_matrix, c_matrix, raw_steps, decay_log, skip_gain, step_bias, norm_gain, out_grad,
):
    rows = mixer_x.shape[0]
    peers = sub_count * tensor_count
    tokens = rows * peers
    chunks = tokens // CHUNK
    per_step = min(2, chunks)
    grid = (chunks // per_step,)
    message = Message(rows)
    owners = [t * sub_count + s for s in range(sub_count) for t in range(tensor_count)]
    sub = lax.axis_index("sub")

    def struct(shape, kind=f32):
        return jax.ShapeDtypeStruct(shape, kind)

    def exchange(array):
        return lax.all_to_all(array, ("sub", "tensor"), split_axis=0, concat_axis=0, tiled=True)

    own_logs = lax.dynamic_slice(decay_log, (sub * HEADS,), (HEADS,))
    own_bias = lax.dynamic_slice(step_bias, (sub * HEADS,), (HEADS,))
    own_skip = lax.dynamic_slice(skip_gain, (sub * HEADS,), (HEADS,))
    own_gain = lax.dynamic_slice(norm_gain, (sub * WIDTH,), (WIDTH,)).reshape(1, WIDTH)
    heads = jnp.broadcast_to(jnp.concatenate([own_logs, own_bias])[:, None], (2 * HEADS, LANES))
    skip_row = jnp.repeat(own_skip, HEAD_DIM).reshape(1, WIDTH)

    first_rows = FIRST * rows + STEP_ROWS
    second_rows = SECOND * rows
    last_rows = LAST * rows + STEP_ROWS

    def packed(kernel, height, *arrays):
        out = struct((peers, height, LANES), bf16)
        moved = 4 * peers * height * LANES
        return call(lambda *refs: kernel(owners, *refs), out, 0, moved)(*arrays)

    first = exchange(packed(pack_first, first_rows, mixer_x, b_matrix, raw_steps))
    second = exchange(packed(pack_second, second_rows, gate_z, out_grad, c_matrix))

    def flow(kernel, shape_specs, flops, moved, in_specs, scratch=()):
        def body(*refs):
            return kernel(message, per_step, *refs)

        shapes = tuple(shape for shape, _ in shape_specs)
        specs = tuple(spec for _, spec in shape_specs)
        return call(body, shapes, flops, moved, grid, in_specs, specs, scratch)

    def spec(block, axis, down=False):
        def index(c):
            at = grid[0] - 1 - c if down else c
            return tuple(at if k == axis else 0 for k in range(len(block)))

        return pl.BlockSpec(block, index)

    span = per_step * CHUNK

    def specs_of(down):
        return dict(
            message=lambda height: spec((per_step * message.per_chunk, height, LANES), 0, down),
            token=lambda width: spec((span, width), 0, down),
            lane=lambda height: spec((height, span), 1, down),
            chunk=lambda *shape: spec((per_step,) + shape, 0, down),
        )

    up, dn = specs_of(False), specs_of(True)

    def whole(*shape):
        return pl.BlockSpec(shape, lambda c: (0,) * len(shape))

    unit = 2 * tokens * CHUNK * WIDTH
    size = tokens * WIDTH

    sm, smt, own, dec, state, decay = flow(
        state_kernel,
        [
            (struct((tokens, LANES)), up["token"](LANES)),
            (struct((KINDS * HEADS, tokens)), up["lane"](KINDS * HEADS)),
            (struct((chunks, STATE, WIDTH)), up["chunk"](STATE, WIDTH)),
            (struct((chunks, 8, WIDTH)), up["chunk"](8, WIDTH)),
            (struct((STATE, WIDTH), bf16), whole(STATE, WIDTH)),
            (struct((8, WIDTH)), whole(8, WIDTH)),
        ],
        2 * unit, size * 8,
        [up["message"](first_rows), whole(2 * HEADS, LANES)],
        [pltpu.VMEM((STATE, WIDTH), f32)],
    )(first, heads)

    before = after = None
    if slab_count > 2:
        before, after = shifted(decay, slab_count, 1), shifted(decay, slab_count, -1)
    inbound = carry_over(state, decay, before, slab_count, 1)

    (within,) = flow(
        within_kernel,
        [(struct((tokens, WIDTH)), up["token"](WIDTH))],
        4 * unit, size * 8,
        [
            up["message"](first_rows), up["message"](second_rows),
            up["token"](LANES), up["lane"](KINDS * HEADS),
        ],
    )(first, second, sm, smt)

    y, starts, sums = flow(
        mix_kernel,
        [
            (struct((tokens, WIDTH)), up["token"](WIDTH)),
            (struct((chunks, STATE, WIDTH)), up["chunk"](STATE, WIDTH)),
            (struct((chunks, 8, LANES)), up["chunk"](8, LANES)),
        ],
        2 * unit, size * 20,
        [
            up["message"](first_rows), up["message"](second_rows), up["token"](WIDTH),
            up["token"](LANES), whole(STATE, WIDTH), up["chunk"](STATE, WIDTH),
            up["chunk"](8, WIDTH), whole(1, WIDTH), whole(1, WIDTH),
        ],
        [pltpu.VMEM((STATE, WIDTH), f32)],
    )(first, second, within, sm, inbound, own, dec, own_gain, skip_row)

    partner = lax.ppermute(sums, "sub", [(i, i ^ 1) for i in range(sub_count)])

    d_gates, d_mixed, e, back, slab_back, readers_part, params = flow(
        norm_kernel,
        [
            (struct((peers, PAIRS * rows, LANES), bf16), up["message"](PAIRS * rows)),
            (struct((tokens, WIDTH), bf16), up["token"](WIDTH)),
            (struct((HEADS, tokens)), up["lane"](HEADS)),
            (struct((chunks, STATE, WIDTH)), up["chunk"](STATE, WIDTH)),
            (struct((STATE, WIDTH), bf16), whole(STATE, WIDTH)),
            (struct((tokens, STATE)), up["token"](STATE)),
            (struct((8, LANES)), whole(8, LANES)),
        ],
        4 * unit, size * 20,
        [
            up["message"](first_rows), up["message"](second_rows), up["token"](WIDTH),
            up["token"](LANES), up["chunk"](STATE, WIDTH), up["chunk"](8, WIDTH),
            up["chunk"](8, LANES), up["chunk"](8, LANES), whole(1, WIDTH), whole(1, WIDTH),
        ],
        [
            pltpu.VMEM((8, WIDTH), f32), pltpu.VMEM((STATE, WIDTH), f32),
            pltpu.VMEM((8, WIDTH), f32), pltpu.VMEM((8, WIDTH), f32),
            pltpu.VMEM((CHUNK, WIDTH), bf16), pltpu.VMEM((CHUNK, WIDTH), bf16),
            pltpu.VMEM((CHUNK, WIDTH), bf16),
        ],
    )(first, second, y, sm, starts, dec, sums, partner, own_gain, skip_row)

    outer = carry_over(slab_back, decay, after, slab_count, -1)
    gates_back = exchange(d_gates)

    d_values, d_sources, d_readers = flow(
        local_kernel,
        [
            (struct((tokens, WIDTH)), up["token"](WIDTH)),
            (struct((tokens, STATE)), up["token"](STATE)),
            (struct((tokens, STATE), bf16), up["token"](STATE)),
        ],
        8 * unit, size * 8,
        [
            up["message"](first_rows), up["message"](second_rows), up["token"](WIDTH),
            up["token"](LANES), up["lane"](KINDS * HEADS), up["token"](STATE),
        ],
    )(first, second, d_mixed, sm, smt, readers_part)

    last, params = flow(
        last_kernel,
        [
            (struct((peers, last_rows, LANES), bf16), dn["message"](last_rows)),
            (struct((8, LANES)), whole(8, LANES)),
        ],
        4 * unit, size * 16,
        [
            dn["message"](first_rows), dn["token"](WIDTH), dn["token"](STATE), dn["token"](STATE),
            dn["token"](WIDTH), dn["lane"](HEADS), dn["token"](LANES), dn["lane"](KINDS * HEADS),
            whole(STATE, WIDTH), dn["chunk"](STATE, WIDTH), dn["chunk"](STATE, WIDTH),
            dn["chunk"](8, WIDTH), whole(1, WIDTH), whole(2 * HEADS, LANES), whole(8, LANES),
        ],
        [
            pltpu.VMEM((STATE, WIDTH), f32), pltpu.VMEM((2 * HEADS, LANES), f32),
            pltpu.VMEM((CHUNK, WIDTH), bf16), pltpu.VMEM((CHUNK, WIDTH), bf16),
            pltpu.VMEM((CHUNK, WIDTH), bf16), pltpu.VMEM((STATE, WIDTH), bf16),
            pltpu.VMEM((16, WIDTH), f32),
        ],
    )(
        first, d_values, d_sources, d_readers, d_mixed, e, sm, smt, outer, back, starts, dec,
        skip_row, heads, params,
    )

    last_back = exchange(last)
    params = sum_over(params, "slab", slab_count)
    mine = lax.broadcasted_iota(jnp.int32, (sub_count, 1, 1), 0) == sub
    params = sum_over(jnp.where(mine, params[None], 0.0), "sub", sub_count)
    grad_gates = call(
        lambda *refs: unpack_gates(owners, *refs),
        struct((rows, CHANNELS), bf16), 0, 4 * rows * CHANNELS,
    )(gates_back)
    grad_x, grad_b, grad_c, grad_steps = call(
        lambda *refs: unpack_last(owners, *refs),
        (
            struct((rows, CHANNELS), bf16), struct((rows, GROUPS * STATE), bf16),
            struct((rows, GROUPS * STATE), bf16), struct((rows, MIXER_HEADS), bf16),
        ),
        0, 6 * rows * CHANNELS,
    )(last_back)
    return (
        grad_x,
        grad_gates,
        grad_b,
        grad_c,
        grad_steps,
        params[:, PAIRS + 1, :HEADS].reshape(-1),
        params[:, PAIRS, :HEADS].reshape(-1),
        params[:, PAIRS + 2, :HEADS].reshape(-1),
        params[:, :PAIRS].reshape(-1),
    )


def solution(mesh):
    tensor_count = mesh.shape["tensor"]
    sub_count = OWNERS // tensor_count
    slab_count = mesh.shape["dp"] // sub_count
    devices = mesh.devices.reshape(slab_count, sub_count, tensor_count)
    split_mesh = Mesh(devices, ("slab", "sub", "tensor"))
    rows = P(("slab", "sub", "tensor"), None)
    param = P("tensor")

    def local(*arrays):
        return on_device(slab_count, sub_count, tensor_count, *arrays)

    return jax.shard_map(
        local,
        mesh=split_mesh,
        in_specs=(rows,) * 5 + (param,) * 4 + (rows,),
        out_specs=(rows,) * 5 + (param,) * 4,
        check_vma=False,
    )
```

time: 179 us -> 167 us (0.933)
  blocking collectives: 29.5 us -> 0 us
  Pallas kernels: 26.7 us -> 54.6 us
  local copies, waits for them, and re-layouts: 33.1 us -> 9.61 us
  waiting for transfers between devices: 45.9 us -> 62.5 us
  other arithmetic: 4.49 us -> 0.32 us
    ppermute x0 -> x5, waiting for transfers between devices: none -> 30.7 us  [the longest x4 29.3 us: sum_over(): lax.ppermute(array, axis, [(i, i ^ step) for i in range(count)])]
    all_to_all x2 -> x0, blocking collectives: 29.5 us -> none  [the longest x1 17.4 us: exchange(): lax.all_to_all(array, ('sub', 'tensor'), split_axis=0, concat_axis=0, til...]
    pallas_call x9 -> x10, Pallas kernels: 26.7 us -> 54.6 us  [the longest x1 9.01 us: on_device(): flow(last_kernel, [(struct((peers, last_rows, LANES), bf16), dn['message'...]
    unnamed x88 -> x22, local copies, waits for them, and re-layouts: 26.8 us -> 4.23 us
    all_to_all x3 -> x4, starting transfers between devices: 12.6 us -> 31.7 us  [exchange(): lax.all_to_all(array, ('sub', 'tensor'), split_axis=0, concat_axis=0, til...]
    ppermute x6 -> x2, waiting for transfers between devices: 13.6 us -> 1.28 us  [shifted(): return lax.ppermute(array, 'slab', pairs)]
    ppermute x6 -> x2, starting transfers between devices: 17.1 us -> 5.79 us  [shifted(): return lax.ppermute(array, 'slab', pairs)]
    all_to_all x1 -> x0, starting transfers between devices: 7.67 us -> none  [gathered(): lax.all_to_all(sent, ('slab', 'sub'), split_axis=0, concat_axis=0, tiled=...]
  transfers between devices with their start and end apart: 10 -> 11, of which waited for: 5 -> 8; matrix products, arithmetic and copies ran while one was open for 6% -> 3% of each run, Pallas kernels for 9% -> 20%
where the time goes in v2:
time: 167 us; the launch traced here: 166 us
  waiting for transfers between devices  62.5 us (37%)
  Pallas kernels  54.6 us (33%)
  starting transfers between devices  38.3 us (23%)
  local copies, waits for them, and re-layouts  9.61 us (6%)
    all_to_all x4, starting transfers between devices, exchange(): lax.all_to_all(array, ('sub', 'tensor'), split_axis=0, concat_axis=0, til...  31.7 us
    all_to_all x4, waiting for transfers between devices, exchange(): lax.all_to_all(array, ('sub', 'tensor'), split_axis=0, concat_axis=0, til...  30.5 us
    ppermute x4, waiting for transfers between devices, sum_over(): lax.ppermute(array, axis, [(i, i ^ step) for i in range(count)])  29.3 us
    pallas_call x1, Pallas kernels, on_device(): flow(last_kernel, [(struct((peers, last_rows, LANES), bf16), dn['message'...  9.01 us
    pallas_call x1, Pallas kernels, on_device(): flow(norm_kernel, [(struct((peers, PAIRS * rows, LANES), bf16), up['messa...  8.49 us
    pallas_call x1, Pallas kernels, on_device(): flow(state_kernel, [(struct((tokens, LANES)), up['token'](LANES)), (struc...  7.71 us
    pallas_call x1, Pallas kernels, on_device(): flow(mix_kernel, [(struct((tokens, WIDTH)), up['token'](WIDTH)), (struct(...  6.85 us
    pallas_call x1, Pallas kernels, on_device(): flow(local_kernel, [(struct((tokens, WIDTH)), up['token'](WIDTH)), (struc...  6.14 us
  transfers between devices with their start and end apart: 11, of which 8 were waited for; matrix products, arithmetic and copies ran while one was open for 3% of the time, Pallas kernels for 20%

profile of v2, /device:TPU:0, one launch (start us, length us, event | category | flops | bytes accessed | tf_op | source)
XLA Modules:
  0.0 166.1 jit_solution(10469489424747173796)
XLA Ops:
  0.6 2.6 %shard_map.169 = bf16[16,336,128]{2,1,0:T(8,128)(2,1)} custom-call(bf16[64,8192]{1,0:T(8,128)(2,1)} %refs_0_.2, bf16[64,1024]{1,0:T(8,128)(2,1)} %refs_1_.2, bf16[64,128]{1,0:T(8,128)(2,1)} %refs_2_.2), custom_call_target="tpu_custom_call" | custom-call | bytes 2752512 | tf_op jit(solution)/shard_map/pallas_call | solution.py:522
  3.3 6.3 %all-to-all-start = ((bf16[16,336,128]{2,1,0:T(8,128)(2,1)}), bf16[16,336,128]{2,1,0:T(8,128)(2,1)S(1)}, u32[]{:S(2)}, u32[]{:S(2)}) async-start(bf16[16,336,128]{2,1,0:T(8,128)(2,1)} %shard_map.169), calls=%async_computation | async-start | bytes 2752512 | tf_op jit(solution)/shard_map/all_to_all | solution.py:506
  9.6 3.4 %shard_map.170 = bf16[16,576,128]{2,1,0:T(8,128)(2,1)} custom-call(bf16[64,8192]{1,0:T(8,128)(2,1)} %refs_0_.3, bf16[64,8192]{1,0:T(8,128)(2,1)} %refs_1_.3, bf16[64,1024]{1,0:T(8,128)(2,1)} %refs_2_.3), custom_call_target="tpu_custom_call" | custom-call | bytes 4718592 | tf_op jit(solution)/shard_map/pallas_call | solution.py:522
  12.9 15.4 %all-to-all-done.refs_0_ = bf16[16,336,128]{2,1,0:T(8,128)(2,1)S(1)} async-done(((bf16[16,336,128]{2,1,0:T(8,128)(2,1)}), bf16[16,336,128]{2,1,0:T(8,128)(2,1)S(1)}, u32[]{:S(2)}, u32[]{:S(2)}) %all-to-all-start) | async-done | bytes 1376288 | tf_op jit(solution)/shard_map/all_to_all | solution.py:506
  29.4 4.4 %all-to-all-start.1 = ((bf16[16,576,128]{2,1,0:T(8,128)(2,1)}), bf16[16,576,128]{2,1,0:T(8,128)(2,1)}, u32[]{:S(2)}, u32[]{:S(2)}) async-start(bf16[16,576,128]{2,1,0:T(8,128)(2,1)} %shard_map.170), calls=%async_computation.1 | async-start | bytes 4718592 | tf_op jit(solution)/shard_map/all_to_all | solution.py:506
  34.8 7.7 %shard_map.171 = (f32[1024,128]{1,0:T(8,128)}, f32[64,1024]{1,0:T(8,128)}, f32[8,128,512]{2,1,0:T(8,128)}, f32[8,8,512]{2,1,0:T(8,128)}, bf16[128,512]{1,0:T(8,128)(2,1)}, /*index=5*/f32[8,512]{1,0:T(8,128)}) custom-call(bf16[16,336,128]{2,1,0:T(8,128)(2,1)} %copy-done, f32[16,128]{1,0:T(8,128)} %broadcast_in_dim.30.refs_1_.refs_13_), custom_call_target="tpu_custom_call" | custom-call | flops 268435456 | bytes 4194304 | tf_op jit(solution)/shard_map/pallas_call | solution.py:560
  42.5 4.5 %collective-permute-start = (bf16[128,512]{1,0:T(8,128)(2,1)}, bf16[128,512]{1,0:T(8,128)(2,1)S(1)}, u32[]{:S(2)}, u32[]{:S(2)}) collective-permute-start(bf16[128,512]{1,0:T(8,128)(2,1)} %get-tuple-element.35), channel_id=1, source_target_pairs={{0,16},{1,17},{2,18},{3,19},{4,20},{5,21},{6,22},{7,23},{8,24},{9,... | collective-permute-start | bytes 393224 | tf_op jit(solution)/shard_map/ppermute | solution.py:453
  47.8 1.3 dynamic_slice.14
  49.1 15.1 %all-to-all-done.1.refs_1_ = bf16[16,576,128]{2,1,0:T(8,128)(2,1)} async-done(((bf16[16,576,128]{2,1,0:T(8,128)(2,1)}), bf16[16,576,128]{2,1,0:T(8,128)(2,1)}, u32[]{:S(2)}, u32[]{:S(2)}) %all-to-all-start.1) | async-done | bytes 2359328 | tf_op jit(solution)/shard_map/all_to_all | solution.py:506
  64.2 5.3 %shard_map.172.refs_2_ = f32[1024,512]{1,0:T(8,128)} custom-call(bf16[16,336,128]{2,1,0:T(8,128)(2,1)} %copy-done, bf16[16,576,128]{2,1,0:T(8,128)(2,1)} %all-to-all-done.1.refs_1_, f32[1024,128]{1,0:T(8,128)} %get-tuple-element.33.refs_2_.refs_3_.refs_6_, f32[64,1024]{1,0:T(8,128)} %get-tuple-element.34.refs_3_.refs_4_.refs_7_), custom_call_target="tpu_custom_call" | custom-call | flops 536870912 | bytes 4194304 | tf_op jit(solution)/shard_map/pallas_call | solution.py:580
  70.2 6.9 %shard_map.173 = (f32[1024,512]{1,0:T(8,128)}, f32[8,128,512]{2,1,0:T(8,128)}, f32[8,8,128]{2,1,0:T(8,128)}) custom-call(bf16[16,336,128]{2,1,0:T(8,128)(2,1)} %copy-done, bf16[16,576,128]{2,1,0:T(8,128)(2,1)} %all-to-all-done.1.refs_1_, f32[1024,512]{1,0:T(8,128)} %shard_map.172.refs_2_, f32[1024,128]{1,0:T(8,128)} %get-tuple-element.33.refs_2_.refs_3_.refs_6_, ...), custom_call_target="tpu_custom_call" | custom-call | flops 268435456 | bytes 10485760 | tf_op jit(solution)/shard_map/pallas_call | solution.py:590
  77.1 1.4 collective-permute-done.1.refs_7_
  79.1 8.5 %shard_map.174 = (bf16[16,256,128]{2,1,0:T(8,128)(2,1)}, bf16[1024,512]{1,0:T(8,128)(2,1)}, f32[8,1024]{1,0:T(8,128)}, f32[8,128,512]{2,1,0:T(8,128)}, bf16[128,...) custom-call(bf16[16,336,128]{2,1,0:T(8,128)(2,1)} %copy-done, ...), custom_call_target="tpu_custom_call" | custom-call | flops 536870912 | bytes 10485760 | tf_op jit(solution)/shard_map/pallas_call | solution.py:608
  87.6 6.1 %all-to-all-start.3 = ((bf16[16,256,128]{2,1,0:T(8,128)(2,1)}), bf16[16,256,128]{2,1,0:T(8,128)(2,1)S(1)}, u32[]{:S(2)}, u32[]{:S(2)}) async-start(bf16[16,256,128]{2,1,0:T(8,128)(2,1)} %get-tuple-element.52), calls=%async_computation.3 | async-start | bytes 2097152 | tf_op jit(solution)/shard_map/all_to_all | solution.py:506
  93.8 1.3 collective-permute-start.2
  95.1 6.1 %shard_map.175 = (f32[1024,512]{1,0:T(8,128)}, f32[1024,128]{1,0:T(8,128)}, bf16[1024,128]{1,0:T(8,128)(2,1)}) custom-call(bf16[16,336,128]{2,1,0:T(8,128)(2,1)} %copy-done, bf16[16,576,128]{2,1,0:T(8,128)(2,1)} %all-to-all-done.1.refs_1_, bf16[1024,512]{1,0:T(8,128)(2,1)} %get-tuple-element.41.refs_2_.refs_4_, ...), custom_call_target="tpu_custom_call" | custom-call | flops 1073741824 | bytes 4194304 | tf_op jit(solution)/shard_map/pallas_call | solution.py:636
  101.2 1.3 collective-permute-done.2.refs_8_
  103.2 9.0 %shard_map.176 = (bf16[16,400,128]{2,1,0:T(8,128)(2,1)}, f32[8,128]{1,0:T(8,128)}) custom-call(bf16[16,336,128]{2,1,0:T(8,128)(2,1)} %copy-done, f32[1024,512]{1,0:T(8,128)} %get-tuple-element.43.refs_1_, f32[1024,128]{1,0:T(8,128)} %get-tuple-element.44.refs_2_, bf16[1024,128]{1,0:T(8,128)(2,1)} %get-tuple-element.45.refs_3_, ...), custom_call_target="tpu_custom_call" | custom-call | flops 536870912 | bytes 8388608 | tf_op jit(solution)/shard_map/pallas_call | solution.py:650
  112.2 14.8 %all-to-all-start.2 = ((bf16[16,400,128]{2,1,0:T(8,128)(2,1)}), bf16[16,400,128]{2,1,0:T(8,128)(2,1)S(1)}, u32[]{:S(2)}, u32[]{:S(2)}) async-start(bf16[16,400,128]{2,1,0:T(8,128)(2,1)} %get-tuple-element.50), calls=%async_computation.2 | async-start | bytes 3276800 | tf_op jit(solution)/shard_map/all_to_all | solution.py:506
  127.1 20.8 %collective-permute-done.3 = f32[8,128]{1,0:T(8,128)S(1)} collective-permute-done((f32[8,128]{1,0:T(8,128)S(1)}, f32[8,128]{1,0:T(8,128)S(1)}, u32[]{:S(2)}, u32[]{:S(2)}) %collective-permute-start.3) | collective-permute-done | bytes 4128 | tf_op jit(solution)/shard_map/ppermute | solution.py:483
  149.4 3.9 %collective-permute-done.5 = f32[8,8,128]{2,1,0:T(8,128)S(1)} collective-permute-done((f32[8,8,128]{2,1,0:T(8,128)S(1)}, f32[8,8,128]{2,1,0:T(8,128)S(1)}, u32[]{:S(2)}, u32[]{:S(2)}) %collective-permute-start.5) | collective-permute-done | bytes 32800 | tf_op jit(solution)/shard_map/ppermute | solution.py:483
  154.0 3.4 %collective-permute-done.6 = f32[8,8,128]{2,1,0:T(8,128)S(1)} collective-permute-done((f32[8,8,128]{2,1,0:T(8,128)S(1)}, f32[8,8,128]{2,1,0:T(8,128)S(1)}, u32[]{:S(2)}, u32[]{:S(2)}) %collective-permute-start.6) | collective-permute-done | bytes 32800 | tf_op jit(solution)/shard_map/ppermute | solution.py:483
  159.8 2.4 %shard_map.178 = bf16[64,8192]{1,0:T(8,128)(2,1)} custom-call(bf16[16,256,128]{2,1,0:T(8,128)(2,1)} %copy-done.2), custom_call_target="tpu_custom_call" | custom-call | bytes 2097152 | tf_op jit(solution)/shard_map/pallas_call | solution.py:678
  163.4 2.7 %shard_map.177 = (bf16[64,8192]{1,0:T(8,128)(2,1)}, bf16[64,1024]{1,0:T(8,128)(2,1)}, bf16[64,1024]{1,0:T(8,128)(2,1)}, bf16[64,128]{1,0:T(8,128)(2,1)}) custom-call(bf16[16,400,128]{2,1,0:T(8,128)(2,1)} %copy-done.1), custom_call_target="tpu_custom_call" | custom-call | bytes 3145728 | tf_op jit(solution)/shard_map/pallas_call | solution.py:682
  (49 shorter events, 10.6 us)
Async XLA Ops:
  3.3 25.1 %all-to-all-start = ((bf16[16,336,128]{2,1,0:T(8,128)(2,1)}), bf16[16,336,128]{2,1,0:T(8,128)(2,1)S(1)}, u32[]{:S(2)}, u32[]{:S(2)}) async-start(bf16[16,336,128]{2,1,0:T(8,128)(2,1)} %shard_map.169), calls=%async_computation | async-start | bytes 2752512 | tf_op jit(solution)/shard_map/all_to_all | solution.py:506
  12.9 20.9 %copy-start.8 = (f32[64]{0:T(128)S(1)}, f32[64]{0:T(128)}, u32[]{:S(2)}) copy-start(f32[64]{0:T(128)} %param.15) | copy-start | bytes 772
  12.9 21.0 %copy-start.9 = (f32[64]{0:T(128)S(1)}, f32[64]{0:T(128)}, u32[]{:S(2)}) copy-start(f32[64]{0:T(128)} %param.17) | copy-start | bytes 772
  12.9 34.1 %copy-start.10 = (f32[64]{0:T(128)S(1)}, f32[64]{0:T(128)}, u32[]{:S(2)}) copy-start(f32[64]{0:T(128)} %param.16) | copy-start | bytes 772
  28.3 1.1 copy-start
  29.4 34.8 %all-to-all-start.1 = ((bf16[16,576,128]{2,1,0:T(8,128)(2,1)}), bf16[16,576,128]{2,1,0:T(8,128)(2,1)}, u32[]{:S(2)}, u32[]{:S(2)}) async-start(bf16[16,576,128]{2,1,0:T(8,128)(2,1)} %shard_map.170), calls=%async_computation.1 | async-start | bytes 4718592 | tf_op jit(solution)/shard_map/all_to_all | solution.py:506
  42.5 27.0 %collective-permute-start = (bf16[128,512]{1,0:T(8,128)(2,1)}, bf16[128,512]{1,0:T(8,128)(2,1)S(1)}, u32[]{:S(2)}, u32[]{:S(2)}) collective-permute-start(bf16[128,512]{1,0:T(8,128)(2,1)} %get-tuple-element.35), channel_id=1, source_target_pairs={{0,16},{1,17},{2,18},{3,19},{4,20},{5,21},{6,22},{7,23},{8,24},{9,... | collective-permute-start | bytes 393224 | tf_op jit(solution)/shard_map/ppermute | solution.py:453
  69.5 0.7 copy-start.3
  77.0 1.5 collective-permute-start.1
  78.5 0.6 copy-start.5
  87.6 6.2 %copy-start.7 = (bf16[128,512]{1,0:T(8,128)(2,1)S(1)}, bf16[128,512]{1,0:T(8,128)(2,1)}, u32[]{:S(2)}) copy-start(bf16[128,512]{1,0:T(8,128)(2,1)} %get-tuple-element.47) | copy-start | bytes 393220
  87.6 24.6 %all-to-all-start.3 = ((bf16[16,256,128]{2,1,0:T(8,128)(2,1)}), bf16[16,256,128]{2,1,0:T(8,128)(2,1)S(1)}, u32[]{:S(2)}, u32[]{:S(2)}) async-start(bf16[16,256,128]{2,1,0:T(8,128)(2,1)} %get-tuple-element.52), calls=%async_computation.3 | async-start | bytes 2097152 | tf_op jit(solution)/shard_map/all_to_all | solution.py:506
  93.8 8.7 %collective-permute-start.2 = (bf16[128,512]{1,0:T(8,128)(2,1)S(1)}, bf16[128,512]{1,0:T(8,128)(2,1)S(1)}, u32[]{:S(2)}, u32[]{:S(2)}) collective-permute-start(bf16[128,512]{1,0:T(8,128)(2,1)S(1)} %copy-done.7), channel_id=1, source_target_pairs={{16,0},{17,1},{18,2},{19,3},{20,4},{21,5},{22,6},{23,7},{24,8},{25... | collective-permute-start | bytes 393224 | tf_op jit(solution)/shard_map/ppermute | solution.py:453
  102.5 0.7 copy-start.4
  112.2 14.8 %copy-start.6 = (f32[8,128]{1,0:T(8,128)S(1)}, f32[8,128]{1,0:T(8,128)}, u32[]{:S(2)}) copy-start(f32[8,128]{1,0:T(8,128)} %get-tuple-element.56) | copy-start | bytes 12292
  112.2 47.6 %copy-start.2 = (bf16[16,256,128]{2,1,0:T(8,128)(2,1)}, bf16[16,256,128]{2,1,0:T(8,128)(2,1)S(1)}, u32[]{:S(2)}) copy-start(bf16[16,256,128]{2,1,0:T(8,128)(2,1)S(1)} %all-to-all-done.3.refs_0_) | copy-start | bytes 3145732
  112.2 50.0 %all-to-all-start.2 = ((bf16[16,400,128]{2,1,0:T(8,128)(2,1)}), bf16[16,400,128]{2,1,0:T(8,128)(2,1)S(1)}, u32[]{:S(2)}, u32[]{:S(2)}) async-start(bf16[16,400,128]{2,1,0:T(8,128)(2,1)} %get-tuple-element.50), calls=%async_computation.2 | async-start | bytes 3276800 | tf_op jit(solution)/shard_map/all_to_all | solution.py:506
  127.0 20.9 %collective-permute-start.3 = (f32[8,128]{1,0:T(8,128)S(1)}, f32[8,128]{1,0:T(8,128)S(1)}, u32[]{:S(2)}, u32[]{:S(2)}) collective-permute-start(f32[8,128]{1,0:T(8,128)S(1)} %copy-done.6), channel_id=1, source_target_pairs={{0,16},{16,0},{1,17},{17,1},{2,18},{18,2},{3,19},{19,3},{4,20},{20... | collective-permute-start | bytes 12296 | tf_op jit(solution)/shard_map/ppermute | solution.py:483
  148.0 1.2 collective-permute-start.4
  149.3 4.0 %collective-permute-start.5 = (f32[8,8,128]{2,1,0:T(8,128)S(1)}, f32[8,8,128]{2,1,0:T(8,128)S(1)}, u32[]{:S(2)}, u32[]{:S(2)}) collective-permute-start(f32[8,8,128]{2,1,0:T(8,128)S(1)} %fusion), channel_id=1, source_target_pairs={{0,4},{2,6},{4,0},{6,2},{8,12},{10,14},{12,8},{14,10},{1,5},{3,7},... | collective-permute-start | bytes 98312 | tf_op jit(solution)/shard_map/ppermute | solution.py:483
  153.4 4.0 %collective-permute-start.6 = (f32[8,8,128]{2,1,0:T(8,128)S(1)}, f32[8,8,128]{2,1,0:T(8,128)S(1)}, u32[]{:S(2)}, u32[]{:S(2)}) collective-permute-start(f32[8,8,128]{2,1,0:T(8,128)S(1)} %fusion.1), channel_id=1, source_target_pairs={{0,8},{2,10},{4,12},{6,14},{8,0},{10,2},{12,4},{14,6},{1,9},{3,11}... | collective-permute-start | bytes 98312 | tf_op jit(solution)/shard_map/ppermute | solution.py:483
  162.2 1.2 copy-start.1

commit v3 on v2

--- a/solution.py
+++ b/solution.py
@@ -105,15 +105,18 @@
         ref[a, b, :] = value.reshape(self.per_chunk, self.rows, LANES)
 
 
-X, B = 0, PAIRS
-FIRST = PAIRS + 1
-Z, GRAD, C = 0, PAIRS, 2 * PAIRS
-SECOND = 2 * PAIRS + 1
-LAST_X, LAST_B, LAST_C = 0, PAIRS, PAIRS + 1
-LAST = PAIRS + 2
-
-
-def pack_first(owners, x_ref, b_ref, steps_ref, out_ref):
+X, B, C = 0, PAIRS, PAIRS + 1
+FIRST = PAIRS + 2
+Z, GRAD = 0, PAIRS
+SECOND = 2 * PAIRS
+GATE_Z, GATE_C = 0, PAIRS
+GATES = PAIRS + 1
+LAST_X, LAST_B = 0, PAIRS
+LAST = PAIRS + 1
+TERMS = 3
+
+
+def pack_first(owners, x_ref, b_ref, c_ref, steps_ref, out_ref):
     r = x_ref.shape[0]
     steps = steps_ref[...].astype(f32)
     padded = jnp.concatenate([steps, jnp.zeros((LANES - r, LANES), f32)], axis=0)
@@ -123,41 +126,87 @@
         for j in range(PAIRS):
             out_ref[peer, j * r : (j + 1) * r, :] = x_ref[:, lanes(own * PAIRS + j)]
         out_ref[peer, B * r : (B + 1) * r, :] = b_ref[:, lanes(own // 2)]
+        out_ref[peer, C * r : (C + 1) * r, :] = c_ref[:, lanes(own // 2)]
         mine = jnp.concatenate([by_head[own * HEADS : (own + 1) * HEADS, :], zero], axis=0)
         out_ref[peer, FIRST * r :, :] = mine.astype(bf16)
 
 
-def pack_second(owners, z_ref, grad_ref, c_ref, out_ref):
+def pack_second(owners, z_ref, grad_ref, out_ref):
     r = z_ref.shape[0]
     for peer, own in enumerate(owners):
         for j in range(PAIRS):
             out_ref[peer, (Z + j) * r : (Z + j + 1) * r, :] = z_ref[:, lanes(own * PAIRS + j)]
             out_ref[peer, (GRAD + j) * r : (GRAD + j + 1) * r, :] = grad_ref[:, lanes(own * PAIRS + j)]
-        out_ref[peer, C * r : (C + 1) * r, :] = c_ref[:, lanes(own // 2)]
-
-
-def unpack_gates(owners, in_ref, out_ref):
+
+
+def add_halves(owners, in_ref, block, out_ref):
+    r = out_ref.shape[0]
+    peer_of = {own: peer for peer, own in enumerate(owners)}
+    for g in range(GROUPS):
+        halves = [
+            in_ref[peer_of[2 * g + k], block * r : (block + 1) * r, :].astype(f32) for k in range(2)
+        ]
+        out_ref[:, lanes(g)] = (halves[0] + halves[1]).astype(bf16)
+
+
+def unpack_gates(owners, in_ref, out_ref, c_ref):
     r = out_ref.shape[0]
     for peer, own in enumerate(owners):
         for j in range(PAIRS):
             out_ref[:, lanes(own * PAIRS + j)] = in_ref[peer, j * r : (j + 1) * r, :]
-
-
-def unpack_last(owners, in_ref, x_ref, b_ref, c_ref, steps_ref):
+    add_halves(owners, in_ref, GATE_C, c_ref)
+
+
+def unpack_last(owners, in_ref, x_ref, b_ref, steps_ref):
     r = x_ref.shape[0]
     peer_of = {own: peer for peer, own in enumerate(owners)}
     for peer, own in enumerate(owners):
         for j in range(PAIRS):
             x_ref[:, lanes(own * PAIRS + j)] = in_ref[peer, j * r : (j + 1) * r, :]
-    for g in range(GROUPS):
-        for block, ref in ((LAST_B, b_ref), (LAST_C, c_ref)):
-            at = slice(block * r, (block + 1) * r)
-            halves = [in_ref[peer_of[2 * g + k], at, :].astype(f32) for k in range(2)]
-            ref[:, lanes(g)] = (halves[0] + halves[1]).astype(bf16)
+    add_halves(owners, in_ref, LAST_B, b_ref)
     by_head = jnp.concatenate(
-        [in_ref[peer_of[own], LAST * r :, :].astype(f32)[:HEADS] for own in range(OWNERS)], axis=0
+        [
+            in_ref[peer_of[own], LAST * r : LAST * r + STEP_ROWS, :].astype(f32)[:HEADS]
+            for own in range(OWNERS)
+        ],
+        axis=0,
     )
     steps_ref[...] = by_head.T[:r, :].astype(bf16)
+
+
+def three_terms(values):
+    high = values.astype(bf16).astype(f32)
+    rest = values - high
+    middle = rest.astype(bf16).astype(f32)
+    return [high, middle, rest - middle]
+
+
+def unpack_params(sub_count, tensor_count, late_ref, early_ref, mine_ref, late_out, gain_out, skip_out):
+    lane = lax.broadcasted_iota(jnp.int32, (1, LANES), 1)
+    late = [jnp.zeros((1, LANES), f32) for _ in range(2)]
+    skip = jnp.zeros((1, LANES), f32)
+
+    def placed(rows, at):
+        total = rows[at : at + 1] + rows[at + 1 : at + 2] + rows[at + 2 : at + 3]
+        return jnp.where(lane < HEADS, total, 0.0)
+
+    for s in range(sub_count):
+        late_rows = jnp.zeros((STEP_ROWS, LANES), f32)
+        early_rows = jnp.zeros((STEP_ROWS, LANES), f32)
+        for t in range(tensor_count):
+            mine = mine_ref[t : t + 1, :] > 0.0
+            peer = s * tensor_count + t
+            late_rows = jnp.where(mine, late_ref[peer].astype(f32), late_rows)
+            early_rows = jnp.where(mine, early_ref[peer].astype(f32), early_rows)
+        for k in range(2):
+            part = placed(late_rows, HEADS + k * TERMS)
+            late[k] = late[k] + (part if s == 0 else pltpu.roll(part, s * HEADS, 1))
+        part = placed(early_rows, TERMS * PAIRS)
+        skip = skip + (part if s == 0 else pltpu.roll(part, s * HEADS, 1))
+        gain = early_rows[:PAIRS] + early_rows[PAIRS : 2 * PAIRS] + early_rows[2 * PAIRS : 3 * PAIRS]
+        gain_out[s * PAIRS : (s + 1) * PAIRS, :] = gain
+    late_out[...] = jnp.concatenate(late + [jnp.zeros((6, LANES), f32)], axis=0)
+    skip_out[...] = skip
 
 
 def state_kernel(
@@ -214,12 +263,12 @@
     state_ref[...] = carry[...].astype(bf16)
 
 
-def within_kernel(message, per_step, first_ref, second_ref, sm_ref, smt_ref, out_ref):
+def within_kernel(message, per_step, first_ref, sm_ref, smt_ref, out_ref):
     t = lax.broadcasted_iota(jnp.int32, (CHUNK, CHUNK), 0)
     s = lax.broadcasted_iota(jnp.int32, (CHUNK, CHUNK), 1)
     for i in range(per_step):
         rows = slice(i * CHUNK, (i + 1) * CHUNK)
-        scores = mm_nt(message.get(second_ref, i, C), message.get(first_ref, i, B))
+        scores = mm_nt(message.get(first_ref, i, C), message.get(first_ref, i, B))
         scores = jnp.where(t >= s, scores, 0.0)
         for j in range(PAIRS):
             weights = []
@@ -246,7 +295,7 @@
     for i in range(per_step):
         rows = slice(i * CHUNK, (i + 1) * CHUNK)
         sm = sm_ref[rows, :]
-        readers = message.get(second_ref, i, C)
+        readers = message.get(first_ref, i, C)
         power = jnp.zeros((CHUNK, LANES), f32)
         cross = jnp.zeros((CHUNK, LANES), f32)
         for j in range(PAIRS):
@@ -286,7 +335,7 @@
     for i in range(per_step):
         rows = slice(i * CHUNK, (i + 1) * CHUNK)
         sm = sm_ref[rows, :]
-        readers = message.get(second_ref, i, C)
+        readers = message.get(first_ref, i, C)
         readers_t = readers.T
         sums = (sums_ref[i] + other_ref[i]) * (1.0 / GROUP_WIDTH)
         inverse_row = lax.rsqrt(sums[0:1] + epsilon)
@@ -337,8 +386,8 @@
 
 def local_kernel(
     message, per_step,
-    first_ref, second_ref, grad_ref, sm_ref, smt_ref, readers_ref,
-    values_out, sources_out, readers_out,
+    first_ref, grad_ref, sm_ref, smt_ref, readers_ref, gate_ref,
+    values_out, sources_out, gates_out,
 ):
     s = lax.broadcasted_iota(jnp.int32, (CHUNK, CHUNK), 0)
     t = lax.broadcasted_iota(jnp.int32, (CHUNK, CHUNK), 1)
@@ -346,7 +395,7 @@
     for i in range(per_step):
         rows = slice(i * CHUNK, (i + 1) * CHUNK)
         sources = message.get(first_ref, i, B)
-        readers = message.get(second_ref, i, C)
+        readers = message.get(first_ref, i, C)
         scores = jnp.where(causal, mm_nt(sources, readers), 0.0)
         total = jnp.zeros((CHUNK, CHUNK), f32)
         for j in range(PAIRS):
@@ -362,14 +411,17 @@
             values_out[rows, lanes(j)] = mm(jnp.concatenate(weights, axis=1), grads)
         total = jnp.where(causal, total, 0.0).astype(bf16)
         sources_out[rows, :] = mm(total, readers)
-        readers_out[rows, :] = (mm_tn(total, sources) + readers_ref[rows, :]).astype(bf16)
+        d_readers = mm_tn(total, sources) + readers_ref[rows, :]
+        message.put(gates_out, i, GATE_C, d_readers.astype(bf16))
+        for j in range(PAIRS):
+            message.put(gates_out, i, GATE_Z + j, message.get(gate_ref, i, j))
 
 
 def last_kernel(
     message, per_step,
-    first_ref, within_ref, sources_ref, readers_ref, grad_ref, e_ref, sm_ref, smt_ref, outer_ref,
+    first_ref, within_ref, sources_ref, grad_ref, e_ref, sm_ref, smt_ref, outer_ref,
     back_ref, start_ref, dec_ref, skip_ref, heads_ref, early_ref,
-    out_ref, param_ref,
+    out_ref,
     carry, sums, high_s, low_s, scaled_s, state_s, flux_s,
 ):
     c = pl.program_id(0)
@@ -385,6 +437,8 @@
     after = lax.broadcasted_iota(jnp.int32, (CHUNK, CHUNK), 1)
     earlier = jnp.where(before < after, 1.0, 0.0)
     decay_rate = jnp.exp(heads_ref[:HEADS, :])
+    first_peer = (pl.num_programs(0) - 1 - c) * per_step * message.per_chunk
+    mine = out_ref.at[pl.ds(first_peer, per_step * message.per_chunk)]
     for i in reversed(range(per_step)):
         rows = slice(i * CHUNK, (i + 1) * CHUNK)
         sm = sm_ref[rows, :]
@@ -398,7 +452,7 @@
             weight = spread_pair(sm, WEIGHT, j)
             grad = within_ref[rows, at] + weight * mm_two(sources, high, low)
             skipped = skip_ref[0:1, at] * grad_ref[rows, at].astype(f32)
-            message.put(out_ref, i, LAST_X + j, (grad + skipped).astype(bf16))
+            message.put(mine, i, LAST_X + j, (grad + skipped).astype(bf16))
             high_s[:, at], low_s[:, at] = two_terms(values * grad)
             scaled_s[:, at] = (values * weight).astype(bf16)
             new = dec_ref[i, 0:1, at] * state + back_ref[i, :, at]
@@ -407,8 +461,7 @@
                 jnp.sum(start_ref[i, :, at] * new, axis=0, keepdims=True), (16, LANES)
             )
         d_sources = sources_ref[rows, :] + mm_nt(scaled_s[...], state_s[...])
-        message.put(out_ref, i, LAST_B, d_sources.astype(bf16))
-        message.put(out_ref, i, LAST_C, readers_ref[rows, :])
+        message.put(mine, i, LAST_B, d_sources.astype(bf16))
         g = (mm_nt(ones, high_s[...]) + mm_nt(ones, low_s[...]))[:HEADS]
         high, low = two_terms(flux_s[...])
         constant = (mm_nt(ones, high) + mm_nt(ones, low))[:HEADS, 0:1]
@@ -422,16 +475,31 @@
         steps = jnp.concatenate([steps, jnp.zeros_like(steps)], axis=0)
         for p in range(message.per_chunk):
             part = steps if p == 0 else pltpu.roll(steps, LANES - p * r, 1)
-            out_ref[i * message.per_chunk + p, LAST * r :, :] = part.astype(bf16)
+            mine[i * message.per_chunk + p, LAST * r : LAST * r + STEP_ROWS, :] = part.astype(bf16)
 
     @pl.when(c == pl.num_programs(0) - 1)
     def _():
-        param_ref[...] = early_ref[...]
+        late = []
         for k in range(2):
             column = jnp.sum(sums[k * HEADS : (k + 1) * HEADS, :], axis=1, keepdims=True)
             block = jnp.broadcast_to(column, (HEADS, LANES))
             block = jnp.concatenate([block, jnp.zeros((LANES - HEADS, LANES), f32)], axis=0)
-            param_ref[PAIRS + 1 + k : PAIRS + 2 + k, :] = block.T[0:1, :]
+            late += three_terms(block.T[0:1, :])
+        late += [jnp.zeros((HEADS - 2 * TERMS, LANES), f32)]
+        late = jnp.concatenate([jnp.zeros((HEADS, LANES), f32)] + late, axis=0)
+        late = late.astype(bf16)
+        early = three_terms(early_ref[:PAIRS, :]) + three_terms(early_ref[PAIRS : PAIRS + 1, :])
+        early += [jnp.zeros((STEP_ROWS - TERMS * (PAIRS + 1), LANES), f32)]
+        early = jnp.concatenate(early, axis=0).astype(bf16)
+        own_rows = lax.broadcasted_iota(jnp.int32, (STEP_ROWS, LANES), 0) < HEADS
+
+        def fill(peer, unused):
+            steps_at = slice(LAST * r, LAST * r + STEP_ROWS)
+            out_ref[peer, steps_at, :] = jnp.where(own_rows, out_ref[peer, steps_at, :], late)
+            out_ref[peer, LAST * r + STEP_ROWS :, :] = early
+            return unused
+
+        lax.fori_loop(0, out_ref.shape[0], fill, 0)
 
 
 def call(kernel, out_shape, flops, moved, grid=None, in_specs=None, out_specs=None, scratch=()):
@@ -442,7 +510,7 @@
         kernel,
         out_shape=out_shape,
         scratch_shapes=list(scratch),
-        compiler_params=pltpu.CompilerParams(vmem_limit_bytes=60 * 1024 * 1024),
+        compiler_params=pltpu.CompilerParams(vmem_limit_bytes=16 * 1024 * 1024),
         cost_estimate=pl.CostEstimate(flops=flops, bytes_accessed=moved, transcendentals=0),
         **extra,
     )
@@ -514,15 +582,16 @@
 
     first_rows = FIRST * rows + STEP_ROWS
     second_rows = SECOND * rows
-    last_rows = LAST * rows + STEP_ROWS
+    gate_rows = GATES * rows
+    last_rows = LAST * rows + 2 * STEP_ROWS
 
     def packed(kernel, height, *arrays):
         out = struct((peers, height, LANES), bf16)
         moved = 4 * peers * height * LANES
         return call(lambda *refs: kernel(owners, *refs), out, 0, moved)(*arrays)
 
-    first = exchange(packed(pack_first, first_rows, mixer_x, b_matrix, raw_steps))
-    second = exchange(packed(pack_second, second_rows, gate_z, out_grad, c_matrix))
+    first = exchange(packed(pack_first, first_rows, mixer_x, b_matrix, c_matrix, raw_steps))
+    second = exchange(packed(pack_second, second_rows, gate_z, out_grad))
 
     def flow(kernel, shape_specs, flops, moved, in_specs, scratch=()):
         def body(*refs):
@@ -582,10 +651,9 @@
         [(struct((tokens, WIDTH)), up["token"](WIDTH))],
         4 * unit, size * 8,
         [
-            up["message"](first_rows), up["message"](second_rows),
-            up["token"](LANES), up["lane"](KINDS * HEADS),
-        ],
-    )(first, second, sm, smt)
+            up["message"](first_rows), up["token"](LANES), up["lane"](KINDS * HEADS),
+        ],
+    )(first, sm, smt)
 
     y, starts, sums = flow(
         mix_kernel,
@@ -631,31 +699,29 @@
     )(first, second, y, sm, starts, dec, sums, partner, own_gain, skip_row)
 
     outer = carry_over(slab_back, decay, after, slab_count, -1)
-    gates_back = exchange(d_gates)
-
-    d_values, d_sources, d_readers = flow(
+    params = sum_over(params, "slab", slab_count)
+
+    d_values, d_sources, gates_message = flow(
         local_kernel,
         [
             (struct((tokens, WIDTH)), up["token"](WIDTH)),
             (struct((tokens, STATE)), up["token"](STATE)),
-            (struct((tokens, STATE), bf16), up["token"](STATE)),
+            (struct((peers, gate_rows, LANES), bf16), up["message"](gate_rows)),
         ],
         8 * unit, size * 8,
         [
-            up["message"](first_rows), up["message"](second_rows), up["token"](WIDTH),
-            up["token"](LANES), up["lane"](KINDS * HEADS), up["token"](STATE),
-        ],
-    )(first, second, d_mixed, sm, smt, readers_part)
-
-    last, params = flow(
+            up["message"](first_rows), up["token"](WIDTH), up["token"](LANES),
+            up["lane"](KINDS * HEADS), up["token"](STATE), up["message"](PAIRS * rows),
+        ],
+    )(first, d_mixed, sm, smt, readers_part, d_gates)
+    gates_back = exchange(gates_message)
+
+    (last,) = flow(
         last_kernel,
-        [
-            (struct((peers, last_rows, LANES), bf16), dn["message"](last_rows)),
-            (struct((8, LANES)), whole(8, LANES)),
-        ],
+        [(struct((peers, last_rows, LANES), bf16), whole(peers, last_rows, LANES))],
         4 * unit, size * 16,
         [
-            dn["message"](first_rows), dn["token"](WIDTH), dn["token"](STATE), dn["token"](STATE),
+            dn["message"](first_rows), dn["token"](WIDTH), dn["token"](STATE),
             dn["token"](WIDTH), dn["lane"](HEADS), dn["token"](LANES), dn["lane"](KINDS * HEADS),
             whole(STATE, WIDTH), dn["chunk"](STATE, WIDTH), dn["chunk"](STATE, WIDTH),
             dn["chunk"](8, WIDTH), whole(1, WIDTH), whole(2 * HEADS, LANES), whole(8, LANES),
@@ -667,36 +733,50 @@
             pltpu.VMEM((16, WIDTH), f32),
         ],
     )(
-        first, d_values, d_sources, d_readers, d_mixed, e, sm, smt, outer, back, starts, dec,
+        first, d_values, d_sources, d_mixed, e, sm, smt, outer, back, starts, dec,
         skip_row, heads, params,
     )
 
     last_back = exchange(last)
-    params = sum_over(params, "slab", slab_count)
-    mine = lax.broadcasted_iota(jnp.int32, (sub_count, 1, 1), 0) == sub
-    params = sum_over(jnp.where(mine, params[None], 0.0), "sub", sub_count)
-    grad_gates = call(
+    grad_gates, grad_c = call(
         lambda *refs: unpack_gates(owners, *refs),
-        struct((rows, CHANNELS), bf16), 0, 4 * rows * CHANNELS,
+        (struct((rows, CHANNELS), bf16), struct((rows, GROUPS * STATE), bf16)),
+        0, 4 * rows * CHANNELS,
     )(gates_back)
-    grad_x, grad_b, grad_c, grad_steps = call(
+
+    tile_at = LAST * rows // STEP_ROWS
+    mine = lax.broadcasted_iota(jnp.int32, (tensor_count, LANES), 0) == lax.axis_index("tensor")
+
+    def tile(at):
+        return pl.BlockSpec((peers, STEP_ROWS, LANES), lambda c: (0, at, 0))
+
+    late, gain, skip = call(
+        lambda *refs: unpack_params(sub_count, tensor_count, *refs),
+        (struct((8, LANES)), struct((sub_count * PAIRS, LANES)), struct((1, LANES))),
+        0, 4 * peers * STEP_ROWS * LANES, (1,),
+        [tile(tile_at), tile(tile_at + 1), whole(tensor_count, LANES)],
+        (whole(8, LANES), whole(sub_count * PAIRS, LANES), whole(1, LANES)),
+    )(last_back, last_back, mine.astype(f32))
+    late = sum_over(late, "slab", slab_count)
+    grad_x, grad_b, grad_steps = call(
         lambda *refs: unpack_last(owners, *refs),
         (
             struct((rows, CHANNELS), bf16), struct((rows, GROUPS * STATE), bf16),
-            struct((rows, GROUPS * STATE), bf16), struct((rows, MIXER_HEADS), bf16),
+            struct((rows, MIXER_HEADS), bf16),
         ),
         0, 6 * rows * CHANNELS,
     )(last_back)
+    count = sub_count * HEADS
     return (
         grad_x,
         grad_gates,
         grad_b,
         grad_c,
         grad_steps,
-        params[:, PAIRS + 1, :HEADS].reshape(-1),
-        params[:, PAIRS, :HEADS].reshape(-1),
-        params[:, PAIRS + 2, :HEADS].reshape(-1),
-        params[:, :PAIRS].reshape(-1),
+        late[0, :count],
+        skip[0, :count],
+        late[1, :count],
+        gain.reshape(-1),
     )
 
 

time: 167 us -> 164 us (0.982)
  Pallas kernels: 54.6 us -> 33.2 us
  local copies, waits for them, and re-layouts: 9.61 us -> 29.1 us
  starting transfers between devices: 38.3 us -> 35.4 us
  waiting for transfers between devices: 62.5 us -> 64.5 us
    unnamed x22 -> x62, local copies, waits for them, and re-layouts: 4.23 us -> 26.8 us
    ppermute x4 -> x2, waiting for transfers between devices: 29.3 us -> 14.9 us  [sum_over(): lax.ppermute(array, axis, [(i, i ^ step) for i in range(count)])]
    ppermute x2, waiting for transfers between devices: 1.28 us -> 11.2 us  [shifted(): return lax.ppermute(array, 'slab', pairs)]
    all_to_all x4, waiting for transfers between devices: 30.5 us -> 37.2 us  [exchange(): lax.all_to_all(array, ('sub', 'tensor'), split_axis=0, concat_axis=0, til...]
    all_to_all x4, starting transfers between devices: 31.7 us -> 25.8 us  [exchange(): lax.all_to_all(array, ('sub', 'tensor'), split_axis=0, concat_axis=0, til...]
    pallas_call x2, Pallas kernels: 6 us -> 1.8 us  [packed(): return call(lambda *refs: kernel(owners, *refs), out, 0, moved)(*arrays)]
    pallas_call x2 -> x3, Pallas kernels: 11.4 us -> 7.75 us  [the longest x1 5.91 us: on_device(): flow(last_kernel, [(struct((peers, last_rows, LANES), bf16), whole(peers,...]
    ppermute x4 -> x2, starting transfers between devices: 0.74 us -> 3.74 us  [sum_over(): lax.ppermute(array, axis, [(i, i ^ step) for i in range(count)])]
  transfers between devices with their start and end apart: 11 -> 9, of which waited for: 8 -> 6; matrix products, arithmetic and copies ran while one was open for 3% -> 1% of each run, Pallas kernels for 20% -> 11%
where the time goes in v3:
time: 164 us; the launch traced here: 163 us
  waiting for transfers between devices  64.5 us (39%)
  starting transfers between devices  35.4 us (22%)
  Pallas kernels  33.2 us (20%)
  local copies, waits for them, and re-layouts  29.1 us (18%)
    all_to_all x4, waiting for transfers between devices, exchange(): lax.all_to_all(array, ('sub', 'tensor'), split_axis=0, concat_axis=0, til...  37.2 us
    unnamed x62, local copies, waits for them, and re-layouts  26.8 us
    all_to_all x4, starting transfers between devices, exchange(): lax.all_to_all(array, ('sub', 'tensor'), split_axis=0, concat_axis=0, til...  25.8 us
    ppermute x2, waiting for transfers between devices, sum_over(): lax.ppermute(array, axis, [(i, i ^ step) for i in range(count)])  14.9 us
    ppermute x2, waiting for transfers between devices, shifted(): return lax.ppermute(array, 'slab', pairs)  11.2 us
    pallas_call x1, Pallas kernels, on_device(): flow(state_kernel, [(struct((tokens, LANES)), up['token'](LANES)), (struc...  6.47 us
    pallas_call x1, Pallas kernels, on_device(): flow(norm_kernel, [(struct((peers, PAIRS * rows, LANES), bf16), up['messa...  6.07 us
    pallas_call x1, Pallas kernels, on_device(): flow(last_kernel, [(struct((peers, last_rows, LANES), bf16), whole(peers,...  5.91 us
  transfers between devices with their start and end apart: 9, of which 6 were waited for; matrix products, arithmetic and copies ran while one was open for 1% of the time, Pallas kernels for 11%

profile of v3, /device:TPU:0, one launch (start us, length us, event | category | flops | bytes accessed | tf_op | source)
XLA Modules:
  0.0 163.3 jit_solution(18180862860509427296)
XLA Ops:
  4.4 1.4 shard_map.169
  5.8 6.4 %all-to-all-start = ((bf16[16,400,128]{2,1,0:T(8,128)(2,1)}), bf16[16,400,128]{2,1,0:T(8,128)(2,1)S(1)}, u32[]{:S(2)}, u32[]{:S(2)}) async-start(bf16[16,400,128]{2,1,0:T(8,128)(2,1)} %shard_map.169), calls=%async_computation | async-start | bytes 3276800 | tf_op jit(solution)/shard_map/all_to_all | solution.py:574
  15.2 18.9 %all-to-all-done.refs_0_ = bf16[16,400,128]{2,1,0:T(8,128)(2,1)S(1)} async-done(((bf16[16,400,128]{2,1,0:T(8,128)(2,1)}), bf16[16,400,128]{2,1,0:T(8,128)(2,1)S(1)}, u32[]{:S(2)}, u32[]{:S(2)}) %all-to-all-start) | async-done | bytes 1638432 | tf_op jit(solution)/shard_map/all_to_all | solution.py:574
  34.1 4.6 %all-to-all-start.1 = ((bf16[16,512,128]{2,1,0:T(8,128)(2,1)}), bf16[16,512,128]{2,1,0:T(8,128)(2,1)}, u32[]{:S(2)}, u32[]{:S(2)}) async-start(bf16[16,512,128]{2,1,0:T(8,128)(2,1)} %copy-done), calls=%async_computation.1 | async-start | bytes 4194304 | tf_op jit(solution)/shard_map/all_to_all | solution.py:574
  39.0 6.5 %shard_map.171 = (f32[1024,128]{1,0:T(8,128)S(1)}, f32[64,1024]{1,0:T(8,128)S(1)}, f32[8,128,512]{2,1,0:T(8,128)S(1)}, f32[8,8,512]{2,1,0:T(8,128)S(1)}, bf16[128,512]{1,0:T(8,128)(2,1)S(1)}, /*index=5*/f32[8,512]{1,0:T(8,128)}) custom-call(bf16[16,400,128]{2,1,0:T(8,128)(2,1)S(1)} %all-to-all-done.refs_0_, f32[16,128]{1,0:T(8,128)S(1)} %broadcast_in_dim.4.refs_1_.refs_12_), custom_call_target="tpu_custom_call" | custom-call | flops 268435456 | bytes 4194304 | tf_op jit(solution)/shard_map/pallas_call | solution.py:629
  46.9 4.5 %collective-permute-start = (bf16[128,512]{1,0:T(8,128)(2,1)S(1)}, bf16[128,512]{1,0:T(8,128)(2,1)S(1)}, u32[]{:S(2)}, u32[]{:S(2)}) collective-permute-start(bf16[128,512]{1,0:T(8,128)(2,1)S(1)} %get-tuple-element.37), channel_id=1, source_target_pairs={{0,16},{1,17},{2,18},{3,19},{4,20},{5,21},{6,22},{7,23},{8,24},{9,... | collective-permute-start | bytes 393224 | tf_op jit(solution)/shard_map/ppermute | solution.py:521
  52.4 2.4 %shard_map.172.refs_2_ = f32[1024,512]{1,0:T(8,128)S(1)} custom-call(bf16[16,400,128]{2,1,0:T(8,128)(2,1)S(1)} %all-to-all-done.refs_0_, f32[1024,128]{1,0:T(8,128)S(1)} %get-tuple-element.35.refs_1_.refs_3_.refs_2_.refs_5_, f32[64,1024]{1,0:T(8,128)S(1)} %get-tuple-element.36.refs_2_.refs_3_.refs_6_), custom_call_target="tpu_custom_call" | custom-call | flops 536870912 | bytes 4194304 | tf_op jit(solution)/shard_map/pallas_call | solution.py:649
  54.8 1.4 copy-done.1
  56.2 11.2 %collective-permute-done.refs_4_ = bf16[128,512]{1,0:T(8,128)(2,1)S(1)} collective-permute-done((bf16[128,512]{1,0:T(8,128)(2,1)S(1)}, bf16[128,512]{1,0:T(8,128)(2,1)S(1)}, u32[]{:S(2)}, u32[]{:S(2)}) %collective-permute-start) | collective-permute-done | bytes 131104 | tf_op jit(solution)/shard_map/ppermute | solution.py:521
  67.4 1.6 copy-done.2
  69.0 1.6 copy-done.13
  70.6 4.1 %shard_map.173 = (f32[1024,512]{1,0:T(8,128)S(1)}, f32[8,128,512]{2,1,0:T(8,128)S(1)}, f32[8,8,128]{2,1,0:T(8,128)S(1)}) custom-call(bf16[16,400,128]{2,1,0:T(8,128)(2,1)S(1)} %all-to-all-done.refs_0_, bf16[16,512,128]{2,1,0:T(8,128)(2,1)} %all-to-all-done.1.refs_1_, f32[1024,512]{1,0:T(8,128)S(1)} %copy-done.2, ...), custom_call_target="tpu_custom_call" | custom-call | flops 268435456 | bytes 10485760 | tf_op jit(solution)/shard_map/pallas_call | solution.py:658
  76.0 6.1 %shard_map.174 = (bf16[16,256,128]{2,1,0:T(8,128)(2,1)S(1)}, bf16[1024,512]{1,0:T(8,128)(2,1)S(1)}, f32[8,1024]{1,0:T(8,128)S(1)}, f32[8,128,512]{2,1,0:T(8,128)...) custom-call(bf16[16,400,128]{2,1,0:T(8,128)(2,1)S(1)} %all-to-all-done.refs_0_, ...), custom_call_target="tpu_custom_call" | custom-call | flops 536870912 | bytes 10485760 | tf_op jit(solution)/shard_map/pallas_call | solution.py:676
  83.4 3.4 %shard_map.175 = (f32[1024,512]{1,0:T(8,128)S(1)}, f32[1024,128]{1,0:T(8,128)S(1)}, bf16[16,320,128]{2,1,0:T(8,128)(2,1)S(1)}) custom-call(bf16[16,400,128]{2,1,0:T(8,128)(2,1)S(1)} %all-to-all-done.refs_0_, bf16[1024,512]{1,0:T(8,128)(2,1)S(1)} %get-tuple-element.43.refs_1_.refs_3_, f32[1024,128]{1,0:T(8,128)S(1)} %get-tuple-element.35.refs_1_.refs_3_.refs_2_.refs_5_, ...), custom_call_target="tpu_custom_call" | custom-call | flops 1073741824 | bytes 4194304 | tf_op jit(solution)/shard_map/pallas_call | solution.py:704
  90.1 4.3 %all-to-all-start.3 = ((bf16[16,320,128]{2,1,0:T(8,128)(2,1)}), bf16[16,320,128]{2,1,0:T(8,128)(2,1)S(1)}, u32[]{:S(2)}, u32[]{:S(2)}) async-start(bf16[16,320,128]{2,1,0:T(8,128)(2,1)} %copy-done.16), calls=%async_computation.3 | async-start | bytes 2621440 | tf_op jit(solution)/shard_map/all_to_all | solution.py:574
  95.7 3.7 %collective-permute-start.3 = (f32[8,128]{1,0:T(8,128)S(1)}, f32[8,128]{1,0:T(8,128)S(1)}, u32[]{:S(2)}, u32[]{:S(2)}) collective-permute-start(f32[8,128]{1,0:T(8,128)S(1)} %get-tuple-element.51), channel_id=1, source_target_pairs={{0,16},{16,0},{1,17},{17,1},{2,18},{18,2},{3,19},{19,3},{4,20},{20... | collective-permute-start | bytes 12296 | tf_op jit(solution)/shard_map/ppermute | solution.py:551
  99.5 12.1 %collective-permute-done.3 = f32[8,128]{1,0:T(8,128)S(1)} collective-permute-done((f32[8,128]{1,0:T(8,128)S(1)}, f32[8,128]{1,0:T(8,128)S(1)}, u32[]{:S(2)}, u32[]{:S(2)}) %collective-permute-start.3) | collective-permute-done | bytes 4128 | tf_op jit(solution)/shard_map/ppermute | solution.py:551
  111.6 1.6 copy-done.4
  115.4 1.6 copy-done.11
  116.9 1.6 copy-done.15
  120.5 5.9 %shard_map.176 = bf16[16,352,128]{2,1,0:T(8,128)(2,1)S(1)} custom-call(bf16[16,400,128]{2,1,0:T(8,128)(2,1)S(1)} %all-to-all-done.refs_0_, f32[1024,512]{1,0:T(8,128)S(1)} %copy-done.15, f32[1024,128]{1,0:T(8,128)S(1)} %copy-done.23, bf16[1024,512]{1,0:T(8,128)(2,1)S(1)} %copy-done.7, f32[8,1024]{1,0:T(8,128)S(1)} %get-tuple-element.48.refs_4_, ...), custom_call_target="tpu_custom_call" | custom-call | flops 536870912 | bytes 8388608 | tf_op jit(solution)/shard_map/pallas_call | solution.py:719
  127.5 10.5 %all-to-all-start.2 = ((bf16[16,352,128]{2,1,0:T(8,128)(2,1)}), bf16[16,352,128]{2,1,0:T(8,128)(2,1)S(1)}, u32[]{:S(2)}, u32[]{:S(2)}) async-start(bf16[16,352,128]{2,1,0:T(8,128)(2,1)} %copy-done.5), calls=%async_computation.2 | async-start | bytes 2883584 | tf_op jit(solution)/shard_map/all_to_all | solution.py:574
  139.2 18.3 %all-to-all-done.2.refs_0_.refs_1_ = bf16[16,352,128]{2,1,0:T(8,128)(2,1)S(1)} async-done(((bf16[16,352,128]{2,1,0:T(8,128)(2,1)}), bf16[16,352,128]{2,1,0:T(8,128)(2,1)S(1)}, u32[]{:S(2)}, u32[]{:S(2)}) %all-to-all-start.2) | async-done | bytes 1441824 | tf_op jit(solution)/shard_map/all_to_all | solution.py:574
  160.0 2.8 %collective-permute-done.4 = f32[8,128]{1,0:T(8,128)S(1)} collective-permute-done((f32[8,128]{1,0:T(8,128)S(1)}, f32[8,128]{1,0:T(8,128)S(1)}, u32[]{:S(2)}, u32[]{:S(2)}) %collective-permute-start.4) | collective-permute-done | bytes 4128 | tf_op jit(solution)/shard_map/ppermute | solution.py:551
  (81 shorter events, 25.9 us)
Async XLA Ops:
  5.8 6.4 %copy-start.20 = (bf16[64,8192]{1,0:T(8,128)(2,1)S(1)}, bf16[64,8192]{1,0:T(8,128)(2,1)}, u32[]{:S(2)}) copy-start(bf16[64,8192]{1,0:T(8,128)(2,1)} %refs_0_.3) | copy-start | bytes 3145732
  5.8 28.2 %all-to-all-start = ((bf16[16,400,128]{2,1,0:T(8,128)(2,1)}), bf16[16,400,128]{2,1,0:T(8,128)(2,1)S(1)}, u32[]{:S(2)}, u32[]{:S(2)}) async-start(bf16[16,400,128]{2,1,0:T(8,128)(2,1)} %shard_map.169), calls=%async_computation | async-start | bytes 3276800 | tf_op jit(solution)/shard_map/all_to_all | solution.py:574
  15.2 23.5 %copy-start.28 = (f32[64]{0:T(128)S(1)}, f32[64]{0:T(128)}, u32[]{:S(2)}) copy-start(f32[64]{0:T(128)} %param.15) | copy-start | bytes 772
  15.2 23.6 %copy-start.29 = (f32[64]{0:T(128)S(1)}, f32[64]{0:T(128)}, u32[]{:S(2)}) copy-start(f32[64]{0:T(128)} %param.17) | copy-start | bytes 772
  15.2 36.1 %copy-start.30 = (f32[64]{0:T(128)S(1)}, f32[64]{0:T(128)}, u32[]{:S(2)}) copy-start(f32[64]{0:T(128)} %param.16) | copy-start | bytes 772
  34.1 33.4 %all-to-all-start.1 = ((bf16[16,512,128]{2,1,0:T(8,128)(2,1)}), bf16[16,512,128]{2,1,0:T(8,128)(2,1)}, u32[]{:S(2)}, u32[]{:S(2)}) async-start(bf16[16,512,128]{2,1,0:T(8,128)(2,1)} %copy-done), calls=%async_computation.1 | async-start | bytes 4194304 | tf_op jit(solution)/shard_map/all_to_all | solution.py:574
  46.9 29.1 %copy-start.17 = (f32[8,8,512]{2,1,0:T(8,128)}, f32[8,8,512]{2,1,0:T(8,128)S(1)}, u32[]{:S(2)}) copy-start(f32[8,8,512]{2,1,0:T(8,128)S(1)} %get-tuple-element.39.refs_6_.refs_5_.refs_10_) | copy-start | bytes 393220
  46.9 36.6 %copy-start.8 = (f32[64,1024]{1,0:T(8,128)}, f32[64,1024]{1,0:T(8,128)S(1)}, u32[]{:S(2)}) copy-start(f32[64,1024]{1,0:T(8,128)S(1)} %get-tuple-element.36.refs_2_.refs_3_.refs_6_) | copy-start | bytes 786436
  46.9 20.6 %collective-permute-start = (bf16[128,512]{1,0:T(8,128)(2,1)S(1)}, bf16[128,512]{1,0:T(8,128)(2,1)S(1)}, u32[]{:S(2)}, u32[]{:S(2)}) collective-permute-start(bf16[128,512]{1,0:T(8,128)(2,1)S(1)} %get-tuple-element.37), channel_id=1, source_target_pairs={{0,16},{1,17},{2,18},{3,19},{4,20},{5,21},{6,22},{7,23},{8,24},{9,... | collective-permute-start | bytes 393224 | tf_op jit(solution)/shard_map/ppermute | solution.py:521
  54.8 1.4 copy-start.1
  67.4 1.6 copy-start.2
  69.0 1.6 copy-start.13
  74.7 7.4 %copy-start.3 = (f32[8,128,512]{2,1,0:T(8,128)}, f32[8,128,512]{2,1,0:T(8,128)S(1)}, u32[]{:S(2)}) copy-start(f32[8,128,512]{2,1,0:T(8,128)S(1)} %get-tuple-element.41.refs_4_.refs_9_) | copy-start | bytes 6291460
  74.7 1.3 collective-permute-start.1
  83.4 3.4 %copy-start.6 = (bf16[1024,512]{1,0:T(8,128)(2,1)}, bf16[1024,512]{1,0:T(8,128)(2,1)S(1)}, u32[]{:S(2)}) copy-start(bf16[1024,512]{1,0:T(8,128)(2,1)S(1)} %get-tuple-element.43.refs_1_.refs_3_) | copy-start | bytes 3145732
  83.4 3.4 %copy-start.27 = (bf16[128,512]{1,0:T(8,128)(2,1)}, bf16[128,512]{1,0:T(8,128)(2,1)S(1)}, u32[]{:S(2)}) copy-start(bf16[128,512]{1,0:T(8,128)(2,1)S(1)} %get-tuple-element.49) | copy-start | bytes 393220
  90.1 37.4 %all-to-all-start.3 = ((bf16[16,320,128]{2,1,0:T(8,128)(2,1)}), bf16[16,320,128]{2,1,0:T(8,128)(2,1)S(1)}, u32[]{:S(2)}, u32[]{:S(2)}) async-start(bf16[16,320,128]{2,1,0:T(8,128)(2,1)} %copy-done.16), calls=%async_computation.3 | async-start | bytes 2621440 | tf_op jit(solution)/shard_map/all_to_all | solution.py:574
  94.4 17.1 %collective-permute-start.2 = (bf16[128,512]{1,0:T(8,128)(2,1)}, bf16[128,512]{1,0:T(8,128)(2,1)S(1)}, u32[]{:S(2)}, u32[]{:S(2)}) collective-permute-start(bf16[128,512]{1,0:T(8,128)(2,1)} %copy-done.27), channel_id=1, source_target_pairs={{16,0},{17,1},{18,2},{19,3},{20,4},{21,5},{22,6},{23,7},{24,8},{25... | collective-permute-start | bytes 393224 | tf_op jit(solution)/shard_map/ppermute | solution.py:521
  95.7 15.8 %collective-permute-start.3 = (f32[8,128]{1,0:T(8,128)S(1)}, f32[8,128]{1,0:T(8,128)S(1)}, u32[]{:S(2)}, u32[]{:S(2)}) collective-permute-start(f32[8,128]{1,0:T(8,128)S(1)} %get-tuple-element.51), channel_id=1, source_target_pairs={{0,16},{16,0},{1,17},{17,1},{2,18},{18,2},{3,19},{19,3},{4,20},{20... | collective-permute-start | bytes 12296 | tf_op jit(solution)/shard_map/ppermute | solution.py:551
  111.6 1.6 copy-start.4
  115.4 1.6 copy-start.11
  116.9 1.6 copy-start.15
  127.5 30.0 %all-to-all-start.2 = ((bf16[16,352,128]{2,1,0:T(8,128)(2,1)}), bf16[16,352,128]{2,1,0:T(8,128)(2,1)S(1)}, u32[]{:S(2)}, u32[]{:S(2)}) async-start(bf16[16,352,128]{2,1,0:T(8,128)(2,1)} %copy-done.5), calls=%async_computation.2 | async-start | bytes 2883584 | tf_op jit(solution)/shard_map/all_to_all | solution.py:574
  158.3 4.5 %collective-permute-start.4 = (f32[8,128]{1,0:T(8,128)S(1)}, f32[8,128]{1,0:T(8,128)S(1)}, u32[]{:S(2)}, u32[]{:S(2)}) collective-permute-start(f32[8,128]{1,0:T(8,128)S(1)} %get-tuple-element.58), channel_id=1, source_target_pairs={{0,16},{16,0},{1,17},{17,1},{2,18},{18,2},{3,19},{19,3},{4,20},{20... | collective-permute-start | bytes 12296 | tf_op jit(solution)/shard_map/ppermute | solution.py:551
  (16 other events, 17.5 us)

commit v4 on v3

--- a/solution.py
+++ b/solution.py
@@ -55,6 +55,10 @@
     return both[:, :width] + both[:, width:]
 
 
+def sigmoid(values):
+    return 0.5 + 0.5 * jnp.tanh(0.5 * values)
+
+
 def low_half(rows):
     return lax.broadcasted_iota(jnp.int32, (rows, LANES), 1) < HEAD_DIM
 
@@ -116,27 +120,34 @@
 TERMS = 3
 
 
-def pack_first(owners, x_ref, b_ref, c_ref, steps_ref, out_ref):
+def pack_first(x_ref, b_ref, c_ref, steps_ref, out_ref, by_head):
     r = x_ref.shape[0]
-    steps = steps_ref[...].astype(f32)
-    padded = jnp.concatenate([steps, jnp.zeros((LANES - r, LANES), f32)], axis=0)
-    by_head = padded.T
+    step = pl.program_id(0)
+    subs = out_ref.shape[0]
+
+    @pl.when(step == 0)
+    def _():
+        steps = steps_ref[...].astype(f32)
+        by_head[...] = jnp.concatenate([steps, jnp.zeros((LANES - r, LANES), f32)], axis=0).T
+
     zero = jnp.zeros((STEP_ROWS - HEADS, LANES), f32)
-    for peer, own in enumerate(owners):
-        for j in range(PAIRS):
-            out_ref[peer, j * r : (j + 1) * r, :] = x_ref[:, lanes(own * PAIRS + j)]
-        out_ref[peer, B * r : (B + 1) * r, :] = b_ref[:, lanes(own // 2)]
-        out_ref[peer, C * r : (C + 1) * r, :] = c_ref[:, lanes(own // 2)]
-        mine = jnp.concatenate([by_head[own * HEADS : (own + 1) * HEADS, :], zero], axis=0)
-        out_ref[peer, FIRST * r :, :] = mine.astype(bf16)
-
-
-def pack_second(owners, z_ref, grad_ref, out_ref):
+    for s in range(subs):
+        for j in range(PAIRS):
+            out_ref[s, 0, j * r : (j + 1) * r, :] = x_ref[:, lanes(s * PAIRS + j)]
+        out_ref[s, 0, B * r : (B + 1) * r, :] = b_ref[:, lanes(s // 2)]
+        out_ref[s, 0, C * r : (C + 1) * r, :] = c_ref[:, lanes(s // 2)]
+        at = pl.multiple_of((step * subs + s) * HEADS, HEADS)
+        mine = jnp.concatenate([by_head[pl.ds(at, HEADS), :], zero], axis=0)
+        out_ref[s, 0, FIRST * r :, :] = mine.astype(bf16)
+
+
+def pack_second(z_ref, grad_ref, out_ref):
     r = z_ref.shape[0]
-    for peer, own in enumerate(owners):
-        for j in range(PAIRS):
-            out_ref[peer, (Z + j) * r : (Z + j + 1) * r, :] = z_ref[:, lanes(own * PAIRS + j)]
-            out_ref[peer, (GRAD + j) * r : (GRAD + j + 1) * r, :] = grad_ref[:, lanes(own * PAIRS + j)]
+    for s in range(out_ref.shape[0]):
+        for j in range(PAIRS):
+            at = lanes(s * PAIRS + j)
+            out_ref[s, 0, (Z + j) * r : (Z + j + 1) * r, :] = z_ref[:, at]
+            out_ref[s, 0, (GRAD + j) * r : (GRAD + j + 1) * r, :] = grad_ref[:, at]
 
 
 def add_halves(owners, in_ref, block, out_ref):
@@ -181,7 +192,7 @@
     return [high, middle, rest - middle]
 
 
-def unpack_params(sub_count, tensor_count, late_ref, early_ref, mine_ref, late_out, gain_out, skip_out):
+def unpack_params(sub_count, tensor_count, late_ref, early_ref, mine_ref, out_ref):
     lane = lax.broadcasted_iota(jnp.int32, (1, LANES), 1)
     late = [jnp.zeros((1, LANES), f32) for _ in range(2)]
     skip = jnp.zeros((1, LANES), f32)
@@ -204,9 +215,8 @@
         part = placed(early_rows, TERMS * PAIRS)
         skip = skip + (part if s == 0 else pltpu.roll(part, s * HEADS, 1))
         gain = early_rows[:PAIRS] + early_rows[PAIRS : 2 * PAIRS] + early_rows[2 * PAIRS : 3 * PAIRS]
-        gain_out[s * PAIRS : (s + 1) * PAIRS, :] = gain
-    late_out[...] = jnp.concatenate(late + [jnp.zeros((6, LANES), f32)], axis=0)
-    skip_out[...] = skip
+        out_ref[8 + s * PAIRS : 8 + (s + 1) * PAIRS, :] = gain
+    out_ref[:8, :] = jnp.concatenate(late + [skip, jnp.zeros((5, LANES), f32)], axis=0)
 
 
 def state_kernel(
@@ -263,14 +273,23 @@
     state_ref[...] = carry[...].astype(bf16)
 
 
-def within_kernel(message, per_step, first_ref, sm_ref, smt_ref, out_ref):
+def forward_kernel(
+    message, per_step,
+    first_ref, sm_ref, smt_ref, inbound_ref, own_ref, dec_ref, y_ref, start_ref, carry,
+):
+    @pl.when(pl.program_id(0) == 0)
+    def _():
+        carry[...] = inbound_ref[...].astype(f32)
+
     t = lax.broadcasted_iota(jnp.int32, (CHUNK, CHUNK), 0)
     s = lax.broadcasted_iota(jnp.int32, (CHUNK, CHUNK), 1)
     for i in range(per_step):
         rows = slice(i * CHUNK, (i + 1) * CHUNK)
-        scores = mm_nt(message.get(first_ref, i, C), message.get(first_ref, i, B))
-        scores = jnp.where(t >= s, scores, 0.0)
-        for j in range(PAIRS):
+        sm = sm_ref[rows, :]
+        readers = message.get(first_ref, i, C)
+        scores = jnp.where(t >= s, mm_nt(readers, message.get(first_ref, i, B)), 0.0)
+        for j in range(PAIRS):
+            at = lanes(j)
             weights = []
             for h in (2 * j, 2 * j + 1):
                 here = sm_ref[rows, CUM * HEADS + h : CUM * HEADS + h + 1]
@@ -279,36 +298,25 @@
                     (scores * jnp.exp(jnp.minimum(here - there, CLAMP))).astype(bf16)
                 )
             values = split_pair(message.get(first_ref, i, X + j))
-            out_ref[rows, lanes(j)] = mm(jnp.concatenate(weights, axis=1), values)
-
-
-def mix_kernel(
-    message, per_step,
-    first_ref, second_ref, within_ref, sm_ref, inbound_ref, own_ref, dec_ref, gain_ref, skip_ref,
-    y_ref, start_ref, sums_ref,
-    carry,
-):
-    @pl.when(pl.program_id(0) == 0)
-    def _():
-        carry[...] = inbound_ref[...].astype(f32)
-
+            within = mm(jnp.concatenate(weights, axis=1), values)
+            state = carry[:, at]
+            start_ref[i, :, at] = state
+            carried = mm_two(readers, *two_terms(state))
+            carry[:, at] = dec_ref[i, 0:1, at] * state + own_ref[i, :, at]
+            y_ref[rows, at] = within + spread_pair(sm, ECUM, j) * carried
+
+
+def mix_kernel(message, per_step, first_ref, second_ref, y_ref, gain_ref, skip_ref, sums_ref):
     for i in range(per_step):
         rows = slice(i * CHUNK, (i + 1) * CHUNK)
-        sm = sm_ref[rows, :]
-        readers = message.get(first_ref, i, C)
         power = jnp.zeros((CHUNK, LANES), f32)
         cross = jnp.zeros((CHUNK, LANES), f32)
         for j in range(PAIRS):
-            state = carry[:, lanes(j)]
-            start_ref[i, :, lanes(j)] = state
-            carried = mm_two(readers, *two_terms(state))
-            carry[:, lanes(j)] = dec_ref[i, 0:1, lanes(j)] * state + own_ref[i, :, lanes(j)]
-            y = within_ref[rows, lanes(j)] + spread_pair(sm, ECUM, j) * carried
-            y_ref[rows, lanes(j)] = y
             values = message.get(first_ref, i, X + j).astype(f32)
             gates = message.get(second_ref, i, Z + j).astype(f32)
             grad = message.get(second_ref, i, GRAD + j).astype(f32)
-            gated = (y + skip_ref[0:1, lanes(j)] * values) * (gates / (1.0 + jnp.exp(-gates)))
+            mixed = y_ref[rows, lanes(j)] + skip_ref[0:1, lanes(j)] * values
+            gated = mixed * (gates * sigmoid(gates))
             power = power + gated * gated
             cross = cross + grad * gain_ref[0:1, lanes(j)] * gated
         sums_ref[i, 0:1, :] = jnp.sum(power.T, axis=0, keepdims=True)
@@ -349,7 +357,7 @@
             grad = message.get(second_ref, i, GRAD + j).astype(f32)
             y = y_ref[rows, at]
             mixed = y + skip_ref[0:1, at] * values
-            sig = 1.0 / (1.0 + jnp.exp(-gates))
+            sig = sigmoid(gates)
             silu = gates * sig
             gated = mixed * silu
             scaled = inverse * grad
@@ -570,6 +578,12 @@
     def struct(shape, kind=f32):
         return jax.ShapeDtypeStruct(shape, kind)
 
+    def hbm(shape, kind=f32):
+        return pltpu.HBM(shape, kind)
+
+    def in_hbm(array):
+        return pltpu.with_memory_space_constraint(array, pltpu.HBM)
+
     def exchange(array):
         return lax.all_to_all(array, ("sub", "tensor"), split_axis=0, concat_axis=0, tiled=True)
 
@@ -585,13 +599,28 @@
     gate_rows = GATES * rows
     last_rows = LAST * rows + 2 * STEP_ROWS
 
-    def packed(kernel, height, *arrays):
-        out = struct((peers, height, LANES), bf16)
+    def packed(kernel, height, arrays, whole_arrays=(), scratch=()):
+        out = hbm((sub_count, tensor_count, height, LANES), bf16)
         moved = 4 * peers * height * LANES
-        return call(lambda *refs: kernel(owners, *refs), out, 0, moved)(*arrays)
-
-    first = exchange(packed(pack_first, first_rows, mixer_x, b_matrix, c_matrix, raw_steps))
-    second = exchange(packed(pack_second, second_rows, gate_z, out_grad))
+        specs = [
+            pl.BlockSpec((rows, a.shape[1] // tensor_count), lambda t: (0, t)) for a in arrays
+        ] + [pl.BlockSpec(a.shape, lambda t: (0, 0)) for a in whole_arrays]
+        out_spec = pl.BlockSpec((sub_count, 1, height, LANES), lambda t: (0, t, 0, 0))
+        made = call(kernel, out, 0, moved, (tensor_count,), specs, out_spec, scratch)(
+            *(in_hbm(a) for a in (*arrays, *whole_arrays))
+        )
+        return made.reshape(peers, height, LANES)
+
+    first = exchange(
+        packed(
+            pack_first, first_rows, (mixer_x, b_matrix, c_matrix), (raw_steps,),
+            [pltpu.VMEM((LANES, LANES), f32)],
+        )
+    )
+    gate_z, heads, skip_row, own_gain = lax.optimization_barrier(
+        (gate_z, heads, skip_row, own_gain)
+    )
+    second = exchange(packed(pack_second, second_rows, (gate_z, out_grad)))
 
     def flow(kernel, shape_specs, flops, moved, in_specs, scratch=()):
         def body(*refs):
@@ -629,10 +658,10 @@
     sm, smt, own, dec, state, decay = flow(
         state_kernel,
         [
-            (struct((tokens, LANES)), up["token"](LANES)),
-            (struct((KINDS * HEADS, tokens)), up["lane"](KINDS * HEADS)),
-            (struct((chunks, STATE, WIDTH)), up["chunk"](STATE, WIDTH)),
-            (struct((chunks, 8, WIDTH)), up["chunk"](8, WIDTH)),
+            (hbm((tokens, LANES)), up["token"](LANES)),
+            (hbm((KINDS * HEADS, tokens)), up["lane"](KINDS * HEADS)),
+            (hbm((chunks, STATE, WIDTH)), up["chunk"](STATE, WIDTH)),
+            (hbm((chunks, 8, WIDTH)), up["chunk"](8, WIDTH)),
             (struct((STATE, WIDTH), bf16), whole(STATE, WIDTH)),
             (struct((8, WIDTH)), whole(8, WIDTH)),
         ],
@@ -646,30 +675,29 @@
         before, after = shifted(decay, slab_count, 1), shifted(decay, slab_count, -1)
     inbound = carry_over(state, decay, before, slab_count, 1)
 
-    (within,) = flow(
-        within_kernel,
-        [(struct((tokens, WIDTH)), up["token"](WIDTH))],
-        4 * unit, size * 8,
+    y, starts = flow(
+        forward_kernel,
+        [
+            (hbm((tokens, WIDTH)), up["token"](WIDTH)),
+            (hbm((chunks, STATE, WIDTH)), up["chunk"](STATE, WIDTH)),
+        ],
+        6 * unit, size * 16,
         [
             up["message"](first_rows), up["token"](LANES), up["lane"](KINDS * HEADS),
-        ],
-    )(first, sm, smt)
-
-    y, starts, sums = flow(
+            whole(STATE, WIDTH), up["chunk"](STATE, WIDTH), up["chunk"](8, WIDTH),
+        ],
+        [pltpu.VMEM((STATE, WIDTH), f32)],
+    )(first, in_hbm(sm), in_hbm(smt), inbound, in_hbm(own), in_hbm(dec))
+
+    (sums,) = flow(
         mix_kernel,
-        [
-            (struct((tokens, WIDTH)), up["token"](WIDTH)),
-            (struct((chunks, STATE, WIDTH)), up["chunk"](STATE, WIDTH)),
-            (struct((chunks, 8, LANES)), up["chunk"](8, LANES)),
-        ],
-        2 * unit, size * 20,
+        [(struct((chunks, 8, LANES)), up["chunk"](8, LANES))],
+        0, size * 12,
         [
             up["message"](first_rows), up["message"](second_rows), up["token"](WIDTH),
-            up["token"](LANES), whole(STATE, WIDTH), up["chunk"](STATE, WIDTH),
-            up["chunk"](8, WIDTH), whole(1, WIDTH), whole(1, WIDTH),
-        ],
-        [pltpu.VMEM((STATE, WIDTH), f32)],
-    )(first, second, within, sm, inbound, own, dec, own_gain, skip_row)
+            whole(1, WIDTH), whole(1, WIDTH),
+        ],
+    )(first, in_hbm(second), in_hbm(y), own_gain, skip_row)
 
     partner = lax.ppermute(sums, "sub", [(i, i ^ 1) for i in range(sub_count)])
 
@@ -677,9 +705,9 @@
         norm_kernel,
         [
             (struct((peers, PAIRS * rows, LANES), bf16), up["message"](PAIRS * rows)),
-            (struct((tokens, WIDTH), bf16), up["token"](WIDTH)),
-            (struct((HEADS, tokens)), up["lane"](HEADS)),
-            (struct((chunks, STATE, WIDTH)), up["chunk"](STATE, WIDTH)),
+            (hbm((tokens, WIDTH), bf16), up["token"](WIDTH)),
+            (hbm((HEADS, tokens)), up["lane"](HEADS)),
+            (hbm((chunks, STATE, WIDTH)), up["chunk"](STATE, WIDTH)),
             (struct((STATE, WIDTH), bf16), whole(STATE, WIDTH)),
             (struct((tokens, STATE)), up["token"](STATE)),
             (struct((8, LANES)), whole(8, LANES)),
@@ -696,29 +724,31 @@
             pltpu.VMEM((CHUNK, WIDTH), bf16), pltpu.VMEM((CHUNK, WIDTH), bf16),
             pltpu.VMEM((CHUNK, WIDTH), bf16),
         ],
-    )(first, second, y, sm, starts, dec, sums, partner, own_gain, skip_row)
+    )(
+        first, in_hbm(second), in_hbm(y), in_hbm(sm), in_hbm(starts), in_hbm(dec), sums, partner,
+        own_gain, skip_row,
+    )
 
     outer = carry_over(slab_back, decay, after, slab_count, -1)
-    params = sum_over(params, "slab", slab_count)
-
     d_values, d_sources, gates_message = flow(
         local_kernel,
         [
-            (struct((tokens, WIDTH)), up["token"](WIDTH)),
-            (struct((tokens, STATE)), up["token"](STATE)),
-            (struct((peers, gate_rows, LANES), bf16), up["message"](gate_rows)),
+            (hbm((tokens, WIDTH)), up["token"](WIDTH)),
+            (hbm((tokens, STATE)), up["token"](STATE)),
+            (hbm((peers, gate_rows, LANES), bf16), up["message"](gate_rows)),
         ],
         8 * unit, size * 8,
         [
             up["message"](first_rows), up["token"](WIDTH), up["token"](LANES),
             up["lane"](KINDS * HEADS), up["token"](STATE), up["message"](PAIRS * rows),
         ],
-    )(first, d_mixed, sm, smt, readers_part, d_gates)
+    )(first, in_hbm(d_mixed), in_hbm(sm), in_hbm(smt), readers_part, d_gates)
+    gates_message, outer = lax.optimization_barrier((gates_message, outer))
     gates_back = exchange(gates_message)
 
     (last,) = flow(
         last_kernel,
-        [(struct((peers, last_rows, LANES), bf16), whole(peers, last_rows, LANES))],
+        [(hbm((peers, last_rows, LANES), bf16), whole(peers, last_rows, LANES))],
         4 * unit, size * 16,
         [
             dn["message"](first_rows), dn["token"](WIDTH), dn["token"](STATE),
@@ -733,8 +763,8 @@
             pltpu.VMEM((16, WIDTH), f32),
         ],
     )(
-        first, d_values, d_sources, d_mixed, e, sm, smt, outer, back, starts, dec,
-        skip_row, heads, params,
+        first, in_hbm(d_values), in_hbm(d_sources), in_hbm(d_mixed), in_hbm(e), in_hbm(sm),
+        in_hbm(smt), outer, in_hbm(back), in_hbm(starts), in_hbm(dec), skip_row, heads, params,
     )
 
     last_back = exchange(last)
@@ -750,14 +780,14 @@
     def tile(at):
         return pl.BlockSpec((peers, STEP_ROWS, LANES), lambda c: (0, at, 0))
 
-    late, gain, skip = call(
+    params = call(
         lambda *refs: unpack_params(sub_count, tensor_count, *refs),
-        (struct((8, LANES)), struct((sub_count * PAIRS, LANES)), struct((1, LANES))),
+        struct((8 + sub_count * PAIRS, LANES)),
         0, 4 * peers * STEP_ROWS * LANES, (1,),
         [tile(tile_at), tile(tile_at + 1), whole(tensor_count, LANES)],
-        (whole(8, LANES), whole(sub_count * PAIRS, LANES), whole(1, LANES)),
+        whole(8 + sub_count * PAIRS, LANES),
     )(last_back, last_back, mine.astype(f32))
-    late = sum_over(late, "slab", slab_count)
+    params = sum_over(params, "slab", slab_count)
     grad_x, grad_b, grad_steps = call(
         lambda *refs: unpack_last(owners, *refs),
         (
@@ -773,10 +803,10 @@
         grad_b,
         grad_c,
         grad_steps,
-        late[0, :count],
-        skip[0, :count],
-        late[1, :count],
-        gain.reshape(-1),
+        params[0, :count],
+        params[2, :count],
+        params[1, :count],
+        params[8:].reshape(-1),
     )
 
 

time: 164 us -> 150 us (0.915)
  local copies, waits for them, and re-layouts: 29.1 us -> 2.42 us
  blocking collectives: 0 us -> 23.6 us
  starting transfers between devices: 35.4 us -> 22.7 us
  Pallas kernels: 33.2 us -> 45.9 us
  waiting for transfers between devices: 64.5 us -> 53.8 us
    unnamed x62 -> x6, local copies, waits for them, and re-layouts: 26.8 us -> 0.01 us
    all_to_all x0 -> x1, blocking collectives: none -> 23.6 us  [exchange(): lax.all_to_all(array, ('sub', 'tensor'), split_axis=0, concat_axis=0, til...]
    ppermute x2 -> x1, waiting for transfers between devices: 14.9 us -> 0.01 us  [sum_over(): lax.ppermute(array, axis, [(i, i ^ step) for i in range(count)])]
    all_to_all x4 -> x3, starting transfers between devices: 25.8 us -> 14.7 us  [exchange(): lax.all_to_all(array, ('sub', 'tensor'), split_axis=0, concat_axis=0, til...]
    pallas_call x8, Pallas kernels: 24.8 us -> 35.8 us  [the longest x1 8.63 us: on_device(): flow(last_kernel, [(hbm((peers, last_rows, LANES), bf16), whole(peers, la...]
    ppermute x2, waiting for transfers between devices: 11.2 us -> 19 us  [shifted(): return lax.ppermute(array, 'slab', pairs)]
    all_to_all x4 -> x3, waiting for transfers between devices: 37.2 us -> 33.6 us  [exchange(): lax.all_to_all(array, ('sub', 'tensor'), split_axis=0, concat_axis=0, til...]
    pallas_call x1, Pallas kernels: 6.07 us -> 7.72 us  [on_device(): flow(norm_kernel, [(struct((peers, PAIRS * rows, LANES), bf16), up['messa...]
  transfers between devices with their start and end apart: 9 -> 7, of which waited for: 6 -> 5; matrix products, arithmetic and copies ran while one was open for 1% -> 1% of each run, Pallas kernels for 11% -> 16%
where the time goes in v4:
time: 150 us; the launch traced here: 149 us
  waiting for transfers between devices  53.8 us (36%)
  Pallas kernels  45.9 us (31%)
  blocking collectives  23.6 us (16%)
  starting transfers between devices  22.7 us (15%)
  local copies, waits for them, and re-layouts  2.42 us (2%)
    all_to_all x3, waiting for transfers between devices, exchange(): lax.all_to_all(array, ('sub', 'tensor'), split_axis=0, concat_axis=0, til...  33.6 us
    all_to_all x1, blocking collectives, exchange(): lax.all_to_all(array, ('sub', 'tensor'), split_axis=0, concat_axis=0, til...  23.6 us
    ppermute x2, waiting for transfers between devices, shifted(): return lax.ppermute(array, 'slab', pairs)  19 us
    all_to_all x3, starting transfers between devices, exchange(): lax.all_to_all(array, ('sub', 'tensor'), split_axis=0, concat_axis=0, til...  14.7 us
    pallas_call x1, Pallas kernels, on_device(): flow(last_kernel, [(hbm((peers, last_rows, LANES), bf16), whole(peers, la...  8.63 us
    pallas_call x1, Pallas kernels, on_device(): flow(norm_kernel, [(struct((peers, PAIRS * rows, LANES), bf16), up['messa...  7.72 us
    pallas_call x1, Pallas kernels, on_device(): flow(state_kernel, [(hbm((tokens, LANES)), up['token'](LANES)), (hbm((KIN...  6.71 us
    pallas_call x1, Pallas kernels, on_device(): flow(forward_kernel, [(hbm((tokens, WIDTH)), up['token'](WIDTH)), (hbm((c...  5.96 us
  transfers between devices with their start and end apart: 7, of which 5 were waited for; matrix products, arithmetic and copies ran while one was open for 1% of the time, Pallas kernels for 16%

profile of v4, /device:TPU:0, one launch (start us, length us, event | category | flops | bytes accessed | tf_op | source)
XLA Modules:
  0.0 149.4 jit_solution(17413273972568318265)
XLA Ops:
  0.6 2.5 %shard_map.169 = bf16[8,2,400,128]{3,2,1,0:T(8,128)(2,1)} custom-call(bf16[64,8192]{1,0:T(8,128)(2,1)} %x_ref.1, bf16[64,1024]{1,0:T(8,128)(2,1)} %b_ref.1, bf16[64,1024]{1,0:T(8,128)(2,1)} %c_ref.1, bf16[64,128]{1,0:T(8,128)(2,1)} %steps_ref.1), custom_call_target="tpu_custom_call" | custom-call | bytes 3276800 | tf_op jit(solution)/shard_map/pallas_call | solution.py:609
  3.2 6.4 %all-to-all-start = ((bf16[16,400,128]{2,1,0:T(8,128)(2,1)}), bf16[16,400,128]{2,1,0:T(8,128)(2,1)S(1)}, u32[]{:S(2)}, u32[]{:S(2)}) async-start(bf16[16,400,128]{2,1,0:T(8,128)(2,1)} %bitcast.14), calls=%async_computation | async-start | bytes 3276800 | tf_op jit(solution)/shard_map/all_to_all | solution.py:588
  10.0 0.8 dynamic_slice.15
  10.9 2.7 %shard_map.170 = bf16[8,2,512,128]{3,2,1,0:T(8,128)(2,1)} custom-call(bf16[64,8192]{1,0:T(8,128)(2,1)} %z_ref, bf16[64,8192]{1,0:T(8,128)(2,1)} %grad_ref.1), custom_call_target="tpu_custom_call" | custom-call | bytes 4194304 | tf_op jit(solution)/shard_map/pallas_call | solution.py:609
  13.6 17.8 %all-to-all-done.refs_0_ = bf16[16,400,128]{2,1,0:T(8,128)(2,1)S(1)} async-done(((bf16[16,400,128]{2,1,0:T(8,128)(2,1)}), bf16[16,400,128]{2,1,0:T(8,128)(2,1)S(1)}, u32[]{:S(2)}, u32[]{:S(2)}) %all-to-all-start) | async-done | bytes 1638432 | tf_op jit(solution)/shard_map/all_to_all | solution.py:588
  31.4 4.6 %all-to-all-start.1 = ((bf16[16,512,128]{2,1,0:T(8,128)(2,1)}), bf16[16,512,128]{2,1,0:T(8,128)(2,1)}, u32[]{:S(2)}, u32[]{:S(2)}) async-start(bf16[16,512,128]{2,1,0:T(8,128)(2,1)} %bitcast.13), calls=%async_computation.1 | async-start | bytes 4194304 | tf_op jit(solution)/shard_map/all_to_all | solution.py:588
  36.0 6.7 %shard_map.171 = (f32[1024,128]{1,0:T(8,128)}, f32[64,1024]{1,0:T(8,128)}, f32[8,128,512]{2,1,0:T(8,128)}, f32[8,8,512]{2,1,0:T(8,128)}, bf16[128,512]{1,0:T(8,128)(2,1)S(1)}, /*index=5*/f32[8,512]{1,0:T(8,128)}) custom-call(bf16[16,400,128]{2,1,0:T(8,128)(2,1)S(1)} %all-to-all-done.refs_0_, f32[16,128]{1,0:T(8,128)S(1)} %broadcast_in_dim.4.refs_1_.refs_12_), custom_call_target="tpu_custom_call" | custom-call | flops 268435456 | bytes 4194304 | tf_op jit(solution)/shard_map/pallas_call | solution.py:658
  42.7 4.5 %collective-permute-start = (bf16[128,512]{1,0:T(8,128)(2,1)S(1)}, bf16[128,512]{1,0:T(8,128)(2,1)S(1)}, u32[]{:S(2)}, u32[]{:S(2)}) collective-permute-start(bf16[128,512]{1,0:T(8,128)(2,1)S(1)} %get-tuple-element.41), channel_id=1, source_target_pairs={{0,16},{1,17},{2,18},{3,19},{4,20},{5,21},{6,22},{7,23},{8,24},{9,... | collective-permute-start | bytes 393224 | tf_op jit(solution)/shard_map/ppermute | solution.py:529
  47.2 17.5 %collective-permute-done.refs_3_ = bf16[128,512]{1,0:T(8,128)(2,1)S(1)} collective-permute-done((bf16[128,512]{1,0:T(8,128)(2,1)S(1)}, bf16[128,512]{1,0:T(8,128)(2,1)S(1)}, u32[]{:S(2)}, u32[]{:S(2)}) %collective-permute-start) | collective-permute-done | bytes 131104 | tf_op jit(solution)/shard_map/ppermute | solution.py:529
  64.8 6.0 %shard_map.172 = (f32[1024,512]{1,0:T(8,128)}, f32[8,128,512]{2,1,0:T(8,128)}) custom-call(bf16[16,400,128]{2,1,0:T(8,128)(2,1)S(1)} %all-to-all-done.refs_0_, f32[1024,128]{1,0:T(8,128)} %get-tuple-element.39.refs_1_.refs_3_.refs_2_.refs_5_, f32[64,1024]{1,0:T(8,128)} %get-tuple-element.40.refs_2_.refs_3_.refs_6_, ...), custom_call_target="tpu_custom_call" | custom-call | flops 805306368 | bytes 8388608 | tf_op jit(solution)/shard_map/pallas_call | solution.py:678
  70.7 3.5 %shard_map.173.refs_6_ = f32[8,8,128]{2,1,0:T(8,128)S(1)} custom-call(bf16[16,400,128]{2,1,0:T(8,128)(2,1)S(1)} %all-to-all-done.refs_0_, bf16[16,512,128]{2,1,0:T(8,128)(2,1)} %all-to-all-done.1.refs_1_, f32[1024,512]{1,0:T(8,128)} %get-tuple-element.44.refs_2_, f32[1,512]{1,0:T(1,128)S(1)} %bitcast.11, f32[1,512]{1,0:T(1,128)S(1)} %reshape_reshape.3.refs_4_.refs_9_.refs_11_), custom_call_target="tpu_custom_call" | custom-call | bytes 6291456 | tf_op jit(solution)/shard_map/pallas_call | solution.py:692
  74.4 1.2 collective-permute-done.1.refs_7_
  75.6 7.7 %shard_map.174 = (bf16[16,256,128]{2,1,0:T(8,128)(2,1)S(1)}, bf16[1024,512]{1,0:T(8,128)(2,1)}, f32[8,1024]{1,0:T(8,128)}, f32[8,128,512]{2,1,0:T(8,128)}, bf16[...) custom-call(bf16[16,400,128]{2,1,0:T(8,128)(2,1)S(1)} %all-to-all-done.refs_0_, ...), custom_call_target="tpu_custom_call" | custom-call | flops 536870912 | bytes 10485760 | tf_op jit(solution)/shard_map/pallas_call | solution.py:704
  83.3 1.3 collective-permute-start.2
  84.6 5.7 %shard_map.175 = (f32[1024,512]{1,0:T(8,128)}, f32[1024,128]{1,0:T(8,128)}, bf16[16,320,128]{2,1,0:T(8,128)(2,1)}) custom-call(bf16[16,400,128]{2,1,0:T(8,128)(2,1)S(1)} %all-to-all-done.refs_0_, bf16[1024,512]{1,0:T(8,128)(2,1)} %get-tuple-element.48.refs_1_.refs_3_, f32[1024,128]{1,0:T(8,128)} %get-tuple-element.39.refs_1_.refs_3_.refs_2_.refs_5_, ...), custom_call_target="tpu_custom_call" | custom-call | flops 1073741824 | bytes 4194304 | tf_op jit(solution)/shard_map/pallas_call | solution.py:733
  90.2 1.5 %collective-permute-done.2.refs_7_ = bf16[128,512]{1,0:T(8,128)(2,1)S(1)} collective-permute-done((bf16[128,512]{1,0:T(8,128)(2,1)S(1)}, bf16[128,512]{1,0:T(8,128)(2,1)S(1)}, u32[]{:S(2)}, u32[]{:S(2)}) %collective-permute-start.2) | collective-permute-done | bytes 131104 | tf_op jit(solution)/shard_map/ppermute | solution.py:529
  91.7 8.6 %shard_map.176 = bf16[16,352,128]{2,1,0:T(8,128)(2,1)} custom-call(bf16[16,400,128]{2,1,0:T(8,128)(2,1)S(1)} %all-to-all-done.refs_0_, f32[1024,512]{1,0:T(8,128)} %get-tuple-element.51.refs_1_, f32[1024,128]{1,0:T(8,128)} %get-tuple-element.52.refs_2_, bf16[1024,512]{1,0:T(8,128)(2,1)} %get-tuple-element.48.refs_1_.refs_3_, ...), custom_call_target="tpu_custom_call" | custom-call | flops 536870912 | bytes 8388608 | tf_op jit(solution)/shard_map/pallas_call | solution.py:749
  100.4 23.6 %all_to_all.20.refs_0_.refs_1_ = bf16[16,352,128]{2,1,0:T(8,128)(2,1)S(1)} all-to-all(bf16[16,352,128]{2,1,0:T(8,128)(2,1)} %shard_map.176), channel_id=1, replica_groups=mesh['slab'=2,'sub'=8,'tensor'=2] {'sub','tensor'}, dimensions={0} | all-to-all | bytes 2883584 | tf_op jit(solution)/shard_map/all_to_all | solution.py:588
  124.0 3.7 %all-to-all-start.3 = ((bf16[16,320,128]{2,1,0:T(8,128)(2,1)}), bf16[16,320,128]{2,1,0:T(8,128)(2,1)S(1)}, u32[]{:S(2)}, u32[]{:S(2)}) async-start(bf16[16,320,128]{2,1,0:T(8,128)(2,1)} %get-tuple-element.60), calls=%async_computation.3 | async-start | bytes 2621440 | tf_op jit(solution)/shard_map/all_to_all | solution.py:588
  127.9 2.1 %collective-permute-start.3 = (f32[40,128]{1,0:T(8,128)S(1)}, f32[40,128]{1,0:T(8,128)S(1)}, u32[]{:S(2)}, u32[]{:S(2)}) collective-permute-start(f32[40,128]{1,0:T(8,128)S(1)} %shard_map.179), channel_id=1, source_target_pairs={{0,16},{16,0},{1,17},{17,1},{2,18},{18,2},{3,19},{19,3},{4,20},{20... | collective-permute-start | bytes 61448 | tf_op jit(solution)/shard_map/ppermute | solution.py:559
  130.1 15.8 %all-to-all-done.3.refs_0_ = bf16[16,320,128]{2,1,0:T(8,128)(2,1)S(1)} async-done(((bf16[16,320,128]{2,1,0:T(8,128)(2,1)}), bf16[16,320,128]{2,1,0:T(8,128)(2,1)S(1)}, u32[]{:S(2)}, u32[]{:S(2)}) %all-to-all-start.3) | async-done | bytes 1310752 | tf_op jit(solution)/shard_map/all_to_all | solution.py:588
  145.9 1.2 shard_map.178
  147.1 1.2 shard_map.177
  148.3 0.6 slice_bitcast_fusion
  (21 shorter events, 1.3 us)
Async XLA Ops:
  3.1 6.5 %copy-start = (f32[64]{0:T(128)S(1)}, f32[64]{0:T(128)}, u32[]{:S(2)}) copy-start(f32[64]{0:T(128)} %param.15) | copy-start | bytes 772
  3.1 6.5 %copy-start.1 = (f32[64]{0:T(128)S(1)}, f32[64]{0:T(128)}, u32[]{:S(2)}) copy-start(f32[64]{0:T(128)} %param.17) | copy-start | bytes 772
  3.2 6.6 %copy-start.2 = (f32[64]{0:T(128)S(1)}, f32[64]{0:T(128)}, u32[]{:S(2)}) copy-start(f32[64]{0:T(128)} %param.16) | copy-start | bytes 772
  3.2 28.3 %all-to-all-start = ((bf16[16,400,128]{2,1,0:T(8,128)(2,1)}), bf16[16,400,128]{2,1,0:T(8,128)(2,1)S(1)}, u32[]{:S(2)}, u32[]{:S(2)}) async-start(bf16[16,400,128]{2,1,0:T(8,128)(2,1)} %bitcast.14), calls=%async_computation | async-start | bytes 3276800 | tf_op jit(solution)/shard_map/all_to_all | solution.py:588
  31.4 39.3 %all-to-all-start.1 = ((bf16[16,512,128]{2,1,0:T(8,128)(2,1)}), bf16[16,512,128]{2,1,0:T(8,128)(2,1)}, u32[]{:S(2)}, u32[]{:S(2)}) async-start(bf16[16,512,128]{2,1,0:T(8,128)(2,1)} %bitcast.13), calls=%async_computation.1 | async-start | bytes 4194304 | tf_op jit(solution)/shard_map/all_to_all | solution.py:588
  42.7 22.0 %collective-permute-start = (bf16[128,512]{1,0:T(8,128)(2,1)S(1)}, bf16[128,512]{1,0:T(8,128)(2,1)S(1)}, u32[]{:S(2)}, u32[]{:S(2)}) collective-permute-start(bf16[128,512]{1,0:T(8,128)(2,1)S(1)} %get-tuple-element.41), channel_id=1, source_target_pairs={{0,16},{1,17},{2,18},{3,19},{4,20},{5,21},{6,22},{7,23},{8,24},{9,... | collective-permute-start | bytes 393224 | tf_op jit(solution)/shard_map/ppermute | solution.py:529
  74.3 1.3 collective-permute-start.1
  83.3 8.5 %collective-permute-start.2 = (bf16[128,512]{1,0:T(8,128)(2,1)S(1)}, bf16[128,512]{1,0:T(8,128)(2,1)S(1)}, u32[]{:S(2)}, u32[]{:S(2)}) collective-permute-start(bf16[128,512]{1,0:T(8,128)(2,1)S(1)} %get-tuple-element.55), channel_id=1, source_target_pairs={{16,0},{17,1},{18,2},{19,3},{20,4},{21,5},{22,6},{23,7},{24,8},{25... | collective-permute-start | bytes 393224 | tf_op jit(solution)/shard_map/ppermute | solution.py:529
  124.0 21.8 %all-to-all-start.3 = ((bf16[16,320,128]{2,1,0:T(8,128)(2,1)}), bf16[16,320,128]{2,1,0:T(8,128)(2,1)S(1)}, u32[]{:S(2)}, u32[]{:S(2)}) async-start(bf16[16,320,128]{2,1,0:T(8,128)(2,1)} %get-tuple-element.60), calls=%async_computation.3 | async-start | bytes 2621440 | tf_op jit(solution)/shard_map/all_to_all | solution.py:588
  127.9 20.3 %collective-permute-start.3 = (f32[40,128]{1,0:T(8,128)S(1)}, f32[40,128]{1,0:T(8,128)S(1)}, u32[]{:S(2)}, u32[]{:S(2)}) collective-permute-start(f32[40,128]{1,0:T(8,128)S(1)} %shard_map.179), channel_id=1, source_target_pairs={{0,16},{16,0},{1,17},{17,1},{2,18},{18,2},{3,19},{19,3},{4,20},{20... | collective-permute-start | bytes 61448 | tf_op jit(solution)/shard_map/ppermute | solution.py:559

commit v5 on v3

--- a/solution.py
+++ b/solution.py
@@ -55,6 +55,10 @@
     return both[:, :width] + both[:, width:]
 
 
+def sigmoid(values):
+    return 0.5 + 0.5 * jnp.tanh(0.5 * values)
+
+
 def low_half(rows):
     return lax.broadcasted_iota(jnp.int32, (rows, LANES), 1) < HEAD_DIM
 
@@ -105,10 +109,10 @@
         ref[a, b, :] = value.reshape(self.per_chunk, self.rows, LANES)
 
 
-X, B, C = 0, PAIRS, PAIRS + 1
-FIRST = PAIRS + 2
-Z, GRAD = 0, PAIRS
-SECOND = 2 * PAIRS
+X, B, C, Z, GRAD = 0, PAIRS, PAIRS + 1, PAIRS + 2, 2 * PAIRS + 2
+SOURCES = PAIRS + 1
+MIXER = PAIRS + 2
+FIRST = 3 * PAIRS + 2
 GATE_Z, GATE_C = 0, PAIRS
 GATES = PAIRS + 1
 LAST_X, LAST_B = 0, PAIRS
@@ -116,27 +120,27 @@
 TERMS = 3
 
 
-def pack_first(owners, x_ref, b_ref, c_ref, steps_ref, out_ref):
+def pack(x_ref, b_ref, c_ref, z_ref, grad_ref, steps_ref, out_ref, by_head):
     r = x_ref.shape[0]
-    steps = steps_ref[...].astype(f32)
-    padded = jnp.concatenate([steps, jnp.zeros((LANES - r, LANES), f32)], axis=0)
-    by_head = padded.T
+    step = pl.program_id(0)
+    subs = out_ref.shape[0]
+
+    @pl.when(step == 0)
+    def _():
+        steps = steps_ref[...].astype(f32)
+        by_head[...] = jnp.concatenate([steps, jnp.zeros((LANES - r, LANES), f32)], axis=0).T
+
     zero = jnp.zeros((STEP_ROWS - HEADS, LANES), f32)
-    for peer, own in enumerate(owners):
-        for j in range(PAIRS):
-            out_ref[peer, j * r : (j + 1) * r, :] = x_ref[:, lanes(own * PAIRS + j)]
-        out_ref[peer, B * r : (B + 1) * r, :] = b_ref[:, lanes(own // 2)]
-        out_ref[peer, C * r : (C + 1) * r, :] = c_ref[:, lanes(own // 2)]
-        mine = jnp.concatenate([by_head[own * HEADS : (own + 1) * HEADS, :], zero], axis=0)
-        out_ref[peer, FIRST * r :, :] = mine.astype(bf16)
-
-
-def pack_second(owners, z_ref, grad_ref, out_ref):
-    r = z_ref.shape[0]
-    for peer, own in enumerate(owners):
-        for j in range(PAIRS):
-            out_ref[peer, (Z + j) * r : (Z + j + 1) * r, :] = z_ref[:, lanes(own * PAIRS + j)]
-            out_ref[peer, (GRAD + j) * r : (GRAD + j + 1) * r, :] = grad_ref[:, lanes(own * PAIRS + j)]
+    for s in range(subs):
+        for j in range(PAIRS):
+            for block, ref in ((X, x_ref), (Z, z_ref), (GRAD, grad_ref)):
+                at = slice((block + j) * r, (block + j + 1) * r)
+                out_ref[s, 0, at, :] = ref[:, lanes(s * PAIRS + j)]
+        out_ref[s, 0, B * r : (B + 1) * r, :] = b_ref[:, lanes(s // 2)]
+        out_ref[s, 0, C * r : (C + 1) * r, :] = c_ref[:, lanes(s // 2)]
+        at = pl.multiple_of((step * subs + s) * HEADS, HEADS)
+        mine = jnp.concatenate([by_head[pl.ds(at, HEADS), :], zero], axis=0)
+        out_ref[s, 0, FIRST * r :, :] = mine.astype(bf16)
 
 
 def add_halves(owners, in_ref, block, out_ref):
@@ -181,7 +185,7 @@
     return [high, middle, rest - middle]
 
 
-def unpack_params(sub_count, tensor_count, late_ref, early_ref, mine_ref, late_out, gain_out, skip_out):
+def unpack_params(sub_count, tensor_count, late_ref, early_ref, mine_ref, out_ref):
     lane = lax.broadcasted_iota(jnp.int32, (1, LANES), 1)
     late = [jnp.zeros((1, LANES), f32) for _ in range(2)]
     skip = jnp.zeros((1, LANES), f32)
@@ -204,49 +208,52 @@
         part = placed(early_rows, TERMS * PAIRS)
         skip = skip + (part if s == 0 else pltpu.roll(part, s * HEADS, 1))
         gain = early_rows[:PAIRS] + early_rows[PAIRS : 2 * PAIRS] + early_rows[2 * PAIRS : 3 * PAIRS]
-        gain_out[s * PAIRS : (s + 1) * PAIRS, :] = gain
-    late_out[...] = jnp.concatenate(late + [jnp.zeros((6, LANES), f32)], axis=0)
-    skip_out[...] = skip
+        out_ref[8 + s * PAIRS : 8 + (s + 1) * PAIRS, :] = gain
+    out_ref[:8, :] = jnp.concatenate(late + [skip, jnp.zeros((5, LANES), f32)], axis=0)
 
 
 def state_kernel(
     message, per_step,
-    first_ref, heads_ref, sm_ref, smt_ref, own_ref, dec_ref, state_ref, whole_ref,
-    carry,
+    first_ref, steps_ref, heads_ref, sm_ref, smt_ref, own_ref, dec_ref, state_ref, whole_ref,
+    carry, rows_s,
 ):
-    @pl.when(pl.program_id(0) == 0)
+    c = pl.program_id(0)
+
+    @pl.when(c == 0)
     def _():
         carry[...] = jnp.zeros_like(carry)
         whole_ref[...] = jnp.ones_like(whole_ref)
-
-    r = message.rows
-    before = lax.broadcasted_iota(jnp.int32, (CHUNK, CHUNK), 0)
-    after = lax.broadcasted_iota(jnp.int32, (CHUNK, CHUNK), 1)
-    up_to = jnp.where(before <= after, 1.0, 0.0)
-    beyond = jnp.where(before > after, 1.0, 0.0)
-    for i in range(per_step):
-        raw = None
-        for p in range(message.per_chunk):
-            part = first_ref[i * message.per_chunk + p, FIRST * r :, :].astype(f32)[:HEADS]
-            part = part if p == 0 else pltpu.roll(part, p * r, 1)
-            raw = part if raw is None else raw + part
-        raw = raw + heads_ref[HEADS:, :]
+        chunks = rows_s.shape[0]
+        before = lax.broadcasted_iota(jnp.int32, (CHUNK, CHUNK), 0)
+        after = lax.broadcasted_iota(jnp.int32, (CHUNK, CHUNK), 1)
+        raws = []
+        for k in range(chunks):
+            raw = heads_ref[HEADS:, :]
+            for p in range(message.per_chunk):
+                part = steps_ref[k * message.per_chunk + p].astype(f32)[:HEADS]
+                raw = raw + (part if p == 0 else pltpu.roll(part, p * message.rows, 1))
+            raws.append(raw)
+        raw = jnp.concatenate(raws, axis=0)
         small = jnp.exp(-jnp.abs(raw))
         series = small * (
             1.0 - small * (0.5 - small * (1.0 / 3 - small * (0.25 - small * 0.2)))
         )
         soft = jnp.maximum(raw, 0.0) + jnp.where(small < 0.015625, series, jnp.log(1.0 + small))
         sig = jnp.where(raw >= 0.0, 1.0, small) / (1.0 + small)
-        rate = -jnp.exp(heads_ref[:HEADS, :]) * soft
-        cum = mm_exact(rate, up_to)
-        rest = mm_exact(rate, beyond)
-        rows = jnp.concatenate(
-            [
-                soft, cum, soft * jnp.exp(rest), cum - jnp.log(soft), jnp.exp(cum), rate, sig,
-                jnp.zeros_like(soft),
-            ],
-            axis=0,
-        )
+        decay_rate = jnp.concatenate([jnp.exp(heads_ref[:HEADS, :])] * chunks, axis=0)
+        rate = -decay_rate * soft
+        cum = mm_exact(rate, jnp.where(before <= after, 1.0, 0.0))
+        rest = mm_exact(rate, jnp.where(before > after, 1.0, 0.0))
+        kinds = [
+            soft, cum, soft * jnp.exp(rest), cum - jnp.log(soft), jnp.exp(cum), rate, sig,
+            jnp.zeros_like(soft),
+        ]
+        for k in range(chunks):
+            at = slice(k * HEADS, (k + 1) * HEADS)
+            rows_s[k] = jnp.concatenate([kind[at] for kind in kinds], axis=0)
+
+    for i in range(per_step):
+        rows = rows_s[c * per_step + i]
         smt_ref[:, lanes(i)] = rows
         sm = jnp.concatenate([rows, jnp.zeros_like(rows)], axis=0).T
         sm_ref[i * CHUNK : (i + 1) * CHUNK, :] = sm
@@ -284,7 +291,7 @@
 
 def mix_kernel(
     message, per_step,
-    first_ref, second_ref, within_ref, sm_ref, inbound_ref, own_ref, dec_ref, gain_ref, skip_ref,
+    first_ref, within_ref, sm_ref, inbound_ref, own_ref, dec_ref, gain_ref, skip_ref,
     y_ref, start_ref, sums_ref,
     carry,
 ):
@@ -306,9 +313,9 @@
             y = within_ref[rows, lanes(j)] + spread_pair(sm, ECUM, j) * carried
             y_ref[rows, lanes(j)] = y
             values = message.get(first_ref, i, X + j).astype(f32)
-            gates = message.get(second_ref, i, Z + j).astype(f32)
-            grad = message.get(second_ref, i, GRAD + j).astype(f32)
-            gated = (y + skip_ref[0:1, lanes(j)] * values) * (gates / (1.0 + jnp.exp(-gates)))
+            gates = message.get(first_ref, i, Z + j).astype(f32)
+            grad = message.get(first_ref, i, GRAD + j).astype(f32)
+            gated = (y + skip_ref[0:1, lanes(j)] * values) * (gates * sigmoid(gates))
             power = power + gated * gated
             cross = cross + grad * gain_ref[0:1, lanes(j)] * gated
         sums_ref[i, 0:1, :] = jnp.sum(power.T, axis=0, keepdims=True)
@@ -318,7 +325,7 @@
 
 def norm_kernel(
     message, per_step,
-    first_ref, second_ref, y_ref, sm_ref, start_ref, dec_ref, sums_ref, other_ref, gain_ref, skip_ref,
+    first_ref, y_ref, sm_ref, start_ref, dec_ref, sums_ref, other_ref, gain_ref, skip_ref,
     gate_ref, mixed_ref, e_ref, back_ref, slab_ref, readers_ref, param_ref,
     pre, back_sum, gain_sum, skip_sum, high_s, low_s, scaled_s,
 ):
@@ -345,11 +352,11 @@
         for j in range(PAIRS):
             at = lanes(j)
             values = message.get(first_ref, i, X + j).astype(f32)
-            gates = message.get(second_ref, i, Z + j).astype(f32)
-            grad = message.get(second_ref, i, GRAD + j).astype(f32)
+            gates = message.get(first_ref, i, Z + j).astype(f32)
+            grad = message.get(first_ref, i, GRAD + j).astype(f32)
             y = y_ref[rows, at]
             mixed = y + skip_ref[0:1, at] * values
-            sig = 1.0 / (1.0 + jnp.exp(-gates))
+            sig = sigmoid(gates)
             silu = gates * sig
             gated = mixed * silu
             scaled = inverse * grad
@@ -570,6 +577,12 @@
     def struct(shape, kind=f32):
         return jax.ShapeDtypeStruct(shape, kind)
 
+    def hbm(shape, kind=f32):
+        return pltpu.HBM(shape, kind)
+
+    def in_hbm(array):
+        return pltpu.with_memory_space_constraint(array, pltpu.HBM)
+
     def exchange(array):
         return lax.all_to_all(array, ("sub", "tensor"), split_axis=0, concat_axis=0, tiled=True)
 
@@ -581,17 +594,22 @@
     skip_row = jnp.repeat(own_skip, HEAD_DIM).reshape(1, WIDTH)
 
     first_rows = FIRST * rows + STEP_ROWS
-    second_rows = SECOND * rows
     gate_rows = GATES * rows
     last_rows = LAST * rows + 2 * STEP_ROWS
 
-    def packed(kernel, height, *arrays):
-        out = struct((peers, height, LANES), bf16)
-        moved = 4 * peers * height * LANES
-        return call(lambda *refs: kernel(owners, *refs), out, 0, moved)(*arrays)
-
-    first = exchange(packed(pack_first, first_rows, mixer_x, b_matrix, c_matrix, raw_steps))
-    second = exchange(packed(pack_second, second_rows, gate_z, out_grad))
+    def packed(arrays, steps):
+        specs = [
+            pl.BlockSpec((rows, a.shape[1] // tensor_count), lambda t: (0, t)) for a in arrays
+        ] + [pl.BlockSpec(steps.shape, lambda t: (0, 0))]
+        made = call(
+            pack, hbm((sub_count, tensor_count, first_rows, LANES), bf16),
+            0, 4 * peers * first_rows * LANES, (tensor_count,), specs,
+            pl.BlockSpec((sub_count, 1, first_rows, LANES), lambda t: (0, t, 0, 0)),
+            [pltpu.VMEM((LANES, LANES), f32)],
+        )(*(in_hbm(a) for a in (*arrays, steps)))
+        return made.reshape(peers, first_rows, LANES)
+
+    first = exchange(packed((mixer_x, b_matrix, c_matrix, gate_z, out_grad), raw_steps))
 
     def flow(kernel, shape_specs, flops, moved, in_specs, scratch=()):
         def body(*refs):
@@ -626,6 +644,8 @@
     unit = 2 * tokens * CHUNK * WIDTH
     size = tokens * WIDTH
 
+    first, heads, skip_row, own_gain = lax.optimization_barrier((first, heads, skip_row, own_gain))
+    first = in_hbm(first)
     sm, smt, own, dec, state, decay = flow(
         state_kernel,
         [
@@ -637,9 +657,13 @@
             (struct((8, WIDTH)), whole(8, WIDTH)),
         ],
         2 * unit, size * 8,
-        [up["message"](first_rows), whole(2 * HEADS, LANES)],
-        [pltpu.VMEM((STATE, WIDTH), f32)],
-    )(first, heads)
+        [
+            up["message"](SOURCES * rows),
+            pl.BlockSpec((peers, STEP_ROWS, LANES), lambda c: (0, FIRST * rows // STEP_ROWS, 0)),
+            whole(2 * HEADS, LANES),
+        ],
+        [pltpu.VMEM((STATE, WIDTH), f32), pltpu.VMEM((chunks, KINDS * HEADS, LANES), f32)],
+    )(first, first, heads)
 
     before = after = None
     if slab_count > 2:
@@ -650,26 +674,24 @@
         within_kernel,
         [(struct((tokens, WIDTH)), up["token"](WIDTH))],
         4 * unit, size * 8,
-        [
-            up["message"](first_rows), up["token"](LANES), up["lane"](KINDS * HEADS),
-        ],
+        [up["message"](MIXER * rows), up["token"](LANES), up["lane"](KINDS * HEADS)],
     )(first, sm, smt)
 
     y, starts, sums = flow(
         mix_kernel,
         [
             (struct((tokens, WIDTH)), up["token"](WIDTH)),
-            (struct((chunks, STATE, WIDTH)), up["chunk"](STATE, WIDTH)),
+            (hbm((chunks, STATE, WIDTH)), up["chunk"](STATE, WIDTH)),
             (struct((chunks, 8, LANES)), up["chunk"](8, LANES)),
         ],
         2 * unit, size * 20,
         [
-            up["message"](first_rows), up["message"](second_rows), up["token"](WIDTH),
-            up["token"](LANES), whole(STATE, WIDTH), up["chunk"](STATE, WIDTH),
-            up["chunk"](8, WIDTH), whole(1, WIDTH), whole(1, WIDTH),
+            up["message"](FIRST * rows), up["token"](WIDTH), up["token"](LANES),
+            whole(STATE, WIDTH), up["chunk"](STATE, WIDTH), up["chunk"](8, WIDTH),
+            whole(1, WIDTH), whole(1, WIDTH),
         ],
         [pltpu.VMEM((STATE, WIDTH), f32)],
-    )(first, second, within, sm, inbound, own, dec, own_gain, skip_row)
+    )(first, within, sm, inbound, own, dec, own_gain, skip_row)
 
     partner = lax.ppermute(sums, "sub", [(i, i ^ 1) for i in range(sub_count)])
 
@@ -677,16 +699,16 @@
         norm_kernel,
         [
             (struct((peers, PAIRS * rows, LANES), bf16), up["message"](PAIRS * rows)),
-            (struct((tokens, WIDTH), bf16), up["token"](WIDTH)),
-            (struct((HEADS, tokens)), up["lane"](HEADS)),
-            (struct((chunks, STATE, WIDTH)), up["chunk"](STATE, WIDTH)),
+            (hbm((tokens, WIDTH), bf16), up["token"](WIDTH)),
+            (hbm((HEADS, tokens)), up["lane"](HEADS)),
+            (hbm((chunks, STATE, WIDTH)), up["chunk"](STATE, WIDTH)),
             (struct((STATE, WIDTH), bf16), whole(STATE, WIDTH)),
             (struct((tokens, STATE)), up["token"](STATE)),
             (struct((8, LANES)), whole(8, LANES)),
         ],
         4 * unit, size * 20,
         [
-            up["message"](first_rows), up["message"](second_rows), up["token"](WIDTH),
+            up["message"](FIRST * rows), up["token"](WIDTH),
             up["token"](LANES), up["chunk"](STATE, WIDTH), up["chunk"](8, WIDTH),
             up["chunk"](8, LANES), up["chunk"](8, LANES), whole(1, WIDTH), whole(1, WIDTH),
         ],
@@ -696,32 +718,33 @@
             pltpu.VMEM((CHUNK, WIDTH), bf16), pltpu.VMEM((CHUNK, WIDTH), bf16),
             pltpu.VMEM((CHUNK, WIDTH), bf16),
         ],
-    )(first, second, y, sm, starts, dec, sums, partner, own_gain, skip_row)
+    )(
+        first, y, sm, in_hbm(starts), dec, sums, partner, own_gain, skip_row,
+    )
 
     outer = carry_over(slab_back, decay, after, slab_count, -1)
-    params = sum_over(params, "slab", slab_count)
-
     d_values, d_sources, gates_message = flow(
         local_kernel,
         [
-            (struct((tokens, WIDTH)), up["token"](WIDTH)),
-            (struct((tokens, STATE)), up["token"](STATE)),
-            (struct((peers, gate_rows, LANES), bf16), up["message"](gate_rows)),
+            (hbm((tokens, WIDTH)), up["token"](WIDTH)),
+            (hbm((tokens, STATE)), up["token"](STATE)),
+            (hbm((peers, gate_rows, LANES), bf16), up["message"](gate_rows)),
         ],
         8 * unit, size * 8,
         [
-            up["message"](first_rows), up["token"](WIDTH), up["token"](LANES),
+            up["message"](MIXER * rows), up["token"](WIDTH), up["token"](LANES),
             up["lane"](KINDS * HEADS), up["token"](STATE), up["message"](PAIRS * rows),
         ],
-    )(first, d_mixed, sm, smt, readers_part, d_gates)
+    )(first, in_hbm(d_mixed), sm, smt, readers_part, d_gates)
+    gates_message, outer = lax.optimization_barrier((gates_message, outer))
     gates_back = exchange(gates_message)
 
     (last,) = flow(
         last_kernel,
-        [(struct((peers, last_rows, LANES), bf16), whole(peers, last_rows, LANES))],
+        [(hbm((peers, last_rows, LANES), bf16), whole(peers, last_rows, LANES))],
         4 * unit, size * 16,
         [
-            dn["message"](first_rows), dn["token"](WIDTH), dn["token"](STATE),
+            dn["message"](SOURCES * rows), dn["token"](WIDTH), dn["token"](STATE),
             dn["token"](WIDTH), dn["lane"](HEADS), dn["token"](LANES), dn["lane"](KINDS * HEADS),
             whole(STATE, WIDTH), dn["chunk"](STATE, WIDTH), dn["chunk"](STATE, WIDTH),
             dn["chunk"](8, WIDTH), whole(1, WIDTH), whole(2 * HEADS, LANES), whole(8, LANES),
@@ -733,10 +756,11 @@
             pltpu.VMEM((16, WIDTH), f32),
         ],
     )(
-        first, d_values, d_sources, d_mixed, e, sm, smt, outer, back, starts, dec,
-        skip_row, heads, params,
+        first, in_hbm(d_values), in_hbm(d_sources), in_hbm(d_mixed), in_hbm(e), sm, smt, outer,
+        in_hbm(back), in_hbm(starts), dec, skip_row, heads, params,
     )
 
+    last, gates_back = lax.optimization_barrier((last, gates_back))
     last_back = exchange(last)
     grad_gates, grad_c = call(
         lambda *refs: unpack_gates(owners, *refs),
@@ -750,14 +774,14 @@
     def tile(at):
         return pl.BlockSpec((peers, STEP_ROWS, LANES), lambda c: (0, at, 0))
 
-    late, gain, skip = call(
+    params = call(
         lambda *refs: unpack_params(sub_count, tensor_count, *refs),
-        (struct((8, LANES)), struct((sub_count * PAIRS, LANES)), struct((1, LANES))),
+        struct((8 + sub_count * PAIRS, LANES)),
         0, 4 * peers * STEP_ROWS * LANES, (1,),
         [tile(tile_at), tile(tile_at + 1), whole(tensor_count, LANES)],
-        (whole(8, LANES), whole(sub_count * PAIRS, LANES), whole(1, LANES)),
+        whole(8 + sub_count * PAIRS, LANES),
     )(last_back, last_back, mine.astype(f32))
-    late = sum_over(late, "slab", slab_count)
+    params = sum_over(params, "slab", slab_count)
     grad_x, grad_b, grad_steps = call(
         lambda *refs: unpack_last(owners, *refs),
         (
@@ -773,10 +797,10 @@
         grad_b,
         grad_c,
         grad_steps,
-        late[0, :count],
-        skip[0, :count],
-        late[1, :count],
-        gain.reshape(-1),
+        params[0, :count],
+        params[2, :count],
+        params[1, :count],
+        params[8:].reshape(-1),
     )
 
 

time: 164 us -> 151 us (0.921)
  local copies, waits for them, and re-layouts: 29.1 us -> 2.42 us
  waiting for transfers between devices: 64.5 us -> 81.2 us
  starting transfers between devices: 35.4 us -> 23.3 us
  Pallas kernels: 33.2 us -> 42.4 us
    all_to_all x4 -> x3, waiting for transfers between devices: 37.2 us -> 74.5 us  [exchange(): lax.all_to_all(array, ('sub', 'tensor'), split_axis=0, concat_axis=0, til...]
    unnamed x62 -> x6, local copies, waits for them, and re-layouts: 26.8 us -> 0.01 us
    ppermute x2 -> x1, waiting for transfers between devices: 14.9 us -> 2.18 us  [sum_over(): lax.ppermute(array, axis, [(i, i ^ step) for i in range(count)])]
    all_to_all x4 -> x3, starting transfers between devices: 25.8 us -> 17.3 us  [exchange(): lax.all_to_all(array, ('sub', 'tensor'), split_axis=0, concat_axis=0, til...]
    ppermute x2, waiting for transfers between devices: 11.2 us -> 3.24 us  [shifted(): return lax.ppermute(array, 'slab', pairs)]
    pallas_call x6 -> x5, Pallas kernels: 15.8 us -> 23.4 us  [the longest x1 8.69 us: on_device(): flow(last_kernel, [(hbm((peers, last_rows, LANES), bf16), whole(peers, la...]
    ppermute x2 -> x1, starting transfers between devices: 3.74 us -> 0.18 us  [sum_over(): lax.ppermute(array, axis, [(i, i ^ step) for i in range(count)])]
  transfers between devices with their start and end apart: 9 -> 7, of which waited for: 6 -> 6; matrix products, arithmetic and copies ran while one was open for 1% -> 1% of each run, Pallas kernels for 11% -> 14%
where the time goes in v5:
time: 151 us; the launch traced here: 150 us
  waiting for transfers between devices  81.2 us (54%)
  Pallas kernels  42.4 us (28%)
  starting transfers between devices  23.3 us (15%)
  local copies, waits for them, and re-layouts  2.42 us (2%)
    all_to_all x3, waiting for transfers between devices, exchange(): lax.all_to_all(array, ('sub', 'tensor'), split_axis=0, concat_axis=0, til...  74.5 us
    all_to_all x3, starting transfers between devices, exchange(): lax.all_to_all(array, ('sub', 'tensor'), split_axis=0, concat_axis=0, til...  17.3 us
    pallas_call x1, Pallas kernels, on_device(): flow(last_kernel, [(hbm((peers, last_rows, LANES), bf16), whole(peers, la...  8.69 us
    pallas_call x1, Pallas kernels, on_device(): flow(norm_kernel, [(struct((peers, PAIRS * rows, LANES), bf16), up['messa...  7.64 us
    ppermute x2, starting transfers between devices, shifted(): return lax.ppermute(array, 'slab', pairs)  5.77 us
    pallas_call x1, Pallas kernels, on_device(): flow(local_kernel, [(hbm((tokens, WIDTH)), up['token'](WIDTH)), (hbm((tok...  5.75 us
    pallas_call x1, Pallas kernels, on_device(): flow(state_kernel, [(struct((tokens, LANES)), up['token'](LANES)), (struc...  5.19 us
    pallas_call x1, Pallas kernels, on_device(): flow(mix_kernel, [(struct((tokens, WIDTH)), up['token'](WIDTH)), (hbm((ch...  5.08 us
  transfers between devices with their start and end apart: 7, of which 6 were waited for; matrix products, arithmetic and copies ran while one was open for 1% of the time, Pallas kernels for 14%

profile of v5, /device:TPU:0, one launch (start us, length us, event | category | flops | bytes accessed | tf_op | source)
XLA Modules:
  0.0 150.1 jit_solution(7076013202027344830)
XLA Ops:
  0.6 3.7 %shard_map.169 = bf16[8,2,912,128]{3,2,1,0:T(8,128)(2,1)} custom-call(bf16[64,8192]{1,0:T(8,128)(2,1)} %x_ref.1, bf16[64,1024]{1,0:T(8,128)(2,1)} %b_ref.1, bf16[64,1024]{1,0:T(8,128)(2,1)} %c_ref.1, bf16[64,8192]{1,0:T(8,128)(2,1)} %z_ref.1, bf16[64,8192]{1,0:T(8,128)(2,1)} %grad_ref.1, bf16[64,128]{1,0:T(8,128)(2,1)} %steps_ref.1), custom_call_target="tpu_custom_call" | custom-call | bytes 7471104 | tf_op jit(solution)/shard_map/pallas_call | solution.py:604
  4.4 6.5 %all-to-all-start = ((bf16[16,912,128]{2,1,0:T(8,128)(2,1)}), bf16[16,912,128]{2,1,0:T(8,128)(2,1)}, u32[]{:S(2)}, u32[]{:S(2)}) async-start(bf16[16,912,128]{2,1,0:T(8,128)(2,1)} %bitcast.12), calls=%async_computation | async-start | bytes 7471104 | tf_op jit(solution)/shard_map/all_to_all | solution.py:587
  11.3 0.8 dynamic_slice.15
  12.1 45.7 %all-to-all-done.refs_0_.refs_1_ = bf16[16,912,128]{2,1,0:T(8,128)(2,1)} async-done(((bf16[16,912,128]{2,1,0:T(8,128)(2,1)}), bf16[16,912,128]{2,1,0:T(8,128)(2,1)}, u32[]{:S(2)}, u32[]{:S(2)}) %all-to-all-start) | async-done | bytes 3735584 | tf_op jit(solution)/shard_map/all_to_all | solution.py:587
  57.9 5.2 %shard_map.170 = (f32[1024,128]{1,0:T(8,128)S(1)}, f32[64,1024]{1,0:T(8,128)S(1)}, f32[8,128,512]{2,1,0:T(8,128)S(1)}, f32[8,8,512]{2,1,0:T(8,128)S(1)}, bf16[128,512]{1,0:T(8,128)(2,1)S(1)}, /*index=5*/f32[8,512]{1,0:T(8,128)}) custom-call(bf16[16,912,128]{2,1,0:T(8,128)(2,1)} %all-to-all-done.refs_0_.refs_1_, ...), custom_call_target="tpu_custom_call" | custom-call | flops 268435456 | bytes 4194304 | tf_op jit(solution)/shard_map/pallas_call | solution.py:649
  63.1 4.5 %collective-permute-start = (bf16[128,512]{1,0:T(8,128)(2,1)S(1)}, bf16[128,512]{1,0:T(8,128)(2,1)S(1)}, u32[]{:S(2)}, u32[]{:S(2)}) collective-permute-start(bf16[128,512]{1,0:T(8,128)(2,1)S(1)} %get-tuple-element.44), channel_id=1, source_target_pairs={{0,16},{1,17},{2,18},{3,19},{4,20},{5,21},{6,22},{7,23},{8,24},{9,... | collective-permute-start | bytes 393224 | tf_op jit(solution)/shard_map/ppermute | solution.py:528
  67.6 3.8 %shard_map.171.refs_1_ = f32[1024,512]{1,0:T(8,128)S(1)} custom-call(bf16[16,912,128]{2,1,0:T(8,128)(2,1)} %all-to-all-done.refs_0_.refs_1_, f32[1024,128]{1,0:T(8,128)S(1)} %get-tuple-element.42.refs_1_.refs_2_.refs_5_, f32[64,1024]{1,0:T(8,128)S(1)} %get-tuple-element.43.refs_2_.refs_3_.refs_6_), custom_call_target="tpu_custom_call" | custom-call | flops 536870912 | bytes 4194304 | tf_op jit(solution)/shard_map/pallas_call | solution.py:673
  71.4 5.1 %shard_map.172 = (f32[1024,512]{1,0:T(8,128)S(1)}, f32[8,128,512]{2,1,0:T(8,128)}, f32[8,8,128]{2,1,0:T(8,128)S(1)}) custom-call(bf16[16,912,128]{2,1,0:T(8,128)(2,1)} %all-to-all-done.refs_0_.refs_1_, f32[1024,512]{1,0:T(8,128)S(1)} %shard_map.171.refs_1_, f32[1024,128]{1,0:T(8,128)S(1)} %get-tuple-element.42.refs_1_.refs_2_.refs_5_, ...), custom_call_target="tpu_custom_call" | custom-call | flops 268435456 | bytes 10485760 | tf_op jit(solution)/shard_map/pallas_call | solution.py:680
  76.5 1.2 collective-permute-done.1.refs_6_
  77.7 7.6 %shard_map.173 = (bf16[16,256,128]{2,1,0:T(8,128)(2,1)S(1)}, bf16[1024,512]{1,0:T(8,128)(2,1)}, f32[8,1024]{1,0:T(8,128)}, f32[8,128,512]{2,1,0:T(8,128)}, bf16[...) custom-call(bf16[16,912,128]{2,1,0:T(8,128)(2,1)} %all-to-all-done.refs_0_.refs_1_, ...), custom_call_target="tpu_custom_call" | custom-call | flops 536870912 | bytes 10485760 | tf_op jit(solution)/shard_map/pallas_call | solution.py:698
  85.4 1.3 collective-permute-start.2
  86.6 5.8 %shard_map.174 = (f32[1024,512]{1,0:T(8,128)}, f32[1024,128]{1,0:T(8,128)}, bf16[16,320,128]{2,1,0:T(8,128)(2,1)}) custom-call(bf16[16,912,128]{2,1,0:T(8,128)(2,1)} %all-to-all-done.refs_0_.refs_1_, bf16[1024,512]{1,0:T(8,128)(2,1)} %get-tuple-element.52.refs_1_.refs_3_, f32[1024,128]{1,0:T(8,128)S(1)} %get-tuple-element.42.refs_1_.refs_2_.refs_5_, ...), custom_call_target="tpu_custom_call" | custom-call | flops 1073741824 | bytes 4194304 | tf_op jit(solution)/shard_map/pallas_call | solution.py:726
  92.4 3.2 %collective-permute-done.2.refs_7_ = bf16[128,512]{1,0:T(8,128)(2,1)S(1)} collective-permute-done((bf16[128,512]{1,0:T(8,128)(2,1)S(1)}, bf16[128,512]{1,0:T(8,128)(2,1)S(1)}, u32[]{:S(2)}, u32[]{:S(2)}) %collective-permute-start.2) | collective-permute-done | bytes 131104 | tf_op jit(solution)/shard_map/ppermute | solution.py:528
  95.6 6.7 %all-to-all-start.1 = ((bf16[16,320,128]{2,1,0:T(8,128)(2,1)}), bf16[16,320,128]{2,1,0:T(8,128)(2,1)S(1)}, u32[]{:S(2)}, u32[]{:S(2)}) async-start(bf16[16,320,128]{2,1,0:T(8,128)(2,1)} %get-tuple-element.63), calls=%async_computation.1 | async-start | bytes 2621440 | tf_op jit(solution)/shard_map/all_to_all | solution.py:587
  102.4 8.7 %shard_map.175 = bf16[16,352,128]{2,1,0:T(8,128)(2,1)} custom-call(bf16[16,912,128]{2,1,0:T(8,128)(2,1)} %all-to-all-done.refs_0_.refs_1_, f32[1024,512]{1,0:T(8,128)} %get-tuple-element.55.refs_1_, f32[1024,128]{1,0:T(8,128)} %get-tuple-element.56.refs_2_, bf16[1024,512]{1,0:T(8,128)(2,1)} %get-tuple-element.52.refs_1_.refs_3_, ...), custom_call_target="tpu_custom_call" | custom-call | flops 536870912 | bytes 8388608 | tf_op jit(solution)/shard_map/pallas_call | solution.py:742
  111.1 9.3 %all-to-all-done.1.refs_0_ = bf16[16,320,128]{2,1,0:T(8,128)(2,1)S(1)} async-done(((bf16[16,320,128]{2,1,0:T(8,128)(2,1)}), bf16[16,320,128]{2,1,0:T(8,128)(2,1)S(1)}, u32[]{:S(2)}, u32[]{:S(2)}) %all-to-all-start.1) | async-done | bytes 1310752 | tf_op jit(solution)/shard_map/all_to_all | solution.py:587
  120.3 4.1 %all-to-all-start.2 = ((bf16[16,352,128]{2,1,0:T(8,128)(2,1)}), bf16[16,352,128]{2,1,0:T(8,128)(2,1)S(1)}, u32[]{:S(2)}, u32[]{:S(2)}) async-start(bf16[16,352,128]{2,1,0:T(8,128)(2,1)} %shard_map.175), calls=%async_computation.2 | async-start | bytes 2883584 | tf_op jit(solution)/shard_map/all_to_all | solution.py:587
  124.5 19.6 %all-to-all-done.2.refs_0_.refs_1_ = bf16[16,352,128]{2,1,0:T(8,128)(2,1)S(1)} async-done(((bf16[16,352,128]{2,1,0:T(8,128)(2,1)}), bf16[16,352,128]{2,1,0:T(8,128)(2,1)S(1)}, u32[]{:S(2)}, u32[]{:S(2)}) %all-to-all-start.2) | async-done | bytes 1441824 | tf_op jit(solution)/shard_map/all_to_all | solution.py:587
  144.2 0.2 collective-permute-start.3
  144.4 1.2 shard_map.177
  145.6 1.2 shard_map.176
  146.8 2.2 %collective-permute-done.3 = f32[40,128]{1,0:T(8,128)S(1)} collective-permute-done((f32[40,128]{1,0:T(8,128)S(1)}, f32[40,128]{1,0:T(8,128)S(1)}, u32[]{:S(2)}, u32[]{:S(2)}) %collective-permute-start.3) | collective-permute-done | bytes 20512 | tf_op jit(solution)/shard_map/ppermute | solution.py:558
  149.0 0.6 slice_bitcast_fusion
  149.6 0.5 slice_bitcast_fusion.1
  (19 shorter events, 0.7 us)
Async XLA Ops:
  4.4 6.5 %copy-start = (f32[64]{0:T(128)S(1)}, f32[64]{0:T(128)}, u32[]{:S(2)}) copy-start(f32[64]{0:T(128)} %param.15) | copy-start | bytes 772
  4.4 6.6 %copy-start.1 = (f32[64]{0:T(128)S(1)}, f32[64]{0:T(128)}, u32[]{:S(2)}) copy-start(f32[64]{0:T(128)} %param.17) | copy-start | bytes 772
  4.4 6.7 %copy-start.2 = (f32[64]{0:T(128)S(1)}, f32[64]{0:T(128)}, u32[]{:S(2)}) copy-start(f32[64]{0:T(128)} %param.16) | copy-start | bytes 772
  4.4 53.4 %all-to-all-start = ((bf16[16,912,128]{2,1,0:T(8,128)(2,1)}), bf16[16,912,128]{2,1,0:T(8,128)(2,1)}, u32[]{:S(2)}, u32[]{:S(2)}) async-start(bf16[16,912,128]{2,1,0:T(8,128)(2,1)} %bitcast.12), calls=%async_computation | async-start | bytes 7471104 | tf_op jit(solution)/shard_map/all_to_all | solution.py:587
  63.1 8.4 %collective-permute-start = (bf16[128,512]{1,0:T(8,128)(2,1)S(1)}, bf16[128,512]{1,0:T(8,128)(2,1)S(1)}, u32[]{:S(2)}, u32[]{:S(2)}) collective-permute-start(bf16[128,512]{1,0:T(8,128)(2,1)S(1)} %get-tuple-element.44), channel_id=1, source_target_pairs={{0,16},{1,17},{2,18},{3,19},{4,20},{5,21},{6,22},{7,23},{8,24},{9,... | collective-permute-start | bytes 393224 | tf_op jit(solution)/shard_map/ppermute | solution.py:528
  76.5 1.2 collective-permute-start.1
  85.4 10.3 %collective-permute-start.2 = (bf16[128,512]{1,0:T(8,128)(2,1)S(1)}, bf16[128,512]{1,0:T(8,128)(2,1)S(1)}, u32[]{:S(2)}, u32[]{:S(2)}) collective-permute-start(bf16[128,512]{1,0:T(8,128)(2,1)S(1)} %get-tuple-element.59), channel_id=1, source_target_pairs={{16,0},{17,1},{18,2},{19,3},{20,4},{21,5},{22,6},{23,7},{24,8},{25... | collective-permute-start | bytes 393224 | tf_op jit(solution)/shard_map/ppermute | solution.py:528
  95.6 24.7 %all-to-all-start.1 = ((bf16[16,320,128]{2,1,0:T(8,128)(2,1)}), bf16[16,320,128]{2,1,0:T(8,128)(2,1)S(1)}, u32[]{:S(2)}, u32[]{:S(2)}) async-start(bf16[16,320,128]{2,1,0:T(8,128)(2,1)} %get-tuple-element.63), calls=%async_computation.1 | async-start | bytes 2621440 | tf_op jit(solution)/shard_map/all_to_all | solution.py:587
  120.3 23.7 %all-to-all-start.2 = ((bf16[16,352,128]{2,1,0:T(8,128)(2,1)}), bf16[16,352,128]{2,1,0:T(8,128)(2,1)S(1)}, u32[]{:S(2)}, u32[]{:S(2)}) async-start(bf16[16,352,128]{2,1,0:T(8,128)(2,1)} %shard_map.175), calls=%async_computation.2 | async-start | bytes 2883584 | tf_op jit(solution)/shard_map/all_to_all | solution.py:587
  144.2 4.8 %collective-permute-start.3 = (f32[40,128]{1,0:T(8,128)S(1)}, f32[40,128]{1,0:T(8,128)S(1)}, u32[]{:S(2)}, u32[]{:S(2)}) collective-permute-start(f32[40,128]{1,0:T(8,128)S(1)} %shard_map.178), channel_id=1, source_target_pairs={{0,16},{16,0},{1,17},{17,1},{2,18},{18,2},{3,19},{19,3},{4,20},{20... | collective-permute-start | bytes 61448 | tf_op jit(solution)/shard_map/ppermute | solution.py:558

commit v6 on v5

--- a/solution.py
+++ b/solution.py
@@ -109,18 +109,17 @@
         ref[a, b, :] = value.reshape(self.per_chunk, self.rows, LANES)
 
 
-X, B, C, Z, GRAD = 0, PAIRS, PAIRS + 1, PAIRS + 2, 2 * PAIRS + 2
+X, B, C = 0, PAIRS, PAIRS + 1
 SOURCES = PAIRS + 1
-MIXER = PAIRS + 2
-FIRST = 3 * PAIRS + 2
-GATE_Z, GATE_C = 0, PAIRS
-GATES = PAIRS + 1
-LAST_X, LAST_B = 0, PAIRS
-LAST = PAIRS + 1
+FIRST = PAIRS + 2
+Z, GRAD = 0, PAIRS
+SECOND = 2 * PAIRS
+LAST_X, LAST_Z, LAST_B, LAST_C = 0, PAIRS, 2 * PAIRS, 2 * PAIRS + 1
+LAST = 2 * PAIRS + 2
 TERMS = 3
 
 
-def pack(x_ref, b_ref, c_ref, z_ref, grad_ref, steps_ref, out_ref, by_head):
+def pack_first(x_ref, b_ref, c_ref, steps_ref, out_ref, by_head):
     r = x_ref.shape[0]
     step = pl.program_id(0)
     subs = out_ref.shape[0]
@@ -133,14 +132,21 @@
     zero = jnp.zeros((STEP_ROWS - HEADS, LANES), f32)
     for s in range(subs):
         for j in range(PAIRS):
-            for block, ref in ((X, x_ref), (Z, z_ref), (GRAD, grad_ref)):
-                at = slice((block + j) * r, (block + j + 1) * r)
-                out_ref[s, 0, at, :] = ref[:, lanes(s * PAIRS + j)]
+            out_ref[s, 0, j * r : (j + 1) * r, :] = x_ref[:, lanes(s * PAIRS + j)]
         out_ref[s, 0, B * r : (B + 1) * r, :] = b_ref[:, lanes(s // 2)]
         out_ref[s, 0, C * r : (C + 1) * r, :] = c_ref[:, lanes(s // 2)]
         at = pl.multiple_of((step * subs + s) * HEADS, HEADS)
         mine = jnp.concatenate([by_head[pl.ds(at, HEADS), :], zero], axis=0)
         out_ref[s, 0, FIRST * r :, :] = mine.astype(bf16)
+
+
+def pack_second(z_ref, grad_ref, out_ref):
+    r = z_ref.shape[0]
+    for s in range(out_ref.shape[0]):
+        for j in range(PAIRS):
+            at = lanes(s * PAIRS + j)
+            out_ref[s, 0, (Z + j) * r : (Z + j + 1) * r, :] = z_ref[:, at]
+            out_ref[s, 0, (GRAD + j) * r : (GRAD + j + 1) * r, :] = grad_ref[:, at]
 
 
 def add_halves(owners, in_ref, block, out_ref):
@@ -153,21 +159,16 @@
         out_ref[:, lanes(g)] = (halves[0] + halves[1]).astype(bf16)
 
 
-def unpack_gates(owners, in_ref, out_ref, c_ref):
-    r = out_ref.shape[0]
-    for peer, own in enumerate(owners):
-        for j in range(PAIRS):
-            out_ref[:, lanes(own * PAIRS + j)] = in_ref[peer, j * r : (j + 1) * r, :]
-    add_halves(owners, in_ref, GATE_C, c_ref)
-
-
-def unpack_last(owners, in_ref, x_ref, b_ref, steps_ref):
+def unpack(owners, in_ref, x_ref, z_ref, b_ref, c_ref, steps_ref):
     r = x_ref.shape[0]
     peer_of = {own: peer for peer, own in enumerate(owners)}
     for peer, own in enumerate(owners):
         for j in range(PAIRS):
-            x_ref[:, lanes(own * PAIRS + j)] = in_ref[peer, j * r : (j + 1) * r, :]
+            for block, ref in ((LAST_X, x_ref), (LAST_Z, z_ref)):
+                at = slice((block + j) * r, (block + j + 1) * r)
+                ref[:, lanes(own * PAIRS + j)] = in_ref[peer, at, :]
     add_halves(owners, in_ref, LAST_B, b_ref)
+    add_halves(owners, in_ref, LAST_C, c_ref)
     by_head = jnp.concatenate(
         [
             in_ref[peer_of[own], LAST * r : LAST * r + STEP_ROWS, :].astype(f32)[:HEADS]
@@ -291,7 +292,7 @@
 
 def mix_kernel(
     message, per_step,
-    first_ref, within_ref, sm_ref, inbound_ref, own_ref, dec_ref, gain_ref, skip_ref,
+    first_ref, second_ref, within_ref, sm_ref, inbound_ref, own_ref, dec_ref, gain_ref, skip_ref,
     y_ref, start_ref, sums_ref,
     carry,
 ):
@@ -313,8 +314,8 @@
             y = within_ref[rows, lanes(j)] + spread_pair(sm, ECUM, j) * carried
             y_ref[rows, lanes(j)] = y
             values = message.get(first_ref, i, X + j).astype(f32)
-            gates = message.get(first_ref, i, Z + j).astype(f32)
-            grad = message.get(first_ref, i, GRAD + j).astype(f32)
+            gates = message.get(second_ref, i, Z + j).astype(f32)
+            grad = message.get(second_ref, i, GRAD + j).astype(f32)
             gated = (y + skip_ref[0:1, lanes(j)] * values) * (gates * sigmoid(gates))
             power = power + gated * gated
             cross = cross + grad * gain_ref[0:1, lanes(j)] * gated
@@ -325,7 +326,7 @@
 
 def norm_kernel(
     message, per_step,
-    first_ref, y_ref, sm_ref, start_ref, dec_ref, sums_ref, other_ref, gain_ref, skip_ref,
+    first_ref, second_ref, y_ref, sm_ref, start_ref, dec_ref, sums_ref, other_ref, gain_ref, skip_ref,
     gate_ref, mixed_ref, e_ref, back_ref, slab_ref, readers_ref, param_ref,
     pre, back_sum, gain_sum, skip_sum, high_s, low_s, scaled_s,
 ):
@@ -352,8 +353,8 @@
         for j in range(PAIRS):
             at = lanes(j)
             values = message.get(first_ref, i, X + j).astype(f32)
-            gates = message.get(first_ref, i, Z + j).astype(f32)
-            grad = message.get(first_ref, i, GRAD + j).astype(f32)
+            gates = message.get(second_ref, i, Z + j).astype(f32)
+            grad = message.get(second_ref, i, GRAD + j).astype(f32)
             y = y_ref[rows, at]
             mixed = y + skip_ref[0:1, at] * values
             sig = sigmoid(gates)
@@ -393,8 +394,7 @@
 
 def local_kernel(
     message, per_step,
-    first_ref, grad_ref, sm_ref, smt_ref, readers_ref, gate_ref,
-    values_out, sources_out, gates_out,
+    first_ref, grad_ref, sm_ref, smt_ref, readers_ref, values_out, sources_out, readers_out,
 ):
     s = lax.broadcasted_iota(jnp.int32, (CHUNK, CHUNK), 0)
     t = lax.broadcasted_iota(jnp.int32, (CHUNK, CHUNK), 1)
@@ -419,14 +419,12 @@
         total = jnp.where(causal, total, 0.0).astype(bf16)
         sources_out[rows, :] = mm(total, readers)
         d_readers = mm_tn(total, sources) + readers_ref[rows, :]
-        message.put(gates_out, i, GATE_C, d_readers.astype(bf16))
-        for j in range(PAIRS):
-            message.put(gates_out, i, GATE_Z + j, message.get(gate_ref, i, j))
+        message.put(readers_out, i, 0, d_readers.astype(bf16))
 
 
 def last_kernel(
     message, per_step,
-    first_ref, within_ref, sources_ref, grad_ref, e_ref, sm_ref, smt_ref, outer_ref,
+    first_ref, within_ref, sources_ref, readers_ref, gate_ref, grad_ref, e_ref, sm_ref, smt_ref, outer_ref,
     back_ref, start_ref, dec_ref, skip_ref, heads_ref, early_ref,
     out_ref,
     carry, sums, high_s, low_s, scaled_s, state_s, flux_s,
@@ -469,6 +467,9 @@
             )
         d_sources = sources_ref[rows, :] + mm_nt(scaled_s[...], state_s[...])
         message.put(mine, i, LAST_B, d_sources.astype(bf16))
+        message.put(mine, i, LAST_C, message.get(readers_ref, i, 0))
+        for j in range(PAIRS):
+            message.put(mine, i, LAST_Z + j, message.get(gate_ref, i, j))
         g = (mm_nt(ones, high_s[...]) + mm_nt(ones, low_s[...]))[:HEADS]
         high, low = two_terms(flux_s[...])
         constant = (mm_nt(ones, high) + mm_nt(ones, low))[:HEADS, 0:1]
@@ -594,22 +595,33 @@
     skip_row = jnp.repeat(own_skip, HEAD_DIM).reshape(1, WIDTH)
 
     first_rows = FIRST * rows + STEP_ROWS
-    gate_rows = GATES * rows
+    second_rows = SECOND * rows
     last_rows = LAST * rows + 2 * STEP_ROWS
 
-    def packed(arrays, steps):
+    def packed(kernel, height, arrays, whole_arrays=(), scratch=()):
+        out = hbm((sub_count, tensor_count, height, LANES), bf16)
+        moved = 4 * peers * height * LANES
         specs = [
             pl.BlockSpec((rows, a.shape[1] // tensor_count), lambda t: (0, t)) for a in arrays
-        ] + [pl.BlockSpec(steps.shape, lambda t: (0, 0))]
-        made = call(
-            pack, hbm((sub_count, tensor_count, first_rows, LANES), bf16),
-            0, 4 * peers * first_rows * LANES, (tensor_count,), specs,
-            pl.BlockSpec((sub_count, 1, first_rows, LANES), lambda t: (0, t, 0, 0)),
+        ] + [pl.BlockSpec(a.shape, lambda t: (0, 0)) for a in whole_arrays]
+        out_spec = pl.BlockSpec((sub_count, 1, height, LANES), lambda t: (0, t, 0, 0))
+        made = call(kernel, out, 0, moved, (tensor_count,), specs, out_spec, scratch)(
+            *(in_hbm(a) for a in (*arrays, *whole_arrays))
+        )
+        return made.reshape(peers, height, LANES)
+
+    first = exchange(
+        packed(
+            pack_first, first_rows, (mixer_x, b_matrix, c_matrix), (raw_steps,),
             [pltpu.VMEM((LANES, LANES), f32)],
-        )(*(in_hbm(a) for a in (*arrays, steps)))
-        return made.reshape(peers, first_rows, LANES)
-
-    first = exchange(packed((mixer_x, b_matrix, c_matrix, gate_z, out_grad), raw_steps))
+        )
+    )
+    tensor_rows = lax.broadcasted_iota(jnp.int32, (tensor_count, LANES), 0)
+    mine = (tensor_rows == lax.axis_index("tensor")).astype(f32)
+    gate_z, heads, skip_row, own_gain, mine = lax.optimization_barrier(
+        (gate_z, heads, skip_row, own_gain, mine)
+    )
+    second = exchange(packed(pack_second, second_rows, (gate_z, out_grad)))
 
     def flow(kernel, shape_specs, flops, moved, in_specs, scratch=()):
         def body(*refs):
@@ -644,15 +656,13 @@
     unit = 2 * tokens * CHUNK * WIDTH
     size = tokens * WIDTH
 
-    first, heads, skip_row, own_gain = lax.optimization_barrier((first, heads, skip_row, own_gain))
-    first = in_hbm(first)
     sm, smt, own, dec, state, decay = flow(
         state_kernel,
         [
-            (struct((tokens, LANES)), up["token"](LANES)),
-            (struct((KINDS * HEADS, tokens)), up["lane"](KINDS * HEADS)),
-            (struct((chunks, STATE, WIDTH)), up["chunk"](STATE, WIDTH)),
-            (struct((chunks, 8, WIDTH)), up["chunk"](8, WIDTH)),
+            (hbm((tokens, LANES)), up["token"](LANES)),
+            (hbm((KINDS * HEADS, tokens)), up["lane"](KINDS * HEADS)),
+            (hbm((chunks, STATE, WIDTH)), up["chunk"](STATE, WIDTH)),
+            (hbm((chunks, 8, WIDTH)), up["chunk"](8, WIDTH)),
             (struct((STATE, WIDTH), bf16), whole(STATE, WIDTH)),
             (struct((8, WIDTH)), whole(8, WIDTH)),
         ],
@@ -672,26 +682,29 @@
 
     (within,) = flow(
         within_kernel,
-        [(struct((tokens, WIDTH)), up["token"](WIDTH))],
+        [(hbm((tokens, WIDTH)), up["token"](WIDTH))],
         4 * unit, size * 8,
-        [up["message"](MIXER * rows), up["token"](LANES), up["lane"](KINDS * HEADS)],
+        [up["message"](FIRST * rows), up["token"](LANES), up["lane"](KINDS * HEADS)],
     )(first, sm, smt)
 
     y, starts, sums = flow(
         mix_kernel,
         [
             (struct((tokens, WIDTH)), up["token"](WIDTH)),
-            (hbm((chunks, STATE, WIDTH)), up["chunk"](STATE, WIDTH)),
+            (struct((chunks, STATE, WIDTH)), up["chunk"](STATE, WIDTH)),
             (struct((chunks, 8, LANES)), up["chunk"](8, LANES)),
         ],
         2 * unit, size * 20,
         [
-            up["message"](FIRST * rows), up["token"](WIDTH), up["token"](LANES),
-            whole(STATE, WIDTH), up["chunk"](STATE, WIDTH), up["chunk"](8, WIDTH),
+            up["message"](FIRST * rows), up["message"](second_rows), up["token"](WIDTH),
+            up["token"](LANES), whole(STATE, WIDTH), up["chunk"](STATE, WIDTH), up["chunk"](8, WIDTH),
             whole(1, WIDTH), whole(1, WIDTH),
         ],
         [pltpu.VMEM((STATE, WIDTH), f32)],
-    )(first, within, sm, inbound, own, dec, own_gain, skip_row)
+    )(
+        first, in_hbm(second), in_hbm(within), in_hbm(sm), inbound, in_hbm(own), in_hbm(dec),
+        own_gain, skip_row,
+    )
 
     partner = lax.ppermute(sums, "sub", [(i, i ^ 1) for i in range(sub_count)])
 
@@ -699,16 +712,16 @@
         norm_kernel,
         [
             (struct((peers, PAIRS * rows, LANES), bf16), up["message"](PAIRS * rows)),
-            (hbm((tokens, WIDTH), bf16), up["token"](WIDTH)),
-            (hbm((HEADS, tokens)), up["lane"](HEADS)),
-            (hbm((chunks, STATE, WIDTH)), up["chunk"](STATE, WIDTH)),
+            (struct((tokens, WIDTH), bf16), up["token"](WIDTH)),
+            (struct((HEADS, tokens)), up["lane"](HEADS)),
+            (struct((chunks, STATE, WIDTH)), up["chunk"](STATE, WIDTH)),
             (struct((STATE, WIDTH), bf16), whole(STATE, WIDTH)),
             (struct((tokens, STATE)), up["token"](STATE)),
             (struct((8, LANES)), whole(8, LANES)),
         ],
         4 * unit, size * 20,
         [
-            up["message"](FIRST * rows), up["token"](WIDTH),
+            up["message"](FIRST * rows), up["message"](second_rows), up["token"](WIDTH),
             up["token"](LANES), up["chunk"](STATE, WIDTH), up["chunk"](8, WIDTH),
             up["chunk"](8, LANES), up["chunk"](8, LANES), whole(1, WIDTH), whole(1, WIDTH),
         ],
@@ -719,25 +732,23 @@
             pltpu.VMEM((CHUNK, WIDTH), bf16),
         ],
     )(
-        first, y, sm, in_hbm(starts), dec, sums, partner, own_gain, skip_row,
+        first, in_hbm(second), y, sm, starts, dec, sums, partner, own_gain, skip_row,
     )
 
     outer = carry_over(slab_back, decay, after, slab_count, -1)
-    d_values, d_sources, gates_message = flow(
+    d_values, d_sources, d_readers = flow(
         local_kernel,
         [
-            (hbm((tokens, WIDTH)), up["token"](WIDTH)),
-            (hbm((tokens, STATE)), up["token"](STATE)),
-            (hbm((peers, gate_rows, LANES), bf16), up["message"](gate_rows)),
+            (struct((tokens, WIDTH)), up["token"](WIDTH)),
+            (struct((tokens, STATE)), up["token"](STATE)),
+            (struct((peers, rows, LANES), bf16), up["message"](rows)),
         ],
         8 * unit, size * 8,
         [
-            up["message"](MIXER * rows), up["token"](WIDTH), up["token"](LANES),
-            up["lane"](KINDS * HEADS), up["token"](STATE), up["message"](PAIRS * rows),
-        ],
-    )(first, in_hbm(d_mixed), sm, smt, readers_part, d_gates)
-    gates_message, outer = lax.optimization_barrier((gates_message, outer))
-    gates_back = exchange(gates_message)
+            up["message"](FIRST * rows), up["token"](WIDTH), up["token"](LANES),
+            up["lane"](KINDS * HEADS), up["token"](STATE),
+        ],
+    )(first, d_mixed, sm, smt, readers_part)
 
     (last,) = flow(
         last_kernel,
@@ -745,6 +756,7 @@
         4 * unit, size * 16,
         [
             dn["message"](SOURCES * rows), dn["token"](WIDTH), dn["token"](STATE),
+            dn["message"](rows), dn["message"](PAIRS * rows),
             dn["token"](WIDTH), dn["lane"](HEADS), dn["token"](LANES), dn["lane"](KINDS * HEADS),
             whole(STATE, WIDTH), dn["chunk"](STATE, WIDTH), dn["chunk"](STATE, WIDTH),
             dn["chunk"](8, WIDTH), whole(1, WIDTH), whole(2 * HEADS, LANES), whole(8, LANES),
@@ -756,21 +768,12 @@
             pltpu.VMEM((16, WIDTH), f32),
         ],
     )(
-        first, in_hbm(d_values), in_hbm(d_sources), in_hbm(d_mixed), in_hbm(e), sm, smt, outer,
-        in_hbm(back), in_hbm(starts), dec, skip_row, heads, params,
-    )
-
-    last, gates_back = lax.optimization_barrier((last, gates_back))
+        first, d_values, d_sources, d_readers, d_gates, d_mixed, e, sm, smt, outer, back, starts,
+        dec, skip_row, heads, params,
+    )
+
     last_back = exchange(last)
-    grad_gates, grad_c = call(
-        lambda *refs: unpack_gates(owners, *refs),
-        (struct((rows, CHANNELS), bf16), struct((rows, GROUPS * STATE), bf16)),
-        0, 4 * rows * CHANNELS,
-    )(gates_back)
-
     tile_at = LAST * rows // STEP_ROWS
-    mine = lax.broadcasted_iota(jnp.int32, (tensor_count, LANES), 0) == lax.axis_index("tensor")
-
     def tile(at):
         return pl.BlockSpec((peers, STEP_ROWS, LANES), lambda c: (0, at, 0))
 
@@ -780,15 +783,13 @@
         0, 4 * peers * STEP_ROWS * LANES, (1,),
         [tile(tile_at), tile(tile_at + 1), whole(tensor_count, LANES)],
         whole(8 + sub_count * PAIRS, LANES),
-    )(last_back, last_back, mine.astype(f32))
+    )(last_back, last_back, mine)
     params = sum_over(params, "slab", slab_count)
-    grad_x, grad_b, grad_steps = call(
-        lambda *refs: unpack_last(owners, *refs),
-        (
-            struct((rows, CHANNELS), bf16), struct((rows, GROUPS * STATE), bf16),
-            struct((rows, MIXER_HEADS), bf16),
-        ),
-        0, 6 * rows * CHANNELS,
+    wide, narrow = struct((rows, CHANNELS), bf16), struct((rows, GROUPS * STATE), bf16)
+    grad_x, grad_gates, grad_b, grad_c, grad_steps = call(
+        lambda *refs: unpack(owners, *refs),
+        (wide, wide, narrow, narrow, struct((rows, MIXER_HEADS), bf16)),
+        0, 10 * rows * CHANNELS,
     )(last_back)
     count = sub_count * HEADS
     return (

time: 151 us -> 141 us (0.934)
  waiting for transfers between devices: 81.2 us -> 42.8 us
  blocking collectives: 0 us -> 38 us
  starting transfers between devices: 23.3 us -> 17 us
  Pallas kernels: 42.4 us -> 37.5 us
  local copies, waits for them, and re-layouts: 2.42 us -> 4.41 us
    all_to_all x3 -> x2, waiting for transfers between devices: 74.5 us -> 17.7 us  [exchange(): lax.all_to_all(array, ('sub', 'tensor'), split_axis=0, concat_axis=0, til...]
    all_to_all x0 -> x1, blocking collectives: none -> 38 us  [exchange(): lax.all_to_all(array, ('sub', 'tensor'), split_axis=0, concat_axis=0, til...]
    ppermute x2, waiting for transfers between devices: 3.24 us -> 20.8 us  [shifted(): return lax.ppermute(array, 'slab', pairs)]
    all_to_all x3 -> x2, starting transfers between devices: 17.3 us -> 11 us  [exchange(): lax.all_to_all(array, ('sub', 'tensor'), split_axis=0, concat_axis=0, til...]
    pallas_call x7, Pallas kernels: 26 us -> 23.5 us  [the longest x2 5.21 us: packed(): call(kernel, out, 0, moved, (tensor_count,), specs, out_spec, scratch)]
    unnamed x6 -> x16, local copies, waits for them, and re-layouts: 0.01 us -> 2.01 us
  transfers between devices with their start and end apart: 7 -> 6, of which waited for: 6 -> 5; matrix products, arithmetic and copies ran while one was open for 1% -> 1% of each run, Pallas kernels for 14% -> 11%
where the time goes in v6:
time: 141 us
  waiting for transfers between devices  42.8 us (30%)
  blocking collectives  38 us (27%)
  Pallas kernels  37.5 us (27%)
  starting transfers between devices  17 us (12%)
  local copies, waits for them, and re-layouts  4.41 us (3%)
    all_to_all x1, blocking collectives, exchange(): lax.all_to_all(array, ('sub', 'tensor'), split_axis=0, concat_axis=0, til...  38 us
    ppermute x2, waiting for transfers between devices, shifted(): return lax.ppermute(array, 'slab', pairs)  20.8 us
    all_to_all x2, waiting for transfers between devices, exchange(): lax.all_to_all(array, ('sub', 'tensor'), split_axis=0, concat_axis=0, til...  17.7 us
    all_to_all x2, starting transfers between devices, exchange(): lax.all_to_all(array, ('sub', 'tensor'), split_axis=0, concat_axis=0, til...  11 us
    pallas_call x1, Pallas kernels, on_device(): flow(last_kernel, [(hbm((peers, last_rows, LANES), bf16), whole(peers, la...  7.6 us
    pallas_call x1, Pallas kernels, on_device(): flow(norm_kernel, [(struct((peers, PAIRS * rows, LANES), bf16), up['messa...  6.26 us
    ppermute x2, starting transfers between devices, shifted(): return lax.ppermute(array, 'slab', pairs)  5.78 us
    pallas_call x2, Pallas kernels, packed(): call(kernel, out, 0, moved, (tensor_count,), specs, out_spec, scratch)  5.21 us
  transfers between devices with their start and end apart: 6, of which 5 were waited for; matrix products, arithmetic and copies ran while one was open for 1% of the time, Pallas kernels for 11%

profile of v6, /device:TPU:0, one launch (start us, length us, event | category | flops | bytes accessed | tf_op | source)
XLA Modules:
  0.0 140.5 jit_solution(643582108001344125)
XLA Ops:
  0.6 2.5 %shard_map.169 = bf16[8,2,400,128]{3,2,1,0:T(8,128)(2,1)} custom-call(bf16[64,8192]{1,0:T(8,128)(2,1)} %x_ref.1, bf16[64,1024]{1,0:T(8,128)(2,1)} %b_ref.1, bf16[64,1024]{1,0:T(8,128)(2,1)} %c_ref.1, bf16[64,128]{1,0:T(8,128)(2,1)} %steps_ref.1), custom_call_target="tpu_custom_call" | custom-call | bytes 3276800 | tf_op jit(solution)/shard_map/pallas_call | solution.py:608
  3.2 6.4 %all-to-all-start = ((bf16[16,400,128]{2,1,0:T(8,128)(2,1)}), bf16[16,400,128]{2,1,0:T(8,128)(2,1)S(1)}, u32[]{:S(2)}, u32[]{:S(2)}) async-start(bf16[16,400,128]{2,1,0:T(8,128)(2,1)} %bitcast.14), calls=%async_computation | async-start | bytes 3276800 | tf_op jit(solution)/shard_map/all_to_all | solution.py:588
  10.0 0.8 dynamic_slice.15
  11.0 2.7 %shard_map.170 = bf16[8,2,512,128]{3,2,1,0:T(8,128)(2,1)} custom-call(bf16[64,8192]{1,0:T(8,128)(2,1)} %z_ref, bf16[64,8192]{1,0:T(8,128)(2,1)} %grad_ref.1), custom_call_target="tpu_custom_call" | custom-call | bytes 4194304 | tf_op jit(solution)/shard_map/pallas_call | solution.py:608
  13.7 17.7 %all-to-all-done.refs_0_.refs_1_ = bf16[16,400,128]{2,1,0:T(8,128)(2,1)S(1)} async-done(((bf16[16,400,128]{2,1,0:T(8,128)(2,1)}), bf16[16,400,128]{2,1,0:T(8,128)(2,1)S(1)}, u32[]{:S(2)}, u32[]{:S(2)}) %all-to-all-start) | async-done | bytes 1638432 | tf_op jit(solution)/shard_map/all_to_all | solution.py:588
  31.4 4.6 %all-to-all-start.1 = ((bf16[16,512,128]{2,1,0:T(8,128)(2,1)}), bf16[16,512,128]{2,1,0:T(8,128)(2,1)}, u32[]{:S(2)}, u32[]{:S(2)}) async-start(bf16[16,512,128]{2,1,0:T(8,128)(2,1)} %bitcast.13), calls=%async_computation.1 | async-start | bytes 4194304 | tf_op jit(solution)/shard_map/all_to_all | solution.py:588
  36.0 4.3 %shard_map.171 = (f32[1024,128]{1,0:T(8,128)}, f32[64,1024]{1,0:T(8,128)}, f32[8,128,512]{2,1,0:T(8,128)}, f32[8,8,512]{2,1,0:T(8,128)}, bf16[128,512]{1,0:T(8,128)(2,1)S(1)}, /*index=5*/f32[8,512]{1,0:T(8,128)}) custom-call(bf16[16,400,128]{2,1,0:T(8,128)(2,1)S(1)} %all-to-all-done.refs_0_.refs_1_, bf16[16,400,128]{2,1,0:T(8,128)(2,1)S(1)} %all-to-all-done.refs_0_.refs_1_, ...), custom_call_target="tpu_custom_call" | custom-call | flops 268435456 | bytes 4194304 | tf_op jit(solution)/shard_map/pallas_call | solution.py:659
  40.4 4.5 %collective-permute-start = (bf16[128,512]{1,0:T(8,128)(2,1)S(1)}, bf16[128,512]{1,0:T(8,128)(2,1)S(1)}, u32[]{:S(2)}, u32[]{:S(2)}) collective-permute-start(bf16[128,512]{1,0:T(8,128)(2,1)S(1)} %get-tuple-element.41), channel_id=1, source_target_pairs={{0,16},{1,17},{2,18},{3,19},{4,20},{5,21},{6,22},{7,23},{8,24},{9,... | collective-permute-start | bytes 393224 | tf_op jit(solution)/shard_map/ppermute | solution.py:529
  44.9 1.0 copy-done
  45.9 0.9 copy-done.2
  46.9 3.6 %shard_map.172.refs_2_ = f32[1024,512]{1,0:T(8,128)} custom-call(bf16[16,400,128]{2,1,0:T(8,128)(2,1)S(1)} %all-to-all-done.refs_0_.refs_1_, f32[1024,128]{1,0:T(8,128)S(1)} %copy-done, f32[64,1024]{1,0:T(8,128)S(1)} %copy-done.2), custom_call_target="tpu_custom_call" | custom-call | flops 536870912 | bytes 4194304 | tf_op jit(solution)/shard_map/pallas_call | solution.py:683
  50.4 14.4 %collective-permute-done.refs_4_ = bf16[128,512]{1,0:T(8,128)(2,1)S(1)} collective-permute-done((bf16[128,512]{1,0:T(8,128)(2,1)S(1)}, bf16[128,512]{1,0:T(8,128)(2,1)S(1)}, u32[]{:S(2)}, u32[]{:S(2)}) %collective-permute-start) | collective-permute-done | bytes 131104 | tf_op jit(solution)/shard_map/ppermute | solution.py:529
  64.8 5.1 %shard_map.173 = (f32[1024,512]{1,0:T(8,128)S(1)}, f32[8,128,512]{2,1,0:T(8,128)S(1)}, f32[8,8,128]{2,1,0:T(8,128)S(1)}) custom-call(bf16[16,400,128]{2,1,0:T(8,128)(2,1)S(1)} %all-to-all-done.refs_0_.refs_1_, bf16[16,512,128]{2,1,0:T(8,128)(2,1)} %all-to-all-done.1.refs_1_, f32[1024,512]{1,0:T(8,128)} %shard_map.172.refs_2_, ...), custom_call_target="tpu_custom_call" | custom-call | flops 268435456 | bytes 10485760 | tf_op jit(solution)/shard_map/pallas_call | solution.py:690
  69.9 1.2 collective-permute-done.1.refs_7_
  71.1 6.3 %shard_map.174 = (bf16[16,256,128]{2,1,0:T(8,128)(2,1)S(1)}, bf16[1024,512]{1,0:T(8,128)(2,1)S(1)}, f32[8,1024]{1,0:T(8,128)S(1)}, f32[8,128,512]{2,1,0:T(8,128)...) custom-call(bf16[16,400,128]{2,1,0:T(8,128)(2,1)S(1)} %all-to-all-done.refs_0_.refs_1_, ...), custom_call_target="tpu_custom_call" | custom-call | flops 536870912 | bytes 10485760 | tf_op jit(solution)/shard_map/pallas_call | solution.py:711
  77.4 1.3 collective-permute-start.2
  78.7 3.5 %shard_map.175 = (f32[1024,512]{1,0:T(8,128)S(1)}, f32[1024,128]{1,0:T(8,128)S(1)}, bf16[16,64,128]{2,1,0:T(8,128)(2,1)S(1)}) custom-call(bf16[16,400,128]{2,1,0:T(8,128)(2,1)S(1)} %all-to-all-done.refs_0_.refs_1_, bf16[1024,512]{1,0:T(8,128)(2,1)S(1)} %get-tuple-element.49.refs_1_.refs_5_, f32[1024,128]{1,0:T(8,128)S(1)} %copy-done.1, ...), custom_call_target="tpu_custom_call" | custom-call | flops 1073741824 | bytes 4194304 | tf_op jit(solution)/shard_map/pallas_call | solution.py:739
  82.2 6.5 %collective-permute-done.2.refs_9_ = bf16[128,512]{1,0:T(8,128)(2,1)S(1)} collective-permute-done((bf16[128,512]{1,0:T(8,128)(2,1)S(1)}, bf16[128,512]{1,0:T(8,128)(2,1)S(1)}, u32[]{:S(2)}, u32[]{:S(2)}) %collective-permute-start.2) | collective-permute-done | bytes 131104 | tf_op jit(solution)/shard_map/ppermute | solution.py:529
  88.7 7.6 %shard_map.176 = bf16[16,672,128]{2,1,0:T(8,128)(2,1)} custom-call(bf16[16,400,128]{2,1,0:T(8,128)(2,1)S(1)} %all-to-all-done.refs_0_.refs_1_, f32[1024,512]{1,0:T(8,128)S(1)} %get-tuple-element.51.refs_1_, f32[1024,128]{1,0:T(8,128)S(1)} %get-tuple-element.52.refs_2_, bf16[16,64,128]{2,1,0:T(8,128)(2,1)S(1)} %get-tuple-element.53.refs_3_, ...), custom_call_target="tpu_custom_call" | custom-call | flops 536870912 | bytes 8388608 | tf_op jit(solution)/shard_map/pallas_call | solution.py:753
  96.3 38.0 %all_to_all.15.refs_0_.refs_1_ = bf16[16,672,128]{2,1,0:T(8,128)(2,1)S(1)} all-to-all(bf16[16,672,128]{2,1,0:T(8,128)(2,1)} %shard_map.176), channel_id=1, replica_groups=mesh['slab'=2,'sub'=8,'tensor'=2] {'sub','tensor'}, dimensions={0} | all-to-all | bytes 5505024 | tf_op jit(solution)/shard_map/all_to_all | solution.py:588
  134.5 1.9 %shard_map.177 = (bf16[64,8192]{1,0:T(8,128)(2,1)}, bf16[64,8192]{1,0:T(8,128)(2,1)}, bf16[64,1024]{1,0:T(8,128)(2,1)}, bf16[64,1024]{1,0:T(8,128)(2,1)}, bf16[64,128]{1,0:T(8,128)(2,1)}) custom-call(bf16[16,672,128]{2,1,0:T(8,128)(2,1)S(1)} %all_to_all.15.refs_0_.refs_1_), custom_call_target="tpu_custom_call" | custom-call | bytes 5242880 | tf_op jit(solution)/shard_map/pallas_call | solution.py:789
  136.4 3.0 %collective-permute-done.3 = f32[40,128]{1,0:T(8,128)S(1)} collective-permute-done((f32[40,128]{1,0:T(8,128)S(1)}, f32[40,128]{1,0:T(8,128)S(1)}, u32[]{:S(2)}, u32[]{:S(2)}) %collective-permute-start.3) | collective-permute-done | bytes 20512 | tf_op jit(solution)/shard_map/ppermute | solution.py:559
  139.4 0.5 slice_bitcast_fusion.1
  139.9 0.6 slice_bitcast_fusion
  (28 shorter events, 0.9 us)
Async XLA Ops:
  3.1 6.5 %copy-start.5 = (f32[64]{0:T(128)S(1)}, f32[64]{0:T(128)}, u32[]{:S(2)}) copy-start(f32[64]{0:T(128)} %param.15) | copy-start | bytes 772
  3.2 6.5 %copy-start.6 = (f32[64]{0:T(128)S(1)}, f32[64]{0:T(128)}, u32[]{:S(2)}) copy-start(f32[64]{0:T(128)} %param.16) | copy-start | bytes 772
  3.2 6.6 %copy-start.7 = (f32[64]{0:T(128)S(1)}, f32[64]{0:T(128)}, u32[]{:S(2)}) copy-start(f32[64]{0:T(128)} %param.17) | copy-start | bytes 772
  3.2 28.3 %all-to-all-start = ((bf16[16,400,128]{2,1,0:T(8,128)(2,1)}), bf16[16,400,128]{2,1,0:T(8,128)(2,1)S(1)}, u32[]{:S(2)}, u32[]{:S(2)}) async-start(bf16[16,400,128]{2,1,0:T(8,128)(2,1)} %bitcast.14), calls=%async_computation | async-start | bytes 3276800 | tf_op jit(solution)/shard_map/all_to_all | solution.py:588
  31.4 33.4 %all-to-all-start.1 = ((bf16[16,512,128]{2,1,0:T(8,128)(2,1)}), bf16[16,512,128]{2,1,0:T(8,128)(2,1)}, u32[]{:S(2)}, u32[]{:S(2)}) async-start(bf16[16,512,128]{2,1,0:T(8,128)(2,1)} %bitcast.13), calls=%async_computation.1 | async-start | bytes 4194304 | tf_op jit(solution)/shard_map/all_to_all | solution.py:588
  40.4 24.4 %collective-permute-start = (bf16[128,512]{1,0:T(8,128)(2,1)S(1)}, bf16[128,512]{1,0:T(8,128)(2,1)S(1)}, u32[]{:S(2)}, u32[]{:S(2)}) collective-permute-start(bf16[128,512]{1,0:T(8,128)(2,1)S(1)} %get-tuple-element.41), channel_id=1, source_target_pairs={{0,16},{1,17},{2,18},{3,19},{4,20},{5,21},{6,22},{7,23},{8,24},{9,... | collective-permute-start | bytes 393224 | tf_op jit(solution)/shard_map/ppermute | solution.py:529
  44.9 1.0 copy-start
  45.9 0.9 copy-start.2
  64.8 6.3 %copy-start.1 = (f32[1024,128]{1,0:T(8,128)S(1)}, f32[1024,128]{1,0:T(8,128)}, u32[]{:S(2)}) copy-start(f32[1024,128]{1,0:T(8,128)} %get-tuple-element.39.refs_1_.refs_3_.refs_2_.refs_7_) | copy-start | bytes 1572868
  64.8 6.3 %copy-start.4 = (f32[8,8,512]{2,1,0:T(8,128)S(1)}, f32[8,8,512]{2,1,0:T(8,128)}, u32[]{:S(2)}) copy-start(f32[8,8,512]{2,1,0:T(8,128)} %get-tuple-element.43.refs_6_.refs_5_.refs_12_) | copy-start | bytes 393220
  69.8 1.3 collective-permute-start.1
  71.1 7.6 %copy-start.3 = (f32[64,1024]{1,0:T(8,128)S(1)}, f32[64,1024]{1,0:T(8,128)}, u32[]{:S(2)}) copy-start(f32[64,1024]{1,0:T(8,128)} %get-tuple-element.40.refs_2_.refs_3_.refs_8_) | copy-start | bytes 786436
  77.4 11.3 %collective-permute-start.2 = (bf16[128,512]{1,0:T(8,128)(2,1)S(1)}, bf16[128,512]{1,0:T(8,128)(2,1)S(1)}, u32[]{:S(2)}, u32[]{:S(2)}) collective-permute-start(bf16[128,512]{1,0:T(8,128)(2,1)S(1)} %get-tuple-element.56), channel_id=1, source_target_pairs={{16,0},{17,1},{18,2},{19,3},{20,4},{21,5},{22,6},{23,7},{24,8},{25... | collective-permute-start | bytes 393224 | tf_op jit(solution)/shard_map/ppermute | solution.py:529
  134.4 5.0 %collective-permute-start.3 = (f32[40,128]{1,0:T(8,128)S(1)}, f32[40,128]{1,0:T(8,128)S(1)}, u32[]{:S(2)}, u32[]{:S(2)}) collective-permute-start(f32[40,128]{1,0:T(8,128)S(1)} %shard_map.178), channel_id=1, source_target_pairs={{0,16},{16,0},{1,17},{17,1},{2,18},{18,2},{3,19},{19,3},{4,20},{20... | collective-permute-start | bytes 61448 | tf_op jit(solution)/shard_map/ppermute | solution.py:559

commit v7 on v6

--- a/solution.py
+++ b/solution.py
@@ -121,7 +121,7 @@
 
 def pack_first(x_ref, b_ref, c_ref, steps_ref, out_ref, by_head):
     r = x_ref.shape[0]
-    step = pl.program_id(0)
+    step = pl.program_id(0) * pl.num_programs(1) + pl.program_id(1)
     subs = out_ref.shape[0]
 
     @pl.when(step == 0)
@@ -427,7 +427,7 @@
     first_ref, within_ref, sources_ref, readers_ref, gate_ref, grad_ref, e_ref, sm_ref, smt_ref, outer_ref,
     back_ref, start_ref, dec_ref, skip_ref, heads_ref, early_ref,
     out_ref,
-    carry, sums, high_s, low_s, scaled_s, state_s, flux_s,
+    carry, sums, high_s, low_s, scaled_s, state_s, flux_s, message_s, sent,
 ):
     c = pl.program_id(0)
 
@@ -443,7 +443,14 @@
     earlier = jnp.where(before < after, 1.0, 0.0)
     decay_rate = jnp.exp(heads_ref[:HEADS, :])
     first_peer = (pl.num_programs(0) - 1 - c) * per_step * message.per_chunk
-    mine = out_ref.at[pl.ds(first_peer, per_step * message.per_chunk)]
+    span = per_step * message.per_chunk
+    mine = message_s.at[pl.ds(first_peer, span)]
+
+    def body_copy(step):
+        peer = (pl.num_programs(0) - 1 - step) * span
+        at = (pl.ds(peer, span), pl.ds(0, LAST * r))
+        return pltpu.make_async_copy(message_s.at[at], out_ref.at[at], sent.at[step])
+
     for i in reversed(range(per_step)):
         rows = slice(i * CHUNK, (i + 1) * CHUNK)
         sm = sm_ref[rows, :]
@@ -484,6 +491,7 @@
         for p in range(message.per_chunk):
             part = steps if p == 0 else pltpu.roll(steps, LANES - p * r, 1)
             mine[i * message.per_chunk + p, LAST * r : LAST * r + STEP_ROWS, :] = part.astype(bf16)
+    body_copy(c).start()
 
     @pl.when(c == pl.num_programs(0) - 1)
     def _():
@@ -503,11 +511,27 @@
 
         def fill(peer, unused):
             steps_at = slice(LAST * r, LAST * r + STEP_ROWS)
-            out_ref[peer, steps_at, :] = jnp.where(own_rows, out_ref[peer, steps_at, :], late)
-            out_ref[peer, LAST * r + STEP_ROWS :, :] = early
+            message_s[peer, steps_at, :] = jnp.where(own_rows, message_s[peer, steps_at, :], late)
+            message_s[peer, LAST * r + STEP_ROWS :, :] = early
             return unused
 
-        lax.fori_loop(0, out_ref.shape[0], fill, 0)
+        lax.fori_loop(0, message_s.shape[0], fill, 0)
+        at = (slice(None), pl.ds(LAST * r, 2 * STEP_ROWS))
+        steps = sent.shape[0] - 1
+        tiles = pltpu.make_async_copy(message_s.at[at], out_ref.at[at], sent.at[steps])
+        tiles.start()
+        for step in range(steps):
+            body_copy(step).wait()
+        tiles.wait()
+
+
+def finish(own_ref, other_ref, logs_ref, skip_ref, bias_ref, gain_ref):
+    total = own_ref[...] + other_ref[...]
+    count = logs_ref.shape[1]
+    logs_ref[...] = total[0:1, :count]
+    bias_ref[...] = total[1:2, :count]
+    skip_ref[...] = total[2:3, :count]
+    gain_ref[...] = total[8:]
 
 
 def call(kernel, out_shape, flops, moved, grid=None, in_specs=None, out_specs=None, scratch=()):
@@ -553,12 +577,13 @@
     return jnp.zeros_like(state) if result is None else result
 
 
-def sum_over(array, axis, count):
-    step = 1
+def two_parts(array, axis, count):
+    step, other = 1, jnp.zeros_like(array)
     while step < count:
-        array = array + lax.ppermute(array, axis, [(i, i ^ step) for i in range(count)])
+        array = array if step == 1 else array + other
+        other = lax.ppermute(array, axis, [(i, i ^ step) for i in range(count)])
         step *= 2
-    return array
+    return array, other
 
 
 def on_device(
@@ -601,11 +626,13 @@
     def packed(kernel, height, arrays, whole_arrays=(), scratch=()):
         out = hbm((sub_count, tensor_count, height, LANES), bf16)
         moved = 4 * peers * height * LANES
+        runs = 2 if sub_count >= 4 else 1
+        parts = tensor_count * runs
         specs = [
-            pl.BlockSpec((rows, a.shape[1] // tensor_count), lambda t: (0, t)) for a in arrays
-        ] + [pl.BlockSpec(a.shape, lambda t: (0, 0)) for a in whole_arrays]
-        out_spec = pl.BlockSpec((sub_count, 1, height, LANES), lambda t: (0, t, 0, 0))
-        made = call(kernel, out, 0, moved, (tensor_count,), specs, out_spec, scratch)(
+            pl.BlockSpec((rows, a.shape[1] // parts), lambda t, k: (0, t * runs + k)) for a in arrays
+        ] + [pl.BlockSpec(a.shape, lambda t, k: (0, 0)) for a in whole_arrays]
+        out_spec = pl.BlockSpec((sub_count // runs, 1, height, LANES), lambda t, k: (k, t, 0, 0))
+        made = call(kernel, out, 0, moved, (tensor_count, runs), specs, out_spec, scratch)(
             *(in_hbm(a) for a in (*arrays, *whole_arrays))
         )
         return made.reshape(peers, height, LANES)
@@ -752,7 +779,7 @@
 
     (last,) = flow(
         last_kernel,
-        [(hbm((peers, last_rows, LANES), bf16), whole(peers, last_rows, LANES))],
+        [(hbm((peers, last_rows, LANES), bf16), pl.BlockSpec(memory_space=pl.ANY))],
         4 * unit, size * 16,
         [
             dn["message"](SOURCES * rows), dn["token"](WIDTH), dn["token"](STATE),
@@ -765,7 +792,8 @@
             pltpu.VMEM((STATE, WIDTH), f32), pltpu.VMEM((2 * HEADS, LANES), f32),
             pltpu.VMEM((CHUNK, WIDTH), bf16), pltpu.VMEM((CHUNK, WIDTH), bf16),
             pltpu.VMEM((CHUNK, WIDTH), bf16), pltpu.VMEM((STATE, WIDTH), bf16),
-            pltpu.VMEM((16, WIDTH), f32),
+            pltpu.VMEM((16, WIDTH), f32), pltpu.VMEM((peers, last_rows, LANES), bf16),
+            pltpu.SemaphoreType.DMA((grid[0] + 1,)),
         ],
     )(
         first, d_values, d_sources, d_readers, d_gates, d_mixed, e, sm, smt, outer, back, starts,
@@ -784,24 +812,27 @@
         [tile(tile_at), tile(tile_at + 1), whole(tensor_count, LANES)],
         whole(8 + sub_count * PAIRS, LANES),
     )(last_back, last_back, mine)
-    params = sum_over(params, "slab", slab_count)
+    own_params, other_params = two_parts(params, "slab", slab_count)
     wide, narrow = struct((rows, CHANNELS), bf16), struct((rows, GROUPS * STATE), bf16)
     grad_x, grad_gates, grad_b, grad_c, grad_steps = call(
         lambda *refs: unpack(owners, *refs),
         (wide, wide, narrow, narrow, struct((rows, MIXER_HEADS), bf16)),
         0, 10 * rows * CHANNELS,
     )(last_back)
-    count = sub_count * HEADS
+    row = struct((1, sub_count * HEADS))
+    grad_logs, grad_skip, grad_bias, grad_gain = call(
+        finish, (row, row, row, struct((sub_count * PAIRS, LANES))), 0, 1 << 16,
+    )(own_params, other_params)
     return (
         grad_x,
         grad_gates,
         grad_b,
         grad_c,
         grad_steps,
-        params[0, :count],
-        params[2, :count],
-        params[1, :count],
-        params[8:].reshape(-1),
+        grad_logs.reshape(-1),
+        grad_skip.reshape(-1),
+        grad_bias.reshape(-1),
+        grad_gain.reshape(-1),
     )
 
 

time: 141 us -> 141 us (level)
  Pallas kernels: 37.5 us -> 39.7 us
    pallas_call x3 -> x4, Pallas kernels: 12.8 us -> 15 us  [the longest x2 7.61 us: packed(): call(kernel, out, 0, moved, (tensor_count, runs), specs, out_spec, scratch)]
  transfers between devices with their start and end apart: 6 -> 6, of which waited for: 5 -> 5; matrix products, arithmetic and copies ran while one was open for 1% -> 1% of each run, Pallas kernels for 11% -> 12%
where the time goes in v7:
time: 141 us; the launch traced here: 140 us
  waiting for transfers between devices  41.6 us (30%)
  Pallas kernels  39.7 us (28%)
  blocking collectives  38 us (27%)
  starting transfers between devices  17 us (12%)
  local copies, waits for them, and re-layouts  3.28 us (2%)
    all_to_all x1, blocking collectives, exchange(): lax.all_to_all(array, ('sub', 'tensor'), split_axis=0, concat_axis=0, til...  38 us
    ppermute x2, waiting for transfers between devices, shifted(): return lax.ppermute(array, 'slab', pairs)  20.8 us
    all_to_all x2, waiting for transfers between devices, exchange(): lax.all_to_all(array, ('sub', 'tensor'), split_axis=0, concat_axis=0, til...  16.6 us
    all_to_all x2, starting transfers between devices, exchange(): lax.all_to_all(array, ('sub', 'tensor'), split_axis=0, concat_axis=0, til...  11 us
    pallas_call x2, Pallas kernels, packed(): call(kernel, out, 0, moved, (tensor_count, runs), specs, out_spec, scratch)  7.61 us
    pallas_call x1, Pallas kernels, on_device(): flow(last_kernel, [(hbm((peers, last_rows, LANES), bf16), pl.BlockSpec(me...  6.8 us
    pallas_call x1, Pallas kernels, on_device(): flow(norm_kernel, [(struct((peers, PAIRS * rows, LANES), bf16), up['messa...  6.26 us
    ppermute x2, starting transfers between devices, shifted(): return lax.ppermute(array, 'slab', pairs)  5.78 us
  transfers between devices with their start and end apart: 6, of which 5 were waited for; matrix products, arithmetic and copies ran while one was open for 1% of the time, Pallas kernels for 12%

profile of v7, /device:TPU:0, one launch (start us, length us, event | category | flops | bytes accessed | tf_op | source)
XLA Modules:
  0.0 140.5 jit_solution(11922226676936790977)
XLA Ops:
  0.6 3.8 %shard_map.169 = bf16[8,2,400,128]{3,2,1,0:T(8,128)(2,1)} custom-call(bf16[64,8192]{1,0:T(8,128)(2,1)} %x_ref.1, bf16[64,1024]{1,0:T(8,128)(2,1)} %b_ref.1, bf16[64,1024]{1,0:T(8,128)(2,1)} %c_ref.1, bf16[64,128]{1,0:T(8,128)(2,1)} %steps_ref.1), custom_call_target="tpu_custom_call" | custom-call | bytes 3276800 | tf_op jit(solution)/shard_map/pallas_call | solution.py:635
  4.4 6.4 %all-to-all-start = ((bf16[16,400,128]{2,1,0:T(8,128)(2,1)}), bf16[16,400,128]{2,1,0:T(8,128)(2,1)S(1)}, u32[]{:S(2)}, u32[]{:S(2)}) async-start(bf16[16,400,128]{2,1,0:T(8,128)(2,1)} %bitcast.10), calls=%async_computation | async-start | bytes 3276800 | tf_op jit(solution)/shard_map/all_to_all | solution.py:613
  11.3 0.8 dynamic_slice.15
  12.2 3.8 %shard_map.170 = bf16[8,2,512,128]{3,2,1,0:T(8,128)(2,1)} custom-call(bf16[64,8192]{1,0:T(8,128)(2,1)} %z_ref, bf16[64,8192]{1,0:T(8,128)(2,1)} %grad_ref.1), custom_call_target="tpu_custom_call" | custom-call | bytes 4194304 | tf_op jit(solution)/shard_map/pallas_call | solution.py:635
  16.1 16.6 %all-to-all-done.refs_0_.refs_1_ = bf16[16,400,128]{2,1,0:T(8,128)(2,1)S(1)} async-done(((bf16[16,400,128]{2,1,0:T(8,128)(2,1)}), bf16[16,400,128]{2,1,0:T(8,128)(2,1)S(1)}, u32[]{:S(2)}, u32[]{:S(2)}) %all-to-all-start) | async-done | bytes 1638432 | tf_op jit(solution)/shard_map/all_to_all | solution.py:613
  32.7 4.6 %all-to-all-start.1 = ((bf16[16,512,128]{2,1,0:T(8,128)(2,1)}), bf16[16,512,128]{2,1,0:T(8,128)(2,1)}, u32[]{:S(2)}, u32[]{:S(2)}) async-start(bf16[16,512,128]{2,1,0:T(8,128)(2,1)} %bitcast.9), calls=%async_computation.1 | async-start | bytes 4194304 | tf_op jit(solution)/shard_map/all_to_all | solution.py:613
  37.3 4.3 %shard_map.171 = (f32[1024,128]{1,0:T(8,128)}, f32[64,1024]{1,0:T(8,128)}, f32[8,128,512]{2,1,0:T(8,128)}, f32[8,8,512]{2,1,0:T(8,128)}, bf16[128,512]{1,0:T(8,128)(2,1)S(1)}, /*index=5*/f32[8,512]{1,0:T(8,128)}) custom-call(bf16[16,400,128]{2,1,0:T(8,128)(2,1)S(1)} %all-to-all-done.refs_0_.refs_1_, bf16[16,400,128]{2,1,0:T(8,128)(2,1)S(1)} %all-to-all-done.refs_0_.refs_1_, ...), custom_call_target="tpu_custom_call" | custom-call | flops 268435456 | bytes 4194304 | tf_op jit(solution)/shard_map/pallas_call | solution.py:686
  41.6 4.5 %collective-permute-start = (bf16[128,512]{1,0:T(8,128)(2,1)S(1)}, bf16[128,512]{1,0:T(8,128)(2,1)S(1)}, u32[]{:S(2)}, u32[]{:S(2)}) collective-permute-start(bf16[128,512]{1,0:T(8,128)(2,1)S(1)} %get-tuple-element.45), channel_id=1, source_target_pairs={{0,16},{1,17},{2,18},{3,19},{4,20},{5,21},{6,22},{7,23},{8,24},{9,... | collective-permute-start | bytes 393224 | tf_op jit(solution)/shard_map/ppermute | solution.py:553
  46.1 1.0 copy-done
  47.2 0.9 copy-done.2
  48.1 3.6 %shard_map.172.refs_2_ = f32[1024,512]{1,0:T(8,128)} custom-call(bf16[16,400,128]{2,1,0:T(8,128)(2,1)S(1)} %all-to-all-done.refs_0_.refs_1_, f32[1024,128]{1,0:T(8,128)S(1)} %copy-done, f32[64,1024]{1,0:T(8,128)S(1)} %copy-done.2), custom_call_target="tpu_custom_call" | custom-call | flops 536870912 | bytes 4194304 | tf_op jit(solution)/shard_map/pallas_call | solution.py:710
  51.7 14.4 %collective-permute-done.refs_4_ = bf16[128,512]{1,0:T(8,128)(2,1)S(1)} collective-permute-done((bf16[128,512]{1,0:T(8,128)(2,1)S(1)}, bf16[128,512]{1,0:T(8,128)(2,1)S(1)}, u32[]{:S(2)}, u32[]{:S(2)}) %collective-permute-start) | collective-permute-done | bytes 131104 | tf_op jit(solution)/shard_map/ppermute | solution.py:553
  66.0 5.1 %shard_map.173 = (f32[1024,512]{1,0:T(8,128)S(1)}, f32[8,128,512]{2,1,0:T(8,128)S(1)}, f32[8,8,128]{2,1,0:T(8,128)S(1)}) custom-call(bf16[16,400,128]{2,1,0:T(8,128)(2,1)S(1)} %all-to-all-done.refs_0_.refs_1_, bf16[16,512,128]{2,1,0:T(8,128)(2,1)} %all-to-all-done.1.refs_1_, f32[1024,512]{1,0:T(8,128)} %shard_map.172.refs_2_, ...), custom_call_target="tpu_custom_call" | custom-call | flops 268435456 | bytes 10485760 | tf_op jit(solution)/shard_map/pallas_call | solution.py:717
  71.2 1.2 collective-permute-done.1.refs_7_
  72.4 6.3 %shard_map.174 = (bf16[16,256,128]{2,1,0:T(8,128)(2,1)S(1)}, bf16[1024,512]{1,0:T(8,128)(2,1)S(1)}, f32[8,1024]{1,0:T(8,128)S(1)}, f32[8,128,512]{2,1,0:T(8,128)...) custom-call(bf16[16,400,128]{2,1,0:T(8,128)(2,1)S(1)} %all-to-all-done.refs_0_.refs_1_, ...), custom_call_target="tpu_custom_call" | custom-call | flops 536870912 | bytes 10485760 | tf_op jit(solution)/shard_map/pallas_call | solution.py:738
  78.7 1.3 collective-permute-start.2
  80.0 3.5 %shard_map.175 = (f32[1024,512]{1,0:T(8,128)S(1)}, f32[1024,128]{1,0:T(8,128)S(1)}, bf16[16,64,128]{2,1,0:T(8,128)(2,1)S(1)}) custom-call(bf16[16,400,128]{2,1,0:T(8,128)(2,1)S(1)} %all-to-all-done.refs_0_.refs_1_, bf16[1024,512]{1,0:T(8,128)(2,1)S(1)} %get-tuple-element.53.refs_1_.refs_5_, f32[1024,128]{1,0:T(8,128)S(1)} %copy-done.1, ...), custom_call_target="tpu_custom_call" | custom-call | flops 1073741824 | bytes 4194304 | tf_op jit(solution)/shard_map/pallas_call | solution.py:766
  83.4 6.5 %collective-permute-done.2.refs_9_ = bf16[128,512]{1,0:T(8,128)(2,1)S(1)} collective-permute-done((bf16[128,512]{1,0:T(8,128)(2,1)S(1)}, bf16[128,512]{1,0:T(8,128)(2,1)S(1)}, u32[]{:S(2)}, u32[]{:S(2)}) %collective-permute-start.2) | collective-permute-done | bytes 131104 | tf_op jit(solution)/shard_map/ppermute | solution.py:553
  89.9 6.8 %shard_map.176 = bf16[16,672,128]{2,1,0:T(8,128)(2,1)} custom-call(bf16[16,400,128]{2,1,0:T(8,128)(2,1)S(1)} %all-to-all-done.refs_0_.refs_1_, f32[1024,512]{1,0:T(8,128)S(1)} %get-tuple-element.55.refs_1_, f32[1024,128]{1,0:T(8,128)S(1)} %get-tuple-element.56.refs_2_, bf16[16,64,128]{2,1,0:T(8,128)(2,1)S(1)} %get-tuple-element.57.refs_3_, ...), custom_call_target="tpu_custom_call" | custom-call | flops 536870912 | bytes 8388608 | tf_op jit(solution)/shard_map/pallas_call | solution.py:780
  96.7 38.0 %all_to_all.15.refs_0_.refs_1_ = bf16[16,672,128]{2,1,0:T(8,128)(2,1)S(1)} all-to-all(bf16[16,672,128]{2,1,0:T(8,128)(2,1)} %shard_map.176), channel_id=1, replica_groups=mesh['slab'=2,'sub'=8,'tensor'=2] {'sub','tensor'}, dimensions={0} | all-to-all | bytes 5505024 | tf_op jit(solution)/shard_map/all_to_all | solution.py:613
  134.8 0.1 shard_map.178.own_ref
  135.0 1.9 %shard_map.177 = (bf16[64,8192]{1,0:T(8,128)(2,1)}, bf16[64,8192]{1,0:T(8,128)(2,1)}, bf16[64,1024]{1,0:T(8,128)(2,1)}, bf16[64,1024]{1,0:T(8,128)(2,1)}, bf16[64,128]{1,0:T(8,128)(2,1)}) custom-call(bf16[16,672,128]{2,1,0:T(8,128)(2,1)S(1)} %all_to_all.15.refs_0_.refs_1_), custom_call_target="tpu_custom_call" | custom-call | bytes 5242880 | tf_op jit(solution)/shard_map/pallas_call | solution.py:817
  136.9 3.0 %collective-permute-done.3.other_ref = f32[40,128]{1,0:T(8,128)S(1)} collective-permute-done((f32[40,128]{1,0:T(8,128)S(1)}, f32[40,128]{1,0:T(8,128)S(1)}, u32[]{:S(2)}, u32[]{:S(2)}) %collective-permute-start.3) | collective-permute-done | bytes 20512 | tf_op jit(solution)/shard_map/ppermute | solution.py:584
  139.9 0.6 shard_map.179
  (26 shorter events, 0.8 us)
Async XLA Ops:
  4.4 6.5 %copy-start.5 = (f32[64]{0:T(128)S(1)}, f32[64]{0:T(128)}, u32[]{:S(2)}) copy-start(f32[64]{0:T(128)} %param.15) | copy-start | bytes 772
  4.4 6.5 %copy-start.6 = (f32[64]{0:T(128)S(1)}, f32[64]{0:T(128)}, u32[]{:S(2)}) copy-start(f32[64]{0:T(128)} %param.16) | copy-start | bytes 772
  4.4 6.6 %copy-start.7 = (f32[64]{0:T(128)S(1)}, f32[64]{0:T(128)}, u32[]{:S(2)}) copy-start(f32[64]{0:T(128)} %param.17) | copy-start | bytes 772
  4.4 28.3 %all-to-all-start = ((bf16[16,400,128]{2,1,0:T(8,128)(2,1)}), bf16[16,400,128]{2,1,0:T(8,128)(2,1)S(1)}, u32[]{:S(2)}, u32[]{:S(2)}) async-start(bf16[16,400,128]{2,1,0:T(8,128)(2,1)} %bitcast.10), calls=%async_computation | async-start | bytes 3276800 | tf_op jit(solution)/shard_map/all_to_all | solution.py:613
  32.7 33.4 %all-to-all-start.1 = ((bf16[16,512,128]{2,1,0:T(8,128)(2,1)}), bf16[16,512,128]{2,1,0:T(8,128)(2,1)}, u32[]{:S(2)}, u32[]{:S(2)}) async-start(bf16[16,512,128]{2,1,0:T(8,128)(2,1)} %bitcast.9), calls=%async_computation.1 | async-start | bytes 4194304 | tf_op jit(solution)/shard_map/all_to_all | solution.py:613
  41.6 24.4 %collective-permute-start = (bf16[128,512]{1,0:T(8,128)(2,1)S(1)}, bf16[128,512]{1,0:T(8,128)(2,1)S(1)}, u32[]{:S(2)}, u32[]{:S(2)}) collective-permute-start(bf16[128,512]{1,0:T(8,128)(2,1)S(1)} %get-tuple-element.45), channel_id=1, source_target_pairs={{0,16},{1,17},{2,18},{3,19},{4,20},{5,21},{6,22},{7,23},{8,24},{9,... | collective-permute-start | bytes 393224 | tf_op jit(solution)/shard_map/ppermute | solution.py:553
  46.1 1.0 copy-start
  47.2 0.9 copy-start.2
  66.0 6.3 %copy-start.1 = (f32[1024,128]{1,0:T(8,128)S(1)}, f32[1024,128]{1,0:T(8,128)}, u32[]{:S(2)}) copy-start(f32[1024,128]{1,0:T(8,128)} %get-tuple-element.43.refs_1_.refs_3_.refs_2_.refs_7_) | copy-start | bytes 1572868
  66.0 6.3 %copy-start.4 = (f32[8,8,512]{2,1,0:T(8,128)S(1)}, f32[8,8,512]{2,1,0:T(8,128)}, u32[]{:S(2)}) copy-start(f32[8,8,512]{2,1,0:T(8,128)} %get-tuple-element.47.refs_6_.refs_5_.refs_12_) | copy-start | bytes 393220
  71.1 1.3 collective-permute-start.1
  72.4 7.6 %copy-start.3 = (f32[64,1024]{1,0:T(8,128)S(1)}, f32[64,1024]{1,0:T(8,128)}, u32[]{:S(2)}) copy-start(f32[64,1024]{1,0:T(8,128)} %get-tuple-element.44.refs_2_.refs_3_.refs_8_) | copy-start | bytes 786436
  78.7 11.3 %collective-permute-start.2 = (bf16[128,512]{1,0:T(8,128)(2,1)S(1)}, bf16[128,512]{1,0:T(8,128)(2,1)S(1)}, u32[]{:S(2)}, u32[]{:S(2)}) collective-permute-start(bf16[128,512]{1,0:T(8,128)(2,1)S(1)} %get-tuple-element.60), channel_id=1, source_target_pairs={{16,0},{17,1},{18,2},{19,3},{20,4},{21,5},{22,6},{23,7},{24,8},{25... | collective-permute-start | bytes 393224 | tf_op jit(solution)/shard_map/ppermute | solution.py:553
  134.9 5.0 %collective-permute-start.3 = (f32[40,128]{1,0:T(8,128)S(1)}, f32[40,128]{1,0:T(8,128)S(1)}, u32[]{:S(2)}, u32[]{:S(2)}) collective-permute-start(f32[40,128]{1,0:T(8,128)S(1)} %shard_map.178.own_ref), channel_id=1, source_target_pairs={{0,16},{16,0},{1,17},{17,1},{2,18},{18,2},{3,19},{19,3},{4,20},{20... | collective-permute-start | bytes 61448 | tf_op jit(solution)/shard_map/ppermute | solution.py:584

commit v8 on v7

--- a/solution.py
+++ b/solution.py
@@ -271,14 +271,26 @@
     state_ref[...] = carry[...].astype(bf16)
 
 
-def within_kernel(message, per_step, first_ref, sm_ref, smt_ref, out_ref):
+def within_kernel(
+    message, per_step,
+    first_ref, sm_ref, smt_ref, own_ref, dec_ref, y_ref, start_ref, pre_ref, carry, pre,
+):
+    @pl.when(pl.program_id(0) == 0)
+    def _():
+        carry[...] = jnp.zeros_like(carry)
+        pre[...] = jnp.ones_like(pre)
+
     t = lax.broadcasted_iota(jnp.int32, (CHUNK, CHUNK), 0)
     s = lax.broadcasted_iota(jnp.int32, (CHUNK, CHUNK), 1)
     for i in range(per_step):
         rows = slice(i * CHUNK, (i + 1) * CHUNK)
-        scores = mm_nt(message.get(first_ref, i, C), message.get(first_ref, i, B))
-        scores = jnp.where(t >= s, scores, 0.0)
-        for j in range(PAIRS):
+        sm = sm_ref[rows, :]
+        readers = message.get(first_ref, i, C)
+        scores = jnp.where(t >= s, mm_nt(readers, message.get(first_ref, i, B)), 0.0)
+        pre_ref[i] = pre[...]
+        pre[...] = pre[...] * dec_ref[i]
+        for j in range(PAIRS):
+            at = lanes(j)
             weights = []
             for h in (2 * j, 2 * j + 1):
                 here = sm_ref[rows, CUM * HEADS + h : CUM * HEADS + h + 1]
@@ -287,72 +299,124 @@
                     (scores * jnp.exp(jnp.minimum(here - there, CLAMP))).astype(bf16)
                 )
             values = split_pair(message.get(first_ref, i, X + j))
-            out_ref[rows, lanes(j)] = mm(jnp.concatenate(weights, axis=1), values)
+            within = mm(jnp.concatenate(weights, axis=1), values)
+            state = carry[:, at]
+            start_ref[i, :, at] = state
+            carried = mm_two(readers, *two_terms(state))
+            y_ref[rows, at] = within + spread_pair(sm, ECUM, j) * carried
+            carry[:, at] = dec_ref[i, 0:1, at] * state + own_ref[i, :, at]
 
 
 def mix_kernel(
     message, per_step,
-    first_ref, second_ref, within_ref, sm_ref, inbound_ref, own_ref, dec_ref, gain_ref, skip_ref,
-    y_ref, start_ref, sums_ref,
-    carry,
+    first_ref, second_ref, within_ref, sm_ref, inbound_ref, pre_ref, gain_ref, skip_ref,
+    y_ref, sums_ref,
+):
+    for i in range(per_step):
+        rows = slice(i * CHUNK, (i + 1) * CHUNK)
+        sm = sm_ref[rows, :]
+        carried = mm(message.get(first_ref, i, C), inbound_ref[...].astype(bf16))
+        power = jnp.zeros((CHUNK, LANES), f32)
+        cross = jnp.zeros((CHUNK, LANES), f32)
+        for j in range(PAIRS):
+            at = lanes(j)
+            decay = spread_pair(sm, ECUM, j) * pre_ref[i, 0:1, at]
+            y = within_ref[rows, at] + decay * carried[:, at]
+            y_ref[rows, at] = y
+            values = message.get(first_ref, i, X + j).astype(f32)
+            gates = message.get(second_ref, i, Z + j).astype(f32)
+            grad = message.get(second_ref, i, GRAD + j).astype(f32)
+            gated = (y + skip_ref[0:1, at] * values) * (gates * sigmoid(gates))
+            power = power + gated * gated
+            cross = cross + grad * gain_ref[0:1, at] * gated
+        sums_ref[i, 0:1, :] = jnp.sum(power.T, axis=0, keepdims=True)
+        sums_ref[i, 1:2, :] = jnp.sum(cross.T, axis=0, keepdims=True)
+        sums_ref[i, 2:, :] = jnp.zeros((6, LANES), f32)
+
+
+def norm_factors(sums):
+    sums = sums * (1.0 / GROUP_WIDTH)
+    inverse = lax.rsqrt(sums[0:1] + epsilon)
+    pull = inverse * inverse * inverse * sums[1:2]
+    return (
+        jnp.broadcast_to(inverse, (CHUNK, LANES)).T,
+        jnp.broadcast_to(pull, (CHUNK, LANES)).T,
+    )
+
+
+def norm_kernel(
+    message, per_step,
+    first_ref, second_ref, y_ref, sm_ref, pre_ref, sums_ref, other_ref, gain_ref, skip_ref,
+    mixed_ref, back_ref, slab_ref,
+    back_sum,
 ):
     @pl.when(pl.program_id(0) == 0)
     def _():
-        carry[...] = inbound_ref[...].astype(f32)
+        back_sum[...] = jnp.zeros_like(back_sum)
 
     for i in range(per_step):
         rows = slice(i * CHUNK, (i + 1) * CHUNK)
         sm = sm_ref[rows, :]
-        readers = message.get(first_ref, i, C)
-        power = jnp.zeros((CHUNK, LANES), f32)
-        cross = jnp.zeros((CHUNK, LANES), f32)
-        for j in range(PAIRS):
-            state = carry[:, lanes(j)]
-            start_ref[i, :, lanes(j)] = state
-            carried = mm_two(readers, *two_terms(state))
-            carry[:, lanes(j)] = dec_ref[i, 0:1, lanes(j)] * state + own_ref[i, :, lanes(j)]
-            y = within_ref[rows, lanes(j)] + spread_pair(sm, ECUM, j) * carried
-            y_ref[rows, lanes(j)] = y
+        readers_t = message.get(first_ref, i, C).T
+        inverse, pull = norm_factors(sums_ref[i] + other_ref[i])
+        for j in range(PAIRS):
+            at = lanes(j)
             values = message.get(first_ref, i, X + j).astype(f32)
             gates = message.get(second_ref, i, Z + j).astype(f32)
             grad = message.get(second_ref, i, GRAD + j).astype(f32)
-            gated = (y + skip_ref[0:1, lanes(j)] * values) * (gates * sigmoid(gates))
-            power = power + gated * gated
-            cross = cross + grad * gain_ref[0:1, lanes(j)] * gated
-        sums_ref[i, 0:1, :] = jnp.sum(power.T, axis=0, keepdims=True)
-        sums_ref[i, 1:2, :] = jnp.sum(cross.T, axis=0, keepdims=True)
-        sums_ref[i, 2:, :] = jnp.zeros((6, LANES), f32)
-
-
-def norm_kernel(
+            silu = gates * sigmoid(gates)
+            gated = (y_ref[rows, at] + skip_ref[0:1, at] * values) * silu
+            d_mixed = (inverse * grad * gain_ref[0:1, at] - pull * gated) * silu
+            mixed_ref[rows, at] = d_mixed.astype(bf16)
+            back = mm_two(readers_t, *two_terms(d_mixed * spread_pair(sm, ECUM, j)))
+            back_ref[i, :, at] = back
+            back_sum[:, at] += pre_ref[i, 0:1, at] * back
+    slab_ref[...] = back_sum[...].astype(bf16)
+
+
+def local_kernel(
     message, per_step,
-    first_ref, second_ref, y_ref, sm_ref, start_ref, dec_ref, sums_ref, other_ref, gain_ref, skip_ref,
-    gate_ref, mixed_ref, e_ref, back_ref, slab_ref, readers_ref, param_ref,
-    pre, back_sum, gain_sum, skip_sum, high_s, low_s, scaled_s,
+    first_ref, second_ref, y_ref, grad_ref, sm_ref, smt_ref, start_ref, pre_ref, inbound_ref,
+    sums_ref, other_ref, gain_ref, skip_ref,
+    values_out, sources_out, readers_out, gate_ref, e_ref, param_ref,
+    gain_sum, skip_sum, high_s, low_s, scaled_s,
 ):
     c = pl.program_id(0)
 
     @pl.when(c == 0)
     def _():
-        pre[...] = jnp.ones_like(pre)
-        back_sum[...] = jnp.zeros_like(back_sum)
         gain_sum[...] = jnp.zeros_like(gain_sum)
         skip_sum[...] = jnp.zeros_like(skip_sum)
 
+    s = lax.broadcasted_iota(jnp.int32, (CHUNK, CHUNK), 0)
+    t = lax.broadcasted_iota(jnp.int32, (CHUNK, CHUNK), 1)
+    causal = t >= s
     ones = head_rows()
+    inbound = inbound_ref[...].astype(f32)
     for i in range(per_step):
         rows = slice(i * CHUNK, (i + 1) * CHUNK)
         sm = sm_ref[rows, :]
+        sources = message.get(first_ref, i, B)
         readers = message.get(first_ref, i, C)
-        readers_t = readers.T
-        sums = (sums_ref[i] + other_ref[i]) * (1.0 / GROUP_WIDTH)
-        inverse_row = lax.rsqrt(sums[0:1] + epsilon)
-        pull_row = inverse_row * inverse_row * inverse_row * sums[1:2]
-        inverse = jnp.broadcast_to(inverse_row, (CHUNK, LANES)).T
-        pull = jnp.broadcast_to(pull_row, (CHUNK, LANES)).T
+        inverse, pull = norm_factors(sums_ref[i] + other_ref[i])
+        scores = jnp.where(causal, mm_nt(sources, readers), 0.0)
+        total = jnp.zeros((CHUNK, CHUNK), f32)
         for j in range(PAIRS):
             at = lanes(j)
-            values = message.get(first_ref, i, X + j).astype(f32)
+            rounded = grad_ref[rows, at]
+            grads = split_pair(rounded)
+            x = message.get(first_ref, i, X + j)
+            weight_grads = mm_nt(x, grads)
+            weights = []
+            for k, h in enumerate((2 * j, 2 * j + 1)):
+                there = sm_ref[rows, SHIFTED * HEADS + h : SHIFTED * HEADS + h + 1]
+                here = smt_ref[CUM * HEADS + h : CUM * HEADS + h + 1, lanes(i)]
+                decay = jnp.exp(jnp.minimum(here - there, CLAMP))
+                weights.append((scores * decay).astype(bf16))
+                total = total + weight_grads[:, lanes(k)] * decay
+            values_out[rows, at] = mm(jnp.concatenate(weights, axis=1), grads)
+
+            values = x.astype(f32)
             gates = message.get(second_ref, i, Z + j).astype(f32)
             grad = message.get(second_ref, i, GRAD + j).astype(f32)
             y = y_ref[rows, at]
@@ -363,22 +427,18 @@
             scaled = inverse * grad
             gain_sum[0:1, at] += jnp.sum(scaled * gated, axis=0, keepdims=True)
             d_gated = scaled * gain_ref[0:1, at] - pull * gated
-            d_mixed = d_gated * silu
             d_gate = d_gated * mixed * (sig + silu * (1.0 - sig))
             message.put(gate_ref, i, j, d_gate.astype(bf16))
-            skip_sum[0:1, at] += jnp.sum(values * d_mixed, axis=0, keepdims=True)
-            rounded = d_mixed.astype(bf16)
-            mixed_ref[rows, at] = rounded
-            high_s[:, at], low_s[:, at] = two_terms(rounded.astype(f32) * y)
-            high, low = two_terms(d_mixed * spread_pair(sm, ECUM, j))
-            scaled_s[:, at] = high
-            back = mm_two(readers_t, high, low)
-            back_ref[i, :, at] = back
-            back_sum[:, at] += pre[0:1, at] * back
-            pre[:, at] = pre[:, at] * dec_ref[i, :, at]
+            skip_sum[0:1, at] += jnp.sum(values * (d_gated * silu), axis=0, keepdims=True)
+            d_mixed = rounded.astype(f32)
+            high_s[:, at], low_s[:, at] = two_terms(d_mixed * y)
+            scaled_s[:, at] = (d_mixed * spread_pair(sm, ECUM, j)).astype(bf16)
         e_ref[:, lanes(i)] = (mm_nt(ones, high_s[...]) + mm_nt(ones, low_s[...]))[:HEADS]
-        readers_ref[rows, :] = mm_nt(scaled_s[...], start_ref[i].astype(bf16))
-    slab_ref[...] = back_sum[...].astype(bf16)
+        total = jnp.where(causal, total, 0.0).astype(bf16)
+        sources_out[rows, :] = mm(total, readers)
+        start = (start_ref[i] + pre_ref[i, 0:1, :] * inbound).astype(bf16)
+        d_readers = mm_tn(total, sources) + mm_nt(scaled_s[...], start)
+        message.put(readers_out, i, 0, d_readers.astype(bf16))
 
     @pl.when(c == pl.num_programs(0) - 1)
     def _():
@@ -392,40 +452,10 @@
         param_ref[PAIRS + 1 :, :] = jnp.zeros((8 - PAIRS - 1, LANES), f32)
 
 
-def local_kernel(
-    message, per_step,
-    first_ref, grad_ref, sm_ref, smt_ref, readers_ref, values_out, sources_out, readers_out,
-):
-    s = lax.broadcasted_iota(jnp.int32, (CHUNK, CHUNK), 0)
-    t = lax.broadcasted_iota(jnp.int32, (CHUNK, CHUNK), 1)
-    causal = t >= s
-    for i in range(per_step):
-        rows = slice(i * CHUNK, (i + 1) * CHUNK)
-        sources = message.get(first_ref, i, B)
-        readers = message.get(first_ref, i, C)
-        scores = jnp.where(causal, mm_nt(sources, readers), 0.0)
-        total = jnp.zeros((CHUNK, CHUNK), f32)
-        for j in range(PAIRS):
-            grads = split_pair(grad_ref[rows, lanes(j)])
-            weight_grads = mm_nt(message.get(first_ref, i, X + j), grads)
-            weights = []
-            for k, h in enumerate((2 * j, 2 * j + 1)):
-                there = sm_ref[rows, SHIFTED * HEADS + h : SHIFTED * HEADS + h + 1]
-                here = smt_ref[CUM * HEADS + h : CUM * HEADS + h + 1, lanes(i)]
-                decay = jnp.exp(jnp.minimum(here - there, CLAMP))
-                weights.append((scores * decay).astype(bf16))
-                total = total + weight_grads[:, lanes(k)] * decay
-            values_out[rows, lanes(j)] = mm(jnp.concatenate(weights, axis=1), grads)
-        total = jnp.where(causal, total, 0.0).astype(bf16)
-        sources_out[rows, :] = mm(total, readers)
-        d_readers = mm_tn(total, sources) + readers_ref[rows, :]
-        message.put(readers_out, i, 0, d_readers.astype(bf16))
-
-
 def last_kernel(
     message, per_step,
     first_ref, within_ref, sources_ref, readers_ref, gate_ref, grad_ref, e_ref, sm_ref, smt_ref, outer_ref,
-    back_ref, start_ref, dec_ref, skip_ref, heads_ref, early_ref,
+    back_ref, start_ref, pre_ref, inbound_ref, dec_ref, skip_ref, heads_ref, early_ref,
     out_ref,
     carry, sums, high_s, low_s, scaled_s, state_s, flux_s, message_s, sent,
 ):
@@ -469,8 +499,9 @@
             scaled_s[:, at] = (values * weight).astype(bf16)
             new = dec_ref[i, 0:1, at] * state + back_ref[i, :, at]
             carry[:, at] = new
+            start = start_ref[i, :, at] + pre_ref[i, 0:1, at] * inbound_ref[:, at].astype(f32)
             flux_s[:, at] = jnp.broadcast_to(
-                jnp.sum(start_ref[i, :, at] * new, axis=0, keepdims=True), (16, LANES)
+                jnp.sum(start * new, axis=0, keepdims=True), (16, LANES)
             )
         d_sources = sources_ref[rows, :] + mm_nt(scaled_s[...], state_s[...])
         message.put(mine, i, LAST_B, d_sources.astype(bf16))
@@ -626,7 +657,7 @@
     def packed(kernel, height, arrays, whole_arrays=(), scratch=()):
         out = hbm((sub_count, tensor_count, height, LANES), bf16)
         moved = 4 * peers * height * LANES
-        runs = 2 if sub_count >= 4 else 1
+        runs = 1
         parts = tensor_count * runs
         specs = [
             pl.BlockSpec((rows, a.shape[1] // parts), lambda t, k: (0, t * runs + k)) for a in arrays
@@ -707,75 +738,83 @@
         before, after = shifted(decay, slab_count, 1), shifted(decay, slab_count, -1)
     inbound = carry_over(state, decay, before, slab_count, 1)
 
-    (within,) = flow(
+    within, starts, pre = flow(
         within_kernel,
-        [(hbm((tokens, WIDTH)), up["token"](WIDTH))],
-        4 * unit, size * 8,
-        [up["message"](FIRST * rows), up["token"](LANES), up["lane"](KINDS * HEADS)],
-    )(first, sm, smt)
-
-    y, starts, sums = flow(
+        [
+            (hbm((tokens, WIDTH)), up["token"](WIDTH)),
+            (hbm((chunks, STATE, WIDTH)), up["chunk"](STATE, WIDTH)),
+            (hbm((chunks, 8, WIDTH)), up["chunk"](8, WIDTH)),
+        ],
+        6 * unit, size * 16,
+        [
+            up["message"](FIRST * rows), up["token"](LANES), up["lane"](KINDS * HEADS),
+            up["chunk"](STATE, WIDTH), up["chunk"](8, WIDTH),
+        ],
+        [pltpu.VMEM((STATE, WIDTH), f32), pltpu.VMEM((8, WIDTH), f32)],
+    )(first, in_hbm(sm), in_hbm(smt), in_hbm(own), in_hbm(dec))
+
+    y, sums = flow(
         mix_kernel,
         [
             (struct((tokens, WIDTH)), up["token"](WIDTH)),
-            (struct((chunks, STATE, WIDTH)), up["chunk"](STATE, WIDTH)),
             (struct((chunks, 8, LANES)), up["chunk"](8, LANES)),
         ],
-        2 * unit, size * 20,
+        unit, size * 16,
         [
             up["message"](FIRST * rows), up["message"](second_rows), up["token"](WIDTH),
-            up["token"](LANES), whole(STATE, WIDTH), up["chunk"](STATE, WIDTH), up["chunk"](8, WIDTH),
+            up["token"](LANES), whole(STATE, WIDTH), up["chunk"](8, WIDTH),
             whole(1, WIDTH), whole(1, WIDTH),
         ],
-        [pltpu.VMEM((STATE, WIDTH), f32)],
     )(
-        first, in_hbm(second), in_hbm(within), in_hbm(sm), inbound, in_hbm(own), in_hbm(dec),
-        own_gain, skip_row,
+        first, in_hbm(second), in_hbm(within), in_hbm(sm), inbound, in_hbm(pre), own_gain, skip_row,
     )
 
     partner = lax.ppermute(sums, "sub", [(i, i ^ 1) for i in range(sub_count)])
 
-    d_gates, d_mixed, e, back, slab_back, readers_part, params = flow(
+    d_mixed, back, slab_back = flow(
         norm_kernel,
         [
-            (struct((peers, PAIRS * rows, LANES), bf16), up["message"](PAIRS * rows)),
             (struct((tokens, WIDTH), bf16), up["token"](WIDTH)),
-            (struct((HEADS, tokens)), up["lane"](HEADS)),
             (struct((chunks, STATE, WIDTH)), up["chunk"](STATE, WIDTH)),
             (struct((STATE, WIDTH), bf16), whole(STATE, WIDTH)),
+        ],
+        2 * unit, size * 12,
+        [
+            up["message"](FIRST * rows), up["message"](second_rows), up["token"](WIDTH),
+            up["token"](LANES), up["chunk"](8, WIDTH), up["chunk"](8, LANES),
+            up["chunk"](8, LANES), whole(1, WIDTH), whole(1, WIDTH),
+        ],
+        [pltpu.VMEM((STATE, WIDTH), f32)],
+    )(first, in_hbm(second), y, sm, in_hbm(pre), sums, partner, own_gain, skip_row)
+
+    outer = carry_over(slab_back, decay, after, slab_count, -1)
+
+    d_values, d_sources, d_readers, d_gates, e, params = flow(
+        local_kernel,
+        [
+            (struct((tokens, WIDTH)), up["token"](WIDTH)),
             (struct((tokens, STATE)), up["token"](STATE)),
+            (struct((peers, rows, LANES), bf16), up["message"](rows)),
+            (struct((peers, PAIRS * rows, LANES), bf16), up["message"](PAIRS * rows)),
+            (struct((HEADS, tokens)), up["lane"](HEADS)),
             (struct((8, LANES)), whole(8, LANES)),
         ],
-        4 * unit, size * 20,
+        10 * unit, size * 16,
         [
             up["message"](FIRST * rows), up["message"](second_rows), up["token"](WIDTH),
-            up["token"](LANES), up["chunk"](STATE, WIDTH), up["chunk"](8, WIDTH),
+            up["token"](WIDTH), up["token"](LANES), up["lane"](KINDS * HEADS),
+            up["chunk"](STATE, WIDTH), up["chunk"](8, WIDTH), whole(STATE, WIDTH),
             up["chunk"](8, LANES), up["chunk"](8, LANES), whole(1, WIDTH), whole(1, WIDTH),
         ],
         [
-            pltpu.VMEM((8, WIDTH), f32), pltpu.VMEM((STATE, WIDTH), f32),
             pltpu.VMEM((8, WIDTH), f32), pltpu.VMEM((8, WIDTH), f32),
             pltpu.VMEM((CHUNK, WIDTH), bf16), pltpu.VMEM((CHUNK, WIDTH), bf16),
             pltpu.VMEM((CHUNK, WIDTH), bf16),
         ],
     )(
-        first, in_hbm(second), y, sm, starts, dec, sums, partner, own_gain, skip_row,
-    )
-
-    outer = carry_over(slab_back, decay, after, slab_count, -1)
-    d_values, d_sources, d_readers = flow(
-        local_kernel,
-        [
-            (struct((tokens, WIDTH)), up["token"](WIDTH)),
-            (struct((tokens, STATE)), up["token"](STATE)),
-            (struct((peers, rows, LANES), bf16), up["message"](rows)),
-        ],
-        8 * unit, size * 8,
-        [
-            up["message"](FIRST * rows), up["token"](WIDTH), up["token"](LANES),
-            up["lane"](KINDS * HEADS), up["token"](STATE),
-        ],
-    )(first, d_mixed, sm, smt, readers_part)
+        first, in_hbm(second), y, d_mixed, sm, smt, in_hbm(starts), in_hbm(pre), inbound,
+        sums, partner, own_gain, skip_row,
+    )
 
     (last,) = flow(
         last_kernel,
@@ -786,7 +825,7 @@
             dn["message"](rows), dn["message"](PAIRS * rows),
             dn["token"](WIDTH), dn["lane"](HEADS), dn["token"](LANES), dn["lane"](KINDS * HEADS),
             whole(STATE, WIDTH), dn["chunk"](STATE, WIDTH), dn["chunk"](STATE, WIDTH),
-            dn["chunk"](8, WIDTH), whole(1, WIDTH), whole(2 * HEADS, LANES), whole(8, LANES),
+            dn["chunk"](8, WIDTH), whole(STATE, WIDTH), dn["chunk"](8, WIDTH), whole(1, WIDTH), whole(2 * HEADS, LANES), whole(8, LANES),
         ],
         [
             pltpu.VMEM((STATE, WIDTH), f32), pltpu.VMEM((2 * HEADS, LANES), f32),
@@ -796,8 +835,8 @@
             pltpu.SemaphoreType.DMA((grid[0] + 1,)),
         ],
     )(
-        first, d_values, d_sources, d_readers, d_gates, d_mixed, e, sm, smt, outer, back, starts,
-        dec, skip_row, heads, params,
+        first, d_values, d_sources, d_readers, d_gates, d_mixed, e, sm, smt, outer, back,
+        in_hbm(starts), in_hbm(pre), inbound, in_hbm(dec), skip_row, heads, params,
     )
 
     last_back = exchange(last)

time: 141 us -> 139 us (0.986)
  waiting for transfers between devices: 41.6 us -> 36.5 us
  Pallas kernels: 39.7 us -> 42.8 us
  local copies, waits for them, and re-layouts: 3.28 us -> 1.29 us
  starting transfers between devices: 17 us -> 18.8 us
    ppermute x2, waiting for transfers between devices: 20.8 us -> 16.4 us  [shifted(): return lax.ppermute(array, 'slab', pairs)]
    pallas_call x1, Pallas kernels: 3.47 us -> 7.53 us  [on_device(): flow(local_kernel, [(struct((tokens, WIDTH)), up['token'](WIDTH)), (struc...]
    pallas_call x2, Pallas kernels: 7.61 us -> 5.21 us  [packed(): call(kernel, out, 0, moved, (tensor_count, runs), specs, out_spec, scratch)]
    unnamed x16 -> x10, local copies, waits for them, and re-layouts: 2.01 us -> 0.02 us
    ppermute x1, starting transfers between devices: 0.07 us -> 1.87 us  [two_parts(): other = lax.ppermute(array, axis, [(i, i ^ step) for i in range(count)])]
    ppermute x1, waiting for transfers between devices: 2.98 us -> 1.19 us  [two_parts(): other = lax.ppermute(array, axis, [(i, i ^ step) for i in range(count)])]
  transfers between devices with their start and end apart: 6 -> 6, of which waited for: 5 -> 5; matrix products, arithmetic and copies ran while one was open for 1% -> 1% of each run, Pallas kernels for 12% -> 16%
where the time goes in v8:
time: 139 us; the launch traced here: 138 us
  Pallas kernels  42.8 us (31%)
  blocking collectives  38 us (27%)
  waiting for transfers between devices  36.5 us (26%)
  starting transfers between devices  18.8 us (14%)
    all_to_all x1, blocking collectives, exchange(): lax.all_to_all(array, ('sub', 'tensor'), split_axis=0, concat_axis=0, til...  38 us
    all_to_all x2, waiting for transfers between devices, exchange(): lax.all_to_all(array, ('sub', 'tensor'), split_axis=0, concat_axis=0, til...  17.7 us
    ppermute x2, waiting for transfers between devices, shifted(): return lax.ppermute(array, 'slab', pairs)  16.4 us
    all_to_all x2, starting transfers between devices, exchange(): lax.all_to_all(array, ('sub', 'tensor'), split_axis=0, concat_axis=0, til...  11 us
    pallas_call x1, Pallas kernels, on_device(): flow(last_kernel, [(hbm((peers, last_rows, LANES), bf16), pl.BlockSpec(me...  7.84 us
    pallas_call x1, Pallas kernels, on_device(): flow(local_kernel, [(struct((tokens, WIDTH)), up['token'](WIDTH)), (struc...  7.53 us
    pallas_call x1, Pallas kernels, on_device(): flow(within_kernel, [(hbm((tokens, WIDTH)), up['token'](WIDTH)), (hbm((ch...  5.98 us
    ppermute x2, starting transfers between devices, shifted(): return lax.ppermute(array, 'slab', pairs)  5.78 us
  transfers between devices with their start and end apart: 6, of which 5 were waited for; matrix products, arithmetic and copies ran while one was open for 1% of the time, Pallas kernels for 16%

profile of v8, /device:TPU:0, one launch (start us, length us, event | category | flops | bytes accessed | tf_op | source)
XLA Modules:
  0.0 138.2 jit_solution(5575275415653789531)
XLA Ops:
  0.6 2.5 %shard_map.169 = bf16[8,2,400,128]{3,2,1,0:T(8,128)(2,1)} custom-call(bf16[64,8192]{1,0:T(8,128)(2,1)} %x_ref.1, bf16[64,1024]{1,0:T(8,128)(2,1)} %b_ref.1, bf16[64,1024]{1,0:T(8,128)(2,1)} %c_ref.1, bf16[64,128]{1,0:T(8,128)(2,1)} %steps_ref.1), custom_call_target="tpu_custom_call" | custom-call | bytes 3276800 | tf_op jit(solution)/shard_map/pallas_call | solution.py:666
  3.2 6.4 %all-to-all-start = ((bf16[16,400,128]{2,1,0:T(8,128)(2,1)}), bf16[16,400,128]{2,1,0:T(8,128)(2,1)S(1)}, u32[]{:S(2)}, u32[]{:S(2)}) async-start(bf16[16,400,128]{2,1,0:T(8,128)(2,1)} %bitcast.11), calls=%async_computation | async-start | bytes 3276800 | tf_op jit(solution)/shard_map/all_to_all | solution.py:644
  9.9 0.1 reshape_reshape.3.refs_7_.refs_8_.refs_12_.refs_15_
  10.0 0.8 dynamic_slice.15
  11.0 2.7 %shard_map.170 = bf16[8,2,512,128]{3,2,1,0:T(8,128)(2,1)} custom-call(bf16[64,8192]{1,0:T(8,128)(2,1)} %z_ref, bf16[64,8192]{1,0:T(8,128)(2,1)} %grad_ref.1), custom_call_target="tpu_custom_call" | custom-call | bytes 4194304 | tf_op jit(solution)/shard_map/pallas_call | solution.py:666
  13.7 17.7 %all-to-all-done.refs_0_.refs_1_ = bf16[16,400,128]{2,1,0:T(8,128)(2,1)S(1)} async-done(((bf16[16,400,128]{2,1,0:T(8,128)(2,1)}), bf16[16,400,128]{2,1,0:T(8,128)(2,1)S(1)}, u32[]{:S(2)}, u32[]{:S(2)}) %all-to-all-start) | async-done | bytes 1638432 | tf_op jit(solution)/shard_map/all_to_all | solution.py:644
  31.4 4.6 %all-to-all-start.1 = ((bf16[16,512,128]{2,1,0:T(8,128)(2,1)}), bf16[16,512,128]{2,1,0:T(8,128)(2,1)}, u32[]{:S(2)}, u32[]{:S(2)}) async-start(bf16[16,512,128]{2,1,0:T(8,128)(2,1)} %bitcast.10), calls=%async_computation.1 | async-start | bytes 4194304 | tf_op jit(solution)/shard_map/all_to_all | solution.py:644
  36.0 4.4 %shard_map.171 = (f32[1024,128]{1,0:T(8,128)}, f32[64,1024]{1,0:T(8,128)}, f32[8,128,512]{2,1,0:T(8,128)}, f32[8,8,512]{2,1,0:T(8,128)}, bf16[128,512]{1,0:T(8,128)(2,1)S(1)}, /*index=5*/f32[8,512]{1,0:T(8,128)}) custom-call(bf16[16,400,128]{2,1,0:T(8,128)(2,1)S(1)} %all-to-all-done.refs_0_.refs_1_, bf16[16,400,128]{2,1,0:T(8,128)(2,1)S(1)} %all-to-all-done.refs_0_.refs_1_, ...), custom_call_target="tpu_custom_call" | custom-call | flops 268435456 | bytes 4194304 | tf_op jit(solution)/shard_map/pallas_call | solution.py:717
  40.4 4.5 %collective-permute-start = (bf16[128,512]{1,0:T(8,128)(2,1)S(1)}, bf16[128,512]{1,0:T(8,128)(2,1)S(1)}, u32[]{:S(2)}, u32[]{:S(2)}) collective-permute-start(bf16[128,512]{1,0:T(8,128)(2,1)S(1)} %get-tuple-element.49), channel_id=1, source_target_pairs={{0,16},{1,17},{2,18},{3,19},{4,20},{5,21},{6,22},{7,23},{8,24},{9,... | collective-permute-start | bytes 393224 | tf_op jit(solution)/shard_map/ppermute | solution.py:584
  44.9 6.0 %shard_map.172 = (f32[1024,512]{1,0:T(8,128)}, f32[8,128,512]{2,1,0:T(8,128)}, f32[8,8,512]{2,1,0:T(8,128)}) custom-call(bf16[16,400,128]{2,1,0:T(8,128)(2,1)S(1)} %all-to-all-done.refs_0_.refs_1_, f32[1024,128]{1,0:T(8,128)} %get-tuple-element.44.refs_1_.refs_3_.refs_4_.refs_7_, f32[64,1024]{1,0:T(8,128)} %get-tuple-element.45.refs_2_.refs_5_.refs_8_, ...), custom_call_target="tpu_custom_call" | custom-call | flops 805306368 | bytes 8388608 | tf_op jit(solution)/shard_map/pallas_call | solution.py:741
  50.9 13.9 %collective-permute-done.refs_4_.refs_8_.refs_13_ = bf16[128,512]{1,0:T(8,128)(2,1)S(1)} collective-permute-done((bf16[128,512]{1,0:T(8,128)(2,1)S(1)}, bf16[128,512]{1,0:T(8,128)(2,1)S(1)}, u32[]{:S(2)}, u32[]{:S(2)}) %collective-permute-start) | collective-permute-done | bytes 131104 | tf_op jit(solution)/shard_map/ppermute | solution.py:584
  64.8 4.6 %shard_map.173 = (f32[1024,512]{1,0:T(8,128)S(1)}, f32[8,8,128]{2,1,0:T(8,128)S(1)}) custom-call(bf16[16,400,128]{2,1,0:T(8,128)(2,1)S(1)} %all-to-all-done.refs_0_.refs_1_, bf16[16,512,128]{2,1,0:T(8,128)(2,1)} %all-to-all-done.1.refs_1_, f32[1024,512]{1,0:T(8,128)} %get-tuple-element.48.refs_2_, ...), custom_call_target="tpu_custom_call" | custom-call | flops 134217728 | bytes 8388608 | tf_op jit(solution)/shard_map/pallas_call | solution.py:756
  69.5 1.2 collective-permute-done.1.refs_6_.refs_10_
  70.7 4.7 %shard_map.174 = (bf16[1024,512]{1,0:T(8,128)(2,1)S(1)}, f32[8,128,512]{2,1,0:T(8,128)S(1)}, bf16[128,512]{1,0:T(8,128)(2,1)S(1)}) custom-call(bf16[16,400,128]{2,1,0:T(8,128)(2,1)S(1)} %all-to-all-done.refs_0_.refs_1_, bf16[16,512,128]{2,1,0:T(8,128)(2,1)} %all-to-all-done.1.refs_1_, f32[1024,512]{1,0:T(8,128)S(1)} %get-tuple-element.53.refs_2_, ...), custom_call_target="tpu_custom_call" | custom-call | flops 268435456 | bytes 6291456 | tf_op jit(solution)/shard_map/pallas_call | solution.py:774
  75.3 1.3 collective-permute-start.2
  76.6 7.5 %shard_map.175 = (f32[1024,512]{1,0:T(8,128)S(1)}, f32[1024,128]{1,0:T(8,128)S(1)}, bf16[16,64,128]{2,1,0:T(8,128)(2,1)S(1)}, bf16[16,256,128]{2,1,0:T(8,128)(2,...) custom-call(bf16[16,400,128]{2,1,0:T(8,128)(2,1)S(1)} %all-to-all-done.refs_0_.refs_1_, ...), custom_call_target="tpu_custom_call" | custom-call | flops 1342177280 | bytes 8388608 | tf_op jit(solution)/shard_map/pallas_call | solution.py:792
  84.2 2.4 %collective-permute-done.2.refs_9_ = bf16[128,512]{1,0:T(8,128)(2,1)S(1)} collective-permute-done((bf16[128,512]{1,0:T(8,128)(2,1)S(1)}, bf16[128,512]{1,0:T(8,128)(2,1)S(1)}, u32[]{:S(2)}, u32[]{:S(2)}) %collective-permute-start.2) | collective-permute-done | bytes 131104 | tf_op jit(solution)/shard_map/ppermute | solution.py:584
  86.6 7.8 %shard_map.176 = bf16[16,672,128]{2,1,0:T(8,128)(2,1)} custom-call(bf16[16,400,128]{2,1,0:T(8,128)(2,1)S(1)} %all-to-all-done.refs_0_.refs_1_, f32[1024,512]{1,0:T(8,128)S(1)} %get-tuple-element.57.refs_1_, f32[1024,128]{1,0:T(8,128)S(1)} %get-tuple-element.58.refs_2_, bf16[16,64,128]{2,1,0:T(8,128)(2,1)S(1)} %get-tuple-element.59.refs_3_, ...), custom_call_target="tpu_custom_call" | custom-call | flops 536870912 | bytes 8388608 | tf_op jit(solution)/shard_map/pallas_call | solution.py:819
  94.5 38.0 %all_to_all.15.refs_0_.refs_1_ = bf16[16,672,128]{2,1,0:T(8,128)(2,1)S(1)} all-to-all(bf16[16,672,128]{2,1,0:T(8,128)(2,1)} %shard_map.176), channel_id=1, replica_groups=mesh['slab'=2,'sub'=8,'tensor'=2] {'sub','tensor'}, dimensions={0} | all-to-all | bytes 5505024 | tf_op jit(solution)/shard_map/all_to_all | solution.py:644
  132.5 0.1 shard_map.178.own_ref
  132.6 1.9 %collective-permute-start.3 = (f32[40,128]{1,0:T(8,128)S(1)}, f32[40,128]{1,0:T(8,128)S(1)}, u32[]{:S(2)}, u32[]{:S(2)}) collective-permute-start(f32[40,128]{1,0:T(8,128)S(1)} %shard_map.178.own_ref), channel_id=1, source_target_pairs={{0,16},{16,0},{1,17},{17,1},{2,18},{18,2},{3,19},{19,3},{4,20},{20... | collective-permute-start | bytes 61448 | tf_op jit(solution)/shard_map/ppermute | solution.py:615
  134.5 1.9 %shard_map.177 = (bf16[64,8192]{1,0:T(8,128)(2,1)}, bf16[64,8192]{1,0:T(8,128)(2,1)}, bf16[64,1024]{1,0:T(8,128)(2,1)}, bf16[64,1024]{1,0:T(8,128)(2,1)}, bf16[64,128]{1,0:T(8,128)(2,1)}) custom-call(bf16[16,672,128]{2,1,0:T(8,128)(2,1)S(1)} %all_to_all.15.refs_0_.refs_1_), custom_call_target="tpu_custom_call" | custom-call | bytes 5242880 | tf_op jit(solution)/shard_map/pallas_call | solution.py:856
  136.4 1.2 collective-permute-done.3.other_ref
  137.6 0.6 shard_map.179
  (20 shorter events, 0.6 us)
Async XLA Ops:
  3.1 6.5 %copy-start.2 = (f32[64]{0:T(128)S(1)}, f32[64]{0:T(128)}, u32[]{:S(2)}) copy-start(f32[64]{0:T(128)} %param.15) | copy-start | bytes 772
  3.2 6.5 %copy-start.3 = (f32[64]{0:T(128)S(1)}, f32[64]{0:T(128)}, u32[]{:S(2)}) copy-start(f32[64]{0:T(128)} %param.16) | copy-start | bytes 772
  3.2 6.6 %copy-start.4 = (f32[64]{0:T(128)S(1)}, f32[64]{0:T(128)}, u32[]{:S(2)}) copy-start(f32[64]{0:T(128)} %param.17) | copy-start | bytes 772
  3.2 28.3 %all-to-all-start = ((bf16[16,400,128]{2,1,0:T(8,128)(2,1)}), bf16[16,400,128]{2,1,0:T(8,128)(2,1)S(1)}, u32[]{:S(2)}, u32[]{:S(2)}) async-start(bf16[16,400,128]{2,1,0:T(8,128)(2,1)} %bitcast.11), calls=%async_computation | async-start | bytes 3276800 | tf_op jit(solution)/shard_map/all_to_all | solution.py:644
  31.4 33.4 %all-to-all-start.1 = ((bf16[16,512,128]{2,1,0:T(8,128)(2,1)}), bf16[16,512,128]{2,1,0:T(8,128)(2,1)}, u32[]{:S(2)}, u32[]{:S(2)}) async-start(bf16[16,512,128]{2,1,0:T(8,128)(2,1)} %bitcast.10), calls=%async_computation.1 | async-start | bytes 4194304 | tf_op jit(solution)/shard_map/all_to_all | solution.py:644
  40.4 24.4 %collective-permute-start = (bf16[128,512]{1,0:T(8,128)(2,1)S(1)}, bf16[128,512]{1,0:T(8,128)(2,1)S(1)}, u32[]{:S(2)}, u32[]{:S(2)}) collective-permute-start(bf16[128,512]{1,0:T(8,128)(2,1)S(1)} %get-tuple-element.49), channel_id=1, source_target_pairs={{0,16},{1,17},{2,18},{3,19},{4,20},{5,21},{6,22},{7,23},{8,24},{9,... | collective-permute-start | bytes 393224 | tf_op jit(solution)/shard_map/ppermute | solution.py:584
  64.8 5.9 %copy-start = (f32[1024,128]{1,0:T(8,128)S(1)}, f32[1024,128]{1,0:T(8,128)}, u32[]{:S(2)}) copy-start(f32[1024,128]{1,0:T(8,128)} %get-tuple-element.44.refs_1_.refs_3_.refs_4_.refs_7_) | copy-start | bytes 1572868
  69.4 1.3 collective-permute-start.1
  70.7 6.0 %copy-start.1 = (f32[64,1024]{1,0:T(8,128)S(1)}, f32[64,1024]{1,0:T(8,128)}, u32[]{:S(2)}) copy-start(f32[64,1024]{1,0:T(8,128)} %get-tuple-element.45.refs_2_.refs_5_.refs_8_) | copy-start | bytes 786436
  75.3 11.3 %collective-permute-start.2 = (bf16[128,512]{1,0:T(8,128)(2,1)S(1)}, bf16[128,512]{1,0:T(8,128)(2,1)S(1)}, u32[]{:S(2)}, u32[]{:S(2)}) collective-permute-start(bf16[128,512]{1,0:T(8,128)(2,1)S(1)} %get-tuple-element.62), channel_id=1, source_target_pairs={{16,0},{17,1},{18,2},{19,3},{20,4},{21,5},{22,6},{23,7},{24,8},{25... | collective-permute-start | bytes 393224 | tf_op jit(solution)/shard_map/ppermute | solution.py:584
  132.6 5.0 %collective-permute-start.3 = (f32[40,128]{1,0:T(8,128)S(1)}, f32[40,128]{1,0:T(8,128)S(1)}, u32[]{:S(2)}, u32[]{:S(2)}) collective-permute-start(f32[40,128]{1,0:T(8,128)S(1)} %shard_map.178.own_ref), channel_id=1, source_target_pairs={{0,16},{16,0},{1,17},{17,1},{2,18},{18,2},{3,19},{19,3},{4,20},{20... | collective-permute-start | bytes 61448 | tf_op jit(solution)/shard_map/ppermute | solution.py:615

commit v9 on v8

--- a/solution.py
+++ b/solution.py
@@ -253,22 +253,34 @@
             at = slice(k * HEADS, (k + 1) * HEADS)
             rows_s[k] = jnp.concatenate([kind[at] for kind in kinds], axis=0)
 
+    made = []
+    state = [carry[:, lanes(j)] for j in range(PAIRS)]
+    decays = [whole_ref[:, lanes(j)] for j in range(PAIRS)]
     for i in range(per_step):
         rows = rows_s[c * per_step + i]
-        smt_ref[:, lanes(i)] = rows
         sm = jnp.concatenate([rows, jnp.zeros_like(rows)], axis=0).T
-        sm_ref[i * CHUNK : (i + 1) * CHUNK, :] = sm
         last = jnp.broadcast_to(sm[CHUNK - 1 : CHUNK, :], (8, LANES))
         sources_t = message.get(first_ref, i, B).T
+        decs, owns = [], []
         for j in range(PAIRS):
             dec = spread_pair(last, ECUM, j)
-            dec_ref[i, :, lanes(j)] = dec
-            whole_ref[:, lanes(j)] = whole_ref[:, lanes(j)] * dec
             scaled = message.get(first_ref, i, X + j).astype(f32) * spread_pair(sm, WEIGHT, j)
             own = mm_two(sources_t, *two_terms(scaled))
-            own_ref[i, :, lanes(j)] = own
-            carry[:, lanes(j)] = dec[0:1] * carry[:, lanes(j)] + own
-    state_ref[...] = carry[...].astype(bf16)
+            state[j] = dec[0:1] * state[j] + own
+            decays[j] = decays[j] * dec
+            decs.append(dec)
+            owns.append(own)
+        made.append((rows, sm, decs, owns))
+    for i, (rows, sm, decs, owns) in enumerate(made):
+        smt_ref[:, lanes(i)] = rows
+        sm_ref[i * CHUNK : (i + 1) * CHUNK, :] = sm
+        for j in range(PAIRS):
+            dec_ref[i, :, lanes(j)] = decs[j]
+            own_ref[i, :, lanes(j)] = owns[j]
+    for j in range(PAIRS):
+        carry[:, lanes(j)] = state[j]
+        whole_ref[:, lanes(j)] = decays[j]
+        state_ref[:, lanes(j)] = state[j].astype(bf16)
 
 
 def within_kernel(
@@ -282,29 +294,40 @@
 
     t = lax.broadcasted_iota(jnp.int32, (CHUNK, CHUNK), 0)
     s = lax.broadcasted_iota(jnp.int32, (CHUNK, CHUNK), 1)
+    made = []
+    states = [carry[:, lanes(j)] for j in range(PAIRS)]
+    before = pre[...]
     for i in range(per_step):
         rows = slice(i * CHUNK, (i + 1) * CHUNK)
         sm = sm_ref[rows, :]
+        smt = smt_ref[:, lanes(i)]
         readers = message.get(first_ref, i, C)
         scores = jnp.where(t >= s, mm_nt(readers, message.get(first_ref, i, B)), 0.0)
-        pre_ref[i] = pre[...]
-        pre[...] = pre[...] * dec_ref[i]
-        for j in range(PAIRS):
-            at = lanes(j)
+        ys = []
+        for j in range(PAIRS):
             weights = []
             for h in (2 * j, 2 * j + 1):
-                here = sm_ref[rows, CUM * HEADS + h : CUM * HEADS + h + 1]
-                there = smt_ref[SHIFTED * HEADS + h : SHIFTED * HEADS + h + 1, lanes(i)]
+                here = sm[:, CUM * HEADS + h : CUM * HEADS + h + 1]
+                there = smt[SHIFTED * HEADS + h : SHIFTED * HEADS + h + 1, :]
                 weights.append(
                     (scores * jnp.exp(jnp.minimum(here - there, CLAMP))).astype(bf16)
                 )
             values = split_pair(message.get(first_ref, i, X + j))
             within = mm(jnp.concatenate(weights, axis=1), values)
-            state = carry[:, at]
-            start_ref[i, :, at] = state
-            carried = mm_two(readers, *two_terms(state))
-            y_ref[rows, at] = within + spread_pair(sm, ECUM, j) * carried
-            carry[:, at] = dec_ref[i, 0:1, at] * state + own_ref[i, :, at]
+            carried = mm_two(readers, *two_terms(states[j]))
+            ys.append(within + spread_pair(sm, ECUM, j) * carried)
+        made.append((ys, list(states), before))
+        for j in range(PAIRS):
+            states[j] = dec_ref[i, 0:1, lanes(j)] * states[j] + own_ref[i, :, lanes(j)]
+        before = before * dec_ref[i]
+    for i, (ys, starts, prefix) in enumerate(made):
+        pre_ref[i] = prefix
+        for j in range(PAIRS):
+            y_ref[i * CHUNK : (i + 1) * CHUNK, lanes(j)] = ys[j]
+            start_ref[i, :, lanes(j)] = starts[j]
+    pre[...] = before
+    for j in range(PAIRS):
+        carry[:, lanes(j)] = states[j]
 
 
 def mix_kernel(
@@ -312,26 +335,33 @@
     first_ref, second_ref, within_ref, sm_ref, inbound_ref, pre_ref, gain_ref, skip_ref,
     y_ref, sums_ref,
 ):
+    made = []
+    inbound = inbound_ref[...].astype(bf16)
     for i in range(per_step):
         rows = slice(i * CHUNK, (i + 1) * CHUNK)
         sm = sm_ref[rows, :]
-        carried = mm(message.get(first_ref, i, C), inbound_ref[...].astype(bf16))
+        carried = mm(message.get(first_ref, i, C), inbound)
         power = jnp.zeros((CHUNK, LANES), f32)
         cross = jnp.zeros((CHUNK, LANES), f32)
+        ys = []
         for j in range(PAIRS):
             at = lanes(j)
             decay = spread_pair(sm, ECUM, j) * pre_ref[i, 0:1, at]
             y = within_ref[rows, at] + decay * carried[:, at]
-            y_ref[rows, at] = y
+            ys.append(y)
             values = message.get(first_ref, i, X + j).astype(f32)
             gates = message.get(second_ref, i, Z + j).astype(f32)
             grad = message.get(second_ref, i, GRAD + j).astype(f32)
             gated = (y + skip_ref[0:1, at] * values) * (gates * sigmoid(gates))
             power = power + gated * gated
             cross = cross + grad * gain_ref[0:1, at] * gated
-        sums_ref[i, 0:1, :] = jnp.sum(power.T, axis=0, keepdims=True)
-        sums_ref[i, 1:2, :] = jnp.sum(cross.T, axis=0, keepdims=True)
-        sums_ref[i, 2:, :] = jnp.zeros((6, LANES), f32)
+        made.append(
+            (ys, jnp.sum(power.T, axis=0, keepdims=True), jnp.sum(cross.T, axis=0, keepdims=True))
+        )
+    for i, (ys, power, cross) in enumerate(made):
+        for j in range(PAIRS):
+            y_ref[i * CHUNK : (i + 1) * CHUNK, lanes(j)] = ys[j]
+        sums_ref[i] = jnp.concatenate([power, cross, jnp.zeros((6, LANES), f32)], axis=0)
 
 
 def norm_factors(sums):
@@ -354,6 +384,8 @@
     def _():
         back_sum[...] = jnp.zeros_like(back_sum)
 
+    made = []
+    sums = [back_sum[:, lanes(j)] for j in range(PAIRS)]
     for i in range(per_step):
         rows = slice(i * CHUNK, (i + 1) * CHUNK)
         sm = sm_ref[rows, :]
@@ -367,19 +399,23 @@
             silu = gates * sigmoid(gates)
             gated = (y_ref[rows, at] + skip_ref[0:1, at] * values) * silu
             d_mixed = (inverse * grad * gain_ref[0:1, at] - pull * gated) * silu
-            mixed_ref[rows, at] = d_mixed.astype(bf16)
             back = mm_two(readers_t, *two_terms(d_mixed * spread_pair(sm, ECUM, j)))
-            back_ref[i, :, at] = back
-            back_sum[:, at] += pre_ref[i, 0:1, at] * back
-    slab_ref[...] = back_sum[...].astype(bf16)
+            sums[j] = sums[j] + pre_ref[i, 0:1, at] * back
+            made.append((i, j, d_mixed.astype(bf16), back))
+    for i, j, d_mixed, back in made:
+        mixed_ref[i * CHUNK : (i + 1) * CHUNK, lanes(j)] = d_mixed
+        back_ref[i, :, lanes(j)] = back
+    for j in range(PAIRS):
+        back_sum[:, lanes(j)] = sums[j]
+        slab_ref[:, lanes(j)] = sums[j].astype(bf16)
 
 
 def local_kernel(
     message, per_step,
     first_ref, second_ref, y_ref, grad_ref, sm_ref, smt_ref, start_ref, pre_ref, inbound_ref,
     sums_ref, other_ref, gain_ref, skip_ref,
-    values_out, sources_out, readers_out, gate_ref, e_ref, param_ref,
-    gain_sum, skip_sum, high_s, low_s, scaled_s,
+    values_out, sources_out, readers_out, gate_ref, e_ref, start_out, param_ref,
+    gain_sum, skip_sum,
 ):
     c = pl.program_id(0)
 
@@ -392,15 +428,19 @@
     t = lax.broadcasted_iota(jnp.int32, (CHUNK, CHUNK), 1)
     causal = t >= s
     ones = head_rows()
-    inbound = inbound_ref[...].astype(f32)
+    made = []
+    gains = [gain_sum[0:1, lanes(j)] for j in range(PAIRS)]
+    skips = [skip_sum[0:1, lanes(j)] for j in range(PAIRS)]
     for i in range(per_step):
         rows = slice(i * CHUNK, (i + 1) * CHUNK)
         sm = sm_ref[rows, :]
+        smt = smt_ref[:, lanes(i)]
         sources = message.get(first_ref, i, B)
         readers = message.get(first_ref, i, C)
         inverse, pull = norm_factors(sums_ref[i] + other_ref[i])
         scores = jnp.where(causal, mm_nt(sources, readers), 0.0)
         total = jnp.zeros((CHUNK, CHUNK), f32)
+        d_values, d_gates, highs, lows, scaleds, starts = [], [], [], [], [], []
         for j in range(PAIRS):
             at = lanes(j)
             rounded = grad_ref[rows, at]
@@ -409,12 +449,12 @@
             weight_grads = mm_nt(x, grads)
             weights = []
             for k, h in enumerate((2 * j, 2 * j + 1)):
-                there = sm_ref[rows, SHIFTED * HEADS + h : SHIFTED * HEADS + h + 1]
-                here = smt_ref[CUM * HEADS + h : CUM * HEADS + h + 1, lanes(i)]
+                there = sm[:, SHIFTED * HEADS + h : SHIFTED * HEADS + h + 1]
+                here = smt[CUM * HEADS + h : CUM * HEADS + h + 1, :]
                 decay = jnp.exp(jnp.minimum(here - there, CLAMP))
                 weights.append((scores * decay).astype(bf16))
                 total = total + weight_grads[:, lanes(k)] * decay
-            values_out[rows, at] = mm(jnp.concatenate(weights, axis=1), grads)
+            d_values.append(mm(jnp.concatenate(weights, axis=1), grads))
 
             values = x.astype(f32)
             gates = message.get(second_ref, i, Z + j).astype(f32)
@@ -425,20 +465,38 @@
             silu = gates * sig
             gated = mixed * silu
             scaled = inverse * grad
-            gain_sum[0:1, at] += jnp.sum(scaled * gated, axis=0, keepdims=True)
+            gains[j] = gains[j] + jnp.sum(scaled * gated, axis=0, keepdims=True)
             d_gated = scaled * gain_ref[0:1, at] - pull * gated
             d_gate = d_gated * mixed * (sig + silu * (1.0 - sig))
-            message.put(gate_ref, i, j, d_gate.astype(bf16))
-            skip_sum[0:1, at] += jnp.sum(values * (d_gated * silu), axis=0, keepdims=True)
+            d_gates.append(d_gate.astype(bf16))
+            skips[j] = skips[j] + jnp.sum(values * (d_gated * silu), axis=0, keepdims=True)
             d_mixed = rounded.astype(f32)
-            high_s[:, at], low_s[:, at] = two_terms(d_mixed * y)
-            scaled_s[:, at] = (d_mixed * spread_pair(sm, ECUM, j)).astype(bf16)
-        e_ref[:, lanes(i)] = (mm_nt(ones, high_s[...]) + mm_nt(ones, low_s[...]))[:HEADS]
+            high, low = two_terms(d_mixed * y)
+            highs.append(high)
+            lows.append(low)
+            scaleds.append((d_mixed * spread_pair(sm, ECUM, j)).astype(bf16))
+            starts.append(
+                start_ref[i, :, at] + pre_ref[i, 0:1, at] * inbound_ref[:, at].astype(f32)
+            )
+        e = mm_nt(ones, jnp.concatenate(highs, axis=1)) + mm_nt(ones, jnp.concatenate(lows, axis=1))
         total = jnp.where(causal, total, 0.0).astype(bf16)
-        sources_out[rows, :] = mm(total, readers)
-        start = (start_ref[i] + pre_ref[i, 0:1, :] * inbound).astype(bf16)
-        d_readers = mm_tn(total, sources) + mm_nt(scaled_s[...], start)
-        message.put(readers_out, i, 0, d_readers.astype(bf16))
+        start = jnp.concatenate([part.astype(bf16) for part in starts], axis=1)
+        d_readers = mm_tn(total, sources) + mm_nt(jnp.concatenate(scaleds, axis=1), start)
+        made.append(
+            (d_values, d_gates, starts, e[:HEADS], mm(total, readers), d_readers.astype(bf16))
+        )
+    for i, (d_values, d_gates, starts, e, d_sources, d_readers) in enumerate(made):
+        rows = slice(i * CHUNK, (i + 1) * CHUNK)
+        for j in range(PAIRS):
+            values_out[rows, lanes(j)] = d_values[j]
+            message.put(gate_ref, i, j, d_gates[j])
+            start_out[i, :, lanes(j)] = starts[j]
+        e_ref[:, lanes(i)] = e
+        sources_out[rows, :] = d_sources
+        message.put(readers_out, i, 0, d_readers)
+    for j in range(PAIRS):
+        gain_sum[0:1, lanes(j)] = gains[j]
+        skip_sum[0:1, lanes(j)] = skips[j]
 
     @pl.when(c == pl.num_programs(0) - 1)
     def _():
@@ -455,9 +513,9 @@
 def last_kernel(
     message, per_step,
     first_ref, within_ref, sources_ref, readers_ref, gate_ref, grad_ref, e_ref, sm_ref, smt_ref, outer_ref,
-    back_ref, start_ref, pre_ref, inbound_ref, dec_ref, skip_ref, heads_ref, early_ref,
+    back_ref, start_ref, dec_ref, skip_ref, heads_ref, early_ref,
     out_ref,
-    carry, sums, high_s, low_s, scaled_s, state_s, flux_s, message_s, sent,
+    carry, sums, message_s, sent,
 ):
     c = pl.program_id(0)
 
@@ -481,47 +539,62 @@
         at = (pl.ds(peer, span), pl.ds(0, LAST * r))
         return pltpu.make_async_copy(message_s.at[at], out_ref.at[at], sent.at[step])
 
+    made = []
+    states = [carry[:, lanes(j)] for j in range(PAIRS)]
+    logs_sum, steps_sum = sums[:HEADS, :], sums[HEADS:, :]
     for i in reversed(range(per_step)):
         rows = slice(i * CHUNK, (i + 1) * CHUNK)
         sm = sm_ref[rows, :]
         sources = message.get(first_ref, i, B)
+        d_values, highs, lows, scaleds, rounded, fluxes = [], [], [], [], [], []
         for j in range(PAIRS):
             at = lanes(j)
-            state = carry[:, at]
-            high, low = two_terms(state)
-            state_s[:, at] = high
+            high, low = two_terms(states[j])
+            rounded.append(high)
             values = message.get(first_ref, i, X + j).astype(f32)
             weight = spread_pair(sm, WEIGHT, j)
             grad = within_ref[rows, at] + weight * mm_two(sources, high, low)
             skipped = skip_ref[0:1, at] * grad_ref[rows, at].astype(f32)
-            message.put(mine, i, LAST_X + j, (grad + skipped).astype(bf16))
-            high_s[:, at], low_s[:, at] = two_terms(values * grad)
-            scaled_s[:, at] = (values * weight).astype(bf16)
-            new = dec_ref[i, 0:1, at] * state + back_ref[i, :, at]
-            carry[:, at] = new
-            start = start_ref[i, :, at] + pre_ref[i, 0:1, at] * inbound_ref[:, at].astype(f32)
-            flux_s[:, at] = jnp.broadcast_to(
-                jnp.sum(start * new, axis=0, keepdims=True), (16, LANES)
+            d_values.append((grad + skipped).astype(bf16))
+            high, low = two_terms(values * grad)
+            highs.append(high)
+            lows.append(low)
+            scaleds.append((values * weight).astype(bf16))
+            states[j] = dec_ref[i, 0:1, at] * states[j] + back_ref[i, :, at]
+            fluxes.append(
+                jnp.broadcast_to(
+                    jnp.sum(start_ref[i, :, at] * states[j], axis=0, keepdims=True), (16, LANES)
+                )
             )
-        d_sources = sources_ref[rows, :] + mm_nt(scaled_s[...], state_s[...])
-        message.put(mine, i, LAST_B, d_sources.astype(bf16))
-        message.put(mine, i, LAST_C, message.get(readers_ref, i, 0))
-        for j in range(PAIRS):
-            message.put(mine, i, LAST_Z + j, message.get(gate_ref, i, j))
-        g = (mm_nt(ones, high_s[...]) + mm_nt(ones, low_s[...]))[:HEADS]
-        high, low = two_terms(flux_s[...])
+        d_sources = sources_ref[rows, :] + mm_nt(
+            jnp.concatenate(scaleds, axis=1), jnp.concatenate(rounded, axis=1)
+        )
+        g = mm_nt(ones, jnp.concatenate(highs, axis=1)) + mm_nt(ones, jnp.concatenate(lows, axis=1))
+        g = g[:HEADS]
+        high, low = two_terms(jnp.concatenate(fluxes, axis=1))
         constant = (mm_nt(ones, high) + mm_nt(ones, low))[:HEADS, 0:1]
         flux = constant + mm_exact(g - e_ref[:, lanes(i)], earlier)
         soft = smt_ref[DT * HEADS : (DT + 1) * HEADS, lanes(i)]
         rate = smt_ref[RATE * HEADS : (RATE + 1) * HEADS, lanes(i)]
         sig = smt_ref[SIG * HEADS : (SIG + 1) * HEADS, lanes(i)]
         steps = (g / soft - decay_rate * flux) * sig
-        sums[:HEADS, :] += flux * rate
-        sums[HEADS:, :] += steps
+        logs_sum = logs_sum + flux * rate
+        steps_sum = steps_sum + steps
         steps = jnp.concatenate([steps, jnp.zeros_like(steps)], axis=0)
+        made.append((i, d_values, d_sources.astype(bf16), steps))
+    for i, d_values, d_sources, steps in made:
+        for j in range(PAIRS):
+            message.put(mine, i, LAST_X + j, d_values[j])
+            message.put(mine, i, LAST_Z + j, message.get(gate_ref, i, j))
+        message.put(mine, i, LAST_B, d_sources)
+        message.put(mine, i, LAST_C, message.get(readers_ref, i, 0))
         for p in range(message.per_chunk):
             part = steps if p == 0 else pltpu.roll(steps, LANES - p * r, 1)
             mine[i * message.per_chunk + p, LAST * r : LAST * r + STEP_ROWS, :] = part.astype(bf16)
+    for j in range(PAIRS):
+        carry[:, lanes(j)] = states[j]
+    sums[:HEADS, :] = logs_sum
+    sums[HEADS:, :] = steps_sum
     body_copy(c).start()
 
     @pl.when(c == pl.num_programs(0) - 1)
@@ -789,7 +862,7 @@
 
     outer = carry_over(slab_back, decay, after, slab_count, -1)
 
-    d_values, d_sources, d_readers, d_gates, e, params = flow(
+    d_values, d_sources, d_readers, d_gates, e, starts, params = flow(
         local_kernel,
         [
             (struct((tokens, WIDTH)), up["token"](WIDTH)),
@@ -797,6 +870,7 @@
             (struct((peers, rows, LANES), bf16), up["message"](rows)),
             (struct((peers, PAIRS * rows, LANES), bf16), up["message"](PAIRS * rows)),
             (struct((HEADS, tokens)), up["lane"](HEADS)),
+            (struct((chunks, STATE, WIDTH)), up["chunk"](STATE, WIDTH)),
             (struct((8, LANES)), whole(8, LANES)),
         ],
         10 * unit, size * 16,
@@ -806,11 +880,7 @@
             up["chunk"](STATE, WIDTH), up["chunk"](8, WIDTH), whole(STATE, WIDTH),
             up["chunk"](8, LANES), up["chunk"](8, LANES), whole(1, WIDTH), whole(1, WIDTH),
         ],
-        [
-            pltpu.VMEM((8, WIDTH), f32), pltpu.VMEM((8, WIDTH), f32),
-            pltpu.VMEM((CHUNK, WIDTH), bf16), pltpu.VMEM((CHUNK, WIDTH), bf16),
-            pltpu.VMEM((CHUNK, WIDTH), bf16),
-        ],
+        [pltpu.VMEM((8, WIDTH), f32), pltpu.VMEM((8, WIDTH), f32)],
     )(
         first, in_hbm(second), y, d_mixed, sm, smt, in_hbm(starts), in_hbm(pre), inbound,
         sums, partner, own_gain, skip_row,
@@ -825,18 +895,16 @@
             dn["message"](rows), dn["message"](PAIRS * rows),
             dn["token"](WIDTH), dn["lane"](HEADS), dn["token"](LANES), dn["lane"](KINDS * HEADS),
             whole(STATE, WIDTH), dn["chunk"](STATE, WIDTH), dn["chunk"](STATE, WIDTH),
-            dn["chunk"](8, WIDTH), whole(STATE, WIDTH), dn["chunk"](8, WIDTH), whole(1, WIDTH), whole(2 * HEADS, LANES), whole(8, LANES),
+            dn["chunk"](8, WIDTH), whole(1, WIDTH), whole(2 * HEADS, LANES), whole(8, LANES),
         ],
         [
             pltpu.VMEM((STATE, WIDTH), f32), pltpu.VMEM((2 * HEADS, LANES), f32),
-            pltpu.VMEM((CHUNK, WIDTH), bf16), pltpu.VMEM((CHUNK, WIDTH), bf16),
-            pltpu.VMEM((CHUNK, WIDTH), bf16), pltpu.VMEM((STATE, WIDTH), bf16),
-            pltpu.VMEM((16, WIDTH), f32), pltpu.VMEM((peers, last_rows, LANES), bf16),
+            pltpu.VMEM((peers, last_rows, LANES), bf16),
             pltpu.SemaphoreType.DMA((grid[0] + 1,)),
         ],
     )(
         first, d_values, d_sources, d_readers, d_gates, d_mixed, e, sm, smt, outer, back,
-        in_hbm(starts), in_hbm(pre), inbound, in_hbm(dec), skip_row, heads, params,
+        starts, in_hbm(dec), skip_row, heads, params,
     )
 
     last_back = exchange(last)

time: 139 us -> 138 us (level)
  Pallas kernels: 42.8 us -> 41.3 us
where the time goes in v9:
time: 138 us; the launch traced here: 137 us
  Pallas kernels  41.3 us (30%)
  blocking collectives  38 us (28%)
  waiting for transfers between devices  37.8 us (27%)
  starting transfers between devices  18.2 us (13%)
    all_to_all x1, blocking collectives, exchange(): lax.all_to_all(array, ('sub', 'tensor'), split_axis=0, concat_axis=0, til...  38 us
    all_to_all x2, waiting for transfers between devices, exchange(): lax.all_to_all(array, ('sub', 'tensor'), split_axis=0, concat_axis=0, til...  17.7 us
    ppermute x2, waiting for transfers between devices, shifted(): return lax.ppermute(array, 'slab', pairs)  17 us
    all_to_all x2, starting transfers between devices, exchange(): lax.all_to_all(array, ('sub', 'tensor'), split_axis=0, concat_axis=0, til...  11 us
    pallas_call x1, Pallas kernels, on_device(): flow(last_kernel, [(hbm((peers, last_rows, LANES), bf16), pl.BlockSpec(me...  6.99 us
    pallas_call x1, Pallas kernels, on_device(): flow(local_kernel, [(struct((tokens, WIDTH)), up['token'](WIDTH)), (struc...  6.92 us
    pallas_call x1, Pallas kernels, on_device(): flow(within_kernel, [(hbm((tokens, WIDTH)), up['token'](WIDTH)), (hbm((ch...  5.89 us
    ppermute x2, starting transfers between devices, shifted(): return lax.ppermute(array, 'slab', pairs)  5.78 us
  transfers between devices with their start and end apart: 6, of which 5 were waited for; matrix products, arithmetic and copies ran while one was open for 1% of the time, Pallas kernels for 16%

profile of v9, /device:TPU:0, one launch (start us, length us, event | category | flops | bytes accessed | tf_op | source)
XLA Modules:
  0.0 137.3 jit_solution(377081066213163224)
XLA Ops:
  0.6 2.5 %shard_map.169 = bf16[8,2,400,128]{3,2,1,0:T(8,128)(2,1)} custom-call(bf16[64,8192]{1,0:T(8,128)(2,1)} %x_ref.1, bf16[64,1024]{1,0:T(8,128)(2,1)} %b_ref.1, bf16[64,1024]{1,0:T(8,128)(2,1)} %c_ref.1, bf16[64,128]{1,0:T(8,128)(2,1)} %steps_ref.1), custom_call_target="tpu_custom_call" | custom-call | bytes 3276800 | tf_op jit(solution)/shard_map/pallas_call | solution.py:739
  3.2 6.4 %all-to-all-start = ((bf16[16,400,128]{2,1,0:T(8,128)(2,1)}), bf16[16,400,128]{2,1,0:T(8,128)(2,1)S(1)}, u32[]{:S(2)}, u32[]{:S(2)}) async-start(bf16[16,400,128]{2,1,0:T(8,128)(2,1)} %bitcast.11), calls=%async_computation | async-start | bytes 3276800 | tf_op jit(solution)/shard_map/all_to_all | solution.py:717
  9.9 0.1 reshape_reshape.3.refs_7_.refs_8_.refs_12_.refs_13_
  10.0 0.8 dynamic_slice.15
  11.0 2.7 %shard_map.170 = bf16[8,2,512,128]{3,2,1,0:T(8,128)(2,1)} custom-call(bf16[64,8192]{1,0:T(8,128)(2,1)} %z_ref, bf16[64,8192]{1,0:T(8,128)(2,1)} %grad_ref.1), custom_call_target="tpu_custom_call" | custom-call | bytes 4194304 | tf_op jit(solution)/shard_map/pallas_call | solution.py:739
  13.7 17.7 %all-to-all-done.refs_0_.refs_1_ = bf16[16,400,128]{2,1,0:T(8,128)(2,1)S(1)} async-done(((bf16[16,400,128]{2,1,0:T(8,128)(2,1)}), bf16[16,400,128]{2,1,0:T(8,128)(2,1)S(1)}, u32[]{:S(2)}, u32[]{:S(2)}) %all-to-all-start) | async-done | bytes 1638432 | tf_op jit(solution)/shard_map/all_to_all | solution.py:717
  31.4 4.6 %all-to-all-start.1 = ((bf16[16,512,128]{2,1,0:T(8,128)(2,1)}), bf16[16,512,128]{2,1,0:T(8,128)(2,1)}, u32[]{:S(2)}, u32[]{:S(2)}) async-start(bf16[16,512,128]{2,1,0:T(8,128)(2,1)} %bitcast.10), calls=%async_computation.1 | async-start | bytes 4194304 | tf_op jit(solution)/shard_map/all_to_all | solution.py:717
  36.0 4.4 %shard_map.171 = (f32[1024,128]{1,0:T(8,128)}, f32[64,1024]{1,0:T(8,128)}, f32[8,128,512]{2,1,0:T(8,128)}, f32[8,8,512]{2,1,0:T(8,128)}, bf16[128,512]{1,0:T(8,128)(2,1)S(1)}, /*index=5*/f32[8,512]{1,0:T(8,128)}) custom-call(bf16[16,400,128]{2,1,0:T(8,128)(2,1)S(1)} %all-to-all-done.refs_0_.refs_1_, bf16[16,400,128]{2,1,0:T(8,128)(2,1)S(1)} %all-to-all-done.refs_0_.refs_1_, ...), custom_call_target="tpu_custom_call" | custom-call | flops 268435456 | bytes 4194304 | tf_op jit(solution)/shard_map/pallas_call | solution.py:790
  40.4 4.5 %collective-permute-start = (bf16[128,512]{1,0:T(8,128)(2,1)S(1)}, bf16[128,512]{1,0:T(8,128)(2,1)S(1)}, u32[]{:S(2)}, u32[]{:S(2)}) collective-permute-start(bf16[128,512]{1,0:T(8,128)(2,1)S(1)} %get-tuple-element.50), channel_id=1, source_target_pairs={{0,16},{1,17},{2,18},{3,19},{4,20},{5,21},{6,22},{7,23},{8,24},{9,... | collective-permute-start | bytes 393224 | tf_op jit(solution)/shard_map/ppermute | solution.py:657
  44.9 5.9 %shard_map.172 = (f32[1024,512]{1,0:T(8,128)}, f32[8,128,512]{2,1,0:T(8,128)}, f32[8,8,512]{2,1,0:T(8,128)}) custom-call(bf16[16,400,128]{2,1,0:T(8,128)(2,1)S(1)} %all-to-all-done.refs_0_.refs_1_, f32[1024,128]{1,0:T(8,128)} %get-tuple-element.45.refs_1_.refs_3_.refs_4_.refs_7_, f32[64,1024]{1,0:T(8,128)} %get-tuple-element.46.refs_2_.refs_5_.refs_8_, ...), custom_call_target="tpu_custom_call" | custom-call | flops 805306368 | bytes 8388608 | tf_op jit(solution)/shard_map/pallas_call | solution.py:814
  50.8 14.0 %collective-permute-done.refs_4_.refs_8_ = bf16[128,512]{1,0:T(8,128)(2,1)S(1)} collective-permute-done((bf16[128,512]{1,0:T(8,128)(2,1)S(1)}, bf16[128,512]{1,0:T(8,128)(2,1)S(1)}, u32[]{:S(2)}, u32[]{:S(2)}) %collective-permute-start) | collective-permute-done | bytes 131104 | tf_op jit(solution)/shard_map/ppermute | solution.py:657
  64.8 4.6 %shard_map.173 = (f32[1024,512]{1,0:T(8,128)S(1)}, f32[8,8,128]{2,1,0:T(8,128)S(1)}) custom-call(bf16[16,400,128]{2,1,0:T(8,128)(2,1)S(1)} %all-to-all-done.refs_0_.refs_1_, bf16[16,512,128]{2,1,0:T(8,128)(2,1)} %all-to-all-done.1.refs_1_, f32[1024,512]{1,0:T(8,128)} %get-tuple-element.49.refs_2_, ...), custom_call_target="tpu_custom_call" | custom-call | flops 134217728 | bytes 8388608 | tf_op jit(solution)/shard_map/pallas_call | solution.py:829
  69.5 1.2 collective-permute-done.1.refs_6_.refs_10_
  70.7 4.6 %shard_map.174 = (bf16[1024,512]{1,0:T(8,128)(2,1)S(1)}, f32[8,128,512]{2,1,0:T(8,128)S(1)}, bf16[128,512]{1,0:T(8,128)(2,1)S(1)}) custom-call(bf16[16,400,128]{2,1,0:T(8,128)(2,1)S(1)} %all-to-all-done.refs_0_.refs_1_, bf16[16,512,128]{2,1,0:T(8,128)(2,1)} %all-to-all-done.1.refs_1_, f32[1024,512]{1,0:T(8,128)S(1)} %get-tuple-element.54.refs_2_, ...), custom_call_target="tpu_custom_call" | custom-call | flops 268435456 | bytes 6291456 | tf_op jit(solution)/shard_map/pallas_call | solution.py:847
  75.3 1.3 collective-permute-start.2
  76.6 6.9 %shard_map.175 = (f32[1024,512]{1,0:T(8,128)S(1)}, f32[1024,128]{1,0:T(8,128)S(1)}, bf16[16,64,128]{2,1,0:T(8,128)(2,1)S(1)}, bf16[16,256,128]{2,1,0:T(8,128)(2,...) custom-call(bf16[16,400,128]{2,1,0:T(8,128)(2,1)S(1)} %all-to-all-done.refs_0_.refs_1_, ...), custom_call_target="tpu_custom_call" | custom-call | flops 1342177280 | bytes 8388608 | tf_op jit(solution)/shard_map/pallas_call | solution.py:865
  83.6 3.0 %collective-permute-done.2.refs_9_ = bf16[128,512]{1,0:T(8,128)(2,1)S(1)} collective-permute-done((bf16[128,512]{1,0:T(8,128)(2,1)S(1)}, bf16[128,512]{1,0:T(8,128)(2,1)S(1)}, u32[]{:S(2)}, u32[]{:S(2)}) %collective-permute-start.2) | collective-permute-done | bytes 131104 | tf_op jit(solution)/shard_map/ppermute | solution.py:657
  86.6 7.0 %shard_map.176 = bf16[16,672,128]{2,1,0:T(8,128)(2,1)} custom-call(bf16[16,400,128]{2,1,0:T(8,128)(2,1)S(1)} %all-to-all-done.refs_0_.refs_1_, f32[1024,512]{1,0:T(8,128)S(1)} %get-tuple-element.58.refs_1_, f32[1024,128]{1,0:T(8,128)S(1)} %get-tuple-element.59.refs_2_, bf16[16,64,128]{2,1,0:T(8,128)(2,1)S(1)} %get-tuple-element.60.refs_3_, ...), custom_call_target="tpu_custom_call" | custom-call | flops 536870912 | bytes 8388608 | tf_op jit(solution)/shard_map/pallas_call | solution.py:889
  93.6 38.0 %all_to_all.15.refs_0_.refs_1_ = bf16[16,672,128]{2,1,0:T(8,128)(2,1)S(1)} all-to-all(bf16[16,672,128]{2,1,0:T(8,128)(2,1)} %shard_map.176), channel_id=1, replica_groups=mesh['slab'=2,'sub'=8,'tensor'=2] {'sub','tensor'}, dimensions={0} | all-to-all | bytes 5505024 | tf_op jit(solution)/shard_map/all_to_all | solution.py:717
  131.7 0.1 shard_map.178.own_ref
  131.8 1.3 collective-permute-start.3
  133.0 1.9 %shard_map.177 = (bf16[64,8192]{1,0:T(8,128)(2,1)}, bf16[64,8192]{1,0:T(8,128)(2,1)}, bf16[64,1024]{1,0:T(8,128)(2,1)}, bf16[64,1024]{1,0:T(8,128)(2,1)}, bf16[64,128]{1,0:T(8,128)(2,1)}) custom-call(bf16[16,672,128]{2,1,0:T(8,128)(2,1)S(1)} %all_to_all.15.refs_0_.refs_1_), custom_call_target="tpu_custom_call" | custom-call | bytes 5242880 | tf_op jit(solution)/shard_map/pallas_call | solution.py:924
  134.9 1.8 %collective-permute-done.3.other_ref = f32[40,128]{1,0:T(8,128)S(1)} collective-permute-done((f32[40,128]{1,0:T(8,128)S(1)}, f32[40,128]{1,0:T(8,128)S(1)}, u32[]{:S(2)}, u32[]{:S(2)}) %collective-permute-start.3) | collective-permute-done | bytes 20512 | tf_op jit(solution)/shard_map/ppermute | solution.py:688
  136.7 0.6 shard_map.179
  (20 shorter events, 0.6 us)
Async XLA Ops:
  3.1 6.5 %copy-start.2 = (f32[64]{0:T(128)S(1)}, f32[64]{0:T(128)}, u32[]{:S(2)}) copy-start(f32[64]{0:T(128)} %param.15) | copy-start | bytes 772
  3.2 6.5 %copy-start.3 = (f32[64]{0:T(128)S(1)}, f32[64]{0:T(128)}, u32[]{:S(2)}) copy-start(f32[64]{0:T(128)} %param.16) | copy-start | bytes 772
  3.2 6.6 %copy-start.4 = (f32[64]{0:T(128)S(1)}, f32[64]{0:T(128)}, u32[]{:S(2)}) copy-start(f32[64]{0:T(128)} %param.17) | copy-start | bytes 772
  3.2 28.3 %all-to-all-start = ((bf16[16,400,128]{2,1,0:T(8,128)(2,1)}), bf16[16,400,128]{2,1,0:T(8,128)(2,1)S(1)}, u32[]{:S(2)}, u32[]{:S(2)}) async-start(bf16[16,400,128]{2,1,0:T(8,128)(2,1)} %bitcast.11), calls=%async_computation | async-start | bytes 3276800 | tf_op jit(solution)/shard_map/all_to_all | solution.py:717
  31.4 33.4 %all-to-all-start.1 = ((bf16[16,512,128]{2,1,0:T(8,128)(2,1)}), bf16[16,512,128]{2,1,0:T(8,128)(2,1)}, u32[]{:S(2)}, u32[]{:S(2)}) async-start(bf16[16,512,128]{2,1,0:T(8,128)(2,1)} %bitcast.10), calls=%async_computation.1 | async-start | bytes 4194304 | tf_op jit(solution)/shard_map/all_to_all | solution.py:717
  40.4 24.4 %collective-permute-start = (bf16[128,512]{1,0:T(8,128)(2,1)S(1)}, bf16[128,512]{1,0:T(8,128)(2,1)S(1)}, u32[]{:S(2)}, u32[]{:S(2)}) collective-permute-start(bf16[128,512]{1,0:T(8,128)(2,1)S(1)} %get-tuple-element.50), channel_id=1, source_target_pairs={{0,16},{1,17},{2,18},{3,19},{4,20},{5,21},{6,22},{7,23},{8,24},{9,... | collective-permute-start | bytes 393224 | tf_op jit(solution)/shard_map/ppermute | solution.py:657
  64.8 5.9 %copy-start = (f32[1024,128]{1,0:T(8,128)S(1)}, f32[1024,128]{1,0:T(8,128)}, u32[]{:S(2)}) copy-start(f32[1024,128]{1,0:T(8,128)} %get-tuple-element.45.refs_1_.refs_3_.refs_4_.refs_7_) | copy-start | bytes 1572868
  69.4 1.3 collective-permute-start.1
  70.7 6.0 %copy-start.1 = (f32[64,1024]{1,0:T(8,128)S(1)}, f32[64,1024]{1,0:T(8,128)}, u32[]{:S(2)}) copy-start(f32[64,1024]{1,0:T(8,128)} %get-tuple-element.46.refs_2_.refs_5_.refs_8_) | copy-start | bytes 786436
  75.3 11.3 %collective-permute-start.2 = (bf16[128,512]{1,0:T(8,128)(2,1)S(1)}, bf16[128,512]{1,0:T(8,128)(2,1)S(1)}, u32[]{:S(2)}, u32[]{:S(2)}) collective-permute-start(bf16[128,512]{1,0:T(8,128)(2,1)S(1)} %get-tuple-element.63), channel_id=1, source_target_pairs={{16,0},{17,1},{18,2},{19,3},{20,4},{21,5},{22,6},{23,7},{24,8},{25... | collective-permute-start | bytes 393224 | tf_op jit(solution)/shard_map/ppermute | solution.py:657
  131.8 5.0 %collective-permute-start.3 = (f32[40,128]{1,0:T(8,128)S(1)}, f32[40,128]{1,0:T(8,128)S(1)}, u32[]{:S(2)}, u32[]{:S(2)}) collective-permute-start(f32[40,128]{1,0:T(8,128)S(1)} %shard_map.178.own_ref), channel_id=1, source_target_pairs={{0,16},{16,0},{1,17},{17,1},{2,18},{18,2},{3,19},{19,3},{4,20},{20... | collective-permute-start | bytes 61448 | tf_op jit(solution)/shard_map/ppermute | solution.py:688

commit v10 on v9

--- a/solution.py
+++ b/solution.py
@@ -49,10 +49,20 @@
     return high, (values - high.astype(f32)).astype(bf16)
 
 
-def mm_two(a, high, low):
-    both = mm(a, jnp.concatenate([high, low], axis=1))
-    width = high.shape[1]
-    return both[:, :width] + both[:, width:]
+def two_terms_each(tiles):
+    return zip(*(two_terms(tile) for tile in tiles))
+
+
+def twice(a):
+    return jnp.concatenate([a, a], axis=1)
+
+
+def mm_two(a_twice, high, low):
+    return mm(a_twice, jnp.concatenate([high, low], axis=0))
+
+
+def sum_heads(ones_twice, highs, lows):
+    return mm_nt(ones_twice, jnp.concatenate([*highs, *lows], axis=1))
 
 
 def sigmoid(values):
@@ -109,9 +119,8 @@
         ref[a, b, :] = value.reshape(self.per_chunk, self.rows, LANES)
 
 
-X, B, C = 0, PAIRS, PAIRS + 1
-SOURCES = PAIRS + 1
-FIRST = PAIRS + 2
+X, HALF = 0, PAIRS
+FIRST = PAIRS + 1
 Z, GRAD = 0, PAIRS
 SECOND = 2 * PAIRS
 LAST_X, LAST_Z, LAST_B, LAST_C = 0, PAIRS, 2 * PAIRS, 2 * PAIRS + 1
@@ -133,8 +142,8 @@
     for s in range(subs):
         for j in range(PAIRS):
             out_ref[s, 0, j * r : (j + 1) * r, :] = x_ref[:, lanes(s * PAIRS + j)]
-        out_ref[s, 0, B * r : (B + 1) * r, :] = b_ref[:, lanes(s // 2)]
-        out_ref[s, 0, C * r : (C + 1) * r, :] = c_ref[:, lanes(s // 2)]
+        half = b_ref if s % 2 == 0 else c_ref
+        out_ref[s, 0, HALF * r : (HALF + 1) * r, :] = half[:, lanes(s // 2)]
         at = pl.multiple_of((step * subs + s) * HEADS, HEADS)
         mine = jnp.concatenate([by_head[pl.ds(at, HEADS), :], zero], axis=0)
         out_ref[s, 0, FIRST * r :, :] = mine.astype(bf16)
@@ -215,7 +224,7 @@
 
 def state_kernel(
     message, per_step,
-    first_ref, steps_ref, heads_ref, sm_ref, smt_ref, own_ref, dec_ref, state_ref, whole_ref,
+    first_ref, sources_ref, steps_ref, heads_ref, sm_ref, smt_ref, own_ref, dec_ref, state_ref, whole_ref,
     carry, rows_s,
 ):
     c = pl.program_id(0)
@@ -260,7 +269,7 @@
         rows = rows_s[c * per_step + i]
         sm = jnp.concatenate([rows, jnp.zeros_like(rows)], axis=0).T
         last = jnp.broadcast_to(sm[CHUNK - 1 : CHUNK, :], (8, LANES))
-        sources_t = message.get(first_ref, i, B).T
+        sources_t = twice(message.get(sources_ref, i, 0).T)
         decs, owns = [], []
         for j in range(PAIRS):
             dec = spread_pair(last, ECUM, j)
@@ -285,7 +294,7 @@
 
 def within_kernel(
     message, per_step,
-    first_ref, sm_ref, smt_ref, own_ref, dec_ref, y_ref, start_ref, pre_ref, carry, pre,
+    first_ref, sources_ref, readers_ref, sm_ref, smt_ref, own_ref, dec_ref, y_ref, start_ref, pre_ref, carry, pre,
 ):
     @pl.when(pl.program_id(0) == 0)
     def _():
@@ -301,8 +310,9 @@
         rows = slice(i * CHUNK, (i + 1) * CHUNK)
         sm = sm_ref[rows, :]
         smt = smt_ref[:, lanes(i)]
-        readers = message.get(first_ref, i, C)
-        scores = jnp.where(t >= s, mm_nt(readers, message.get(first_ref, i, B)), 0.0)
+        readers = message.get(readers_ref, i, 0)
+        readers_twice = twice(readers)
+        scores = jnp.where(t >= s, mm_nt(readers, message.get(sources_ref, i, 0)), 0.0)
         ys = []
         for j in range(PAIRS):
             weights = []
@@ -314,7 +324,7 @@
                 )
             values = split_pair(message.get(first_ref, i, X + j))
             within = mm(jnp.concatenate(weights, axis=1), values)
-            carried = mm_two(readers, *two_terms(states[j]))
+            carried = mm_two(readers_twice, *two_terms(states[j]))
             ys.append(within + spread_pair(sm, ECUM, j) * carried)
         made.append((ys, list(states), before))
         for j in range(PAIRS):
@@ -332,7 +342,7 @@
 
 def mix_kernel(
     message, per_step,
-    first_ref, second_ref, within_ref, sm_ref, inbound_ref, pre_ref, gain_ref, skip_ref,
+    first_ref, readers_ref, second_ref, within_ref, sm_ref, inbound_ref, pre_ref, gain_ref, skip_ref,
     y_ref, sums_ref,
 ):
     made = []
@@ -340,7 +350,7 @@
     for i in range(per_step):
         rows = slice(i * CHUNK, (i + 1) * CHUNK)
         sm = sm_ref[rows, :]
-        carried = mm(message.get(first_ref, i, C), inbound)
+        carried = mm(message.get(readers_ref, i, 0), inbound)
         power = jnp.zeros((CHUNK, LANES), f32)
         cross = jnp.zeros((CHUNK, LANES), f32)
         ys = []
@@ -376,7 +386,7 @@
 
 def norm_kernel(
     message, per_step,
-    first_ref, second_ref, y_ref, sm_ref, pre_ref, sums_ref, other_ref, gain_ref, skip_ref,
+    first_ref, readers_ref, second_ref, y_ref, sm_ref, pre_ref, sums_ref, other_ref, gain_ref, skip_ref,
     mixed_ref, back_ref, slab_ref,
     back_sum,
 ):
@@ -389,7 +399,7 @@
     for i in range(per_step):
         rows = slice(i * CHUNK, (i + 1) * CHUNK)
         sm = sm_ref[rows, :]
-        readers_t = message.get(first_ref, i, C).T
+        readers_t = twice(message.get(readers_ref, i, 0).T)
         inverse, pull = norm_factors(sums_ref[i] + other_ref[i])
         for j in range(PAIRS):
             at = lanes(j)
@@ -412,7 +422,7 @@
 
 def local_kernel(
     message, per_step,
-    first_ref, second_ref, y_ref, grad_ref, sm_ref, smt_ref, start_ref, pre_ref, inbound_ref,
+    first_ref, sources_ref, readers_ref, second_ref, y_ref, grad_ref, sm_ref, smt_ref, start_ref, pre_ref, inbound_ref,
     sums_ref, other_ref, gain_ref, skip_ref,
     values_out, sources_out, readers_out, gate_ref, e_ref, start_out, param_ref,
     gain_sum, skip_sum,
@@ -428,6 +438,7 @@
     t = lax.broadcasted_iota(jnp.int32, (CHUNK, CHUNK), 1)
     causal = t >= s
     ones = head_rows()
+    ones_twice = twice(ones)
     made = []
     gains = [gain_sum[0:1, lanes(j)] for j in range(PAIRS)]
     skips = [skip_sum[0:1, lanes(j)] for j in range(PAIRS)]
@@ -435,8 +446,8 @@
         rows = slice(i * CHUNK, (i + 1) * CHUNK)
         sm = sm_ref[rows, :]
         smt = smt_ref[:, lanes(i)]
-        sources = message.get(first_ref, i, B)
-        readers = message.get(first_ref, i, C)
+        sources = message.get(sources_ref, i, 0)
+        readers = message.get(readers_ref, i, 0)
         inverse, pull = norm_factors(sums_ref[i] + other_ref[i])
         scores = jnp.where(causal, mm_nt(sources, readers), 0.0)
         total = jnp.zeros((CHUNK, CHUNK), f32)
@@ -478,7 +489,7 @@
             starts.append(
                 start_ref[i, :, at] + pre_ref[i, 0:1, at] * inbound_ref[:, at].astype(f32)
             )
-        e = mm_nt(ones, jnp.concatenate(highs, axis=1)) + mm_nt(ones, jnp.concatenate(lows, axis=1))
+        e = sum_heads(ones_twice, highs, lows)
         total = jnp.where(causal, total, 0.0).astype(bf16)
         start = jnp.concatenate([part.astype(bf16) for part in starts], axis=1)
         d_readers = mm_tn(total, sources) + mm_nt(jnp.concatenate(scaleds, axis=1), start)
@@ -512,7 +523,7 @@
 
 def last_kernel(
     message, per_step,
-    first_ref, within_ref, sources_ref, readers_ref, gate_ref, grad_ref, e_ref, sm_ref, smt_ref, outer_ref,
+    first_ref, sources_ref, within_ref, d_sources_ref, d_readers_ref, gate_ref, grad_ref, e_ref, sm_ref, smt_ref, outer_ref,
     back_ref, start_ref, dec_ref, skip_ref, heads_ref, early_ref,
     out_ref,
     carry, sums, message_s, sent,
@@ -526,6 +537,7 @@
 
     r = message.rows
     ones = head_rows()
+    ones_twice = twice(ones)
     before = lax.broadcasted_iota(jnp.int32, (CHUNK, CHUNK), 0)
     after = lax.broadcasted_iota(jnp.int32, (CHUNK, CHUNK), 1)
     earlier = jnp.where(before < after, 1.0, 0.0)
@@ -545,7 +557,7 @@
     for i in reversed(range(per_step)):
         rows = slice(i * CHUNK, (i + 1) * CHUNK)
         sm = sm_ref[rows, :]
-        sources = message.get(first_ref, i, B)
+        sources_twice = twice(message.get(sources_ref, i, 0))
         d_values, highs, lows, scaleds, rounded, fluxes = [], [], [], [], [], []
         for j in range(PAIRS):
             at = lanes(j)
@@ -553,7 +565,7 @@
             rounded.append(high)
             values = message.get(first_ref, i, X + j).astype(f32)
             weight = spread_pair(sm, WEIGHT, j)
-            grad = within_ref[rows, at] + weight * mm_two(sources, high, low)
+            grad = within_ref[rows, at] + weight * mm_two(sources_twice, high, low)
             skipped = skip_ref[0:1, at] * grad_ref[rows, at].astype(f32)
             d_values.append((grad + skipped).astype(bf16))
             high, low = two_terms(values * grad)
@@ -566,13 +578,11 @@
                     jnp.sum(start_ref[i, :, at] * states[j], axis=0, keepdims=True), (16, LANES)
                 )
             )
-        d_sources = sources_ref[rows, :] + mm_nt(
+        d_sources = d_sources_ref[rows, :] + mm_nt(
             jnp.concatenate(scaleds, axis=1), jnp.concatenate(rounded, axis=1)
         )
-        g = mm_nt(ones, jnp.concatenate(highs, axis=1)) + mm_nt(ones, jnp.concatenate(lows, axis=1))
-        g = g[:HEADS]
-        high, low = two_terms(jnp.concatenate(fluxes, axis=1))
-        constant = (mm_nt(ones, high) + mm_nt(ones, low))[:HEADS, 0:1]
+        g = sum_heads(ones_twice, highs, lows)[:HEADS]
+        constant = sum_heads(ones_twice, *two_terms_each(fluxes))[:HEADS, 0:1]
         flux = constant + mm_exact(g - e_ref[:, lanes(i)], earlier)
         soft = smt_ref[DT * HEADS : (DT + 1) * HEADS, lanes(i)]
         rate = smt_ref[RATE * HEADS : (RATE + 1) * HEADS, lanes(i)]
@@ -587,7 +597,7 @@
             message.put(mine, i, LAST_X + j, d_values[j])
             message.put(mine, i, LAST_Z + j, message.get(gate_ref, i, j))
         message.put(mine, i, LAST_B, d_sources)
-        message.put(mine, i, LAST_C, message.get(readers_ref, i, 0))
+        message.put(mine, i, LAST_C, message.get(d_readers_ref, i, 0))
         for p in range(message.per_chunk):
             part = steps if p == 0 else pltpu.roll(steps, LANES - p * r, 1)
             mine[i * message.per_chunk + p, LAST * r : LAST * r + STEP_ROWS, :] = part.astype(bf16)
@@ -749,6 +759,10 @@
     )
     tensor_rows = lax.broadcasted_iota(jnp.int32, (tensor_count, LANES), 0)
     mine = (tensor_rows == lax.axis_index("tensor")).astype(f32)
+    half = first[:, HALF * rows : (HALF + 1) * rows, :]
+    other_half = lax.ppermute(half, "sub", [(i, i ^ 1) for i in range(sub_count)])
+    even = sub % 2 == 0
+    sources, readers = jnp.where(even, half, other_half), jnp.where(even, other_half, half)
     gate_z, heads, skip_row, own_gain, mine = lax.optimization_barrier(
         (gate_z, heads, skip_row, own_gain, mine)
     )
@@ -799,12 +813,12 @@
         ],
         2 * unit, size * 8,
         [
-            up["message"](SOURCES * rows),
+            up["message"](PAIRS * rows), up["message"](rows),
             pl.BlockSpec((peers, STEP_ROWS, LANES), lambda c: (0, FIRST * rows // STEP_ROWS, 0)),
             whole(2 * HEADS, LANES),
         ],
         [pltpu.VMEM((STATE, WIDTH), f32), pltpu.VMEM((chunks, KINDS * HEADS, LANES), f32)],
-    )(first, first, heads)
+    )(first, sources, first, heads)
 
     before = after = None
     if slab_count > 2:
@@ -820,11 +834,12 @@
         ],
         6 * unit, size * 16,
         [
-            up["message"](FIRST * rows), up["token"](LANES), up["lane"](KINDS * HEADS),
+            up["message"](PAIRS * rows), up["message"](rows), up["message"](rows),
+            up["token"](LANES), up["lane"](KINDS * HEADS),
             up["chunk"](STATE, WIDTH), up["chunk"](8, WIDTH),
         ],
         [pltpu.VMEM((STATE, WIDTH), f32), pltpu.VMEM((8, WIDTH), f32)],
-    )(first, in_hbm(sm), in_hbm(smt), in_hbm(own), in_hbm(dec))
+    )(first, sources, readers, in_hbm(sm), in_hbm(smt), in_hbm(own), in_hbm(dec))
 
     y, sums = flow(
         mix_kernel,
@@ -834,12 +849,13 @@
         ],
         unit, size * 16,
         [
-            up["message"](FIRST * rows), up["message"](second_rows), up["token"](WIDTH),
-            up["token"](LANES), whole(STATE, WIDTH), up["chunk"](8, WIDTH),
+            up["message"](PAIRS * rows), up["message"](rows), up["message"](second_rows),
+            up["token"](WIDTH), up["token"](LANES), whole(STATE, WIDTH), up["chunk"](8, WIDTH),
             whole(1, WIDTH), whole(1, WIDTH),
         ],
     )(
-        first, in_hbm(second), in_hbm(within), in_hbm(sm), inbound, in_hbm(pre), own_gain, skip_row,
+        first, readers, in_hbm(second), in_hbm(within), in_hbm(sm), inbound, in_hbm(pre),
+        own_gain, skip_row,
     )
 
     partner = lax.ppermute(sums, "sub", [(i, i ^ 1) for i in range(sub_count)])
@@ -853,12 +869,12 @@
         ],
         2 * unit, size * 12,
         [
-            up["message"](FIRST * rows), up["message"](second_rows), up["token"](WIDTH),
-            up["token"](LANES), up["chunk"](8, WIDTH), up["chunk"](8, LANES),
+            up["message"](PAIRS * rows), up["message"](rows), up["message"](second_rows),
+            up["token"](WIDTH), up["token"](LANES), up["chunk"](8, WIDTH), up["chunk"](8, LANES),
             up["chunk"](8, LANES), whole(1, WIDTH), whole(1, WIDTH),
         ],
         [pltpu.VMEM((STATE, WIDTH), f32)],
-    )(first, in_hbm(second), y, sm, in_hbm(pre), sums, partner, own_gain, skip_row)
+    )(first, readers, in_hbm(second), y, sm, in_hbm(pre), sums, partner, own_gain, skip_row)
 
     outer = carry_over(slab_back, decay, after, slab_count, -1)
 
@@ -875,14 +891,15 @@
         ],
         10 * unit, size * 16,
         [
-            up["message"](FIRST * rows), up["message"](second_rows), up["token"](WIDTH),
-            up["token"](WIDTH), up["token"](LANES), up["lane"](KINDS * HEADS),
+            up["message"](PAIRS * rows), up["message"](rows), up["message"](rows),
+            up["message"](second_rows), up["token"](WIDTH), up["token"](WIDTH), up["token"](LANES),
+            up["lane"](KINDS * HEADS),
             up["chunk"](STATE, WIDTH), up["chunk"](8, WIDTH), whole(STATE, WIDTH),
             up["chunk"](8, LANES), up["chunk"](8, LANES), whole(1, WIDTH), whole(1, WIDTH),
         ],
         [pltpu.VMEM((8, WIDTH), f32), pltpu.VMEM((8, WIDTH), f32)],
     )(
-        first, in_hbm(second), y, d_mixed, sm, smt, in_hbm(starts), in_hbm(pre), inbound,
+        first, sources, readers, in_hbm(second), y, d_mixed, sm, smt, in_hbm(starts), in_hbm(pre), inbound,
         sums, partner, own_gain, skip_row,
     )
 
@@ -891,7 +908,7 @@
         [(hbm((peers, last_rows, LANES), bf16), pl.BlockSpec(memory_space=pl.ANY))],
         4 * unit, size * 16,
         [
-            dn["message"](SOURCES * rows), dn["token"](WIDTH), dn["token"](STATE),
+            dn["message"](PAIRS * rows), dn["message"](rows), dn["token"](WIDTH), dn["token"](STATE),
             dn["message"](rows), dn["message"](PAIRS * rows),
             dn["token"](WIDTH), dn["lane"](HEADS), dn["token"](LANES), dn["lane"](KINDS * HEADS),
             whole(STATE, WIDTH), dn["chunk"](STATE, WIDTH), dn["chunk"](STATE, WIDTH),
@@ -903,7 +920,7 @@
             pltpu.SemaphoreType.DMA((grid[0] + 1,)),
         ],
     )(
-        first, d_values, d_sources, d_readers, d_gates, d_mixed, e, sm, smt, outer, back,
+        first, sources, d_values, d_sources, d_readers, d_gates, d_mixed, e, sm, smt, outer, back,
         starts, in_hbm(dec), skip_row, heads, params,
     )
 

time: 138 us -> 135 us (0.978)
  waiting for transfers between devices: 37.8 us -> 33.2 us
    all_to_all x2, waiting for transfers between devices: 17.7 us -> 14.7 us  [exchange(): lax.all_to_all(array, ('sub', 'tensor'), split_axis=0, concat_axis=0, til...]
    ppermute x2, waiting for transfers between devices: 17 us -> 14.7 us  [shifted(): return lax.ppermute(array, 'slab', pairs)]
  transfers between devices with their start and end apart: 6 -> 7, of which waited for: 5 -> 6; matrix products, arithmetic and copies ran while one was open for 1% -> 1% of each run, Pallas kernels for 16% -> 17%
where the time goes in v10:
time: 135 us; the launch traced here: 134 us
  Pallas kernels  41.9 us (31%)
  blocking collectives  38 us (28%)
  waiting for transfers between devices  33.2 us (25%)
  starting transfers between devices  18.6 us (14%)
    all_to_all x1, blocking collectives, exchange(): lax.all_to_all(array, ('sub', 'tensor'), split_axis=0, concat_axis=0, til...  38 us
    ppermute x2, waiting for transfers between devices, shifted(): return lax.ppermute(array, 'slab', pairs)  14.7 us
    all_to_all x2, waiting for transfers between devices, exchange(): lax.all_to_all(array, ('sub', 'tensor'), split_axis=0, concat_axis=0, til...  14.7 us
    all_to_all x2, starting transfers between devices, exchange(): lax.all_to_all(array, ('sub', 'tensor'), split_axis=0, concat_axis=0, til...  10.7 us
    pallas_call x1, Pallas kernels, on_device(): flow(local_kernel, [(struct((tokens, WIDTH)), up['token'](WIDTH)), (struc...  7.46 us
    pallas_call x1, Pallas kernels, on_device(): flow(last_kernel, [(hbm((peers, last_rows, LANES), bf16), pl.BlockSpec(me...  7.07 us
    pallas_call x1, Pallas kernels, on_device(): flow(within_kernel, [(hbm((tokens, WIDTH)), up['token'](WIDTH)), (hbm((ch...  5.91 us
    ppermute x2, starting transfers between devices, shifted(): return lax.ppermute(array, 'slab', pairs)  5.78 us
  transfers between devices with their start and end apart: 7, of which 6 were waited for; matrix products, arithmetic and copies ran while one was open for 1% of the time, Pallas kernels for 17%

profile of v10, /device:TPU:0, one launch (start us, length us, event | category | flops | bytes accessed | tf_op | source)
XLA Modules:
  0.0 134.0 jit_solution(1782067589962003586)
XLA Ops:
  0.7 2.4 %shard_map.169 = bf16[8,2,336,128]{3,2,1,0:T(8,128)(2,1)} custom-call(bf16[64,8192]{1,0:T(8,128)(2,1)} %x_ref.1, bf16[64,1024]{1,0:T(8,128)(2,1)} %b_ref.1, bf16[64,1024]{1,0:T(8,128)(2,1)} %c_ref.1, bf16[64,128]{1,0:T(8,128)(2,1)} %steps_ref.1), custom_call_target="tpu_custom_call" | custom-call | bytes 2752512 | tf_op jit(solution)/shard_map/pallas_call | solution.py:749
  3.1 6.3 %all-to-all-start = ((bf16[16,336,128]{2,1,0:T(8,128)(2,1)}), bf16[16,336,128]{2,1,0:T(8,128)(2,1)S(1)}, u32[]{:S(2)}, u32[]{:S(2)}) async-start(bf16[16,336,128]{2,1,0:T(8,128)(2,1)} %bitcast.11), calls=%async_computation | async-start | bytes 2752512 | tf_op jit(solution)/shard_map/all_to_all | solution.py:727
  9.8 0.8 dynamic_slice.15
  10.8 2.7 %shard_map.170 = bf16[8,2,512,128]{3,2,1,0:T(8,128)(2,1)} custom-call(bf16[64,8192]{1,0:T(8,128)(2,1)} %z_ref, bf16[64,8192]{1,0:T(8,128)(2,1)} %grad_ref.1), custom_call_target="tpu_custom_call" | custom-call | bytes 4194304 | tf_op jit(solution)/shard_map/pallas_call | solution.py:749
  13.5 14.7 %all-to-all-done.refs_0_.refs_2_ = bf16[16,336,128]{2,1,0:T(8,128)(2,1)S(1)} async-done(((bf16[16,336,128]{2,1,0:T(8,128)(2,1)}), bf16[16,336,128]{2,1,0:T(8,128)(2,1)S(1)}, u32[]{:S(2)}, u32[]{:S(2)}) %all-to-all-start) | async-done | bytes 1376288 | tf_op jit(solution)/shard_map/all_to_all | solution.py:727
  28.1 4.4 %all-to-all-start.1 = ((bf16[16,512,128]{2,1,0:T(8,128)(2,1)}), bf16[16,512,128]{2,1,0:T(8,128)(2,1)}, u32[]{:S(2)}, u32[]{:S(2)}) async-start(bf16[16,512,128]{2,1,0:T(8,128)(2,1)} %bitcast.10), calls=%async_computation.1 | async-start | bytes 4194304 | tf_op jit(solution)/shard_map/all_to_all | solution.py:727
  32.6 0.3 collective-permute-start
  32.9 1.3 collective-permute-done
  34.2 4.4 %shard_map.171 = (f32[1024,128]{1,0:T(8,128)}, f32[64,1024]{1,0:T(8,128)}, f32[8,128,512]{2,1,0:T(8,128)}, f32[8,8,512]{2,1,0:T(8,128)}, bf16[128,512]{1,0:T(8,128)(2,1)S(1)}, /*index=5*/f32[8,512]{1,0:T(8,128)}) custom-call(bf16[16,336,128]{2,1,0:T(8,128)(2,1)S(1)} %all-to-all-done.refs_0_.refs_2_, bf16[16,64,128]{2,1,0:T(8,128)(2,1)S(1)} %get-tuple-element.78.refs_1_, ...), custom_call_target="tpu_custom_call" | custom-call | flops 268435456 | bytes 4194304 | tf_op jit(solution)/shard_map/pallas_call | solution.py:804
  38.6 4.5 %collective-permute-start.1 = (bf16[128,512]{1,0:T(8,128)(2,1)S(1)}, bf16[128,512]{1,0:T(8,128)(2,1)S(1)}, u32[]{:S(2)}, u32[]{:S(2)}) collective-permute-start(bf16[128,512]{1,0:T(8,128)(2,1)S(1)} %get-tuple-element.50), channel_id=1, source_target_pairs={{0,16},{1,17},{2,18},{3,19},{4,20},{5,21},{6,22},{7,23},{8,24},{9,... | collective-permute-start | bytes 393224 | tf_op jit(solution)/shard_map/ppermute | solution.py:667
  43.1 5.9 %shard_map.172 = (f32[1024,512]{1,0:T(8,128)}, f32[8,128,512]{2,1,0:T(8,128)}, f32[8,8,512]{2,1,0:T(8,128)}) custom-call(bf16[16,336,128]{2,1,0:T(8,128)(2,1)S(1)} %all-to-all-done.refs_0_.refs_2_, bf16[16,64,128]{2,1,0:T(8,128)(2,1)S(1)} %get-tuple-element.78.refs_1_, bf16[16,64,128]{2,1,0:T(8,128)(2,1)S(1)} %get-tuple-element.77.refs_2_.refs_1_, ...), custom_call_target="tpu_custom_call" | custom-call | flops 805306368 | bytes 8388608 | tf_op jit(solution)/shard_map/pallas_call | solution.py:828
  49.0 12.2 %collective-permute-done.1.refs_5_.refs_10_ = bf16[128,512]{1,0:T(8,128)(2,1)S(1)} collective-permute-done((bf16[128,512]{1,0:T(8,128)(2,1)S(1)}, bf16[128,512]{1,0:T(8,128)(2,1)S(1)}, u32[]{:S(2)}, u32[]{:S(2)}) %collective-permute-start.1) | collective-permute-done | bytes 131104 | tf_op jit(solution)/shard_map/ppermute | solution.py:667
  61.2 4.6 %shard_map.173 = (f32[1024,512]{1,0:T(8,128)S(1)}, f32[8,8,128]{2,1,0:T(8,128)S(1)}) custom-call(bf16[16,336,128]{2,1,0:T(8,128)(2,1)S(1)} %all-to-all-done.refs_0_.refs_2_, bf16[16,64,128]{2,1,0:T(8,128)(2,1)S(1)} %get-tuple-element.77.refs_2_.refs_1_, bf16[16,512,128]{2,1,0:T(8,128)(2,1)} %all-to-all-done.1.refs_2_.refs_3_, ...), custom_call_target="tpu_custom_call" | custom-call | flops 134217728 | bytes 8388608 | tf_op jit(solution)/shard_map/pallas_call | solution.py:844
  66.0 1.2 collective-permute-done.2.refs_7_.refs_12_
  67.2 4.7 %shard_map.174 = (bf16[1024,512]{1,0:T(8,128)(2,1)S(1)}, f32[8,128,512]{2,1,0:T(8,128)S(1)}, bf16[128,512]{1,0:T(8,128)(2,1)S(1)}) custom-call(bf16[16,336,128]{2,1,0:T(8,128)(2,1)S(1)} %all-to-all-done.refs_0_.refs_2_, bf16[16,64,128]{2,1,0:T(8,128)(2,1)S(1)} %get-tuple-element.77.refs_2_.refs_1_, bf16[16,512,128]{2,1,0:T(8,128)(2,1)} %all-to-all-done.1.refs_2_.refs_3_, ...), custom_call_target="tpu_custom_call" | custom-call | flops 268435456 | bytes 6291456 | tf_op jit(solution)/shard_map/pallas_call | solution.py:863
  71.9 1.3 collective-permute-start.3
  73.2 7.5 %shard_map.175 = (f32[1024,512]{1,0:T(8,128)S(1)}, f32[1024,128]{1,0:T(8,128)S(1)}, bf16[16,64,128]{2,1,0:T(8,128)(2,1)S(1)}, bf16[16,256,128]{2,1,0:T(8,128)(2,...) custom-call(bf16[16,336,128]{2,1,0:T(8,128)(2,1)S(1)} %all-to-all-done.refs_0_.refs_2_, ...), custom_call_target="tpu_custom_call" | custom-call | flops 1342177280 | bytes 8388608 | tf_op jit(solution)/shard_map/pallas_call | solution.py:881
  80.7 2.5 %collective-permute-done.3.refs_10_ = bf16[128,512]{1,0:T(8,128)(2,1)S(1)} collective-permute-done((bf16[128,512]{1,0:T(8,128)(2,1)S(1)}, bf16[128,512]{1,0:T(8,128)(2,1)S(1)}, u32[]{:S(2)}, u32[]{:S(2)}) %collective-permute-start.3) | collective-permute-done | bytes 131104 | tf_op jit(solution)/shard_map/ppermute | solution.py:667
  83.2 7.1 %shard_map.176 = bf16[16,672,128]{2,1,0:T(8,128)(2,1)} custom-call(bf16[16,336,128]{2,1,0:T(8,128)(2,1)S(1)} %all-to-all-done.refs_0_.refs_2_, bf16[16,64,128]{2,1,0:T(8,128)(2,1)S(1)} %get-tuple-element.78.refs_1_, f32[1024,512]{1,0:T(8,128)S(1)} %get-tuple-element.58.refs_2_, f32[1024,128]{1,0:T(8,128)S(1)} %get-tuple-element.59.refs_3_, ...), custom_call_target="tpu_custom_call" | custom-call | flops 536870912 | bytes 8388608 | tf_op jit(solution)/shard_map/pallas_call | solution.py:906
  90.2 38.0 %all_to_all.15.refs_0_.refs_1_ = bf16[16,672,128]{2,1,0:T(8,128)(2,1)S(1)} all-to-all(bf16[16,672,128]{2,1,0:T(8,128)(2,1)} %shard_map.176), channel_id=1, replica_groups=mesh['slab'=2,'sub'=8,'tensor'=2] {'sub','tensor'}, dimensions={0} | all-to-all | bytes 5505024 | tf_op jit(solution)/shard_map/all_to_all | solution.py:727
  128.4 1.7 %collective-permute-start.4 = (f32[40,128]{1,0:T(8,128)S(1)}, f32[40,128]{1,0:T(8,128)S(1)}, u32[]{:S(2)}, u32[]{:S(2)}) collective-permute-start(f32[40,128]{1,0:T(8,128)S(1)} %shard_map.178.own_ref), channel_id=1, source_target_pairs={{0,16},{16,0},{1,17},{17,1},{2,18},{18,2},{3,19},{19,3},{4,20},{20... | collective-permute-start | bytes 61448 | tf_op jit(solution)/shard_map/ppermute | solution.py:698
  130.1 1.9 %shard_map.177 = (bf16[64,8192]{1,0:T(8,128)(2,1)}, bf16[64,8192]{1,0:T(8,128)(2,1)}, bf16[64,1024]{1,0:T(8,128)(2,1)}, bf16[64,1024]{1,0:T(8,128)(2,1)}, bf16[64,128]{1,0:T(8,128)(2,1)}) custom-call(bf16[16,672,128]{2,1,0:T(8,128)(2,1)S(1)} %all_to_all.15.refs_0_.refs_1_), custom_call_target="tpu_custom_call" | custom-call | bytes 5242880 | tf_op jit(solution)/shard_map/pallas_call | solution.py:941
  132.0 1.3 collective-permute-done.4.other_ref
  133.3 0.6 shard_map.179
  (24 shorter events, 0.9 us)
Async XLA Ops:
  0.6 8.7 %copy-start.2 = (f32[64]{0:T(128)S(1)}, f32[64]{0:T(128)}, u32[]{:S(2)}) copy-start(f32[64]{0:T(128)} %param.15) | copy-start | bytes 772
  0.7 8.8 %copy-start.3 = (f32[64]{0:T(128)S(1)}, f32[64]{0:T(128)}, u32[]{:S(2)}) copy-start(f32[64]{0:T(128)} %param.16) | copy-start | bytes 772
  0.7 8.9 %copy-start.4 = (f32[64]{0:T(128)S(1)}, f32[64]{0:T(128)}, u32[]{:S(2)}) copy-start(f32[64]{0:T(128)} %param.17) | copy-start | bytes 772
  3.1 25.1 %all-to-all-start = ((bf16[16,336,128]{2,1,0:T(8,128)(2,1)}), bf16[16,336,128]{2,1,0:T(8,128)(2,1)S(1)}, u32[]{:S(2)}, u32[]{:S(2)}) async-start(bf16[16,336,128]{2,1,0:T(8,128)(2,1)} %bitcast.11), calls=%async_computation | async-start | bytes 2752512 | tf_op jit(solution)/shard_map/all_to_all | solution.py:727
  28.1 33.1 %all-to-all-start.1 = ((bf16[16,512,128]{2,1,0:T(8,128)(2,1)}), bf16[16,512,128]{2,1,0:T(8,128)(2,1)}, u32[]{:S(2)}, u32[]{:S(2)}) async-start(bf16[16,512,128]{2,1,0:T(8,128)(2,1)} %bitcast.10), calls=%async_computation.1 | async-start | bytes 4194304 | tf_op jit(solution)/shard_map/all_to_all | solution.py:727
  32.6 1.6 %collective-permute-start = (bf16[16,64,128]{2,1,0:T(8,128)(2,1)S(1)}, bf16[16,64,128]{2,1,0:T(8,128)(2,1)S(1)}, u32[]{:S(2)}, u32[]{:S(2)}) collective-permute-start(bf16[16,64,128]{2,1,0:T(8,128)(2,1)S(1)} %slice.4), channel_id=1, source_target_pairs={{0,2},{2,0},{4,6},{6,4},{8,10},{10,8},{12,14},{14,12},{1,3},{3,1},... | collective-permute-start | bytes 786440 | tf_op jit(solution)/shard_map/ppermute | solution.py:763
  38.6 22.6 %collective-permute-start.1 = (bf16[128,512]{1,0:T(8,128)(2,1)S(1)}, bf16[128,512]{1,0:T(8,128)(2,1)S(1)}, u32[]{:S(2)}, u32[]{:S(2)}) collective-permute-start(bf16[128,512]{1,0:T(8,128)(2,1)S(1)} %get-tuple-element.50), channel_id=1, source_target_pairs={{0,16},{1,17},{2,18},{3,19},{4,20},{5,21},{6,22},{7,23},{8,24},{9,... | collective-permute-start | bytes 393224 | tf_op jit(solution)/shard_map/ppermute | solution.py:667
  61.2 5.9 %copy-start = (f32[1024,128]{1,0:T(8,128)S(1)}, f32[1024,128]{1,0:T(8,128)}, u32[]{:S(2)}) copy-start(f32[1024,128]{1,0:T(8,128)} %get-tuple-element.45.refs_3_.refs_4_.refs_6_.refs_8_) | copy-start | bytes 1572868
  65.9 1.3 collective-permute-start.2
  67.2 6.0 %copy-start.1 = (f32[64,1024]{1,0:T(8,128)S(1)}, f32[64,1024]{1,0:T(8,128)}, u32[]{:S(2)}) copy-start(f32[64,1024]{1,0:T(8,128)} %get-tuple-element.46.refs_4_.refs_7_.refs_9_) | copy-start | bytes 786436
  71.9 11.3 %collective-permute-start.3 = (bf16[128,512]{1,0:T(8,128)(2,1)S(1)}, bf16[128,512]{1,0:T(8,128)(2,1)S(1)}, u32[]{:S(2)}, u32[]{:S(2)}) collective-permute-start(bf16[128,512]{1,0:T(8,128)(2,1)S(1)} %get-tuple-element.63), channel_id=1, source_target_pairs={{16,0},{17,1},{18,2},{19,3},{20,4},{21,5},{22,6},{23,7},{24,8},{25... | collective-permute-start | bytes 393224 | tf_op jit(solution)/shard_map/ppermute | solution.py:667
  128.4 5.0 %collective-permute-start.4 = (f32[40,128]{1,0:T(8,128)S(1)}, f32[40,128]{1,0:T(8,128)S(1)}, u32[]{:S(2)}, u32[]{:S(2)}) collective-permute-start(f32[40,128]{1,0:T(8,128)S(1)} %shard_map.178.own_ref), channel_id=1, source_target_pairs={{0,16},{16,0},{1,17},{17,1},{2,18},{18,2},{3,19},{19,3},{4,20},{20... | collective-permute-start | bytes 61448 | tf_op jit(solution)/shard_map/ppermute | solution.py:698

commit v11 on v10

--- a/solution.py
+++ b/solution.py
@@ -125,7 +125,6 @@
 SECOND = 2 * PAIRS
 LAST_X, LAST_Z, LAST_B, LAST_C = 0, PAIRS, 2 * PAIRS, 2 * PAIRS + 1
 LAST = 2 * PAIRS + 2
-TERMS = 3
 
 
 def pack_first(x_ref, b_ref, c_ref, steps_ref, out_ref, by_head):
@@ -188,38 +187,22 @@
     steps_ref[...] = by_head.T[:r, :].astype(bf16)
 
 
-def three_terms(values):
-    high = values.astype(bf16).astype(f32)
-    rest = values - high
-    middle = rest.astype(bf16).astype(f32)
-    return [high, middle, rest - middle]
-
-
-def unpack_params(sub_count, tensor_count, late_ref, early_ref, mine_ref, out_ref):
+GAIN_ROW, SKIP_ROW, LOGS_ROW, BIAS_ROW = HEADS, HEADS + PAIRS, HEADS + PAIRS + 1, HEADS + PAIRS + 2
+
+
+def unpack_params(sub_count, tensor_count, tile_ref, mine_ref, out_ref):
     lane = lax.broadcasted_iota(jnp.int32, (1, LANES), 1)
-    late = [jnp.zeros((1, LANES), f32) for _ in range(2)]
-    skip = jnp.zeros((1, LANES), f32)
-
-    def placed(rows, at):
-        total = rows[at : at + 1] + rows[at + 1 : at + 2] + rows[at + 2 : at + 3]
-        return jnp.where(lane < HEADS, total, 0.0)
-
+    totals = [jnp.zeros((1, LANES), f32) for _ in range(3)]
     for s in range(sub_count):
-        late_rows = jnp.zeros((STEP_ROWS, LANES), f32)
-        early_rows = jnp.zeros((STEP_ROWS, LANES), f32)
+        rows = jnp.zeros((STEP_ROWS, LANES), f32)
         for t in range(tensor_count):
             mine = mine_ref[t : t + 1, :] > 0.0
-            peer = s * tensor_count + t
-            late_rows = jnp.where(mine, late_ref[peer].astype(f32), late_rows)
-            early_rows = jnp.where(mine, early_ref[peer].astype(f32), early_rows)
-        for k in range(2):
-            part = placed(late_rows, HEADS + k * TERMS)
-            late[k] = late[k] + (part if s == 0 else pltpu.roll(part, s * HEADS, 1))
-        part = placed(early_rows, TERMS * PAIRS)
-        skip = skip + (part if s == 0 else pltpu.roll(part, s * HEADS, 1))
-        gain = early_rows[:PAIRS] + early_rows[PAIRS : 2 * PAIRS] + early_rows[2 * PAIRS : 3 * PAIRS]
-        out_ref[8 + s * PAIRS : 8 + (s + 1) * PAIRS, :] = gain
-    out_ref[:8, :] = jnp.concatenate(late + [skip, jnp.zeros((5, LANES), f32)], axis=0)
+            rows = jnp.where(mine, tile_ref[s * tensor_count + t].astype(f32), rows)
+        for k, at in enumerate((LOGS_ROW, BIAS_ROW, SKIP_ROW)):
+            part = jnp.where(lane < HEADS, rows[at : at + 1], 0.0)
+            totals[k] = totals[k] + (part if s == 0 else pltpu.roll(part, s * HEADS, 1))
+        out_ref[8 + s * PAIRS : 8 + (s + 1) * PAIRS, :] = rows[GAIN_ROW : GAIN_ROW + PAIRS]
+    out_ref[:8, :] = jnp.concatenate(totals + [jnp.zeros((5, LANES), f32)], axis=0)
 
 
 def state_kernel(
@@ -343,8 +326,9 @@
 def mix_kernel(
     message, per_step,
     first_ref, readers_ref, second_ref, within_ref, sm_ref, inbound_ref, pre_ref, gain_ref, skip_ref,
-    y_ref, sums_ref,
+    y_ref, sums_ref, second_out,
 ):
+    second_out[...] = second_ref[...]
     made = []
     inbound = inbound_ref[...].astype(bf16)
     for i in range(per_step):
@@ -614,23 +598,21 @@
             column = jnp.sum(sums[k * HEADS : (k + 1) * HEADS, :], axis=1, keepdims=True)
             block = jnp.broadcast_to(column, (HEADS, LANES))
             block = jnp.concatenate([block, jnp.zeros((LANES - HEADS, LANES), f32)], axis=0)
-            late += three_terms(block.T[0:1, :])
-        late += [jnp.zeros((HEADS - 2 * TERMS, LANES), f32)]
-        late = jnp.concatenate([jnp.zeros((HEADS, LANES), f32)] + late, axis=0)
-        late = late.astype(bf16)
-        early = three_terms(early_ref[:PAIRS, :]) + three_terms(early_ref[PAIRS : PAIRS + 1, :])
-        early += [jnp.zeros((STEP_ROWS - TERMS * (PAIRS + 1), LANES), f32)]
-        early = jnp.concatenate(early, axis=0).astype(bf16)
+            late.append(block.T[0:1, :])
+        small = [
+            jnp.zeros((HEADS, LANES), f32), early_ref[: PAIRS + 1, :], *late,
+            jnp.zeros((STEP_ROWS - BIAS_ROW - 1, LANES), f32),
+        ]
+        small = jnp.concatenate(small, axis=0).astype(bf16)
         own_rows = lax.broadcasted_iota(jnp.int32, (STEP_ROWS, LANES), 0) < HEADS
 
         def fill(peer, unused):
             steps_at = slice(LAST * r, LAST * r + STEP_ROWS)
-            message_s[peer, steps_at, :] = jnp.where(own_rows, message_s[peer, steps_at, :], late)
-            message_s[peer, LAST * r + STEP_ROWS :, :] = early
+            message_s[peer, steps_at, :] = jnp.where(own_rows, message_s[peer, steps_at, :], small)
             return unused
 
         lax.fori_loop(0, message_s.shape[0], fill, 0)
-        at = (slice(None), pl.ds(LAST * r, 2 * STEP_ROWS))
+        at = (slice(None), pl.ds(LAST * r, STEP_ROWS))
         steps = sent.shape[0] - 1
         tiles = pltpu.make_async_copy(message_s.at[at], out_ref.at[at], sent.at[steps])
         tiles.start()
@@ -735,7 +717,7 @@
 
     first_rows = FIRST * rows + STEP_ROWS
     second_rows = SECOND * rows
-    last_rows = LAST * rows + 2 * STEP_ROWS
+    last_rows = LAST * rows + STEP_ROWS
 
     def packed(kernel, height, arrays, whole_arrays=(), scratch=()):
         out = hbm((sub_count, tensor_count, height, LANES), bf16)
@@ -841,11 +823,12 @@
         [pltpu.VMEM((STATE, WIDTH), f32), pltpu.VMEM((8, WIDTH), f32)],
     )(first, sources, readers, in_hbm(sm), in_hbm(smt), in_hbm(own), in_hbm(dec))
 
-    y, sums = flow(
+    y, sums, second = flow(
         mix_kernel,
         [
             (struct((tokens, WIDTH)), up["token"](WIDTH)),
             (struct((chunks, 8, LANES)), up["chunk"](8, LANES)),
+            (struct((peers, second_rows, LANES), bf16), up["message"](second_rows)),
         ],
         unit, size * 16,
         [
@@ -874,7 +857,7 @@
             up["chunk"](8, LANES), whole(1, WIDTH), whole(1, WIDTH),
         ],
         [pltpu.VMEM((STATE, WIDTH), f32)],
-    )(first, readers, in_hbm(second), y, sm, in_hbm(pre), sums, partner, own_gain, skip_row)
+    )(first, readers, second, y, sm, pre, sums, partner, own_gain, skip_row)
 
     outer = carry_over(slab_back, decay, after, slab_count, -1)
 
@@ -899,7 +882,7 @@
         ],
         [pltpu.VMEM((8, WIDTH), f32), pltpu.VMEM((8, WIDTH), f32)],
     )(
-        first, sources, readers, in_hbm(second), y, d_mixed, sm, smt, in_hbm(starts), in_hbm(pre), inbound,
+        first, sources, readers, second, y, d_mixed, sm, smt, starts, pre, inbound,
         sums, partner, own_gain, skip_row,
     )
 
@@ -921,7 +904,7 @@
         ],
     )(
         first, sources, d_values, d_sources, d_readers, d_gates, d_mixed, e, sm, smt, outer, back,
-        starts, in_hbm(dec), skip_row, heads, params,
+        starts, dec, skip_row, heads, params,
     )
 
     last_back = exchange(last)
@@ -933,9 +916,9 @@
         lambda *refs: unpack_params(sub_count, tensor_count, *refs),
         struct((8 + sub_count * PAIRS, LANES)),
         0, 4 * peers * STEP_ROWS * LANES, (1,),
-        [tile(tile_at), tile(tile_at + 1), whole(tensor_count, LANES)],
+        [tile(tile_at), whole(tensor_count, LANES)],
         whole(8 + sub_count * PAIRS, LANES),
-    )(last_back, last_back, mine)
+    )(last_back, mine)
     own_params, other_params = two_parts(params, "slab", slab_count)
     wide, narrow = struct((rows, CHANNELS), bf16), struct((rows, GROUPS * STATE), bf16)
     grad_x, grad_gates, grad_b, grad_c, grad_steps = call(

time: 135 us -> 132 us (0.978)
  Pallas kernels: 41.9 us -> 38.6 us
  waiting for transfers between devices: 33.2 us -> 35.4 us
  transfers between devices with their start and end apart: 7 -> 7, of which waited for: 6 -> 6; matrix products, arithmetic and copies ran while one was open for 1% -> 1% of each run, Pallas kernels for 17% -> 16%
where the time goes in v11:
time: 132 us; the launch traced here: 131 us
  Pallas kernels  38.6 us (29%)
  blocking collectives  37.5 us (28%)
  waiting for transfers between devices  35.4 us (27%)
  starting transfers between devices  17.5 us (13%)
  local copies, waits for them, and re-layouts  1.32 us (1%)
    all_to_all x1, blocking collectives, exchange(): lax.all_to_all(array, ('sub', 'tensor'), split_axis=0, concat_axis=0, til...  37.5 us
    ppermute x2, waiting for transfers between devices, shifted(): return lax.ppermute(array, 'slab', pairs)  15.8 us
    all_to_all x2, waiting for transfers between devices, exchange(): lax.all_to_all(array, ('sub', 'tensor'), split_axis=0, concat_axis=0, til...  14.7 us
    all_to_all x2, starting transfers between devices, exchange(): lax.all_to_all(array, ('sub', 'tensor'), split_axis=0, concat_axis=0, til...  10.7 us
    pallas_call x1, Pallas kernels, on_device(): flow(local_kernel, [(struct((tokens, WIDTH)), up['token'](WIDTH)), (struc...  6.35 us
    pallas_call x1, Pallas kernels, on_device(): flow(last_kernel, [(hbm((peers, last_rows, LANES), bf16), pl.BlockSpec(me...  6.31 us
    pallas_call x1, Pallas kernels, on_device(): flow(within_kernel, [(hbm((tokens, WIDTH)), up['token'](WIDTH)), (hbm((ch...  5.88 us
    ppermute x2, starting transfers between devices, shifted(): return lax.ppermute(array, 'slab', pairs)  5.78 us
  transfers between devices with their start and end apart: 7, of which 6 were waited for; matrix products, arithmetic and copies ran while one was open for 1% of the time, Pallas kernels for 16%

profile of v11, /device:TPU:0, one launch (start us, length us, event | category | flops | bytes accessed | tf_op | source)
XLA Modules:
  0.0 131.3 jit_solution(1935639471932801984)
XLA Ops:
  0.7 2.4 %shard_map.169 = bf16[8,2,336,128]{3,2,1,0:T(8,128)(2,1)} custom-call(bf16[64,8192]{1,0:T(8,128)(2,1)} %x_ref.1, bf16[64,1024]{1,0:T(8,128)(2,1)} %b_ref.1, bf16[64,1024]{1,0:T(8,128)(2,1)} %c_ref.1, bf16[64,128]{1,0:T(8,128)(2,1)} %steps_ref.1), custom_call_target="tpu_custom_call" | custom-call | bytes 2752512 | tf_op jit(solution)/shard_map/pallas_call | solution.py:731
  3.1 6.3 %all-to-all-start = ((bf16[16,336,128]{2,1,0:T(8,128)(2,1)}), bf16[16,336,128]{2,1,0:T(8,128)(2,1)S(1)}, u32[]{:S(2)}, u32[]{:S(2)}) async-start(bf16[16,336,128]{2,1,0:T(8,128)(2,1)} %bitcast.11), calls=%async_computation | async-start | bytes 2752512 | tf_op jit(solution)/shard_map/all_to_all | solution.py:709
  9.8 0.8 dynamic_slice.15
  10.8 2.7 %shard_map.170 = bf16[8,2,512,128]{3,2,1,0:T(8,128)(2,1)} custom-call(bf16[64,8192]{1,0:T(8,128)(2,1)} %z_ref, bf16[64,8192]{1,0:T(8,128)(2,1)} %grad_ref.1), custom_call_target="tpu_custom_call" | custom-call | bytes 4194304 | tf_op jit(solution)/shard_map/pallas_call | solution.py:731
  13.5 14.7 %all-to-all-done.refs_0_.refs_2_ = bf16[16,336,128]{2,1,0:T(8,128)(2,1)S(1)} async-done(((bf16[16,336,128]{2,1,0:T(8,128)(2,1)}), bf16[16,336,128]{2,1,0:T(8,128)(2,1)S(1)}, u32[]{:S(2)}, u32[]{:S(2)}) %all-to-all-start) | async-done | bytes 1376288 | tf_op jit(solution)/shard_map/all_to_all | solution.py:709
  28.1 4.5 %all-to-all-start.1 = ((bf16[16,512,128]{2,1,0:T(8,128)(2,1)}), bf16[16,512,128]{2,1,0:T(8,128)(2,1)}, u32[]{:S(2)}, u32[]{:S(2)}) async-start(bf16[16,512,128]{2,1,0:T(8,128)(2,1)} %bitcast.10), calls=%async_computation.1 | async-start | bytes 4194304 | tf_op jit(solution)/shard_map/all_to_all | solution.py:709
  32.6 0.3 collective-permute-start
  32.9 1.3 collective-permute-done
  34.3 4.4 %shard_map.171 = (f32[1024,128]{1,0:T(8,128)}, f32[64,1024]{1,0:T(8,128)}, f32[8,128,512]{2,1,0:T(8,128)}, f32[8,8,512]{2,1,0:T(8,128)}, bf16[128,512]{1,0:T(8,128)(2,1)S(1)}, /*index=5*/f32[8,512]{1,0:T(8,128)}) custom-call(bf16[16,336,128]{2,1,0:T(8,128)(2,1)S(1)} %all-to-all-done.refs_0_.refs_2_, bf16[16,64,128]{2,1,0:T(8,128)(2,1)S(1)} %get-tuple-element.80.refs_1_, ...), custom_call_target="tpu_custom_call" | custom-call | flops 268435456 | bytes 4194304 | tf_op jit(solution)/shard_map/pallas_call | solution.py:786
  38.7 4.5 %collective-permute-start.1 = (bf16[128,512]{1,0:T(8,128)(2,1)S(1)}, bf16[128,512]{1,0:T(8,128)(2,1)S(1)}, u32[]{:S(2)}, u32[]{:S(2)}) collective-permute-start(bf16[128,512]{1,0:T(8,128)(2,1)S(1)} %get-tuple-element.51), channel_id=1, source_target_pairs={{0,16},{1,17},{2,18},{3,19},{4,20},{5,21},{6,22},{7,23},{8,24},{9,... | collective-permute-start | bytes 393224 | tf_op jit(solution)/shard_map/ppermute | solution.py:649
  43.2 5.9 %shard_map.172 = (f32[1024,512]{1,0:T(8,128)}, f32[8,128,512]{2,1,0:T(8,128)}, f32[8,8,512]{2,1,0:T(8,128)}) custom-call(bf16[16,336,128]{2,1,0:T(8,128)(2,1)S(1)} %all-to-all-done.refs_0_.refs_2_, bf16[16,64,128]{2,1,0:T(8,128)(2,1)S(1)} %get-tuple-element.80.refs_1_, bf16[16,64,128]{2,1,0:T(8,128)(2,1)S(1)} %get-tuple-element.79.refs_2_.refs_1_, ...), custom_call_target="tpu_custom_call" | custom-call | flops 805306368 | bytes 8388608 | tf_op jit(solution)/shard_map/pallas_call | solution.py:810
  49.0 12.2 %collective-permute-done.1.refs_5_.refs_10_ = bf16[128,512]{1,0:T(8,128)(2,1)S(1)} collective-permute-done((bf16[128,512]{1,0:T(8,128)(2,1)S(1)}, bf16[128,512]{1,0:T(8,128)(2,1)S(1)}, u32[]{:S(2)}, u32[]{:S(2)}) %collective-permute-start.1) | collective-permute-done | bytes 131104 | tf_op jit(solution)/shard_map/ppermute | solution.py:649
  61.3 4.5 %shard_map.173 = (f32[1024,512]{1,0:T(8,128)S(1)}, f32[8,8,128]{2,1,0:T(8,128)S(1)}, bf16[16,512,128]{2,1,0:T(8,128)(2,1)S(1)}) custom-call(bf16[16,336,128]{2,1,0:T(8,128)(2,1)S(1)} %all-to-all-done.refs_0_.refs_2_, bf16[16,64,128]{2,1,0:T(8,128)(2,1)S(1)} %get-tuple-element.79.refs_2_.refs_1_, bf16[16,512,128]{2,1,0:T(8,128)(2,1)} %all-to-all-done.1.refs_2_, ...), custom_call_target="tpu_custom_call" | custom-call | flops 134217728 | bytes 8388608 | tf_op jit(solution)/shard_map/pallas_call | solution.py:826
  65.9 1.2 collective-permute-done.2.refs_7_.refs_12_
  67.1 3.4 %shard_map.174 = (bf16[1024,512]{1,0:T(8,128)(2,1)S(1)}, f32[8,128,512]{2,1,0:T(8,128)S(1)}, bf16[128,512]{1,0:T(8,128)(2,1)S(1)}) custom-call(bf16[16,336,128]{2,1,0:T(8,128)(2,1)S(1)} %all-to-all-done.refs_0_.refs_2_, bf16[16,64,128]{2,1,0:T(8,128)(2,1)S(1)} %get-tuple-element.79.refs_2_.refs_1_, ...), custom_call_target="tpu_custom_call" | custom-call | flops 268435456 | bytes 6291456 | tf_op jit(solution)/shard_map/pallas_call | solution.py:846
  70.5 1.3 collective-permute-start.3
  71.9 6.3 %shard_map.175 = (f32[1024,512]{1,0:T(8,128)S(1)}, f32[1024,128]{1,0:T(8,128)S(1)}, bf16[16,64,128]{2,1,0:T(8,128)(2,1)S(1)}, bf16[16,256,128]{2,1,0:T(8,128)(2,...) custom-call(bf16[16,336,128]{2,1,0:T(8,128)(2,1)S(1)} %all-to-all-done.refs_0_.refs_2_, ...), custom_call_target="tpu_custom_call" | custom-call | flops 1342177280 | bytes 8388608 | tf_op jit(solution)/shard_map/pallas_call | solution.py:864
  78.2 3.6 %collective-permute-done.3.refs_10_ = bf16[128,512]{1,0:T(8,128)(2,1)S(1)} collective-permute-done((bf16[128,512]{1,0:T(8,128)(2,1)S(1)}, bf16[128,512]{1,0:T(8,128)(2,1)S(1)}, u32[]{:S(2)}, u32[]{:S(2)}) %collective-permute-start.3) | collective-permute-done | bytes 131104 | tf_op jit(solution)/shard_map/ppermute | solution.py:649
  81.8 6.3 %shard_map.176 = bf16[16,656,128]{2,1,0:T(8,128)(2,1)} custom-call(bf16[16,336,128]{2,1,0:T(8,128)(2,1)S(1)} %all-to-all-done.refs_0_.refs_2_, bf16[16,64,128]{2,1,0:T(8,128)(2,1)S(1)} %get-tuple-element.80.refs_1_, f32[1024,512]{1,0:T(8,128)S(1)} %get-tuple-element.60.refs_2_, f32[1024,128]{1,0:T(8,128)S(1)} %get-tuple-element.61.refs_3_, ...), custom_call_target="tpu_custom_call" | custom-call | flops 536870912 | bytes 8388608 | tf_op jit(solution)/shard_map/pallas_call | solution.py:889
  88.1 37.5 %all_to_all.15.refs_0_ = bf16[16,656,128]{2,1,0:T(8,128)(2,1)S(1)} all-to-all(bf16[16,656,128]{2,1,0:T(8,128)(2,1)} %shard_map.176), channel_id=1, replica_groups=mesh['slab'=2,'sub'=8,'tensor'=2] {'sub','tensor'}, dimensions={0} | all-to-all | bytes 5373952 | tf_op jit(solution)/shard_map/all_to_all | solution.py:709
  125.7 0.7 collective-permute-start.4
  126.3 1.9 %shard_map.177 = (bf16[64,8192]{1,0:T(8,128)(2,1)}, bf16[64,8192]{1,0:T(8,128)(2,1)}, bf16[64,1024]{1,0:T(8,128)(2,1)}, bf16[64,1024]{1,0:T(8,128)(2,1)}, bf16[64,128]{1,0:T(8,128)(2,1)}) custom-call(bf16[16,656,128]{2,1,0:T(8,128)(2,1)S(1)} %all_to_all.15.refs_0_), custom_call_target="tpu_custom_call" | custom-call | bytes 5242880 | tf_op jit(solution)/shard_map/pallas_call | solution.py:924
  128.2 2.4 %collective-permute-done.4.other_ref = f32[40,128]{1,0:T(8,128)S(1)} collective-permute-done((f32[40,128]{1,0:T(8,128)S(1)}, f32[40,128]{1,0:T(8,128)S(1)}, u32[]{:S(2)}, u32[]{:S(2)}) %collective-permute-start.4) | collective-permute-done | bytes 20512 | tf_op jit(solution)/shard_map/ppermute | solution.py:680
  130.7 0.6 shard_map.179
  (30 shorter events, 0.9 us)
Async XLA Ops:
  0.6 8.7 %copy-start.5 = (f32[64]{0:T(128)S(1)}, f32[64]{0:T(128)}, u32[]{:S(2)}) copy-start(f32[64]{0:T(128)} %param.15) | copy-start | bytes 772
  0.7 8.8 %copy-start.6 = (f32[64]{0:T(128)S(1)}, f32[64]{0:T(128)}, u32[]{:S(2)}) copy-start(f32[64]{0:T(128)} %param.16) | copy-start | bytes 772
  0.7 8.9 %copy-start.7 = (f32[64]{0:T(128)S(1)}, f32[64]{0:T(128)}, u32[]{:S(2)}) copy-start(f32[64]{0:T(128)} %param.17) | copy-start | bytes 772
  3.1 25.1 %all-to-all-start = ((bf16[16,336,128]{2,1,0:T(8,128)(2,1)}), bf16[16,336,128]{2,1,0:T(8,128)(2,1)S(1)}, u32[]{:S(2)}, u32[]{:S(2)}) async-start(bf16[16,336,128]{2,1,0:T(8,128)(2,1)} %bitcast.11), calls=%async_computation | async-start | bytes 2752512 | tf_op jit(solution)/shard_map/all_to_all | solution.py:709
  28.1 33.1 %all-to-all-start.1 = ((bf16[16,512,128]{2,1,0:T(8,128)(2,1)}), bf16[16,512,128]{2,1,0:T(8,128)(2,1)}, u32[]{:S(2)}, u32[]{:S(2)}) async-start(bf16[16,512,128]{2,1,0:T(8,128)(2,1)} %bitcast.10), calls=%async_computation.1 | async-start | bytes 4194304 | tf_op jit(solution)/shard_map/all_to_all | solution.py:709
  32.6 1.6 %collective-permute-start = (bf16[16,64,128]{2,1,0:T(8,128)(2,1)S(1)}, bf16[16,64,128]{2,1,0:T(8,128)(2,1)S(1)}, u32[]{:S(2)}, u32[]{:S(2)}) collective-permute-start(bf16[16,64,128]{2,1,0:T(8,128)(2,1)S(1)} %slice.4), channel_id=1, source_target_pairs={{0,2},{2,0},{4,6},{6,4},{8,10},{10,8},{12,14},{14,12},{1,3},{3,1},... | collective-permute-start | bytes 786440 | tf_op jit(solution)/shard_map/ppermute | solution.py:745
  38.7 22.6 %collective-permute-start.1 = (bf16[128,512]{1,0:T(8,128)(2,1)S(1)}, bf16[128,512]{1,0:T(8,128)(2,1)S(1)}, u32[]{:S(2)}, u32[]{:S(2)}) collective-permute-start(bf16[128,512]{1,0:T(8,128)(2,1)S(1)} %get-tuple-element.51), channel_id=1, source_target_pairs={{0,16},{1,17},{2,18},{3,19},{4,20},{5,21},{6,22},{7,23},{8,24},{9,... | collective-permute-start | bytes 393224 | tf_op jit(solution)/shard_map/ppermute | solution.py:649
  61.3 5.8 %copy-start = (f32[1024,128]{1,0:T(8,128)S(1)}, f32[1024,128]{1,0:T(8,128)}, u32[]{:S(2)}) copy-start(f32[1024,128]{1,0:T(8,128)} %get-tuple-element.46.refs_3_.refs_4_.refs_6_.refs_8_) | copy-start | bytes 1572868
  61.3 5.8 %copy-start.3 = (f32[8,8,512]{2,1,0:T(8,128)S(1)}, f32[8,8,512]{2,1,0:T(8,128)}, u32[]{:S(2)}) copy-start(f32[8,8,512]{2,1,0:T(8,128)} %get-tuple-element.52.refs_6_.refs_5_.refs_9_) | copy-start | bytes 393220
  65.8 1.3 collective-permute-start.2
  67.1 4.7 %copy-start.1 = (f32[64,1024]{1,0:T(8,128)S(1)}, f32[64,1024]{1,0:T(8,128)}, u32[]{:S(2)}) copy-start(f32[64,1024]{1,0:T(8,128)} %get-tuple-element.47.refs_4_.refs_7_.refs_9_) | copy-start | bytes 786436
  67.1 4.8 %copy-start.2 = (f32[8,128,512]{2,1,0:T(8,128)S(1)}, f32[8,128,512]{2,1,0:T(8,128)}, u32[]{:S(2)}) copy-start(f32[8,128,512]{2,1,0:T(8,128)} %get-tuple-element.59.refs_8_) | copy-start | bytes 6291460
  70.5 11.3 %collective-permute-start.3 = (bf16[128,512]{1,0:T(8,128)(2,1)S(1)}, bf16[128,512]{1,0:T(8,128)(2,1)S(1)}, u32[]{:S(2)}, u32[]{:S(2)}) collective-permute-start(bf16[128,512]{1,0:T(8,128)(2,1)S(1)} %get-tuple-element.65), channel_id=1, source_target_pairs={{16,0},{17,1},{18,2},{19,3},{20,4},{21,5},{22,6},{23,7},{24,8},{25... | collective-permute-start | bytes 393224 | tf_op jit(solution)/shard_map/ppermute | solution.py:649
  71.8 10.0 %copy-start.4 = (f32[8,8,512]{2,1,0:T(8,128)S(1)}, f32[8,8,512]{2,1,0:T(8,128)}, u32[]{:S(2)}) copy-start(f32[8,8,512]{2,1,0:T(8,128)} %get-tuple-element.49.refs_6_.refs_13_) | copy-start | bytes 393220
  125.7 5.0 %collective-permute-start.4 = (f32[40,128]{1,0:T(8,128)S(1)}, f32[40,128]{1,0:T(8,128)S(1)}, u32[]{:S(2)}, u32[]{:S(2)}) collective-permute-start(f32[40,128]{1,0:T(8,128)S(1)} %shard_map.178.own_ref), channel_id=1, source_target_pairs={{0,16},{16,0},{1,17},{17,1},{2,18},{18,2},{3,19},{19,3},{4,20},{20... | collective-permute-start | bytes 61448 | tf_op jit(solution)/shard_map/ppermute | solution.py:680

commit v12 on v11

--- a/solution.py
+++ b/solution.py
@@ -123,7 +123,7 @@
 FIRST = PAIRS + 1
 Z, GRAD = 0, PAIRS
 SECOND = 2 * PAIRS
-LAST_X, LAST_Z, LAST_B, LAST_C = 0, PAIRS, 2 * PAIRS, 2 * PAIRS + 1
+LAST_X, LAST_B, LAST_Z, LAST_C = 0, PAIRS, PAIRS + 1, 2 * PAIRS + 1
 LAST = 2 * PAIRS + 2
 
 
@@ -325,37 +325,51 @@
 
 def mix_kernel(
     message, per_step,
-    first_ref, readers_ref, second_ref, within_ref, sm_ref, inbound_ref, pre_ref, gain_ref, skip_ref,
-    y_ref, sums_ref, second_out,
+    first_ref, readers_ref, second_hbm, within_hbm, sm_ref, inbound_ref, pre_ref, gain_ref, skip_ref,
+    y_ref, sums_ref, second_ref, arrived,
 ):
-    second_out[...] = second_ref[...]
-    made = []
+    c = pl.program_id(0)
+    peers, tokens = per_step * message.per_chunk, per_step * CHUNK
+
+    def copies(step):
+        at = pl.ds(step * peers, peers)
+        rows = pl.ds(step * tokens, tokens)
+        return (
+            pltpu.make_async_copy(within_hbm.at[rows], y_ref.at[rows], arrived.at[0, step]),
+            pltpu.make_async_copy(second_hbm.at[at], second_ref.at[at], arrived.at[1, step]),
+        )
+
+    @pl.when(c == 0)
+    def _():
+        for step in range(arrived.shape[1]):
+            for copy in copies(step):
+                copy.start()
+
+    for copy in copies(c):
+        copy.wait()
+    mine = second_ref.at[pl.ds(c * peers, peers)]
     inbound = inbound_ref[...].astype(bf16)
     for i in range(per_step):
         rows = slice(i * CHUNK, (i + 1) * CHUNK)
+        y_rows = pl.ds(pl.multiple_of(c * tokens + i * CHUNK, CHUNK), CHUNK)
         sm = sm_ref[rows, :]
         carried = mm(message.get(readers_ref, i, 0), inbound)
         power = jnp.zeros((CHUNK, LANES), f32)
         cross = jnp.zeros((CHUNK, LANES), f32)
-        ys = []
         for j in range(PAIRS):
             at = lanes(j)
             decay = spread_pair(sm, ECUM, j) * pre_ref[i, 0:1, at]
-            y = within_ref[rows, at] + decay * carried[:, at]
-            ys.append(y)
+            y = y_ref[y_rows, at] + decay * carried[:, at]
+            y_ref[y_rows, at] = y
             values = message.get(first_ref, i, X + j).astype(f32)
-            gates = message.get(second_ref, i, Z + j).astype(f32)
-            grad = message.get(second_ref, i, GRAD + j).astype(f32)
+            gates = message.get(mine, i, Z + j).astype(f32)
+            grad = message.get(mine, i, GRAD + j).astype(f32)
             gated = (y + skip_ref[0:1, at] * values) * (gates * sigmoid(gates))
             power = power + gated * gated
             cross = cross + grad * gain_ref[0:1, at] * gated
-        made.append(
-            (ys, jnp.sum(power.T, axis=0, keepdims=True), jnp.sum(cross.T, axis=0, keepdims=True))
-        )
-    for i, (ys, power, cross) in enumerate(made):
-        for j in range(PAIRS):
-            y_ref[i * CHUNK : (i + 1) * CHUNK, lanes(j)] = ys[j]
-        sums_ref[i] = jnp.concatenate([power, cross, jnp.zeros((6, LANES), f32)], axis=0)
+        sums_ref[i, 0:1, :] = jnp.sum(power.T, axis=0, keepdims=True)
+        sums_ref[i, 1:2, :] = jnp.sum(cross.T, axis=0, keepdims=True)
+        sums_ref[i, 2:, :] = jnp.zeros((6, LANES), f32)
 
 
 def norm_factors(sums):
@@ -378,7 +392,6 @@
     def _():
         back_sum[...] = jnp.zeros_like(back_sum)
 
-    made = []
     sums = [back_sum[:, lanes(j)] for j in range(PAIRS)]
     for i in range(per_step):
         rows = slice(i * CHUNK, (i + 1) * CHUNK)
@@ -395,10 +408,8 @@
             d_mixed = (inverse * grad * gain_ref[0:1, at] - pull * gated) * silu
             back = mm_two(readers_t, *two_terms(d_mixed * spread_pair(sm, ECUM, j)))
             sums[j] = sums[j] + pre_ref[i, 0:1, at] * back
-            made.append((i, j, d_mixed.astype(bf16), back))
-    for i, j, d_mixed, back in made:
-        mixed_ref[i * CHUNK : (i + 1) * CHUNK, lanes(j)] = d_mixed
-        back_ref[i, :, lanes(j)] = back
+            mixed_ref[rows, at] = d_mixed.astype(bf16)
+            back_ref[i, :, at] = back
     for j in range(PAIRS):
         back_sum[:, lanes(j)] = sums[j]
         slab_ref[:, lanes(j)] = sums[j].astype(bf16)
@@ -423,7 +434,6 @@
     causal = t >= s
     ones = head_rows()
     ones_twice = twice(ones)
-    made = []
     gains = [gain_sum[0:1, lanes(j)] for j in range(PAIRS)]
     skips = [skip_sum[0:1, lanes(j)] for j in range(PAIRS)]
     for i in range(per_step):
@@ -477,18 +487,13 @@
         total = jnp.where(causal, total, 0.0).astype(bf16)
         start = jnp.concatenate([part.astype(bf16) for part in starts], axis=1)
         d_readers = mm_tn(total, sources) + mm_nt(jnp.concatenate(scaleds, axis=1), start)
-        made.append(
-            (d_values, d_gates, starts, e[:HEADS], mm(total, readers), d_readers.astype(bf16))
-        )
-    for i, (d_values, d_gates, starts, e, d_sources, d_readers) in enumerate(made):
-        rows = slice(i * CHUNK, (i + 1) * CHUNK)
         for j in range(PAIRS):
             values_out[rows, lanes(j)] = d_values[j]
             message.put(gate_ref, i, j, d_gates[j])
             start_out[i, :, lanes(j)] = starts[j]
-        e_ref[:, lanes(i)] = e
-        sources_out[rows, :] = d_sources
-        message.put(readers_out, i, 0, d_readers)
+        e_ref[:, lanes(i)] = e[:HEADS]
+        sources_out[rows, :] = mm(total, readers)
+        message.put(readers_out, i, 0, d_readers.astype(bf16))
     for j in range(PAIRS):
         gain_sum[0:1, lanes(j)] = gains[j]
         skip_sum[0:1, lanes(j)] = skips[j]
@@ -527,15 +532,25 @@
     earlier = jnp.where(before < after, 1.0, 0.0)
     decay_rate = jnp.exp(heads_ref[:HEADS, :])
     first_peer = (pl.num_programs(0) - 1 - c) * per_step * message.per_chunk
-    span = per_step * message.per_chunk
-    mine = message_s.at[pl.ds(first_peer, span)]
-
-    def body_copy(step):
-        peer = (pl.num_programs(0) - 1 - step) * span
-        at = (pl.ds(peer, span), pl.ds(0, LAST * r))
-        return pltpu.make_async_copy(message_s.at[at], out_ref.at[at], sent.at[step])
-
-    made = []
+    mine = message_s.at[pl.ds(first_peer, per_step * message.per_chunk)]
+    chunks = sent.shape[0] - 3
+
+    def body_copy(chunk):
+        at = (pl.ds(chunk * message.per_chunk, message.per_chunk), pl.ds(0, LAST_Z * r))
+        return pltpu.make_async_copy(message_s.at[at], out_ref.at[at], sent.at[chunk])
+
+    gates_copy = pltpu.make_async_copy(
+        gate_ref, out_ref.at[:, pl.ds(LAST_Z * r, PAIRS * r)], sent.at[chunks]
+    )
+    readers_copy = pltpu.make_async_copy(
+        d_readers_ref, out_ref.at[:, pl.ds(LAST_C * r, r)], sent.at[chunks + 1]
+    )
+
+    @pl.when(c == 0)
+    def _():
+        gates_copy.start()
+        readers_copy.start()
+
     states = [carry[:, lanes(j)] for j in range(PAIRS)]
     logs_sum, steps_sum = sums[:HEADS, :], sums[HEADS:, :]
     for i in reversed(range(per_step)):
@@ -575,21 +590,17 @@
         logs_sum = logs_sum + flux * rate
         steps_sum = steps_sum + steps
         steps = jnp.concatenate([steps, jnp.zeros_like(steps)], axis=0)
-        made.append((i, d_values, d_sources.astype(bf16), steps))
-    for i, d_values, d_sources, steps in made:
         for j in range(PAIRS):
             message.put(mine, i, LAST_X + j, d_values[j])
-            message.put(mine, i, LAST_Z + j, message.get(gate_ref, i, j))
-        message.put(mine, i, LAST_B, d_sources)
-        message.put(mine, i, LAST_C, message.get(d_readers_ref, i, 0))
+        message.put(mine, i, LAST_B, d_sources.astype(bf16))
         for p in range(message.per_chunk):
             part = steps if p == 0 else pltpu.roll(steps, LANES - p * r, 1)
             mine[i * message.per_chunk + p, LAST * r : LAST * r + STEP_ROWS, :] = part.astype(bf16)
+        body_copy((pl.num_programs(0) - 1 - c) * per_step + i).start()
     for j in range(PAIRS):
         carry[:, lanes(j)] = states[j]
     sums[:HEADS, :] = logs_sum
     sums[HEADS:, :] = steps_sum
-    body_copy(c).start()
 
     @pl.when(c == pl.num_programs(0) - 1)
     def _():
@@ -613,11 +624,12 @@
 
         lax.fori_loop(0, message_s.shape[0], fill, 0)
         at = (slice(None), pl.ds(LAST * r, STEP_ROWS))
-        steps = sent.shape[0] - 1
-        tiles = pltpu.make_async_copy(message_s.at[at], out_ref.at[at], sent.at[steps])
+        tiles = pltpu.make_async_copy(message_s.at[at], out_ref.at[at], sent.at[chunks + 2])
         tiles.start()
-        for step in range(steps):
-            body_copy(step).wait()
+        for chunk in range(chunks):
+            body_copy(chunk).wait()
+        gates_copy.wait()
+        readers_copy.wait()
         tiles.wait()
 
 
@@ -638,7 +650,7 @@
         kernel,
         out_shape=out_shape,
         scratch_shapes=list(scratch),
-        compiler_params=pltpu.CompilerParams(vmem_limit_bytes=16 * 1024 * 1024),
+        compiler_params=pltpu.CompilerParams(vmem_limit_bytes=28 * 1024 * 1024),
         cost_estimate=pl.CostEstimate(flops=flops, bytes_accessed=moved, transcendentals=0),
         **extra,
     )
@@ -690,8 +702,6 @@
     peers = sub_count * tensor_count
     tokens = rows * peers
     chunks = tokens // CHUNK
-    per_step = min(2, chunks)
-    grid = (chunks // per_step,)
     message = Message(rows)
     owners = [t * sub_count + s for s in range(sub_count) for t in range(tensor_count)]
     sub = lax.axis_index("sub")
@@ -750,32 +760,37 @@
     )
     second = exchange(packed(pack_second, second_rows, (gate_z, out_grad)))
 
-    def flow(kernel, shape_specs, flops, moved, in_specs, scratch=()):
+    def flow(kernel, shape_specs, flops, moved, in_specs, scratch=(), per=2):
+        per = min(per, chunks)
+
         def body(*refs):
-            return kernel(message, per_step, *refs)
+            return kernel(message, per, *refs)
 
         shapes = tuple(shape for shape, _ in shape_specs)
         specs = tuple(spec for _, spec in shape_specs)
-        return call(body, shapes, flops, moved, grid, in_specs, specs, scratch)
-
-    def spec(block, axis, down=False):
-        def index(c):
-            at = grid[0] - 1 - c if down else c
-            return tuple(at if k == axis else 0 for k in range(len(block)))
-
-        return pl.BlockSpec(block, index)
-
-    span = per_step * CHUNK
-
-    def specs_of(down):
+        return call(body, shapes, flops, moved, (chunks // per,), in_specs, specs, scratch)
+
+    def specs_of(per, down=False):
+        per = min(per, chunks)
+        steps = chunks // per
+
+        def spec(block, axis):
+            def index(c):
+                at = steps - 1 - c if down else c
+                return tuple(at if k == axis else 0 for k in range(len(block)))
+
+            return pl.BlockSpec(block, index)
+
         return dict(
-            message=lambda height: spec((per_step * message.per_chunk, height, LANES), 0, down),
-            token=lambda width: spec((span, width), 0, down),
-            lane=lambda height: spec((height, span), 1, down),
-            chunk=lambda *shape: spec((per_step,) + shape, 0, down),
+            message=lambda height: spec((per * message.per_chunk, height, LANES), 0),
+            token=lambda width: spec((per * CHUNK, width), 0),
+            lane=lambda height: spec((height, per * CHUNK), 1),
+            chunk=lambda *shape: spec((per,) + shape, 0),
         )
 
-    up, dn = specs_of(False), specs_of(True)
+    up = specs_of(2)
+    many = specs_of(4)
+    dn = specs_of(8, down=True)
 
     def whole(*shape):
         return pl.BlockSpec(shape, lambda c: (0,) * len(shape))
@@ -823,19 +838,21 @@
         [pltpu.VMEM((STATE, WIDTH), f32), pltpu.VMEM((8, WIDTH), f32)],
     )(first, sources, readers, in_hbm(sm), in_hbm(smt), in_hbm(own), in_hbm(dec))
 
+    anywhere = pl.BlockSpec(memory_space=pl.ANY)
     y, sums, second = flow(
         mix_kernel,
         [
-            (struct((tokens, WIDTH)), up["token"](WIDTH)),
+            (struct((tokens, WIDTH)), whole(tokens, WIDTH)),
             (struct((chunks, 8, LANES)), up["chunk"](8, LANES)),
-            (struct((peers, second_rows, LANES), bf16), up["message"](second_rows)),
+            (struct((peers, second_rows, LANES), bf16), whole(peers, second_rows, LANES)),
         ],
         unit, size * 16,
         [
-            up["message"](PAIRS * rows), up["message"](rows), up["message"](second_rows),
-            up["token"](WIDTH), up["token"](LANES), whole(STATE, WIDTH), up["chunk"](8, WIDTH),
+            up["message"](PAIRS * rows), up["message"](rows), anywhere, anywhere,
+            up["token"](LANES), whole(STATE, WIDTH), up["chunk"](8, WIDTH),
             whole(1, WIDTH), whole(1, WIDTH),
         ],
+        [pltpu.SemaphoreType.DMA((2, chunks // min(2, chunks)))],
     )(
         first, readers, in_hbm(second), in_hbm(within), in_hbm(sm), inbound, in_hbm(pre),
         own_gain, skip_row,
@@ -846,17 +863,18 @@
     d_mixed, back, slab_back = flow(
         norm_kernel,
         [
-            (struct((tokens, WIDTH), bf16), up["token"](WIDTH)),
-            (struct((chunks, STATE, WIDTH)), up["chunk"](STATE, WIDTH)),
+            (struct((tokens, WIDTH), bf16), many["token"](WIDTH)),
+            (struct((chunks, STATE, WIDTH)), many["chunk"](STATE, WIDTH)),
             (struct((STATE, WIDTH), bf16), whole(STATE, WIDTH)),
         ],
         2 * unit, size * 12,
         [
-            up["message"](PAIRS * rows), up["message"](rows), up["message"](second_rows),
-            up["token"](WIDTH), up["token"](LANES), up["chunk"](8, WIDTH), up["chunk"](8, LANES),
-            up["chunk"](8, LANES), whole(1, WIDTH), whole(1, WIDTH),
+            many["message"](PAIRS * rows), many["message"](rows), many["message"](second_rows),
+            many["token"](WIDTH), many["token"](LANES), many["chunk"](8, WIDTH), many["chunk"](8, LANES),
+            many["chunk"](8, LANES), whole(1, WIDTH), whole(1, WIDTH),
         ],
         [pltpu.VMEM((STATE, WIDTH), f32)],
+        per=4,
     )(first, readers, second, y, sm, pre, sums, partner, own_gain, skip_row)
 
     outer = carry_over(slab_back, decay, after, slab_count, -1)
@@ -864,23 +882,24 @@
     d_values, d_sources, d_readers, d_gates, e, starts, params = flow(
         local_kernel,
         [
-            (struct((tokens, WIDTH)), up["token"](WIDTH)),
-            (struct((tokens, STATE)), up["token"](STATE)),
-            (struct((peers, rows, LANES), bf16), up["message"](rows)),
-            (struct((peers, PAIRS * rows, LANES), bf16), up["message"](PAIRS * rows)),
-            (struct((HEADS, tokens)), up["lane"](HEADS)),
-            (struct((chunks, STATE, WIDTH)), up["chunk"](STATE, WIDTH)),
+            (struct((tokens, WIDTH)), many["token"](WIDTH)),
+            (struct((tokens, STATE)), many["token"](STATE)),
+            (struct((peers, rows, LANES), bf16), many["message"](rows)),
+            (struct((peers, PAIRS * rows, LANES), bf16), many["message"](PAIRS * rows)),
+            (struct((HEADS, tokens)), many["lane"](HEADS)),
+            (struct((chunks, STATE, WIDTH)), many["chunk"](STATE, WIDTH)),
             (struct((8, LANES)), whole(8, LANES)),
         ],
         10 * unit, size * 16,
         [
-            up["message"](PAIRS * rows), up["message"](rows), up["message"](rows),
-            up["message"](second_rows), up["token"](WIDTH), up["token"](WIDTH), up["token"](LANES),
-            up["lane"](KINDS * HEADS),
-            up["chunk"](STATE, WIDTH), up["chunk"](8, WIDTH), whole(STATE, WIDTH),
-            up["chunk"](8, LANES), up["chunk"](8, LANES), whole(1, WIDTH), whole(1, WIDTH),
+            many["message"](PAIRS * rows), many["message"](rows), many["message"](rows),
+            many["message"](second_rows), many["token"](WIDTH), many["token"](WIDTH), many["token"](LANES),
+            many["lane"](KINDS * HEADS),
+            many["chunk"](STATE, WIDTH), many["chunk"](8, WIDTH), whole(STATE, WIDTH),
+            many["chunk"](8, LANES), many["chunk"](8, LANES), whole(1, WIDTH), whole(1, WIDTH),
         ],
         [pltpu.VMEM((8, WIDTH), f32), pltpu.VMEM((8, WIDTH), f32)],
+        per=4,
     )(
         first, sources, readers, second, y, d_mixed, sm, smt, starts, pre, inbound,
         sums, partner, own_gain, skip_row,
@@ -888,11 +907,11 @@
 
     (last,) = flow(
         last_kernel,
-        [(hbm((peers, last_rows, LANES), bf16), pl.BlockSpec(memory_space=pl.ANY))],
+        [(hbm((peers, last_rows, LANES), bf16), anywhere)],
         4 * unit, size * 16,
         [
             dn["message"](PAIRS * rows), dn["message"](rows), dn["token"](WIDTH), dn["token"](STATE),
-            dn["message"](rows), dn["message"](PAIRS * rows),
+            anywhere, anywhere,
             dn["token"](WIDTH), dn["lane"](HEADS), dn["token"](LANES), dn["lane"](KINDS * HEADS),
             whole(STATE, WIDTH), dn["chunk"](STATE, WIDTH), dn["chunk"](STATE, WIDTH),
             dn["chunk"](8, WIDTH), whole(1, WIDTH), whole(2 * HEADS, LANES), whole(8, LANES),
@@ -900,8 +919,9 @@
         [
             pltpu.VMEM((STATE, WIDTH), f32), pltpu.VMEM((2 * HEADS, LANES), f32),
             pltpu.VMEM((peers, last_rows, LANES), bf16),
-            pltpu.SemaphoreType.DMA((grid[0] + 1,)),
-        ],
+            pltpu.SemaphoreType.DMA((chunks + 3,)),
+        ],
+        per=8,
     )(
         first, sources, d_values, d_sources, d_readers, d_gates, d_mixed, e, sm, smt, outer, back,
         starts, dec, skip_row, heads, params,

time: 132 us -> 131 us (level)
  no operation moved by 1% of the time
where the time goes in v12:
time: 131 us
  blocking collectives  37.5 us (29%)
  Pallas kernels  37.4 us (29%)
  waiting for transfers between devices  36.3 us (28%)
  starting transfers between devices  17.1 us (13%)
  local copies, waits for them, and re-layouts  1.32 us (1%)
    all_to_all x1, blocking collectives, exchange(): lax.all_to_all(array, ('sub', 'tensor'), split_axis=0, concat_axis=0, til...  37.5 us
    ppermute x2, waiting for transfers between devices, shifted(): return lax.ppermute(array, 'slab', pairs)  16.3 us
    all_to_all x2, waiting for transfers between devices, exchange(): lax.all_to_all(array, ('sub', 'tensor'), split_axis=0, concat_axis=0, til...  14.7 us
    all_to_all x2, starting transfers between devices, exchange(): lax.all_to_all(array, ('sub', 'tensor'), split_axis=0, concat_axis=0, til...  10.7 us
    pallas_call x1, Pallas kernels, on_device(): flow(local_kernel, [(struct((tokens, WIDTH)), many['token'](WIDTH)), (str...  5.9 us
    pallas_call x1, Pallas kernels, on_device(): flow(within_kernel, [(hbm((tokens, WIDTH)), up['token'](WIDTH)), (hbm((ch...  5.88 us
    ppermute x2, starting transfers between devices, shifted(): return lax.ppermute(array, 'slab', pairs)  5.78 us
    pallas_call x1, Pallas kernels, on_device(): flow(last_kernel, [(hbm((peers, last_rows, LANES), bf16), anywhere)], 4 *...  5.51 us
  transfers between devices with their start and end apart: 7, of which 6 were waited for; matrix products, arithmetic and copies ran while one was open for 1% of the time, Pallas kernels for 16%

profile of v12, /device:TPU:0, one launch (start us, length us, event | category | flops | bytes accessed | tf_op | source)
XLA Modules:
  0.0 130.5 jit_solution(10596256626372909554)
XLA Ops:
  0.7 2.4 %shard_map.169 = bf16[8,2,336,128]{3,2,1,0:T(8,128)(2,1)} custom-call(bf16[64,8192]{1,0:T(8,128)(2,1)} %x_ref.1, bf16[64,1024]{1,0:T(8,128)(2,1)} %b_ref.1, bf16[64,1024]{1,0:T(8,128)(2,1)} %c_ref.1, bf16[64,128]{1,0:T(8,128)(2,1)} %steps_ref.1), custom_call_target="tpu_custom_call" | custom-call | bytes 2752512 | tf_op jit(solution)/shard_map/pallas_call | solution.py:741
  3.1 6.3 %all-to-all-start = ((bf16[16,336,128]{2,1,0:T(8,128)(2,1)}), bf16[16,336,128]{2,1,0:T(8,128)(2,1)S(1)}, u32[]{:S(2)}, u32[]{:S(2)}) async-start(bf16[16,336,128]{2,1,0:T(8,128)(2,1)} %bitcast.11), calls=%async_computation | async-start | bytes 2752512 | tf_op jit(solution)/shard_map/all_to_all | solution.py:719
  9.8 0.8 dynamic_slice.15
  10.8 2.7 %shard_map.170 = bf16[8,2,512,128]{3,2,1,0:T(8,128)(2,1)} custom-call(bf16[64,8192]{1,0:T(8,128)(2,1)} %z_ref, bf16[64,8192]{1,0:T(8,128)(2,1)} %grad_ref.1), custom_call_target="tpu_custom_call" | custom-call | bytes 4194304 | tf_op jit(solution)/shard_map/pallas_call | solution.py:741
  13.5 14.7 %all-to-all-done.refs_0_.refs_2_ = bf16[16,336,128]{2,1,0:T(8,128)(2,1)S(1)} async-done(((bf16[16,336,128]{2,1,0:T(8,128)(2,1)}), bf16[16,336,128]{2,1,0:T(8,128)(2,1)S(1)}, u32[]{:S(2)}, u32[]{:S(2)}) %all-to-all-start) | async-done | bytes 1376288 | tf_op jit(solution)/shard_map/all_to_all | solution.py:719
  28.1 4.5 %all-to-all-start.1 = ((bf16[16,512,128]{2,1,0:T(8,128)(2,1)}), bf16[16,512,128]{2,1,0:T(8,128)(2,1)}, u32[]{:S(2)}, u32[]{:S(2)}) async-start(bf16[16,512,128]{2,1,0:T(8,128)(2,1)} %bitcast.10), calls=%async_computation.1 | async-start | bytes 4194304 | tf_op jit(solution)/shard_map/all_to_all | solution.py:719
  32.6 0.3 collective-permute-start
  32.9 1.3 collective-permute-done
  34.3 4.4 %shard_map.171 = (f32[1024,128]{1,0:T(8,128)}, f32[64,1024]{1,0:T(8,128)}, f32[8,128,512]{2,1,0:T(8,128)}, f32[8,8,512]{2,1,0:T(8,128)}, bf16[128,512]{1,0:T(8,128)(2,1)S(1)}, /*index=5*/f32[8,512]{1,0:T(8,128)}) custom-call(bf16[16,336,128]{2,1,0:T(8,128)(2,1)S(1)} %all-to-all-done.refs_0_.refs_2_, bf16[16,64,128]{2,1,0:T(8,128)(2,1)S(1)} %get-tuple-element.80.refs_1_, ...), custom_call_target="tpu_custom_call" | custom-call | flops 268435456 | bytes 4194304 | tf_op jit(solution)/shard_map/pallas_call | solution.py:801
  38.7 4.5 %collective-permute-start.1 = (bf16[128,512]{1,0:T(8,128)(2,1)S(1)}, bf16[128,512]{1,0:T(8,128)(2,1)S(1)}, u32[]{:S(2)}, u32[]{:S(2)}) collective-permute-start(bf16[128,512]{1,0:T(8,128)(2,1)S(1)} %get-tuple-element.51), channel_id=1, source_target_pairs={{0,16},{1,17},{2,18},{3,19},{4,20},{5,21},{6,22},{7,23},{8,24},{9,... | collective-permute-start | bytes 393224 | tf_op jit(solution)/shard_map/ppermute | solution.py:661
  43.2 5.9 %shard_map.172 = (f32[1024,512]{1,0:T(8,128)}, f32[8,128,512]{2,1,0:T(8,128)}, f32[8,8,512]{2,1,0:T(8,128)}) custom-call(bf16[16,336,128]{2,1,0:T(8,128)(2,1)S(1)} %all-to-all-done.refs_0_.refs_2_, bf16[16,64,128]{2,1,0:T(8,128)(2,1)S(1)} %get-tuple-element.80.refs_1_, bf16[16,64,128]{2,1,0:T(8,128)(2,1)S(1)} %get-tuple-element.79.refs_2_.refs_1_, ...), custom_call_target="tpu_custom_call" | custom-call | flops 805306368 | bytes 8388608 | tf_op jit(solution)/shard_map/pallas_call | solution.py:825
  49.0 12.2 %collective-permute-done.1.refs_5_.refs_10_ = bf16[128,512]{1,0:T(8,128)(2,1)S(1)} collective-permute-done((bf16[128,512]{1,0:T(8,128)(2,1)S(1)}, bf16[128,512]{1,0:T(8,128)(2,1)S(1)}, u32[]{:S(2)}, u32[]{:S(2)}) %collective-permute-start.1) | collective-permute-done | bytes 131104 | tf_op jit(solution)/shard_map/ppermute | solution.py:661
  61.3 5.2 %shard_map.173 = (f32[1024,512]{1,0:T(8,128)S(1)}, f32[8,8,128]{2,1,0:T(8,128)S(1)}, bf16[16,512,128]{2,1,0:T(8,128)(2,1)S(1)}) custom-call(bf16[16,336,128]{2,1,0:T(8,128)(2,1)S(1)} %all-to-all-done.refs_0_.refs_2_, bf16[16,64,128]{2,1,0:T(8,128)(2,1)S(1)} %get-tuple-element.79.refs_2_.refs_1_, bf16[16,512,128]{2,1,0:T(8,128)(2,1)} %all-to-all-done.1.refs_2_, ...), custom_call_target="tpu_custom_call" | custom-call | flops 134217728 | bytes 8388608 | tf_op jit(solution)/shard_map/pallas_call | solution.py:842
  66.6 1.2 collective-permute-done.2.refs_7_.refs_12_
  67.8 2.8 %shard_map.174 = (bf16[1024,512]{1,0:T(8,128)(2,1)S(1)}, f32[8,128,512]{2,1,0:T(8,128)S(1)}, bf16[128,512]{1,0:T(8,128)(2,1)S(1)}) custom-call(bf16[16,336,128]{2,1,0:T(8,128)(2,1)S(1)} %all-to-all-done.refs_0_.refs_2_, bf16[16,64,128]{2,1,0:T(8,128)(2,1)S(1)} %get-tuple-element.79.refs_2_.refs_1_, ...), custom_call_target="tpu_custom_call" | custom-call | flops 268435456 | bytes 6291456 | tf_op jit(solution)/shard_map/pallas_call | solution.py:863
  70.6 1.3 collective-permute-start.3
  71.9 5.9 %shard_map.175 = (f32[1024,512]{1,0:T(8,128)S(1)}, f32[1024,128]{1,0:T(8,128)S(1)}, bf16[16,64,128]{2,1,0:T(8,128)(2,1)S(1)}, bf16[16,256,128]{2,1,0:T(8,128)(2,...) custom-call(bf16[16,336,128]{2,1,0:T(8,128)(2,1)S(1)} %all-to-all-done.refs_0_.refs_2_, ...), custom_call_target="tpu_custom_call" | custom-call | flops 1342177280 | bytes 8388608 | tf_op jit(solution)/shard_map/pallas_call | solution.py:882
  77.8 4.0 %collective-permute-done.3.refs_10_ = bf16[128,512]{1,0:T(8,128)(2,1)S(1)} collective-permute-done((bf16[128,512]{1,0:T(8,128)(2,1)S(1)}, bf16[128,512]{1,0:T(8,128)(2,1)S(1)}, u32[]{:S(2)}, u32[]{:S(2)}) %collective-permute-start.3) | collective-permute-done | bytes 131104 | tf_op jit(solution)/shard_map/ppermute | solution.py:661
  81.9 5.5 %shard_map.176 = bf16[16,656,128]{2,1,0:T(8,128)(2,1)} custom-call(bf16[16,336,128]{2,1,0:T(8,128)(2,1)S(1)} %all-to-all-done.refs_0_.refs_2_, bf16[16,64,128]{2,1,0:T(8,128)(2,1)S(1)} %get-tuple-element.80.refs_1_, f32[1024,512]{1,0:T(8,128)S(1)} %get-tuple-element.60.refs_2_, f32[1024,128]{1,0:T(8,128)S(1)} %get-tuple-element.61.refs_3_, ...), custom_call_target="tpu_custom_call" | custom-call | flops 536870912 | bytes 8388608 | tf_op jit(solution)/shard_map/pallas_call | solution.py:908
  87.4 37.5 %all_to_all.15.refs_0_ = bf16[16,656,128]{2,1,0:T(8,128)(2,1)S(1)} all-to-all(bf16[16,656,128]{2,1,0:T(8,128)(2,1)} %shard_map.176), channel_id=1, replica_groups=mesh['slab'=2,'sub'=8,'tensor'=2] {'sub','tensor'}, dimensions={0} | all-to-all | bytes 5373952 | tf_op jit(solution)/shard_map/all_to_all | solution.py:719
  124.9 0.2 collective-permute-start.4
  125.1 1.9 %shard_map.177 = (bf16[64,8192]{1,0:T(8,128)(2,1)}, bf16[64,8192]{1,0:T(8,128)(2,1)}, bf16[64,1024]{1,0:T(8,128)(2,1)}, bf16[64,1024]{1,0:T(8,128)(2,1)}, bf16[64,128]{1,0:T(8,128)(2,1)}) custom-call(bf16[16,656,128]{2,1,0:T(8,128)(2,1)S(1)} %all_to_all.15.refs_0_), custom_call_target="tpu_custom_call" | custom-call | bytes 5242880 | tf_op jit(solution)/shard_map/pallas_call | solution.py:944
  127.0 2.9 %collective-permute-done.4.other_ref = f32[40,128]{1,0:T(8,128)S(1)} collective-permute-done((f32[40,128]{1,0:T(8,128)S(1)}, f32[40,128]{1,0:T(8,128)S(1)}, u32[]{:S(2)}, u32[]{:S(2)}) %collective-permute-start.4) | collective-permute-done | bytes 20512 | tf_op jit(solution)/shard_map/ppermute | solution.py:692
  129.9 0.6 shard_map.179
  (30 shorter events, 0.9 us)
Async XLA Ops:
  0.6 8.7 %copy-start.5 = (f32[64]{0:T(128)S(1)}, f32[64]{0:T(128)}, u32[]{:S(2)}) copy-start(f32[64]{0:T(128)} %param.15) | copy-start | bytes 772
  0.7 8.8 %copy-start.6 = (f32[64]{0:T(128)S(1)}, f32[64]{0:T(128)}, u32[]{:S(2)}) copy-start(f32[64]{0:T(128)} %param.16) | copy-start | bytes 772
  0.7 8.9 %copy-start.7 = (f32[64]{0:T(128)S(1)}, f32[64]{0:T(128)}, u32[]{:S(2)}) copy-start(f32[64]{0:T(128)} %param.17) | copy-start | bytes 772
  3.1 25.1 %all-to-all-start = ((bf16[16,336,128]{2,1,0:T(8,128)(2,1)}), bf16[16,336,128]{2,1,0:T(8,128)(2,1)S(1)}, u32[]{:S(2)}, u32[]{:S(2)}) async-start(bf16[16,336,128]{2,1,0:T(8,128)(2,1)} %bitcast.11), calls=%async_computation | async-start | bytes 2752512 | tf_op jit(solution)/shard_map/all_to_all | solution.py:719
  28.1 33.1 %all-to-all-start.1 = ((bf16[16,512,128]{2,1,0:T(8,128)(2,1)}), bf16[16,512,128]{2,1,0:T(8,128)(2,1)}, u32[]{:S(2)}, u32[]{:S(2)}) async-start(bf16[16,512,128]{2,1,0:T(8,128)(2,1)} %bitcast.10), calls=%async_computation.1 | async-start | bytes 4194304 | tf_op jit(solution)/shard_map/all_to_all | solution.py:719
  32.6 1.6 %collective-permute-start = (bf16[16,64,128]{2,1,0:T(8,128)(2,1)S(1)}, bf16[16,64,128]{2,1,0:T(8,128)(2,1)S(1)}, u32[]{:S(2)}, u32[]{:S(2)}) collective-permute-start(bf16[16,64,128]{2,1,0:T(8,128)(2,1)S(1)} %slice.4), channel_id=1, source_target_pairs={{0,2},{2,0},{4,6},{6,4},{8,10},{10,8},{12,14},{14,12},{1,3},{3,1},... | collective-permute-start | bytes 786440 | tf_op jit(solution)/shard_map/ppermute | solution.py:755
  38.7 22.6 %collective-permute-start.1 = (bf16[128,512]{1,0:T(8,128)(2,1)S(1)}, bf16[128,512]{1,0:T(8,128)(2,1)S(1)}, u32[]{:S(2)}, u32[]{:S(2)}) collective-permute-start(bf16[128,512]{1,0:T(8,128)(2,1)S(1)} %get-tuple-element.51), channel_id=1, source_target_pairs={{0,16},{1,17},{2,18},{3,19},{4,20},{5,21},{6,22},{7,23},{8,24},{9,... | collective-permute-start | bytes 393224 | tf_op jit(solution)/shard_map/ppermute | solution.py:661
  61.3 6.5 %copy-start = (f32[1024,128]{1,0:T(8,128)S(1)}, f32[1024,128]{1,0:T(8,128)}, u32[]{:S(2)}) copy-start(f32[1024,128]{1,0:T(8,128)} %get-tuple-element.46.refs_3_.refs_4_.refs_6_.refs_8_) | copy-start | bytes 1572868
  61.3 6.5 %copy-start.3 = (f32[8,8,512]{2,1,0:T(8,128)S(1)}, f32[8,8,512]{2,1,0:T(8,128)}, u32[]{:S(2)}) copy-start(f32[8,8,512]{2,1,0:T(8,128)} %get-tuple-element.52.refs_6_.refs_5_.refs_9_) | copy-start | bytes 393220
  66.5 1.3 collective-permute-start.2
  67.8 4.1 %copy-start.1 = (f32[64,1024]{1,0:T(8,128)S(1)}, f32[64,1024]{1,0:T(8,128)}, u32[]{:S(2)}) copy-start(f32[64,1024]{1,0:T(8,128)} %get-tuple-element.47.refs_4_.refs_7_.refs_9_) | copy-start | bytes 786436
  67.8 4.1 %copy-start.2 = (f32[8,128,512]{2,1,0:T(8,128)S(1)}, f32[8,128,512]{2,1,0:T(8,128)}, u32[]{:S(2)}) copy-start(f32[8,128,512]{2,1,0:T(8,128)} %get-tuple-element.59.refs_8_) | copy-start | bytes 6291460
  70.6 11.3 %collective-permute-start.3 = (bf16[128,512]{1,0:T(8,128)(2,1)S(1)}, bf16[128,512]{1,0:T(8,128)(2,1)S(1)}, u32[]{:S(2)}, u32[]{:S(2)}) collective-permute-start(bf16[128,512]{1,0:T(8,128)(2,1)S(1)} %get-tuple-element.65), channel_id=1, source_target_pairs={{16,0},{17,1},{18,2},{19,3},{20,4},{21,5},{22,6},{23,7},{24,8},{25... | collective-permute-start | bytes 393224 | tf_op jit(solution)/shard_map/ppermute | solution.py:661
  71.9 10.0 %copy-start.4 = (f32[8,8,512]{2,1,0:T(8,128)S(1)}, f32[8,8,512]{2,1,0:T(8,128)}, u32[]{:S(2)}) copy-start(f32[8,8,512]{2,1,0:T(8,128)} %get-tuple-element.49.refs_6_.refs_13_) | copy-start | bytes 393220
  124.9 5.0 %collective-permute-start.4 = (f32[40,128]{1,0:T(8,128)S(1)}, f32[40,128]{1,0:T(8,128)S(1)}, u32[]{:S(2)}, u32[]{:S(2)}) collective-permute-start(f32[40,128]{1,0:T(8,128)S(1)} %shard_map.178.own_ref), channel_id=1, source_target_pairs={{0,16},{16,0},{1,17},{17,1},{2,18},{18,2},{3,19},{19,3},{4,20},{20... | collective-permute-start | bytes 61448 | tf_op jit(solution)/shard_map/ppermute | solution.py:692

commit v13 on v12

--- a/solution.py
+++ b/solution.py
@@ -325,45 +325,25 @@
 
 def mix_kernel(
     message, per_step,
-    first_ref, readers_ref, second_hbm, within_hbm, sm_ref, inbound_ref, pre_ref, gain_ref, skip_ref,
-    y_ref, sums_ref, second_ref, arrived,
+    first_ref, readers_ref, second_ref, within_ref, ecum_ref, inbound_ref, pre_ref, gain_ref, skip_ref,
+    y_ref, sums_ref,
 ):
-    c = pl.program_id(0)
-    peers, tokens = per_step * message.per_chunk, per_step * CHUNK
-
-    def copies(step):
-        at = pl.ds(step * peers, peers)
-        rows = pl.ds(step * tokens, tokens)
-        return (
-            pltpu.make_async_copy(within_hbm.at[rows], y_ref.at[rows], arrived.at[0, step]),
-            pltpu.make_async_copy(second_hbm.at[at], second_ref.at[at], arrived.at[1, step]),
-        )
-
-    @pl.when(c == 0)
-    def _():
-        for step in range(arrived.shape[1]):
-            for copy in copies(step):
-                copy.start()
-
-    for copy in copies(c):
-        copy.wait()
-    mine = second_ref.at[pl.ds(c * peers, peers)]
     inbound = inbound_ref[...].astype(bf16)
+    fill = jnp.zeros((LANES - HEADS, CHUNK), f32)
     for i in range(per_step):
         rows = slice(i * CHUNK, (i + 1) * CHUNK)
-        y_rows = pl.ds(pl.multiple_of(c * tokens + i * CHUNK, CHUNK), CHUNK)
-        sm = sm_ref[rows, :]
+        ecum = jnp.concatenate([ecum_ref[:, lanes(i)], fill], axis=0).T
         carried = mm(message.get(readers_ref, i, 0), inbound)
         power = jnp.zeros((CHUNK, LANES), f32)
         cross = jnp.zeros((CHUNK, LANES), f32)
         for j in range(PAIRS):
             at = lanes(j)
-            decay = spread_pair(sm, ECUM, j) * pre_ref[i, 0:1, at]
-            y = y_ref[y_rows, at] + decay * carried[:, at]
-            y_ref[y_rows, at] = y
+            decay = spread_pair(ecum, 0, j) * pre_ref[i, 0:1, at]
+            y = within_ref[rows, at] + decay * carried[:, at]
+            y_ref[rows, at] = y
             values = message.get(first_ref, i, X + j).astype(f32)
-            gates = message.get(mine, i, Z + j).astype(f32)
-            grad = message.get(mine, i, GRAD + j).astype(f32)
+            gates = message.get(second_ref, i, Z + j).astype(f32)
+            grad = message.get(second_ref, i, GRAD + j).astype(f32)
             gated = (y + skip_ref[0:1, at] * values) * (gates * sigmoid(gates))
             power = power + gated * gated
             cross = cross + grad * gain_ref[0:1, at] * gated
@@ -815,7 +795,7 @@
             whole(2 * HEADS, LANES),
         ],
         [pltpu.VMEM((STATE, WIDTH), f32), pltpu.VMEM((chunks, KINDS * HEADS, LANES), f32)],
-    )(first, sources, first, heads)
+    )(first, in_hbm(sources), first, heads)
 
     before = after = None
     if slab_count > 2:
@@ -836,25 +816,26 @@
             up["chunk"](STATE, WIDTH), up["chunk"](8, WIDTH),
         ],
         [pltpu.VMEM((STATE, WIDTH), f32), pltpu.VMEM((8, WIDTH), f32)],
-    )(first, sources, readers, in_hbm(sm), in_hbm(smt), in_hbm(own), in_hbm(dec))
+    )(first, in_hbm(sources), in_hbm(readers), in_hbm(sm), in_hbm(smt), in_hbm(own), in_hbm(dec))
 
     anywhere = pl.BlockSpec(memory_space=pl.ANY)
-    y, sums, second = flow(
+    per_mix = min(2, chunks)
+    ecum_block = pl.BlockSpec((HEADS, per_mix * CHUNK), lambda c: (ECUM, c))
+    y, sums = flow(
         mix_kernel,
         [
-            (struct((tokens, WIDTH)), whole(tokens, WIDTH)),
+            (struct((tokens, WIDTH)), up["token"](WIDTH)),
             (struct((chunks, 8, LANES)), up["chunk"](8, LANES)),
-            (struct((peers, second_rows, LANES), bf16), whole(peers, second_rows, LANES)),
         ],
         unit, size * 16,
         [
-            up["message"](PAIRS * rows), up["message"](rows), anywhere, anywhere,
-            up["token"](LANES), whole(STATE, WIDTH), up["chunk"](8, WIDTH),
+            up["message"](PAIRS * rows), up["message"](rows), up["message"](second_rows),
+            up["token"](WIDTH), ecum_block, whole(STATE, WIDTH), up["chunk"](8, WIDTH),
             whole(1, WIDTH), whole(1, WIDTH),
         ],
-        [pltpu.SemaphoreType.DMA((2, chunks // min(2, chunks)))],
+        per=per_mix,
     )(
-        first, readers, in_hbm(second), in_hbm(within), in_hbm(sm), inbound, in_hbm(pre),
+        first, in_hbm(readers), second, in_hbm(within), in_hbm(smt), inbound, in_hbm(pre),
         own_gain, skip_row,
     )
 

time: 131 us -> 132 us (level)
  waiting for transfers between devices: 36.3 us -> 32.7 us
  local copies, waits for them, and re-layouts: 1.32 us -> 3.6 us
  other arithmetic: 0.12 us -> 1.87 us
    ppermute x2, waiting for transfers between devices: 16.3 us -> 12.6 us  [shifted(): return lax.ppermute(array, 'slab', pairs)]
    select_n x1, other arithmetic: 0.05 us -> 1.8 us  [on_device(): jnp.where(even, other_half, half)]
    unnamed x16 -> x26, local copies, waits for them, and re-layouts: 0.03 us -> 1.6 us
  transfers between devices with their start and end apart: 7 -> 7, of which waited for: 6 -> 6; matrix products, arithmetic and copies ran while one was open for 1% -> 3% of each run, Pallas kernels for 16% -> 17%
where the time goes in v13:
time: 132 us
  Pallas kernels  38.2 us (29%)
  blocking collectives  37.5 us (28%)
  waiting for transfers between devices  32.7 us (25%)
  starting transfers between devices  17 us (13%)
  local copies, waits for them, and re-layouts  3.6 us (3%)
  other arithmetic  1.87 us (1%)
    all_to_all x1, blocking collectives, exchange(): lax.all_to_all(array, ('sub', 'tensor'), split_axis=0, concat_axis=0, til...  37.5 us
    all_to_all x2, waiting for transfers between devices, exchange(): lax.all_to_all(array, ('sub', 'tensor'), split_axis=0, concat_axis=0, til...  14.7 us
    ppermute x2, waiting for transfers between devices, shifted(): return lax.ppermute(array, 'slab', pairs)  12.6 us
    all_to_all x2, starting transfers between devices, exchange(): lax.all_to_all(array, ('sub', 'tensor'), split_axis=0, concat_axis=0, til...  10.4 us
    pallas_call x1, Pallas kernels, on_device(): flow(within_kernel, [(hbm((tokens, WIDTH)), up['token'](WIDTH)), (hbm((ch...  5.99 us
    pallas_call x1, Pallas kernels, on_device(): flow(local_kernel, [(struct((tokens, WIDTH)), many['token'](WIDTH)), (str...  5.88 us
    ppermute x2, starting transfers between devices, shifted(): return lax.ppermute(array, 'slab', pairs)  5.8 us
    pallas_call x1, Pallas kernels, on_device(): flow(last_kernel, [(hbm((peers, last_rows, LANES), bf16), anywhere)], 4 *...  5.55 us
  transfers between devices with their start and end apart: 7, of which 6 were waited for; matrix products, arithmetic and copies ran while one was open for 3% of the time, Pallas kernels for 17%

profile of v13, /device:TPU:0, one launch (start us, length us, event | category | flops | bytes accessed | tf_op | source)
XLA Modules:
  0.0 131.7 jit_solution(15966394925320437610)
XLA Ops:
  0.7 2.4 %shard_map.169 = bf16[8,2,336,128]{3,2,1,0:T(8,128)(2,1)} custom-call(bf16[64,8192]{1,0:T(8,128)(2,1)} %x_ref.1, bf16[64,1024]{1,0:T(8,128)(2,1)} %b_ref.1, bf16[64,1024]{1,0:T(8,128)(2,1)} %c_ref.1, bf16[64,128]{1,0:T(8,128)(2,1)} %steps_ref.1), custom_call_target="tpu_custom_call" | custom-call | bytes 2752512 | tf_op jit(solution)/shard_map/pallas_call | solution.py:721
  3.1 6.3 %all-to-all-start = ((bf16[16,336,128]{2,1,0:T(8,128)(2,1)}), bf16[16,336,128]{2,1,0:T(8,128)(2,1)S(1)}, u32[]{:S(2)}, u32[]{:S(2)}) async-start(bf16[16,336,128]{2,1,0:T(8,128)(2,1)} %bitcast.11), calls=%async_computation | async-start | bytes 2752512 | tf_op jit(solution)/shard_map/all_to_all | solution.py:699
  9.8 0.8 dynamic_slice.15
  10.8 2.7 %shard_map.170 = bf16[8,2,512,128]{3,2,1,0:T(8,128)(2,1)} custom-call(bf16[64,8192]{1,0:T(8,128)(2,1)} %z_ref, bf16[64,8192]{1,0:T(8,128)(2,1)} %grad_ref.1), custom_call_target="tpu_custom_call" | custom-call | bytes 4194304 | tf_op jit(solution)/shard_map/pallas_call | solution.py:721
  13.5 14.6 %all-to-all-done.refs_0_.refs_2_ = bf16[16,336,128]{2,1,0:T(8,128)(2,1)S(1)} async-done(((bf16[16,336,128]{2,1,0:T(8,128)(2,1)}), bf16[16,336,128]{2,1,0:T(8,128)(2,1)S(1)}, u32[]{:S(2)}, u32[]{:S(2)}) %all-to-all-start) | async-done | bytes 1376288 | tf_op jit(solution)/shard_map/all_to_all | solution.py:699
  28.2 4.1 %all-to-all-start.1 = ((bf16[16,512,128]{2,1,0:T(8,128)(2,1)}), bf16[16,512,128]{2,1,0:T(8,128)(2,1)S(1)}, u32[]{:S(2)}, u32[]{:S(2)}) async-start(bf16[16,512,128]{2,1,0:T(8,128)(2,1)} %bitcast.10), calls=%async_computation.1 | async-start | bytes 4194304 | tf_op jit(solution)/shard_map/all_to_all | solution.py:699
  32.3 0.7 slice.4
  33.4 1.5 %collective-permute-done = bf16[16,64,128]{2,1,0:T(8,128)(2,1)} collective-permute-done((bf16[16,64,128]{2,1,0:T(8,128)(2,1)}, bf16[16,64,128]{2,1,0:T(8,128)(2,1)}, u32[]{:S(2)}, u32[]{:S(2)}) %collective-permute-start) | collective-permute-done | bytes 262176 | tf_op jit(solution)/shard_map/ppermute | solution.py:735
  34.9 1.8 %broadcast_select_fusion = (bf16[16,64,128]{2,1,0:T(8,128)(2,1)}, bf16[16,64,128]{2,1,0:T(8,128)(2,1)}) fusion(bf16[16,64,128]{2,1,0:T(8,128)(2,1)} %collective-permute-done, pred[]{:T(512)S(6)} %eq.12, bf16[16,336,128]{2,1,0:T(8,128)(2,1)S(1)} %all-to-all-done.refs_0_.refs_2_), kind=kLoop, calls=%fused_computation | loop fusion | flops 262144 | bytes 1048577 | tf_op jit(solution)/shard_map/jit(_where)/select_n | solution.py:737
  36.7 5.3 %shard_map.171 = (f32[1024,128]{1,0:T(8,128)}, f32[64,1024]{1,0:T(8,128)}, f32[8,128,512]{2,1,0:T(8,128)}, f32[8,8,512]{2,1,0:T(8,128)}, bf16[128,512]{1,0:T(8,128)(2,1)S(1)}, /*index=5*/f32[8,512]{1,0:T(8,128)}) custom-call(bf16[16,336,128]{2,1,0:T(8,128)(2,1)S(1)} %all-to-all-done.refs_0_.refs_2_, bf16[16,64,128]{2,1,0:T(8,128)(2,1)} %get-tuple-element.78.refs_1_, ...), custom_call_target="tpu_custom_call" | custom-call | flops 268435456 | bytes 4194304 | tf_op jit(solution)/shard_map/pallas_call | solution.py:781
  42.0 4.5 %collective-permute-start.1 = (bf16[128,512]{1,0:T(8,128)(2,1)S(1)}, bf16[128,512]{1,0:T(8,128)(2,1)S(1)}, u32[]{:S(2)}, u32[]{:S(2)}) collective-permute-start(bf16[128,512]{1,0:T(8,128)(2,1)S(1)} %get-tuple-element.50), channel_id=1, source_target_pairs={{0,16},{1,17},{2,18},{3,19},{4,20},{5,21},{6,22},{7,23},{8,24},{9,... | collective-permute-start | bytes 393224 | tf_op jit(solution)/shard_map/ppermute | solution.py:641
  46.5 6.0 %shard_map.172 = (f32[1024,512]{1,0:T(8,128)}, f32[8,128,512]{2,1,0:T(8,128)}, f32[8,8,512]{2,1,0:T(8,128)}) custom-call(bf16[16,336,128]{2,1,0:T(8,128)(2,1)S(1)} %all-to-all-done.refs_0_.refs_2_, bf16[16,64,128]{2,1,0:T(8,128)(2,1)} %get-tuple-element.78.refs_1_, bf16[16,64,128]{2,1,0:T(8,128)(2,1)} %get-tuple-element.77.refs_2_.refs_1_, ...), custom_call_target="tpu_custom_call" | custom-call | flops 805306368 | bytes 8388608 | tf_op jit(solution)/shard_map/pallas_call | solution.py:805
  52.5 8.6 %collective-permute-done.1.refs_5_.refs_10_ = bf16[128,512]{1,0:T(8,128)(2,1)S(1)} collective-permute-done((bf16[128,512]{1,0:T(8,128)(2,1)S(1)}, bf16[128,512]{1,0:T(8,128)(2,1)S(1)}, u32[]{:S(2)}, u32[]{:S(2)}) %collective-permute-start.1) | collective-permute-done | bytes 131104 | tf_op jit(solution)/shard_map/ppermute | solution.py:641
  61.7 0.9 copy-done.8
  62.6 4.9 %shard_map.173 = (f32[1024,512]{1,0:T(8,128)S(1)}, f32[8,8,128]{2,1,0:T(8,128)S(1)}) custom-call(bf16[16,336,128]{2,1,0:T(8,128)(2,1)S(1)} %all-to-all-done.refs_0_.refs_2_, bf16[16,64,128]{2,1,0:T(8,128)(2,1)} %get-tuple-element.77.refs_2_.refs_1_, bf16[16,512,128]{2,1,0:T(8,128)(2,1)S(1)} %all-to-all-done.1.refs_2_.refs_3_, ...), custom_call_target="tpu_custom_call" | custom-call | flops 134217728 | bytes 8388608 | tf_op jit(solution)/shard_map/pallas_call | solution.py:824
  67.6 1.2 collective-permute-done.2.refs_7_.refs_12_
  68.9 2.8 %shard_map.174 = (bf16[1024,512]{1,0:T(8,128)(2,1)S(1)}, f32[8,128,512]{2,1,0:T(8,128)S(1)}, bf16[128,512]{1,0:T(8,128)(2,1)S(1)}) custom-call(bf16[16,336,128]{2,1,0:T(8,128)(2,1)S(1)} %all-to-all-done.refs_0_.refs_2_, bf16[16,64,128]{2,1,0:T(8,128)(2,1)S(1)} %copy-done.2, bf16[16,512,128]{2,1,0:T(8,128)(2,1)S(1)} %all-to-all-done.1.refs_2_.refs_3_, ...), custom_call_target="tpu_custom_call" | custom-call | flops 268435456 | bytes 6291456 | tf_op jit(solution)/shard_map/pallas_call | solution.py:844
  71.7 1.3 collective-permute-start.3
  73.0 5.9 %shard_map.175 = (f32[1024,512]{1,0:T(8,128)S(1)}, f32[1024,128]{1,0:T(8,128)S(1)}, bf16[16,64,128]{2,1,0:T(8,128)(2,1)S(1)}, bf16[16,256,128]{2,1,0:T(8,128)(2,...) custom-call(bf16[16,336,128]{2,1,0:T(8,128)(2,1)S(1)} %all-to-all-done.refs_0_.refs_2_, ...), custom_call_target="tpu_custom_call" | custom-call | flops 1342177280 | bytes 8388608 | tf_op jit(solution)/shard_map/pallas_call | solution.py:863
  78.9 4.0 %collective-permute-done.3.refs_10_ = bf16[128,512]{1,0:T(8,128)(2,1)S(1)} collective-permute-done((bf16[128,512]{1,0:T(8,128)(2,1)S(1)}, bf16[128,512]{1,0:T(8,128)(2,1)S(1)}, u32[]{:S(2)}, u32[]{:S(2)}) %collective-permute-start.3) | collective-permute-done | bytes 131104 | tf_op jit(solution)/shard_map/ppermute | solution.py:641
  83.0 5.6 %shard_map.176 = bf16[16,656,128]{2,1,0:T(8,128)(2,1)} custom-call(bf16[16,336,128]{2,1,0:T(8,128)(2,1)S(1)} %all-to-all-done.refs_0_.refs_2_, bf16[16,64,128]{2,1,0:T(8,128)(2,1)S(1)} %copy-done.1, f32[1024,512]{1,0:T(8,128)S(1)} %get-tuple-element.58.refs_2_, f32[1024,128]{1,0:T(8,128)S(1)} %get-tuple-element.59.refs_3_, ...), custom_call_target="tpu_custom_call" | custom-call | flops 536870912 | bytes 8388608 | tf_op jit(solution)/shard_map/pallas_call | solution.py:889
  88.5 37.5 %all_to_all.15.refs_0_ = bf16[16,656,128]{2,1,0:T(8,128)(2,1)S(1)} all-to-all(bf16[16,656,128]{2,1,0:T(8,128)(2,1)} %shard_map.176), channel_id=1, replica_groups=mesh['slab'=2,'sub'=8,'tensor'=2] {'sub','tensor'}, dimensions={0} | all-to-all | bytes 5373952 | tf_op jit(solution)/shard_map/all_to_all | solution.py:699
  126.4 1.9 %shard_map.177 = (bf16[64,8192]{1,0:T(8,128)(2,1)}, bf16[64,8192]{1,0:T(8,128)(2,1)}, bf16[64,1024]{1,0:T(8,128)(2,1)}, bf16[64,1024]{1,0:T(8,128)(2,1)}, bf16[64,128]{1,0:T(8,128)(2,1)}) custom-call(bf16[16,656,128]{2,1,0:T(8,128)(2,1)S(1)} %all_to_all.15.refs_0_), custom_call_target="tpu_custom_call" | custom-call | bytes 5242880 | tf_op jit(solution)/shard_map/pallas_call | solution.py:925
  128.3 2.7 %collective-permute-done.4.other_ref = f32[40,128]{1,0:T(8,128)S(1)} collective-permute-done((f32[40,128]{1,0:T(8,128)S(1)}, f32[40,128]{1,0:T(8,128)S(1)}, u32[]{:S(2)}, u32[]{:S(2)}) %collective-permute-start.4) | collective-permute-done | bytes 20512 | tf_op jit(solution)/shard_map/ppermute | solution.py:672
  (40 shorter events, 2.9 us)
Async XLA Ops:
  0.6 8.8 %copy-start.10 = (f32[64]{0:T(128)S(1)}, f32[64]{0:T(128)}, u32[]{:S(2)}) copy-start(f32[64]{0:T(128)} %param.15) | copy-start | bytes 772
  0.7 8.8 %copy-start.11 = (f32[64]{0:T(128)S(1)}, f32[64]{0:T(128)}, u32[]{:S(2)}) copy-start(f32[64]{0:T(128)} %param.16) | copy-start | bytes 772
  0.7 8.9 %copy-start.12 = (f32[64]{0:T(128)S(1)}, f32[64]{0:T(128)}, u32[]{:S(2)}) copy-start(f32[64]{0:T(128)} %param.17) | copy-start | bytes 772
  3.1 25.1 %all-to-all-start = ((bf16[16,336,128]{2,1,0:T(8,128)(2,1)}), bf16[16,336,128]{2,1,0:T(8,128)(2,1)S(1)}, u32[]{:S(2)}, u32[]{:S(2)}) async-start(bf16[16,336,128]{2,1,0:T(8,128)(2,1)} %bitcast.11), calls=%async_computation | async-start | bytes 2752512 | tf_op jit(solution)/shard_map/all_to_all | solution.py:699
  28.2 33.6 %all-to-all-start.1 = ((bf16[16,512,128]{2,1,0:T(8,128)(2,1)}), bf16[16,512,128]{2,1,0:T(8,128)(2,1)S(1)}, u32[]{:S(2)}, u32[]{:S(2)}) async-start(bf16[16,512,128]{2,1,0:T(8,128)(2,1)} %bitcast.10), calls=%async_computation.1 | async-start | bytes 4194304 | tf_op jit(solution)/shard_map/all_to_all | solution.py:699
  33.0 1.9 %collective-permute-start = (bf16[16,64,128]{2,1,0:T(8,128)(2,1)}, bf16[16,64,128]{2,1,0:T(8,128)(2,1)}, u32[]{:S(2)}, u32[]{:S(2)}) collective-permute-start(bf16[16,64,128]{2,1,0:T(8,128)(2,1)} %slice.4), channel_id=1, source_target_pairs={{0,2},{2,0},{4,6},{6,4},{8,10},{10,8},{12,14},{14,12},{1,3},{3,1},... | collective-permute-start | bytes 786440 | tf_op jit(solution)/shard_map/ppermute | solution.py:735
  42.0 19.1 %collective-permute-start.1 = (bf16[128,512]{1,0:T(8,128)(2,1)S(1)}, bf16[128,512]{1,0:T(8,128)(2,1)S(1)}, u32[]{:S(2)}, u32[]{:S(2)}) collective-permute-start(bf16[128,512]{1,0:T(8,128)(2,1)S(1)} %get-tuple-element.50), channel_id=1, source_target_pairs={{0,16},{1,17},{2,18},{3,19},{4,20},{5,21},{6,22},{7,23},{8,24},{9,... | collective-permute-start | bytes 393224 | tf_op jit(solution)/shard_map/ppermute | solution.py:641
  61.1 0.7 copy-start.7
  61.7 0.9 copy-start.8
  62.6 6.2 %copy-start = (f32[1024,128]{1,0:T(8,128)S(1)}, f32[1024,128]{1,0:T(8,128)}, u32[]{:S(2)}) copy-start(f32[1024,128]{1,0:T(8,128)} %get-tuple-element.45.refs_3_.refs_4_.refs_6_.refs_8_) | copy-start | bytes 1572868
  62.6 6.2 %copy-start.2 = (bf16[16,64,128]{2,1,0:T(8,128)(2,1)S(1)}, bf16[16,64,128]{2,1,0:T(8,128)(2,1)}, u32[]{:S(2)}) copy-start(bf16[16,64,128]{2,1,0:T(8,128)(2,1)} %get-tuple-element.77.refs_2_.refs_1_) | copy-start | bytes 786436
  62.6 6.2 %copy-start.5 = (f32[8,8,512]{2,1,0:T(8,128)S(1)}, f32[8,8,512]{2,1,0:T(8,128)}, u32[]{:S(2)}) copy-start(f32[8,8,512]{2,1,0:T(8,128)} %get-tuple-element.51.refs_6_.refs_5_.refs_9_) | copy-start | bytes 393220
  67.6 1.3 collective-permute-start.2
  68.9 4.1 %copy-start.1 = (bf16[16,64,128]{2,1,0:T(8,128)(2,1)S(1)}, bf16[16,64,128]{2,1,0:T(8,128)(2,1)}, u32[]{:S(2)}) copy-start(bf16[16,64,128]{2,1,0:T(8,128)(2,1)} %get-tuple-element.78.refs_1_) | copy-start | bytes 786436
  68.9 4.1 %copy-start.3 = (f32[64,1024]{1,0:T(8,128)S(1)}, f32[64,1024]{1,0:T(8,128)}, u32[]{:S(2)}) copy-start(f32[64,1024]{1,0:T(8,128)} %get-tuple-element.46.refs_4_.refs_7_.refs_9_) | copy-start | bytes 786436
  68.9 4.1 %copy-start.4 = (f32[8,128,512]{2,1,0:T(8,128)S(1)}, f32[8,128,512]{2,1,0:T(8,128)}, u32[]{:S(2)}) copy-start(f32[8,128,512]{2,1,0:T(8,128)} %get-tuple-element.57.refs_8_) | copy-start | bytes 6291460
  68.9 4.1 %copy-start.9 = (bf16[128,512]{1,0:T(8,128)(2,1)S(1)}, bf16[128,512]{1,0:T(8,128)(2,1)}, u32[]{:S(2)}) copy-start(bf16[128,512]{1,0:T(8,128)(2,1)} %copy-done.7) | copy-start | bytes 393220
  71.7 11.3 %collective-permute-start.3 = (bf16[128,512]{1,0:T(8,128)(2,1)S(1)}, bf16[128,512]{1,0:T(8,128)(2,1)S(1)}, u32[]{:S(2)}, u32[]{:S(2)}) collective-permute-start(bf16[128,512]{1,0:T(8,128)(2,1)S(1)} %get-tuple-element.63), channel_id=1, source_target_pairs={{16,0},{17,1},{18,2},{19,3},{20,4},{21,5},{22,6},{23,7},{24,8},{25... | collective-permute-start | bytes 393224 | tf_op jit(solution)/shard_map/ppermute | solution.py:641
  73.0 9.9 %copy-start.6 = (f32[8,8,512]{2,1,0:T(8,128)S(1)}, f32[8,8,512]{2,1,0:T(8,128)}, u32[]{:S(2)}) copy-start(f32[8,8,512]{2,1,0:T(8,128)} %get-tuple-element.48.refs_6_.refs_13_) | copy-start | bytes 393220
  126.1 5.0 %collective-permute-start.4 = (f32[40,128]{1,0:T(8,128)S(1)}, f32[40,128]{1,0:T(8,128)S(1)}, u32[]{:S(2)}, u32[]{:S(2)}) collective-permute-start(f32[40,128]{1,0:T(8,128)S(1)} %shard_map.178.own_ref), channel_id=1, source_target_pairs={{0,16},{16,0},{1,17},{17,1},{2,18},{18,2},{3,19},{19,3},{4,20},{20... | collective-permute-start | bytes 61448 | tf_op jit(solution)/shard_map/ppermute | solution.py:672

commit v14 on v13

--- a/solution.py
+++ b/solution.py
@@ -819,23 +819,23 @@
     )(first, in_hbm(sources), in_hbm(readers), in_hbm(sm), in_hbm(smt), in_hbm(own), in_hbm(dec))
 
     anywhere = pl.BlockSpec(memory_space=pl.ANY)
-    per_mix = min(2, chunks)
+    per_mix = min(4, chunks)
     ecum_block = pl.BlockSpec((HEADS, per_mix * CHUNK), lambda c: (ECUM, c))
     y, sums = flow(
         mix_kernel,
         [
-            (struct((tokens, WIDTH)), up["token"](WIDTH)),
-            (struct((chunks, 8, LANES)), up["chunk"](8, LANES)),
+            (struct((tokens, WIDTH)), many["token"](WIDTH)),
+            (struct((chunks, 8, LANES)), many["chunk"](8, LANES)),
         ],
         unit, size * 16,
         [
-            up["message"](PAIRS * rows), up["message"](rows), up["message"](second_rows),
-            up["token"](WIDTH), ecum_block, whole(STATE, WIDTH), up["chunk"](8, WIDTH),
+            many["message"](PAIRS * rows), many["message"](rows), many["message"](second_rows),
+            many["token"](WIDTH), ecum_block, whole(STATE, WIDTH), many["chunk"](8, WIDTH),
             whole(1, WIDTH), whole(1, WIDTH),
         ],
         per=per_mix,
     )(
-        first, in_hbm(readers), second, in_hbm(within), in_hbm(smt), inbound, in_hbm(pre),
+        first, in_hbm(readers), second, in_hbm(within), in_hbm(smt), in_hbm(inbound), in_hbm(pre),
         own_gain, skip_row,
     )
 
@@ -882,7 +882,7 @@
         [pltpu.VMEM((8, WIDTH), f32), pltpu.VMEM((8, WIDTH), f32)],
         per=4,
     )(
-        first, sources, readers, second, y, d_mixed, sm, smt, starts, pre, inbound,
+        first, sources, readers, second, y, d_mixed, sm, smt, in_hbm(starts), pre, in_hbm(inbound),
         sums, partner, own_gain, skip_row,
     )
 

time: 132 us -> 131 us (level)
  waiting for transfers between devices: 32.7 us -> 29.1 us
  starting transfers between devices: 17 us -> 19.7 us
  local copies, waits for them, and re-layouts: 3.6 us -> 2.04 us
    ppermute x1, waiting for transfers between devices: 2.7 us -> 0.89 us  [two_parts(): other = lax.ppermute(array, axis, [(i, i ^ step) for i in range(count)])]
    ppermute x1, starting transfers between devices: 0.36 us -> 2.17 us  [two_parts(): other = lax.ppermute(array, axis, [(i, i ^ step) for i in range(count)])]
    ppermute x2, waiting for transfers between devices: 12.6 us -> 10.8 us  [shifted(): return lax.ppermute(array, 'slab', pairs)]
    unnamed x26 -> x18, local copies, waits for them, and re-layouts: 1.6 us -> 0.04 us
  transfers between devices with their start and end apart: 7 -> 7, of which waited for: 6 -> 6; matrix products, arithmetic and copies ran while one was open for 3% -> 3% of each run, Pallas kernels for 17% -> 18%
where the time goes in v14:
time: 131 us; the launch traced here: 130 us
  Pallas kernels  39.2 us (30%)
  blocking collectives  37.5 us (29%)
  waiting for transfers between devices  29.1 us (22%)
  starting transfers between devices  19.7 us (15%)
  local copies, waits for them, and re-layouts  2.04 us (2%)
  other arithmetic  1.87 us (1%)
    all_to_all x1, blocking collectives, exchange(): lax.all_to_all(array, ('sub', 'tensor'), split_axis=0, concat_axis=0, til...  37.5 us
    all_to_all x2, waiting for transfers between devices, exchange(): lax.all_to_all(array, ('sub', 'tensor'), split_axis=0, concat_axis=0, til...  14.7 us
    ppermute x2, waiting for transfers between devices, shifted(): return lax.ppermute(array, 'slab', pairs)  10.8 us
    all_to_all x2, starting transfers between devices, exchange(): lax.all_to_all(array, ('sub', 'tensor'), split_axis=0, concat_axis=0, til...  10.4 us
    pallas_call x1, Pallas kernels, on_device(): flow(local_kernel, [(struct((tokens, WIDTH)), many['token'](WIDTH)), (str...  7.03 us
    ppermute x2, starting transfers between devices, shifted(): return lax.ppermute(array, 'slab', pairs)  6.61 us
    pallas_call x1, Pallas kernels, on_device(): flow(within_kernel, [(hbm((tokens, WIDTH)), up['token'](WIDTH)), (hbm((ch...  6.01 us
    pallas_call x1, Pallas kernels, on_device(): flow(last_kernel, [(hbm((peers, last_rows, LANES), bf16), anywhere)], 4 *...  5.5 us
  transfers between devices with their start and end apart: 7, of which 6 were waited for; matrix products, arithmetic and copies ran while one was open for 3% of the time, Pallas kernels for 18%

profile of v14, /device:TPU:0, one launch (start us, length us, event | category | flops | bytes accessed | tf_op | source)
XLA Modules:
  0.0 130.1 jit_solution(3685008349621566314)
XLA Ops:
  0.7 2.5 %shard_map.169 = bf16[8,2,336,128]{3,2,1,0:T(8,128)(2,1)} custom-call(bf16[64,8192]{1,0:T(8,128)(2,1)} %x_ref.1, bf16[64,1024]{1,0:T(8,128)(2,1)} %b_ref.1, bf16[64,1024]{1,0:T(8,128)(2,1)} %c_ref.1, bf16[64,128]{1,0:T(8,128)(2,1)} %steps_ref.1), custom_call_target="tpu_custom_call" | custom-call | bytes 2752512 | tf_op jit(solution)/shard_map/pallas_call | solution.py:721
  3.2 6.3 %all-to-all-start = ((bf16[16,336,128]{2,1,0:T(8,128)(2,1)}), bf16[16,336,128]{2,1,0:T(8,128)(2,1)S(1)}, u32[]{:S(2)}, u32[]{:S(2)}) async-start(bf16[16,336,128]{2,1,0:T(8,128)(2,1)} %bitcast.11), calls=%async_computation | async-start | bytes 2752512 | tf_op jit(solution)/shard_map/all_to_all | solution.py:699
  9.9 0.8 dynamic_slice.15
  10.8 2.7 %shard_map.170 = bf16[8,2,512,128]{3,2,1,0:T(8,128)(2,1)} custom-call(bf16[64,8192]{1,0:T(8,128)(2,1)} %z_ref, bf16[64,8192]{1,0:T(8,128)(2,1)} %grad_ref.1), custom_call_target="tpu_custom_call" | custom-call | bytes 4194304 | tf_op jit(solution)/shard_map/pallas_call | solution.py:721
  13.5 14.7 %all-to-all-done.refs_0_.refs_2_ = bf16[16,336,128]{2,1,0:T(8,128)(2,1)S(1)} async-done(((bf16[16,336,128]{2,1,0:T(8,128)(2,1)}), bf16[16,336,128]{2,1,0:T(8,128)(2,1)S(1)}, u32[]{:S(2)}, u32[]{:S(2)}) %all-to-all-start) | async-done | bytes 1376288 | tf_op jit(solution)/shard_map/all_to_all | solution.py:699
  28.2 4.1 %all-to-all-start.1 = ((bf16[16,512,128]{2,1,0:T(8,128)(2,1)}), bf16[16,512,128]{2,1,0:T(8,128)(2,1)S(1)}, u32[]{:S(2)}, u32[]{:S(2)}) async-start(bf16[16,512,128]{2,1,0:T(8,128)(2,1)} %bitcast.10), calls=%async_computation.1 | async-start | bytes 4194304 | tf_op jit(solution)/shard_map/all_to_all | solution.py:699
  32.3 0.7 slice.4
  33.5 1.5 %collective-permute-done = bf16[16,64,128]{2,1,0:T(8,128)(2,1)} collective-permute-done((bf16[16,64,128]{2,1,0:T(8,128)(2,1)}, bf16[16,64,128]{2,1,0:T(8,128)(2,1)}, u32[]{:S(2)}, u32[]{:S(2)}) %collective-permute-start) | collective-permute-done | bytes 262176 | tf_op jit(solution)/shard_map/ppermute | solution.py:735
  35.0 1.8 %broadcast_select_fusion = (bf16[16,64,128]{2,1,0:T(8,128)(2,1)}, bf16[16,64,128]{2,1,0:T(8,128)(2,1)}) fusion(bf16[16,64,128]{2,1,0:T(8,128)(2,1)} %collective-permute-done, pred[]{:T(512)S(6)} %eq.12, bf16[16,336,128]{2,1,0:T(8,128)(2,1)S(1)} %all-to-all-done.refs_0_.refs_2_), kind=kLoop, calls=%fused_computation | loop fusion | flops 262144 | bytes 1048577 | tf_op jit(solution)/shard_map/jit(_where)/select_n | solution.py:737
  36.8 5.2 %shard_map.171 = (f32[1024,128]{1,0:T(8,128)}, f32[64,1024]{1,0:T(8,128)}, f32[8,128,512]{2,1,0:T(8,128)}, f32[8,8,512]{2,1,0:T(8,128)}, bf16[128,512]{1,0:T(8,128)(2,1)S(1)}, /*index=5*/f32[8,512]{1,0:T(8,128)}) custom-call(bf16[16,336,128]{2,1,0:T(8,128)(2,1)S(1)} %all-to-all-done.refs_0_.refs_2_, bf16[16,64,128]{2,1,0:T(8,128)(2,1)} %get-tuple-element.78.refs_1_, ...), custom_call_target="tpu_custom_call" | custom-call | flops 268435456 | bytes 4194304 | tf_op jit(solution)/shard_map/pallas_call | solution.py:781
  42.0 5.1 %collective-permute-start.1 = (bf16[128,512]{1,0:T(8,128)(2,1)S(1)}, bf16[128,512]{1,0:T(8,128)(2,1)}, u32[]{:S(2)}, u32[]{:S(2)}) collective-permute-start(bf16[128,512]{1,0:T(8,128)(2,1)S(1)} %get-tuple-element.50), channel_id=1, source_target_pairs={{0,16},{1,17},{2,18},{3,19},{4,20},{5,21},{6,22},{7,23},{8,24},{9,... | collective-permute-start | bytes 393224 | tf_op jit(solution)/shard_map/ppermute | solution.py:641
  47.1 6.0 %shard_map.172 = (f32[1024,512]{1,0:T(8,128)}, f32[8,128,512]{2,1,0:T(8,128)}, f32[8,8,512]{2,1,0:T(8,128)}) custom-call(bf16[16,336,128]{2,1,0:T(8,128)(2,1)S(1)} %all-to-all-done.refs_0_.refs_2_, bf16[16,64,128]{2,1,0:T(8,128)(2,1)} %get-tuple-element.78.refs_1_, bf16[16,64,128]{2,1,0:T(8,128)(2,1)} %get-tuple-element.77.refs_2_.refs_1_, ...), custom_call_target="tpu_custom_call" | custom-call | flops 805306368 | bytes 8388608 | tf_op jit(solution)/shard_map/pallas_call | solution.py:805
  53.2 8.0 %collective-permute-done.1.refs_5_.refs_10_ = bf16[128,512]{1,0:T(8,128)(2,1)} collective-permute-done((bf16[128,512]{1,0:T(8,128)(2,1)S(1)}, bf16[128,512]{1,0:T(8,128)(2,1)}, u32[]{:S(2)}, u32[]{:S(2)}) %collective-permute-start.1) | collective-permute-done | bytes 131104 | tf_op jit(solution)/shard_map/ppermute | solution.py:641
  61.1 4.9 %shard_map.173 = (f32[1024,512]{1,0:T(8,128)S(1)}, f32[8,8,128]{2,1,0:T(8,128)S(1)}) custom-call(bf16[16,336,128]{2,1,0:T(8,128)(2,1)S(1)} %all-to-all-done.refs_0_.refs_2_, bf16[16,64,128]{2,1,0:T(8,128)(2,1)} %get-tuple-element.77.refs_2_.refs_1_, bf16[16,512,128]{2,1,0:T(8,128)(2,1)S(1)} %all-to-all-done.1.refs_2_.refs_3_, ...), custom_call_target="tpu_custom_call" | custom-call | flops 134217728 | bytes 8388608 | tf_op jit(solution)/shard_map/pallas_call | solution.py:824
  66.1 1.2 collective-permute-done.2.refs_7_.refs_12_
  67.3 2.8 %shard_map.174 = (bf16[1024,512]{1,0:T(8,128)(2,1)S(1)}, f32[8,128,512]{2,1,0:T(8,128)S(1)}, bf16[128,512]{1,0:T(8,128)(2,1)S(1)}) custom-call(bf16[16,336,128]{2,1,0:T(8,128)(2,1)S(1)} %all-to-all-done.refs_0_.refs_2_, bf16[16,64,128]{2,1,0:T(8,128)(2,1)S(1)} %copy-done.2, bf16[16,512,128]{2,1,0:T(8,128)(2,1)S(1)} %all-to-all-done.1.refs_2_.refs_3_, ...), custom_call_target="tpu_custom_call" | custom-call | flops 268435456 | bytes 6291456 | tf_op jit(solution)/shard_map/pallas_call | solution.py:844
  70.1 1.5 %collective-permute-start.3 = (bf16[128,512]{1,0:T(8,128)(2,1)S(1)}, bf16[128,512]{1,0:T(8,128)(2,1)S(1)}, u32[]{:S(2)}, u32[]{:S(2)}) collective-permute-start(bf16[128,512]{1,0:T(8,128)(2,1)S(1)} %get-tuple-element.63), channel_id=1, source_target_pairs={{16,0},{17,1},{18,2},{19,3},{20,4},{21,5},{22,6},{23,7},{24,8},{25... | collective-permute-start | bytes 393224 | tf_op jit(solution)/shard_map/ppermute | solution.py:641
  71.6 7.0 %shard_map.175 = (f32[1024,512]{1,0:T(8,128)S(1)}, f32[1024,128]{1,0:T(8,128)S(1)}, bf16[16,64,128]{2,1,0:T(8,128)(2,1)S(1)}, bf16[16,256,128]{2,1,0:T(8,128)(2,...) custom-call(bf16[16,336,128]{2,1,0:T(8,128)(2,1)S(1)} %all-to-all-done.refs_0_.refs_2_, ...), custom_call_target="tpu_custom_call" | custom-call | flops 1342177280 | bytes 8388608 | tf_op jit(solution)/shard_map/pallas_call | solution.py:863
  78.6 2.8 %collective-permute-done.3.refs_10_ = bf16[128,512]{1,0:T(8,128)(2,1)S(1)} collective-permute-done((bf16[128,512]{1,0:T(8,128)(2,1)S(1)}, bf16[128,512]{1,0:T(8,128)(2,1)S(1)}, u32[]{:S(2)}, u32[]{:S(2)}) %collective-permute-start.3) | collective-permute-done | bytes 131104 | tf_op jit(solution)/shard_map/ppermute | solution.py:641
  81.5 5.5 %shard_map.176 = bf16[16,656,128]{2,1,0:T(8,128)(2,1)} custom-call(bf16[16,336,128]{2,1,0:T(8,128)(2,1)S(1)} %all-to-all-done.refs_0_.refs_2_, bf16[16,64,128]{2,1,0:T(8,128)(2,1)S(1)} %copy-done.1, f32[1024,512]{1,0:T(8,128)S(1)} %get-tuple-element.58.refs_2_, f32[1024,128]{1,0:T(8,128)S(1)} %get-tuple-element.59.refs_3_, ...), custom_call_target="tpu_custom_call" | custom-call | flops 536870912 | bytes 8388608 | tf_op jit(solution)/shard_map/pallas_call | solution.py:889
  87.0 37.5 %all_to_all.15.refs_0_ = bf16[16,656,128]{2,1,0:T(8,128)(2,1)S(1)} all-to-all(bf16[16,656,128]{2,1,0:T(8,128)(2,1)} %shard_map.176), channel_id=1, replica_groups=mesh['slab'=2,'sub'=8,'tensor'=2] {'sub','tensor'}, dimensions={0} | all-to-all | bytes 5373952 | tf_op jit(solution)/shard_map/all_to_all | solution.py:699
  124.6 2.2 %collective-permute-start.4 = (f32[40,128]{1,0:T(8,128)S(1)}, f32[40,128]{1,0:T(8,128)S(1)}, u32[]{:S(2)}, u32[]{:S(2)}) collective-permute-start(f32[40,128]{1,0:T(8,128)S(1)} %shard_map.178.own_ref), channel_id=1, source_target_pairs={{0,16},{16,0},{1,17},{17,1},{2,18},{18,2},{3,19},{19,3},{4,20},{20... | collective-permute-start | bytes 61448 | tf_op jit(solution)/shard_map/ppermute | solution.py:672
  126.7 1.9 %shard_map.177 = (bf16[64,8192]{1,0:T(8,128)(2,1)}, bf16[64,8192]{1,0:T(8,128)(2,1)}, bf16[64,1024]{1,0:T(8,128)(2,1)}, bf16[64,1024]{1,0:T(8,128)(2,1)}, bf16[64,128]{1,0:T(8,128)(2,1)}) custom-call(bf16[16,656,128]{2,1,0:T(8,128)(2,1)S(1)} %all_to_all.15.refs_0_), custom_call_target="tpu_custom_call" | custom-call | bytes 5242880 | tf_op jit(solution)/shard_map/pallas_call | solution.py:925
  128.6 0.9 collective-permute-done.4.other_ref
  (32 shorter events, 1.8 us)
Async XLA Ops:
  0.6 8.8 %copy-start.6 = (f32[64]{0:T(128)S(1)}, f32[64]{0:T(128)}, u32[]{:S(2)}) copy-start(f32[64]{0:T(128)} %param.15) | copy-start | bytes 772
  0.7 8.9 %copy-start.7 = (f32[64]{0:T(128)S(1)}, f32[64]{0:T(128)}, u32[]{:S(2)}) copy-start(f32[64]{0:T(128)} %param.16) | copy-start | bytes 772
  0.7 9.0 %copy-start.8 = (f32[64]{0:T(128)S(1)}, f32[64]{0:T(128)}, u32[]{:S(2)}) copy-start(f32[64]{0:T(128)} %param.17) | copy-start | bytes 772
  3.2 25.1 %all-to-all-start = ((bf16[16,336,128]{2,1,0:T(8,128)(2,1)}), bf16[16,336,128]{2,1,0:T(8,128)(2,1)S(1)}, u32[]{:S(2)}, u32[]{:S(2)}) async-start(bf16[16,336,128]{2,1,0:T(8,128)(2,1)} %bitcast.11), calls=%async_computation | async-start | bytes 2752512 | tf_op jit(solution)/shard_map/all_to_all | solution.py:699
  28.2 32.9 %all-to-all-start.1 = ((bf16[16,512,128]{2,1,0:T(8,128)(2,1)}), bf16[16,512,128]{2,1,0:T(8,128)(2,1)S(1)}, u32[]{:S(2)}, u32[]{:S(2)}) async-start(bf16[16,512,128]{2,1,0:T(8,128)(2,1)} %bitcast.10), calls=%async_computation.1 | async-start | bytes 4194304 | tf_op jit(solution)/shard_map/all_to_all | solution.py:699
  33.1 1.9 %collective-permute-start = (bf16[16,64,128]{2,1,0:T(8,128)(2,1)}, bf16[16,64,128]{2,1,0:T(8,128)(2,1)}, u32[]{:S(2)}, u32[]{:S(2)}) collective-permute-start(bf16[16,64,128]{2,1,0:T(8,128)(2,1)} %slice.4), channel_id=1, source_target_pairs={{0,2},{2,0},{4,6},{6,4},{8,10},{10,8},{12,14},{14,12},{1,3},{3,1},... | collective-permute-start | bytes 786440 | tf_op jit(solution)/shard_map/ppermute | solution.py:735
  42.0 19.1 %collective-permute-start.1 = (bf16[128,512]{1,0:T(8,128)(2,1)S(1)}, bf16[128,512]{1,0:T(8,128)(2,1)}, u32[]{:S(2)}, u32[]{:S(2)}) collective-permute-start(bf16[128,512]{1,0:T(8,128)(2,1)S(1)} %get-tuple-element.50), channel_id=1, source_target_pairs={{0,16},{1,17},{2,18},{3,19},{4,20},{5,21},{6,22},{7,23},{8,24},{9,... | collective-permute-start | bytes 393224 | tf_op jit(solution)/shard_map/ppermute | solution.py:641
  61.1 6.2 %copy-start = (f32[1024,128]{1,0:T(8,128)S(1)}, f32[1024,128]{1,0:T(8,128)}, u32[]{:S(2)}) copy-start(f32[1024,128]{1,0:T(8,128)} %get-tuple-element.45.refs_3_.refs_4_.refs_6_.refs_8_) | copy-start | bytes 1572868
  61.1 6.2 %copy-start.2 = (bf16[16,64,128]{2,1,0:T(8,128)(2,1)S(1)}, bf16[16,64,128]{2,1,0:T(8,128)(2,1)}, u32[]{:S(2)}) copy-start(bf16[16,64,128]{2,1,0:T(8,128)(2,1)} %get-tuple-element.77.refs_2_.refs_1_) | copy-start | bytes 786436
  61.1 6.2 %copy-start.4 = (f32[8,8,512]{2,1,0:T(8,128)S(1)}, f32[8,8,512]{2,1,0:T(8,128)}, u32[]{:S(2)}) copy-start(f32[8,8,512]{2,1,0:T(8,128)} %get-tuple-element.51.refs_6_.refs_5_.refs_9_) | copy-start | bytes 393220
  66.0 1.3 collective-permute-start.2
  67.3 4.3 %copy-start.1 = (bf16[16,64,128]{2,1,0:T(8,128)(2,1)S(1)}, bf16[16,64,128]{2,1,0:T(8,128)(2,1)}, u32[]{:S(2)}) copy-start(bf16[16,64,128]{2,1,0:T(8,128)(2,1)} %get-tuple-element.78.refs_1_) | copy-start | bytes 786436
  67.3 4.3 %copy-start.3 = (f32[64,1024]{1,0:T(8,128)S(1)}, f32[64,1024]{1,0:T(8,128)}, u32[]{:S(2)}) copy-start(f32[64,1024]{1,0:T(8,128)} %get-tuple-element.46.refs_4_.refs_7_.refs_9_) | copy-start | bytes 786436
  70.1 11.4 %collective-permute-start.3 = (bf16[128,512]{1,0:T(8,128)(2,1)S(1)}, bf16[128,512]{1,0:T(8,128)(2,1)S(1)}, u32[]{:S(2)}, u32[]{:S(2)}) collective-permute-start(bf16[128,512]{1,0:T(8,128)(2,1)S(1)} %get-tuple-element.63), channel_id=1, source_target_pairs={{16,0},{17,1},{18,2},{19,3},{20,4},{21,5},{22,6},{23,7},{24,8},{25... | collective-permute-start | bytes 393224 | tf_op jit(solution)/shard_map/ppermute | solution.py:641
  71.6 9.9 %copy-start.5 = (f32[8,8,512]{2,1,0:T(8,128)S(1)}, f32[8,8,512]{2,1,0:T(8,128)}, u32[]{:S(2)}) copy-start(f32[8,8,512]{2,1,0:T(8,128)} %get-tuple-element.48.refs_6_.refs_13_) | copy-start | bytes 393220
  124.6 5.0 %collective-permute-start.4 = (f32[40,128]{1,0:T(8,128)S(1)}, f32[40,128]{1,0:T(8,128)S(1)}, u32[]{:S(2)}, u32[]{:S(2)}) collective-permute-start(f32[40,128]{1,0:T(8,128)S(1)} %shard_map.178.own_ref), channel_id=1, source_target_pairs={{0,16},{16,0},{1,17},{17,1},{2,18},{18,2},{3,19},{19,3},{4,20},{20... | collective-permute-start | bytes 61448 | tf_op jit(solution)/shard_map/ppermute | solution.py:672

commit v15 on v13

--- a/solution.py
+++ b/solution.py
@@ -326,8 +326,9 @@
 def mix_kernel(
     message, per_step,
     first_ref, readers_ref, second_ref, within_ref, ecum_ref, inbound_ref, pre_ref, gain_ref, skip_ref,
-    y_ref, sums_ref,
+    y_ref, sums_ref, second_out,
 ):
+    second_out[...] = second_ref[...]
     inbound = inbound_ref[...].astype(bf16)
     fill = jnp.zeros((LANES - HEADS, CHUNK), f32)
     for i in range(per_step):
@@ -770,6 +771,7 @@
 
     up = specs_of(2)
     many = specs_of(4)
+    all_at_once = specs_of(8)
     dn = specs_of(8, down=True)
 
     def whole(*shape):
@@ -795,7 +797,7 @@
             whole(2 * HEADS, LANES),
         ],
         [pltpu.VMEM((STATE, WIDTH), f32), pltpu.VMEM((chunks, KINDS * HEADS, LANES), f32)],
-    )(first, in_hbm(sources), first, heads)
+    )(first, sources, first, heads)
 
     before = after = None
     if slab_count > 2:
@@ -816,16 +818,17 @@
             up["chunk"](STATE, WIDTH), up["chunk"](8, WIDTH),
         ],
         [pltpu.VMEM((STATE, WIDTH), f32), pltpu.VMEM((8, WIDTH), f32)],
-    )(first, in_hbm(sources), in_hbm(readers), in_hbm(sm), in_hbm(smt), in_hbm(own), in_hbm(dec))
+    )(first, sources, readers, in_hbm(sm), in_hbm(smt), in_hbm(own), in_hbm(dec))
 
     anywhere = pl.BlockSpec(memory_space=pl.ANY)
     per_mix = min(2, chunks)
     ecum_block = pl.BlockSpec((HEADS, per_mix * CHUNK), lambda c: (ECUM, c))
-    y, sums = flow(
+    y, sums, second = flow(
         mix_kernel,
         [
             (struct((tokens, WIDTH)), up["token"](WIDTH)),
             (struct((chunks, 8, LANES)), up["chunk"](8, LANES)),
+            (struct((peers, second_rows, LANES), bf16), up["message"](second_rows)),
         ],
         unit, size * 16,
         [
@@ -835,7 +838,7 @@
         ],
         per=per_mix,
     )(
-        first, in_hbm(readers), second, in_hbm(within), in_hbm(smt), inbound, in_hbm(pre),
+        first, readers, in_hbm(second), in_hbm(within), in_hbm(smt), inbound, in_hbm(pre),
         own_gain, skip_row,
     )
 
@@ -844,18 +847,18 @@
     d_mixed, back, slab_back = flow(
         norm_kernel,
         [
-            (struct((tokens, WIDTH), bf16), many["token"](WIDTH)),
-            (struct((chunks, STATE, WIDTH)), many["chunk"](STATE, WIDTH)),
+            (struct((tokens, WIDTH), bf16), all_at_once["token"](WIDTH)),
+            (struct((chunks, STATE, WIDTH)), all_at_once["chunk"](STATE, WIDTH)),
             (struct((STATE, WIDTH), bf16), whole(STATE, WIDTH)),
         ],
         2 * unit, size * 12,
         [
-            many["message"](PAIRS * rows), many["message"](rows), many["message"](second_rows),
-            many["token"](WIDTH), many["token"](LANES), many["chunk"](8, WIDTH), many["chunk"](8, LANES),
-            many["chunk"](8, LANES), whole(1, WIDTH), whole(1, WIDTH),
+            all_at_once["message"](PAIRS * rows), all_at_once["message"](rows), all_at_once["message"](second_rows),
+            all_at_once["token"](WIDTH), all_at_once["token"](LANES), all_at_once["chunk"](8, WIDTH), all_at_once["chunk"](8, LANES),
+            all_at_once["chunk"](8, LANES), whole(1, WIDTH), whole(1, WIDTH),
         ],
         [pltpu.VMEM((STATE, WIDTH), f32)],
-        per=4,
+        per=8,
     )(first, readers, second, y, sm, pre, sums, partner, own_gain, skip_row)
 
     outer = carry_over(slab_back, decay, after, slab_count, -1)

time: 132 us -> 131 us (level)
  waiting for transfers between devices: 32.7 us -> 36 us
  local copies, waits for them, and re-layouts: 3.6 us -> 1.32 us
  other arithmetic: 1.87 us -> 0.12 us
    ppermute x2, waiting for transfers between devices: 12.6 us -> 16.1 us  [shifted(): return lax.ppermute(array, 'slab', pairs)]
    select_n x1, other arithmetic: 1.8 us -> 0.05 us  [on_device(): jnp.where(even, other_half, half)]
    unnamed x26 -> x16, local copies, waits for them, and re-layouts: 1.6 us -> 0.03 us
  transfers between devices with their start and end apart: 7 -> 7, of which waited for: 6 -> 6; matrix products, arithmetic and copies ran while one was open for 3% -> 1% of each run, Pallas kernels for 17% -> 16%
where the time goes in v15:
time: 131 us; the launch traced here: 130 us
  blocking collectives  37.5 us (29%)
  Pallas kernels  37.3 us (28%)
  waiting for transfers between devices  36 us (27%)
  starting transfers between devices  17.4 us (13%)
  local copies, waits for them, and re-layouts  1.32 us (1%)
    all_to_all x1, blocking collectives, exchange(): lax.all_to_all(array, ('sub', 'tensor'), split_axis=0, concat_axis=0, til...  37.5 us
    ppermute x2, waiting for transfers between devices, shifted(): return lax.ppermute(array, 'slab', pairs)  16.1 us
    all_to_all x2, waiting for transfers between devices, exchange(): lax.all_to_all(array, ('sub', 'tensor'), split_axis=0, concat_axis=0, til...  14.7 us
    all_to_all x2, starting transfers between devices, exchange(): lax.all_to_all(array, ('sub', 'tensor'), split_axis=0, concat_axis=0, til...  10.7 us
    ppermute x2, starting transfers between devices, shifted(): return lax.ppermute(array, 'slab', pairs)  5.96 us
    pallas_call x1, Pallas kernels, on_device(): flow(local_kernel, [(struct((tokens, WIDTH)), many['token'](WIDTH)), (str...  5.9 us
    pallas_call x1, Pallas kernels, on_device(): flow(within_kernel, [(hbm((tokens, WIDTH)), up['token'](WIDTH)), (hbm((ch...  5.88 us
    pallas_call x1, Pallas kernels, on_device(): flow(last_kernel, [(hbm((peers, last_rows, LANES), bf16), anywhere)], 4 *...  5.51 us
  transfers between devices with their start and end apart: 7, of which 6 were waited for; matrix products, arithmetic and copies ran while one was open for 1% of the time, Pallas kernels for 16%

profile of v15, /device:TPU:0, one launch (start us, length us, event | category | flops | bytes accessed | tf_op | source)
XLA Modules:
  0.0 130.4 jit_solution(8557772634340002161)
XLA Ops:
  0.7 2.4 %shard_map.169 = bf16[8,2,336,128]{3,2,1,0:T(8,128)(2,1)} custom-call(bf16[64,8192]{1,0:T(8,128)(2,1)} %x_ref.1, bf16[64,1024]{1,0:T(8,128)(2,1)} %b_ref.1, bf16[64,1024]{1,0:T(8,128)(2,1)} %c_ref.1, bf16[64,128]{1,0:T(8,128)(2,1)} %steps_ref.1), custom_call_target="tpu_custom_call" | custom-call | bytes 2752512 | tf_op jit(solution)/shard_map/pallas_call | solution.py:722
  3.1 6.3 %all-to-all-start = ((bf16[16,336,128]{2,1,0:T(8,128)(2,1)}), bf16[16,336,128]{2,1,0:T(8,128)(2,1)S(1)}, u32[]{:S(2)}, u32[]{:S(2)}) async-start(bf16[16,336,128]{2,1,0:T(8,128)(2,1)} %bitcast.11), calls=%async_computation | async-start | bytes 2752512 | tf_op jit(solution)/shard_map/all_to_all | solution.py:700
  9.8 0.8 dynamic_slice.15
  10.8 2.7 %shard_map.170 = bf16[8,2,512,128]{3,2,1,0:T(8,128)(2,1)} custom-call(bf16[64,8192]{1,0:T(8,128)(2,1)} %z_ref, bf16[64,8192]{1,0:T(8,128)(2,1)} %grad_ref.1), custom_call_target="tpu_custom_call" | custom-call | bytes 4194304 | tf_op jit(solution)/shard_map/pallas_call | solution.py:722
  13.5 14.7 %all-to-all-done.refs_0_.refs_2_ = bf16[16,336,128]{2,1,0:T(8,128)(2,1)S(1)} async-done(((bf16[16,336,128]{2,1,0:T(8,128)(2,1)}), bf16[16,336,128]{2,1,0:T(8,128)(2,1)S(1)}, u32[]{:S(2)}, u32[]{:S(2)}) %all-to-all-start) | async-done | bytes 1376288 | tf_op jit(solution)/shard_map/all_to_all | solution.py:700
  28.1 4.5 %all-to-all-start.1 = ((bf16[16,512,128]{2,1,0:T(8,128)(2,1)}), bf16[16,512,128]{2,1,0:T(8,128)(2,1)}, u32[]{:S(2)}, u32[]{:S(2)}) async-start(bf16[16,512,128]{2,1,0:T(8,128)(2,1)} %bitcast.10), calls=%async_computation.1 | async-start | bytes 4194304 | tf_op jit(solution)/shard_map/all_to_all | solution.py:700
  32.6 0.3 collective-permute-start
  32.9 1.3 collective-permute-done
  34.3 4.4 %shard_map.171 = (f32[1024,128]{1,0:T(8,128)}, f32[64,1024]{1,0:T(8,128)}, f32[8,128,512]{2,1,0:T(8,128)}, f32[8,8,512]{2,1,0:T(8,128)}, bf16[128,512]{1,0:T(8,128)(2,1)S(1)}, /*index=5*/f32[8,512]{1,0:T(8,128)}) custom-call(bf16[16,336,128]{2,1,0:T(8,128)(2,1)S(1)} %all-to-all-done.refs_0_.refs_2_, bf16[16,64,128]{2,1,0:T(8,128)(2,1)S(1)} %get-tuple-element.80.refs_1_, ...), custom_call_target="tpu_custom_call" | custom-call | flops 268435456 | bytes 4194304 | tf_op jit(solution)/shard_map/pallas_call | solution.py:783
  38.7 4.5 %collective-permute-start.1 = (bf16[128,512]{1,0:T(8,128)(2,1)S(1)}, bf16[128,512]{1,0:T(8,128)(2,1)S(1)}, u32[]{:S(2)}, u32[]{:S(2)}) collective-permute-start(bf16[128,512]{1,0:T(8,128)(2,1)S(1)} %get-tuple-element.51), channel_id=1, source_target_pairs={{0,16},{1,17},{2,18},{3,19},{4,20},{5,21},{6,22},{7,23},{8,24},{9,... | collective-permute-start | bytes 393224 | tf_op jit(solution)/shard_map/ppermute | solution.py:642
  43.2 5.9 %shard_map.172 = (f32[1024,512]{1,0:T(8,128)}, f32[8,128,512]{2,1,0:T(8,128)}, f32[8,8,512]{2,1,0:T(8,128)}) custom-call(bf16[16,336,128]{2,1,0:T(8,128)(2,1)S(1)} %all-to-all-done.refs_0_.refs_2_, bf16[16,64,128]{2,1,0:T(8,128)(2,1)S(1)} %get-tuple-element.80.refs_1_, bf16[16,64,128]{2,1,0:T(8,128)(2,1)S(1)} %get-tuple-element.79.refs_2_.refs_1_, ...), custom_call_target="tpu_custom_call" | custom-call | flops 805306368 | bytes 8388608 | tf_op jit(solution)/shard_map/pallas_call | solution.py:807
  49.0 12.2 %collective-permute-done.1.refs_5_.refs_10_ = bf16[128,512]{1,0:T(8,128)(2,1)S(1)} collective-permute-done((bf16[128,512]{1,0:T(8,128)(2,1)S(1)}, bf16[128,512]{1,0:T(8,128)(2,1)S(1)}, u32[]{:S(2)}, u32[]{:S(2)}) %collective-permute-start.1) | collective-permute-done | bytes 131104 | tf_op jit(solution)/shard_map/ppermute | solution.py:642
  61.3 5.2 %shard_map.173 = (f32[1024,512]{1,0:T(8,128)S(1)}, f32[8,8,128]{2,1,0:T(8,128)S(1)}, bf16[16,512,128]{2,1,0:T(8,128)(2,1)S(1)}) custom-call(bf16[16,336,128]{2,1,0:T(8,128)(2,1)S(1)} %all-to-all-done.refs_0_.refs_2_, bf16[16,64,128]{2,1,0:T(8,128)(2,1)S(1)} %get-tuple-element.79.refs_2_.refs_1_, bf16[16,512,128]{2,1,0:T(8,128)(2,1)} %all-to-all-done.1.refs_2_, ...), custom_call_target="tpu_custom_call" | custom-call | flops 134217728 | bytes 8388608 | tf_op jit(solution)/shard_map/pallas_call | solution.py:826
  66.6 1.2 collective-permute-done.2.refs_7_.refs_12_
  67.8 2.6 %shard_map.174 = (bf16[1024,512]{1,0:T(8,128)(2,1)S(1)}, f32[8,128,512]{2,1,0:T(8,128)S(1)}, bf16[128,512]{1,0:T(8,128)(2,1)S(1)}) custom-call(bf16[16,336,128]{2,1,0:T(8,128)(2,1)S(1)} %all-to-all-done.refs_0_.refs_2_, bf16[16,64,128]{2,1,0:T(8,128)(2,1)S(1)} %get-tuple-element.79.refs_2_.refs_1_, ...), custom_call_target="tpu_custom_call" | custom-call | flops 268435456 | bytes 6291456 | tf_op jit(solution)/shard_map/pallas_call | solution.py:847
  70.4 1.5 %collective-permute-start.3 = (bf16[128,512]{1,0:T(8,128)(2,1)S(1)}, bf16[128,512]{1,0:T(8,128)(2,1)S(1)}, u32[]{:S(2)}, u32[]{:S(2)}) collective-permute-start(bf16[128,512]{1,0:T(8,128)(2,1)S(1)} %get-tuple-element.65), channel_id=1, source_target_pairs={{16,0},{17,1},{18,2},{19,3},{20,4},{21,5},{22,6},{23,7},{24,8},{25... | collective-permute-start | bytes 393224 | tf_op jit(solution)/shard_map/ppermute | solution.py:642
  72.0 5.9 %shard_map.175 = (f32[1024,512]{1,0:T(8,128)S(1)}, f32[1024,128]{1,0:T(8,128)S(1)}, bf16[16,64,128]{2,1,0:T(8,128)(2,1)S(1)}, bf16[16,256,128]{2,1,0:T(8,128)(2,...) custom-call(bf16[16,336,128]{2,1,0:T(8,128)(2,1)S(1)} %all-to-all-done.refs_0_.refs_2_, ...), custom_call_target="tpu_custom_call" | custom-call | flops 1342177280 | bytes 8388608 | tf_op jit(solution)/shard_map/pallas_call | solution.py:866
  77.9 3.9 %collective-permute-done.3.refs_10_ = bf16[128,512]{1,0:T(8,128)(2,1)S(1)} collective-permute-done((bf16[128,512]{1,0:T(8,128)(2,1)S(1)}, bf16[128,512]{1,0:T(8,128)(2,1)S(1)}, u32[]{:S(2)}, u32[]{:S(2)}) %collective-permute-start.3) | collective-permute-done | bytes 131104 | tf_op jit(solution)/shard_map/ppermute | solution.py:642
  81.7 5.5 %shard_map.176 = bf16[16,656,128]{2,1,0:T(8,128)(2,1)} custom-call(bf16[16,336,128]{2,1,0:T(8,128)(2,1)S(1)} %all-to-all-done.refs_0_.refs_2_, bf16[16,64,128]{2,1,0:T(8,128)(2,1)S(1)} %get-tuple-element.80.refs_1_, f32[1024,512]{1,0:T(8,128)S(1)} %get-tuple-element.60.refs_2_, f32[1024,128]{1,0:T(8,128)S(1)} %get-tuple-element.61.refs_3_, ...), custom_call_target="tpu_custom_call" | custom-call | flops 536870912 | bytes 8388608 | tf_op jit(solution)/shard_map/pallas_call | solution.py:892
  87.3 37.5 %all_to_all.15.refs_0_ = bf16[16,656,128]{2,1,0:T(8,128)(2,1)S(1)} all-to-all(bf16[16,656,128]{2,1,0:T(8,128)(2,1)} %shard_map.176), channel_id=1, replica_groups=mesh['slab'=2,'sub'=8,'tensor'=2] {'sub','tensor'}, dimensions={0} | all-to-all | bytes 5373952 | tf_op jit(solution)/shard_map/all_to_all | solution.py:700
  124.8 0.4 collective-permute-start.4
  125.2 1.9 %shard_map.177 = (bf16[64,8192]{1,0:T(8,128)(2,1)}, bf16[64,8192]{1,0:T(8,128)(2,1)}, bf16[64,1024]{1,0:T(8,128)(2,1)}, bf16[64,1024]{1,0:T(8,128)(2,1)}, bf16[64,128]{1,0:T(8,128)(2,1)}) custom-call(bf16[16,656,128]{2,1,0:T(8,128)(2,1)S(1)} %all_to_all.15.refs_0_), custom_call_target="tpu_custom_call" | custom-call | bytes 5242880 | tf_op jit(solution)/shard_map/pallas_call | solution.py:928
  127.1 2.7 %collective-permute-done.4.other_ref = f32[40,128]{1,0:T(8,128)S(1)} collective-permute-done((f32[40,128]{1,0:T(8,128)S(1)}, f32[40,128]{1,0:T(8,128)S(1)}, u32[]{:S(2)}, u32[]{:S(2)}) %collective-permute-start.4) | collective-permute-done | bytes 20512 | tf_op jit(solution)/shard_map/ppermute | solution.py:673
  129.8 0.6 shard_map.179
  (30 shorter events, 0.9 us)
Async XLA Ops:
  0.6 8.7 %copy-start.5 = (f32[64]{0:T(128)S(1)}, f32[64]{0:T(128)}, u32[]{:S(2)}) copy-start(f32[64]{0:T(128)} %param.15) | copy-start | bytes 772
  0.7 8.8 %copy-start.6 = (f32[64]{0:T(128)S(1)}, f32[64]{0:T(128)}, u32[]{:S(2)}) copy-start(f32[64]{0:T(128)} %param.16) | copy-start | bytes 772
  0.7 8.9 %copy-start.7 = (f32[64]{0:T(128)S(1)}, f32[64]{0:T(128)}, u32[]{:S(2)}) copy-start(f32[64]{0:T(128)} %param.17) | copy-start | bytes 772
  3.1 25.1 %all-to-all-start = ((bf16[16,336,128]{2,1,0:T(8,128)(2,1)}), bf16[16,336,128]{2,1,0:T(8,128)(2,1)S(1)}, u32[]{:S(2)}, u32[]{:S(2)}) async-start(bf16[16,336,128]{2,1,0:T(8,128)(2,1)} %bitcast.11), calls=%async_computation | async-start | bytes 2752512 | tf_op jit(solution)/shard_map/all_to_all | solution.py:700
  28.1 33.1 %all-to-all-start.1 = ((bf16[16,512,128]{2,1,0:T(8,128)(2,1)}), bf16[16,512,128]{2,1,0:T(8,128)(2,1)}, u32[]{:S(2)}, u32[]{:S(2)}) async-start(bf16[16,512,128]{2,1,0:T(8,128)(2,1)} %bitcast.10), calls=%async_computation.1 | async-start | bytes 4194304 | tf_op jit(solution)/shard_map/all_to_all | solution.py:700
  32.6 1.6 %collective-permute-start = (bf16[16,64,128]{2,1,0:T(8,128)(2,1)S(1)}, bf16[16,64,128]{2,1,0:T(8,128)(2,1)S(1)}, u32[]{:S(2)}, u32[]{:S(2)}) collective-permute-start(bf16[16,64,128]{2,1,0:T(8,128)(2,1)S(1)} %slice.4), channel_id=1, source_target_pairs={{0,2},{2,0},{4,6},{6,4},{8,10},{10,8},{12,14},{14,12},{1,3},{3,1},... | collective-permute-start | bytes 786440 | tf_op jit(solution)/shard_map/ppermute | solution.py:736
  38.7 22.6 %collective-permute-start.1 = (bf16[128,512]{1,0:T(8,128)(2,1)S(1)}, bf16[128,512]{1,0:T(8,128)(2,1)S(1)}, u32[]{:S(2)}, u32[]{:S(2)}) collective-permute-start(bf16[128,512]{1,0:T(8,128)(2,1)S(1)} %get-tuple-element.51), channel_id=1, source_target_pairs={{0,16},{1,17},{2,18},{3,19},{4,20},{5,21},{6,22},{7,23},{8,24},{9,... | collective-permute-start | bytes 393224 | tf_op jit(solution)/shard_map/ppermute | solution.py:642
  61.3 6.5 %copy-start = (f32[1024,128]{1,0:T(8,128)S(1)}, f32[1024,128]{1,0:T(8,128)}, u32[]{:S(2)}) copy-start(f32[1024,128]{1,0:T(8,128)} %get-tuple-element.46.refs_3_.refs_4_.refs_6_.refs_8_) | copy-start | bytes 1572868
  61.3 6.5 %copy-start.3 = (f32[8,8,512]{2,1,0:T(8,128)S(1)}, f32[8,8,512]{2,1,0:T(8,128)}, u32[]{:S(2)}) copy-start(f32[8,8,512]{2,1,0:T(8,128)} %get-tuple-element.52.refs_6_.refs_5_.refs_9_) | copy-start | bytes 393220
  66.5 1.3 collective-permute-start.2
  67.8 4.1 %copy-start.1 = (f32[64,1024]{1,0:T(8,128)S(1)}, f32[64,1024]{1,0:T(8,128)}, u32[]{:S(2)}) copy-start(f32[64,1024]{1,0:T(8,128)} %get-tuple-element.47.refs_4_.refs_7_.refs_9_) | copy-start | bytes 786436
  67.8 4.1 %copy-start.2 = (f32[8,128,512]{2,1,0:T(8,128)S(1)}, f32[8,128,512]{2,1,0:T(8,128)}, u32[]{:S(2)}) copy-start(f32[8,128,512]{2,1,0:T(8,128)} %get-tuple-element.59.refs_8_) | copy-start | bytes 6291460
  70.4 11.3 %collective-permute-start.3 = (bf16[128,512]{1,0:T(8,128)(2,1)S(1)}, bf16[128,512]{1,0:T(8,128)(2,1)S(1)}, u32[]{:S(2)}, u32[]{:S(2)}) collective-permute-start(bf16[128,512]{1,0:T(8,128)(2,1)S(1)} %get-tuple-element.65), channel_id=1, source_target_pairs={{16,0},{17,1},{18,2},{19,3},{20,4},{21,5},{22,6},{23,7},{24,8},{25... | collective-permute-start | bytes 393224 | tf_op jit(solution)/shard_map/ppermute | solution.py:642
  71.9 9.8 %copy-start.4 = (f32[8,8,512]{2,1,0:T(8,128)S(1)}, f32[8,8,512]{2,1,0:T(8,128)}, u32[]{:S(2)}) copy-start(f32[8,8,512]{2,1,0:T(8,128)} %get-tuple-element.49.refs_6_.refs_13_) | copy-start | bytes 393220
  124.8 5.0 %collective-permute-start.4 = (f32[40,128]{1,0:T(8,128)S(1)}, f32[40,128]{1,0:T(8,128)S(1)}, u32[]{:S(2)}, u32[]{:S(2)}) collective-permute-start(f32[40,128]{1,0:T(8,128)S(1)} %shard_map.178.own_ref), channel_id=1, source_target_pairs={{0,16},{16,0},{1,17},{17,1},{2,18},{18,2},{3,19},{19,3},{4,20},{20... | collective-permute-start | bytes 61448 | tf_op jit(solution)/shard_map/ppermute | solution.py:673

commit v16 on v15

--- a/solution.py
+++ b/solution.py
@@ -325,21 +325,21 @@
 
 def mix_kernel(
     message, per_step,
-    first_ref, readers_ref, second_ref, within_ref, ecum_ref, inbound_ref, pre_ref, gain_ref, skip_ref,
+    first_ref, readers_ref, second_ref, within_ref, sm_ref, inbound_ref, pre_ref, gain_ref, skip_ref,
     y_ref, sums_ref, second_out,
 ):
     second_out[...] = second_ref[...]
     inbound = inbound_ref[...].astype(bf16)
-    fill = jnp.zeros((LANES - HEADS, CHUNK), f32)
+    ones = jnp.ones((16, 2 * LANES), bf16)
     for i in range(per_step):
         rows = slice(i * CHUNK, (i + 1) * CHUNK)
-        ecum = jnp.concatenate([ecum_ref[:, lanes(i)], fill], axis=0).T
+        sm = sm_ref[rows, :]
         carried = mm(message.get(readers_ref, i, 0), inbound)
         power = jnp.zeros((CHUNK, LANES), f32)
         cross = jnp.zeros((CHUNK, LANES), f32)
         for j in range(PAIRS):
             at = lanes(j)
-            decay = spread_pair(ecum, 0, j) * pre_ref[i, 0:1, at]
+            decay = spread_pair(sm, ECUM, j) * pre_ref[i, 0:1, at]
             y = within_ref[rows, at] + decay * carried[:, at]
             y_ref[rows, at] = y
             values = message.get(first_ref, i, X + j).astype(f32)
@@ -348,8 +348,9 @@
             gated = (y + skip_ref[0:1, at] * values) * (gates * sigmoid(gates))
             power = power + gated * gated
             cross = cross + grad * gain_ref[0:1, at] * gated
-        sums_ref[i, 0:1, :] = jnp.sum(power.T, axis=0, keepdims=True)
-        sums_ref[i, 1:2, :] = jnp.sum(cross.T, axis=0, keepdims=True)
+        for k, tile in enumerate((power, cross)):
+            terms = jnp.concatenate(two_terms(tile), axis=1)
+            sums_ref[i, k : k + 1, :] = mm_nt(ones, terms)[0:1]
         sums_ref[i, 2:, :] = jnp.zeros((6, LANES), f32)
 
 
@@ -822,7 +823,6 @@
 
     anywhere = pl.BlockSpec(memory_space=pl.ANY)
     per_mix = min(2, chunks)
-    ecum_block = pl.BlockSpec((HEADS, per_mix * CHUNK), lambda c: (ECUM, c))
     y, sums, second = flow(
         mix_kernel,
         [
@@ -833,12 +833,12 @@
         unit, size * 16,
         [
             up["message"](PAIRS * rows), up["message"](rows), up["message"](second_rows),
-            up["token"](WIDTH), ecum_block, whole(STATE, WIDTH), up["chunk"](8, WIDTH),
+            up["token"](WIDTH), up["token"](LANES), whole(STATE, WIDTH), up["chunk"](8, WIDTH),
             whole(1, WIDTH), whole(1, WIDTH),
         ],
         per=per_mix,
     )(
-        first, readers, in_hbm(second), in_hbm(within), in_hbm(smt), inbound, in_hbm(pre),
+        first, readers, in_hbm(second), in_hbm(within), in_hbm(sm), inbound, in_hbm(pre),
         own_gain, skip_row,
     )
 

time: 131 us -> 130 us (level)
  no operation moved by 1% of the time
where the time goes in v16:
time: 130 us
  blocking collectives  37.5 us (29%)
  Pallas kernels  36.9 us (28%)
  waiting for transfers between devices  36 us (28%)
  starting transfers between devices  17.4 us (13%)
  local copies, waits for them, and re-layouts  1.32 us (1%)
    all_to_all x1, blocking collectives, exchange(): lax.all_to_all(array, ('sub', 'tensor'), split_axis=0, concat_axis=0, til...  37.5 us
    ppermute x2, waiting for transfers between devices, shifted(): return lax.ppermute(array, 'slab', pairs)  16.1 us
    all_to_all x2, waiting for transfers between devices, exchange(): lax.all_to_all(array, ('sub', 'tensor'), split_axis=0, concat_axis=0, til...  14.7 us
    all_to_all x2, starting transfers between devices, exchange(): lax.all_to_all(array, ('sub', 'tensor'), split_axis=0, concat_axis=0, til...  10.7 us
    ppermute x2, starting transfers between devices, shifted(): return lax.ppermute(array, 'slab', pairs)  5.96 us
    pallas_call x1, Pallas kernels, on_device(): flow(local_kernel, [(struct((tokens, WIDTH)), many['token'](WIDTH)), (str...  5.9 us
    pallas_call x1, Pallas kernels, on_device(): flow(within_kernel, [(hbm((tokens, WIDTH)), up['token'](WIDTH)), (hbm((ch...  5.88 us
    pallas_call x1, Pallas kernels, on_device(): flow(last_kernel, [(hbm((peers, last_rows, LANES), bf16), anywhere)], 4 *...  5.51 us
  transfers between devices with their start and end apart: 7, of which 6 were waited for; matrix products, arithmetic and copies ran while one was open for 1% of the time, Pallas kernels for 16%

profile of v16, /device:TPU:0, one launch (start us, length us, event | category | flops | bytes accessed | tf_op | source)
XLA Modules:
  0.0 129.9 jit_solution(2194360170475463761)
XLA Ops:
  0.7 2.4 %shard_map.169 = bf16[8,2,336,128]{3,2,1,0:T(8,128)(2,1)} custom-call(bf16[64,8192]{1,0:T(8,128)(2,1)} %x_ref.1, bf16[64,1024]{1,0:T(8,128)(2,1)} %b_ref.1, bf16[64,1024]{1,0:T(8,128)(2,1)} %c_ref.1, bf16[64,128]{1,0:T(8,128)(2,1)} %steps_ref.1), custom_call_target="tpu_custom_call" | custom-call | bytes 2752512 | tf_op jit(solution)/shard_map/pallas_call | solution.py:723
  3.1 6.3 %all-to-all-start = ((bf16[16,336,128]{2,1,0:T(8,128)(2,1)}), bf16[16,336,128]{2,1,0:T(8,128)(2,1)S(1)}, u32[]{:S(2)}, u32[]{:S(2)}) async-start(bf16[16,336,128]{2,1,0:T(8,128)(2,1)} %bitcast.11), calls=%async_computation | async-start | bytes 2752512 | tf_op jit(solution)/shard_map/all_to_all | solution.py:701
  9.8 0.8 dynamic_slice.15
  10.8 2.7 %shard_map.170 = bf16[8,2,512,128]{3,2,1,0:T(8,128)(2,1)} custom-call(bf16[64,8192]{1,0:T(8,128)(2,1)} %z_ref, bf16[64,8192]{1,0:T(8,128)(2,1)} %grad_ref.1), custom_call_target="tpu_custom_call" | custom-call | bytes 4194304 | tf_op jit(solution)/shard_map/pallas_call | solution.py:723
  13.5 14.7 %all-to-all-done.refs_0_.refs_2_ = bf16[16,336,128]{2,1,0:T(8,128)(2,1)S(1)} async-done(((bf16[16,336,128]{2,1,0:T(8,128)(2,1)}), bf16[16,336,128]{2,1,0:T(8,128)(2,1)S(1)}, u32[]{:S(2)}, u32[]{:S(2)}) %all-to-all-start) | async-done | bytes 1376288 | tf_op jit(solution)/shard_map/all_to_all | solution.py:701
  28.1 4.5 %all-to-all-start.1 = ((bf16[16,512,128]{2,1,0:T(8,128)(2,1)}), bf16[16,512,128]{2,1,0:T(8,128)(2,1)}, u32[]{:S(2)}, u32[]{:S(2)}) async-start(bf16[16,512,128]{2,1,0:T(8,128)(2,1)} %bitcast.10), calls=%async_computation.1 | async-start | bytes 4194304 | tf_op jit(solution)/shard_map/all_to_all | solution.py:701
  32.6 0.3 collective-permute-start
  32.9 1.3 %collective-permute-done = bf16[16,64,128]{2,1,0:T(8,128)(2,1)S(1)} collective-permute-done((bf16[16,64,128]{2,1,0:T(8,128)(2,1)S(1)}, bf16[16,64,128]{2,1,0:T(8,128)(2,1)S(1)}, u32[]{:S(2)}, u32[]{:S(2)}) %collective-permute-start) | collective-permute-done | bytes 262176 | tf_op jit(solution)/shard_map/ppermute | solution.py:737
  34.3 4.4 %shard_map.171 = (f32[1024,128]{1,0:T(8,128)}, f32[64,1024]{1,0:T(8,128)}, f32[8,128,512]{2,1,0:T(8,128)}, f32[8,8,512]{2,1,0:T(8,128)}, bf16[128,512]{1,0:T(8,128)(2,1)S(1)}, /*index=5*/f32[8,512]{1,0:T(8,128)}) custom-call(bf16[16,336,128]{2,1,0:T(8,128)(2,1)S(1)} %all-to-all-done.refs_0_.refs_2_, bf16[16,64,128]{2,1,0:T(8,128)(2,1)S(1)} %get-tuple-element.80.refs_1_, ...), custom_call_target="tpu_custom_call" | custom-call | flops 268435456 | bytes 4194304 | tf_op jit(solution)/shard_map/pallas_call | solution.py:784
  38.7 4.5 %collective-permute-start.1 = (bf16[128,512]{1,0:T(8,128)(2,1)S(1)}, bf16[128,512]{1,0:T(8,128)(2,1)S(1)}, u32[]{:S(2)}, u32[]{:S(2)}) collective-permute-start(bf16[128,512]{1,0:T(8,128)(2,1)S(1)} %get-tuple-element.51), channel_id=1, source_target_pairs={{0,16},{1,17},{2,18},{3,19},{4,20},{5,21},{6,22},{7,23},{8,24},{9,... | collective-permute-start | bytes 393224 | tf_op jit(solution)/shard_map/ppermute | solution.py:643
  43.2 5.9 %shard_map.172 = (f32[1024,512]{1,0:T(8,128)}, f32[8,128,512]{2,1,0:T(8,128)}, f32[8,8,512]{2,1,0:T(8,128)}) custom-call(bf16[16,336,128]{2,1,0:T(8,128)(2,1)S(1)} %all-to-all-done.refs_0_.refs_2_, bf16[16,64,128]{2,1,0:T(8,128)(2,1)S(1)} %get-tuple-element.80.refs_1_, bf16[16,64,128]{2,1,0:T(8,128)(2,1)S(1)} %get-tuple-element.79.refs_2_.refs_1_, ...), custom_call_target="tpu_custom_call" | custom-call | flops 805306368 | bytes 8388608 | tf_op jit(solution)/shard_map/pallas_call | solution.py:808
  49.0 12.2 %collective-permute-done.1.refs_5_.refs_10_ = bf16[128,512]{1,0:T(8,128)(2,1)S(1)} collective-permute-done((bf16[128,512]{1,0:T(8,128)(2,1)S(1)}, bf16[128,512]{1,0:T(8,128)(2,1)S(1)}, u32[]{:S(2)}, u32[]{:S(2)}) %collective-permute-start.1) | collective-permute-done | bytes 131104 | tf_op jit(solution)/shard_map/ppermute | solution.py:643
  61.3 4.8 %shard_map.173 = (f32[1024,512]{1,0:T(8,128)S(1)}, f32[8,8,128]{2,1,0:T(8,128)S(1)}, bf16[16,512,128]{2,1,0:T(8,128)(2,1)S(1)}) custom-call(bf16[16,336,128]{2,1,0:T(8,128)(2,1)S(1)} %all-to-all-done.refs_0_.refs_2_, bf16[16,64,128]{2,1,0:T(8,128)(2,1)S(1)} %get-tuple-element.79.refs_2_.refs_1_, bf16[16,512,128]{2,1,0:T(8,128)(2,1)} %all-to-all-done.1.refs_2_, ...), custom_call_target="tpu_custom_call" | custom-call | flops 134217728 | bytes 8388608 | tf_op jit(solution)/shard_map/pallas_call | solution.py:826
  66.1 1.2 collective-permute-done.2.refs_7_.refs_12_
  67.3 2.6 %shard_map.174 = (bf16[1024,512]{1,0:T(8,128)(2,1)S(1)}, f32[8,128,512]{2,1,0:T(8,128)S(1)}, bf16[128,512]{1,0:T(8,128)(2,1)S(1)}) custom-call(bf16[16,336,128]{2,1,0:T(8,128)(2,1)S(1)} %all-to-all-done.refs_0_.refs_2_, bf16[16,64,128]{2,1,0:T(8,128)(2,1)S(1)} %get-tuple-element.79.refs_2_.refs_1_, ...), custom_call_target="tpu_custom_call" | custom-call | flops 268435456 | bytes 6291456 | tf_op jit(solution)/shard_map/pallas_call | solution.py:847
  70.0 1.5 %collective-permute-start.3 = (bf16[128,512]{1,0:T(8,128)(2,1)S(1)}, bf16[128,512]{1,0:T(8,128)(2,1)S(1)}, u32[]{:S(2)}, u32[]{:S(2)}) collective-permute-start(bf16[128,512]{1,0:T(8,128)(2,1)S(1)} %get-tuple-element.65), channel_id=1, source_target_pairs={{16,0},{17,1},{18,2},{19,3},{20,4},{21,5},{22,6},{23,7},{24,8},{25... | collective-permute-start | bytes 393224 | tf_op jit(solution)/shard_map/ppermute | solution.py:643
  71.5 5.9 %shard_map.175 = (f32[1024,512]{1,0:T(8,128)S(1)}, f32[1024,128]{1,0:T(8,128)S(1)}, bf16[16,64,128]{2,1,0:T(8,128)(2,1)S(1)}, bf16[16,256,128]{2,1,0:T(8,128)(2,...) custom-call(bf16[16,336,128]{2,1,0:T(8,128)(2,1)S(1)} %all-to-all-done.refs_0_.refs_2_, ...), custom_call_target="tpu_custom_call" | custom-call | flops 1342177280 | bytes 8388608 | tf_op jit(solution)/shard_map/pallas_call | solution.py:866
  77.4 3.9 %collective-permute-done.3.refs_10_ = bf16[128,512]{1,0:T(8,128)(2,1)S(1)} collective-permute-done((bf16[128,512]{1,0:T(8,128)(2,1)S(1)}, bf16[128,512]{1,0:T(8,128)(2,1)S(1)}, u32[]{:S(2)}, u32[]{:S(2)}) %collective-permute-start.3) | collective-permute-done | bytes 131104 | tf_op jit(solution)/shard_map/ppermute | solution.py:643
  81.3 5.5 %shard_map.176 = bf16[16,656,128]{2,1,0:T(8,128)(2,1)} custom-call(bf16[16,336,128]{2,1,0:T(8,128)(2,1)S(1)} %all-to-all-done.refs_0_.refs_2_, bf16[16,64,128]{2,1,0:T(8,128)(2,1)S(1)} %get-tuple-element.80.refs_1_, f32[1024,512]{1,0:T(8,128)S(1)} %get-tuple-element.60.refs_2_, f32[1024,128]{1,0:T(8,128)S(1)} %get-tuple-element.61.refs_3_, ...), custom_call_target="tpu_custom_call" | custom-call | flops 536870912 | bytes 8388608 | tf_op jit(solution)/shard_map/pallas_call | solution.py:892
  86.8 37.5 %all_to_all.15.refs_0_ = bf16[16,656,128]{2,1,0:T(8,128)(2,1)S(1)} all-to-all(bf16[16,656,128]{2,1,0:T(8,128)(2,1)} %shard_map.176), channel_id=1, replica_groups=mesh['slab'=2,'sub'=8,'tensor'=2] {'sub','tensor'}, dimensions={0} | all-to-all | bytes 5373952 | tf_op jit(solution)/shard_map/all_to_all | solution.py:701
  124.3 0.4 collective-permute-start.4
  124.7 1.9 %shard_map.177 = (bf16[64,8192]{1,0:T(8,128)(2,1)}, bf16[64,8192]{1,0:T(8,128)(2,1)}, bf16[64,1024]{1,0:T(8,128)(2,1)}, bf16[64,1024]{1,0:T(8,128)(2,1)}, bf16[64,128]{1,0:T(8,128)(2,1)}) custom-call(bf16[16,656,128]{2,1,0:T(8,128)(2,1)S(1)} %all_to_all.15.refs_0_), custom_call_target="tpu_custom_call" | custom-call | bytes 5242880 | tf_op jit(solution)/shard_map/pallas_call | solution.py:928
  126.6 2.7 %collective-permute-done.4.other_ref = f32[40,128]{1,0:T(8,128)S(1)} collective-permute-done((f32[40,128]{1,0:T(8,128)S(1)}, f32[40,128]{1,0:T(8,128)S(1)}, u32[]{:S(2)}, u32[]{:S(2)}) %collective-permute-start.4) | collective-permute-done | bytes 20512 | tf_op jit(solution)/shard_map/ppermute | solution.py:674
  129.3 0.6 shard_map.179
  (30 shorter events, 0.8 us)
Async XLA Ops:
  0.6 8.7 %copy-start.5 = (f32[64]{0:T(128)S(1)}, f32[64]{0:T(128)}, u32[]{:S(2)}) copy-start(f32[64]{0:T(128)} %param.15) | copy-start | bytes 772
  0.7 8.8 %copy-start.6 = (f32[64]{0:T(128)S(1)}, f32[64]{0:T(128)}, u32[]{:S(2)}) copy-start(f32[64]{0:T(128)} %param.16) | copy-start | bytes 772
  0.7 8.9 %copy-start.7 = (f32[64]{0:T(128)S(1)}, f32[64]{0:T(128)}, u32[]{:S(2)}) copy-start(f32[64]{0:T(128)} %param.17) | copy-start | bytes 772
  3.1 25.1 %all-to-all-start = ((bf16[16,336,128]{2,1,0:T(8,128)(2,1)}), bf16[16,336,128]{2,1,0:T(8,128)(2,1)S(1)}, u32[]{:S(2)}, u32[]{:S(2)}) async-start(bf16[16,336,128]{2,1,0:T(8,128)(2,1)} %bitcast.11), calls=%async_computation | async-start | bytes 2752512 | tf_op jit(solution)/shard_map/all_to_all | solution.py:701
  28.1 33.1 %all-to-all-start.1 = ((bf16[16,512,128]{2,1,0:T(8,128)(2,1)}), bf16[16,512,128]{2,1,0:T(8,128)(2,1)}, u32[]{:S(2)}, u32[]{:S(2)}) async-start(bf16[16,512,128]{2,1,0:T(8,128)(2,1)} %bitcast.10), calls=%async_computation.1 | async-start | bytes 4194304 | tf_op jit(solution)/shard_map/all_to_all | solution.py:701
  32.6 1.6 %collective-permute-start = (bf16[16,64,128]{2,1,0:T(8,128)(2,1)S(1)}, bf16[16,64,128]{2,1,0:T(8,128)(2,1)S(1)}, u32[]{:S(2)}, u32[]{:S(2)}) collective-permute-start(bf16[16,64,128]{2,1,0:T(8,128)(2,1)S(1)} %slice.4), channel_id=1, source_target_pairs={{0,2},{2,0},{4,6},{6,4},{8,10},{10,8},{12,14},{14,12},{1,3},{3,1},... | collective-permute-start | bytes 786440 | tf_op jit(solution)/shard_map/ppermute | solution.py:737
  38.7 22.6 %collective-permute-start.1 = (bf16[128,512]{1,0:T(8,128)(2,1)S(1)}, bf16[128,512]{1,0:T(8,128)(2,1)S(1)}, u32[]{:S(2)}, u32[]{:S(2)}) collective-permute-start(bf16[128,512]{1,0:T(8,128)(2,1)S(1)} %get-tuple-element.51), channel_id=1, source_target_pairs={{0,16},{1,17},{2,18},{3,19},{4,20},{5,21},{6,22},{7,23},{8,24},{9,... | collective-permute-start | bytes 393224 | tf_op jit(solution)/shard_map/ppermute | solution.py:643
  61.3 6.0 %copy-start = (f32[1024,128]{1,0:T(8,128)S(1)}, f32[1024,128]{1,0:T(8,128)}, u32[]{:S(2)}) copy-start(f32[1024,128]{1,0:T(8,128)} %get-tuple-element.46.refs_3_.refs_4_.refs_6_.refs_8_) | copy-start | bytes 1572868
  61.3 6.0 %copy-start.3 = (f32[8,8,512]{2,1,0:T(8,128)S(1)}, f32[8,8,512]{2,1,0:T(8,128)}, u32[]{:S(2)}) copy-start(f32[8,8,512]{2,1,0:T(8,128)} %get-tuple-element.52.refs_6_.refs_5_.refs_9_) | copy-start | bytes 393220
  66.1 1.2 collective-permute-start.2
  67.3 4.1 %copy-start.1 = (f32[64,1024]{1,0:T(8,128)S(1)}, f32[64,1024]{1,0:T(8,128)}, u32[]{:S(2)}) copy-start(f32[64,1024]{1,0:T(8,128)} %get-tuple-element.47.refs_4_.refs_7_.refs_9_) | copy-start | bytes 786436
  67.3 4.1 %copy-start.2 = (f32[8,128,512]{2,1,0:T(8,128)S(1)}, f32[8,128,512]{2,1,0:T(8,128)}, u32[]{:S(2)}) copy-start(f32[8,128,512]{2,1,0:T(8,128)} %get-tuple-element.59.refs_8_) | copy-start | bytes 6291460
  70.0 11.3 %collective-permute-start.3 = (bf16[128,512]{1,0:T(8,128)(2,1)S(1)}, bf16[128,512]{1,0:T(8,128)(2,1)S(1)}, u32[]{:S(2)}, u32[]{:S(2)}) collective-permute-start(bf16[128,512]{1,0:T(8,128)(2,1)S(1)} %get-tuple-element.65), channel_id=1, source_target_pairs={{16,0},{17,1},{18,2},{19,3},{20,4},{21,5},{22,6},{23,7},{24,8},{25... | collective-permute-start | bytes 393224 | tf_op jit(solution)/shard_map/ppermute | solution.py:643
  71.5 9.8 %copy-start.4 = (f32[8,8,512]{2,1,0:T(8,128)S(1)}, f32[8,8,512]{2,1,0:T(8,128)}, u32[]{:S(2)}) copy-start(f32[8,8,512]{2,1,0:T(8,128)} %get-tuple-element.49.refs_6_.refs_13_) | copy-start | bytes 393220
  124.3 5.0 %collective-permute-start.4 = (f32[40,128]{1,0:T(8,128)S(1)}, f32[40,128]{1,0:T(8,128)S(1)}, u32[]{:S(2)}, u32[]{:S(2)}) collective-permute-start(f32[40,128]{1,0:T(8,128)S(1)} %shard_map.178.own_ref), channel_id=1, source_target_pairs={{0,16},{16,0},{1,17},{17,1},{2,18},{18,2},{3,19},{19,3},{4,20},{20... | collective-permute-start | bytes 61448 | tf_op jit(solution)/shard_map/ppermute | solution.py:674

commit v17 on v16

--- a/solution.py
+++ b/solution.py
@@ -330,7 +330,6 @@
 ):
     second_out[...] = second_ref[...]
     inbound = inbound_ref[...].astype(bf16)
-    ones = jnp.ones((16, 2 * LANES), bf16)
     for i in range(per_step):
         rows = slice(i * CHUNK, (i + 1) * CHUNK)
         sm = sm_ref[rows, :]
@@ -348,9 +347,8 @@
             gated = (y + skip_ref[0:1, at] * values) * (gates * sigmoid(gates))
             power = power + gated * gated
             cross = cross + grad * gain_ref[0:1, at] * gated
-        for k, tile in enumerate((power, cross)):
-            terms = jnp.concatenate(two_terms(tile), axis=1)
-            sums_ref[i, k : k + 1, :] = mm_nt(ones, terms)[0:1]
+        sums_ref[i, 0:1, :] = jnp.sum(power.T, axis=0, keepdims=True)
+        sums_ref[i, 1:2, :] = jnp.sum(cross.T, axis=0, keepdims=True)
         sums_ref[i, 2:, :] = jnp.zeros((6, LANES), f32)
 
 

time: 130 us -> 130 us (level)
  no operation moved by 1% of the time
where the time goes in v17:
time: 130 us
  blocking collectives  37.5 us (29%)
  Pallas kernels  36.6 us (28%)
  waiting for transfers between devices  36 us (28%)
  starting transfers between devices  17.4 us (13%)
  local copies, waits for them, and re-layouts  1.32 us (1%)
    all_to_all x1, blocking collectives, exchange(): lax.all_to_all(array, ('sub', 'tensor'), split_axis=0, concat_axis=0, til...  37.5 us
    ppermute x2, waiting for transfers between devices, shifted(): return lax.ppermute(array, 'slab', pairs)  16.1 us
    all_to_all x2, waiting for transfers between devices, exchange(): lax.all_to_all(array, ('sub', 'tensor'), split_axis=0, concat_axis=0, til...  14.7 us
    all_to_all x2, starting transfers between devices, exchange(): lax.all_to_all(array, ('sub', 'tensor'), split_axis=0, concat_axis=0, til...  10.7 us
    ppermute x2, starting transfers between devices, shifted(): return lax.ppermute(array, 'slab', pairs)  5.96 us
    pallas_call x1, Pallas kernels, on_device(): flow(local_kernel, [(struct((tokens, WIDTH)), many['token'](WIDTH)), (str...  5.9 us
    pallas_call x1, Pallas kernels, on_device(): flow(within_kernel, [(hbm((tokens, WIDTH)), up['token'](WIDTH)), (hbm((ch...  5.88 us
    pallas_call x1, Pallas kernels, on_device(): flow(last_kernel, [(hbm((peers, last_rows, LANES), bf16), anywhere)], 4 *...  5.51 us
  transfers between devices with their start and end apart: 7, of which 6 were waited for; matrix products, arithmetic and copies ran while one was open for 1% of the time, Pallas kernels for 16%

profile of v17, /device:TPU:0, one launch (start us, length us, event | category | flops | bytes accessed | tf_op | source)
XLA Modules:
  0.0 129.7 jit_solution(13779791624892744637)
XLA Ops:
  0.7 2.4 %shard_map.169 = bf16[8,2,336,128]{3,2,1,0:T(8,128)(2,1)} custom-call(bf16[64,8192]{1,0:T(8,128)(2,1)} %x_ref.1, bf16[64,1024]{1,0:T(8,128)(2,1)} %b_ref.1, bf16[64,1024]{1,0:T(8,128)(2,1)} %c_ref.1, bf16[64,128]{1,0:T(8,128)(2,1)} %steps_ref.1), custom_call_target="tpu_custom_call" | custom-call | bytes 2752512 | tf_op jit(solution)/shard_map/pallas_call | solution.py:721
  3.1 6.3 %all-to-all-start = ((bf16[16,336,128]{2,1,0:T(8,128)(2,1)}), bf16[16,336,128]{2,1,0:T(8,128)(2,1)S(1)}, u32[]{:S(2)}, u32[]{:S(2)}) async-start(bf16[16,336,128]{2,1,0:T(8,128)(2,1)} %bitcast.11), calls=%async_computation | async-start | bytes 2752512 | tf_op jit(solution)/shard_map/all_to_all | solution.py:699
  9.8 0.8 dynamic_slice.15
  10.8 2.7 %shard_map.170 = bf16[8,2,512,128]{3,2,1,0:T(8,128)(2,1)} custom-call(bf16[64,8192]{1,0:T(8,128)(2,1)} %z_ref, bf16[64,8192]{1,0:T(8,128)(2,1)} %grad_ref.1), custom_call_target="tpu_custom_call" | custom-call | bytes 4194304 | tf_op jit(solution)/shard_map/pallas_call | solution.py:721
  13.5 14.7 %all-to-all-done.refs_0_.refs_2_ = bf16[16,336,128]{2,1,0:T(8,128)(2,1)S(1)} async-done(((bf16[16,336,128]{2,1,0:T(8,128)(2,1)}), bf16[16,336,128]{2,1,0:T(8,128)(2,1)S(1)}, u32[]{:S(2)}, u32[]{:S(2)}) %all-to-all-start) | async-done | bytes 1376288 | tf_op jit(solution)/shard_map/all_to_all | solution.py:699
  28.1 4.5 %all-to-all-start.1 = ((bf16[16,512,128]{2,1,0:T(8,128)(2,1)}), bf16[16,512,128]{2,1,0:T(8,128)(2,1)}, u32[]{:S(2)}, u32[]{:S(2)}) async-start(bf16[16,512,128]{2,1,0:T(8,128)(2,1)} %bitcast.10), calls=%async_computation.1 | async-start | bytes 4194304 | tf_op jit(solution)/shard_map/all_to_all | solution.py:699
  32.6 0.3 collective-permute-start
  32.9 1.3 %collective-permute-done = bf16[16,64,128]{2,1,0:T(8,128)(2,1)S(1)} collective-permute-done((bf16[16,64,128]{2,1,0:T(8,128)(2,1)S(1)}, bf16[16,64,128]{2,1,0:T(8,128)(2,1)S(1)}, u32[]{:S(2)}, u32[]{:S(2)}) %collective-permute-start) | collective-permute-done | bytes 262176 | tf_op jit(solution)/shard_map/ppermute | solution.py:735
  34.3 4.4 %shard_map.171 = (f32[1024,128]{1,0:T(8,128)}, f32[64,1024]{1,0:T(8,128)}, f32[8,128,512]{2,1,0:T(8,128)}, f32[8,8,512]{2,1,0:T(8,128)}, bf16[128,512]{1,0:T(8,128)(2,1)S(1)}, /*index=5*/f32[8,512]{1,0:T(8,128)}) custom-call(bf16[16,336,128]{2,1,0:T(8,128)(2,1)S(1)} %all-to-all-done.refs_0_.refs_2_, bf16[16,64,128]{2,1,0:T(8,128)(2,1)S(1)} %get-tuple-element.80.refs_1_, ...), custom_call_target="tpu_custom_call" | custom-call | flops 268435456 | bytes 4194304 | tf_op jit(solution)/shard_map/pallas_call | solution.py:782
  38.7 4.5 %collective-permute-start.1 = (bf16[128,512]{1,0:T(8,128)(2,1)S(1)}, bf16[128,512]{1,0:T(8,128)(2,1)S(1)}, u32[]{:S(2)}, u32[]{:S(2)}) collective-permute-start(bf16[128,512]{1,0:T(8,128)(2,1)S(1)} %get-tuple-element.51), channel_id=1, source_target_pairs={{0,16},{1,17},{2,18},{3,19},{4,20},{5,21},{6,22},{7,23},{8,24},{9,... | collective-permute-start | bytes 393224 | tf_op jit(solution)/shard_map/ppermute | solution.py:641
  43.2 5.9 %shard_map.172 = (f32[1024,512]{1,0:T(8,128)}, f32[8,128,512]{2,1,0:T(8,128)}, f32[8,8,512]{2,1,0:T(8,128)}) custom-call(bf16[16,336,128]{2,1,0:T(8,128)(2,1)S(1)} %all-to-all-done.refs_0_.refs_2_, bf16[16,64,128]{2,1,0:T(8,128)(2,1)S(1)} %get-tuple-element.80.refs_1_, bf16[16,64,128]{2,1,0:T(8,128)(2,1)S(1)} %get-tuple-element.79.refs_2_.refs_1_, ...), custom_call_target="tpu_custom_call" | custom-call | flops 805306368 | bytes 8388608 | tf_op jit(solution)/shard_map/pallas_call | solution.py:806
  49.0 12.2 %collective-permute-done.1.refs_5_.refs_10_ = bf16[128,512]{1,0:T(8,128)(2,1)S(1)} collective-permute-done((bf16[128,512]{1,0:T(8,128)(2,1)S(1)}, bf16[128,512]{1,0:T(8,128)(2,1)S(1)}, u32[]{:S(2)}, u32[]{:S(2)}) %collective-permute-start.1) | collective-permute-done | bytes 131104 | tf_op jit(solution)/shard_map/ppermute | solution.py:641
  61.3 4.5 %shard_map.173 = (f32[1024,512]{1,0:T(8,128)S(1)}, f32[8,8,128]{2,1,0:T(8,128)S(1)}, bf16[16,512,128]{2,1,0:T(8,128)(2,1)S(1)}) custom-call(bf16[16,336,128]{2,1,0:T(8,128)(2,1)S(1)} %all-to-all-done.refs_0_.refs_2_, bf16[16,64,128]{2,1,0:T(8,128)(2,1)S(1)} %get-tuple-element.79.refs_2_.refs_1_, bf16[16,512,128]{2,1,0:T(8,128)(2,1)} %all-to-all-done.1.refs_2_, ...), custom_call_target="tpu_custom_call" | custom-call | flops 134217728 | bytes 8388608 | tf_op jit(solution)/shard_map/pallas_call | solution.py:824
  65.9 1.2 collective-permute-done.2.refs_7_.refs_12_
  67.1 2.6 %shard_map.174 = (bf16[1024,512]{1,0:T(8,128)(2,1)S(1)}, f32[8,128,512]{2,1,0:T(8,128)S(1)}, bf16[128,512]{1,0:T(8,128)(2,1)S(1)}) custom-call(bf16[16,336,128]{2,1,0:T(8,128)(2,1)S(1)} %all-to-all-done.refs_0_.refs_2_, bf16[16,64,128]{2,1,0:T(8,128)(2,1)S(1)} %get-tuple-element.79.refs_2_.refs_1_, ...), custom_call_target="tpu_custom_call" | custom-call | flops 268435456 | bytes 6291456 | tf_op jit(solution)/shard_map/pallas_call | solution.py:845
  69.7 1.5 %collective-permute-start.3 = (bf16[128,512]{1,0:T(8,128)(2,1)S(1)}, bf16[128,512]{1,0:T(8,128)(2,1)S(1)}, u32[]{:S(2)}, u32[]{:S(2)}) collective-permute-start(bf16[128,512]{1,0:T(8,128)(2,1)S(1)} %get-tuple-element.65), channel_id=1, source_target_pairs={{16,0},{17,1},{18,2},{19,3},{20,4},{21,5},{22,6},{23,7},{24,8},{25... | collective-permute-start | bytes 393224 | tf_op jit(solution)/shard_map/ppermute | solution.py:641
  71.2 5.9 %shard_map.175 = (f32[1024,512]{1,0:T(8,128)S(1)}, f32[1024,128]{1,0:T(8,128)S(1)}, bf16[16,64,128]{2,1,0:T(8,128)(2,1)S(1)}, bf16[16,256,128]{2,1,0:T(8,128)(2,...) custom-call(bf16[16,336,128]{2,1,0:T(8,128)(2,1)S(1)} %all-to-all-done.refs_0_.refs_2_, ...), custom_call_target="tpu_custom_call" | custom-call | flops 1342177280 | bytes 8388608 | tf_op jit(solution)/shard_map/pallas_call | solution.py:864
  77.1 3.9 %collective-permute-done.3.refs_10_ = bf16[128,512]{1,0:T(8,128)(2,1)S(1)} collective-permute-done((bf16[128,512]{1,0:T(8,128)(2,1)S(1)}, bf16[128,512]{1,0:T(8,128)(2,1)S(1)}, u32[]{:S(2)}, u32[]{:S(2)}) %collective-permute-start.3) | collective-permute-done | bytes 131104 | tf_op jit(solution)/shard_map/ppermute | solution.py:641
  81.0 5.5 %shard_map.176 = bf16[16,656,128]{2,1,0:T(8,128)(2,1)} custom-call(bf16[16,336,128]{2,1,0:T(8,128)(2,1)S(1)} %all-to-all-done.refs_0_.refs_2_, bf16[16,64,128]{2,1,0:T(8,128)(2,1)S(1)} %get-tuple-element.80.refs_1_, f32[1024,512]{1,0:T(8,128)S(1)} %get-tuple-element.60.refs_2_, f32[1024,128]{1,0:T(8,128)S(1)} %get-tuple-element.61.refs_3_, ...), custom_call_target="tpu_custom_call" | custom-call | flops 536870912 | bytes 8388608 | tf_op jit(solution)/shard_map/pallas_call | solution.py:890
  86.5 37.5 %all_to_all.15.refs_0_ = bf16[16,656,128]{2,1,0:T(8,128)(2,1)S(1)} all-to-all(bf16[16,656,128]{2,1,0:T(8,128)(2,1)} %shard_map.176), channel_id=1, replica_groups=mesh['slab'=2,'sub'=8,'tensor'=2] {'sub','tensor'}, dimensions={0} | all-to-all | bytes 5373952 | tf_op jit(solution)/shard_map/all_to_all | solution.py:699
  124.1 0.4 collective-permute-start.4
  124.5 1.9 %shard_map.177 = (bf16[64,8192]{1,0:T(8,128)(2,1)}, bf16[64,8192]{1,0:T(8,128)(2,1)}, bf16[64,1024]{1,0:T(8,128)(2,1)}, bf16[64,1024]{1,0:T(8,128)(2,1)}, bf16[64,128]{1,0:T(8,128)(2,1)}) custom-call(bf16[16,656,128]{2,1,0:T(8,128)(2,1)S(1)} %all_to_all.15.refs_0_), custom_call_target="tpu_custom_call" | custom-call | bytes 5242880 | tf_op jit(solution)/shard_map/pallas_call | solution.py:926
  126.4 2.7 %collective-permute-done.4.other_ref = f32[40,128]{1,0:T(8,128)S(1)} collective-permute-done((f32[40,128]{1,0:T(8,128)S(1)}, f32[40,128]{1,0:T(8,128)S(1)}, u32[]{:S(2)}, u32[]{:S(2)}) %collective-permute-start.4) | collective-permute-done | bytes 20512 | tf_op jit(solution)/shard_map/ppermute | solution.py:672
  129.1 0.6 shard_map.179
  (30 shorter events, 0.9 us)
Async XLA Ops:
  0.6 8.7 %copy-start.5 = (f32[64]{0:T(128)S(1)}, f32[64]{0:T(128)}, u32[]{:S(2)}) copy-start(f32[64]{0:T(128)} %param.15) | copy-start | bytes 772
  0.7 8.8 %copy-start.6 = (f32[64]{0:T(128)S(1)}, f32[64]{0:T(128)}, u32[]{:S(2)}) copy-start(f32[64]{0:T(128)} %param.16) | copy-start | bytes 772
  0.7 8.9 %copy-start.7 = (f32[64]{0:T(128)S(1)}, f32[64]{0:T(128)}, u32[]{:S(2)}) copy-start(f32[64]{0:T(128)} %param.17) | copy-start | bytes 772
  3.1 25.1 %all-to-all-start = ((bf16[16,336,128]{2,1,0:T(8,128)(2,1)}), bf16[16,336,128]{2,1,0:T(8,128)(2,1)S(1)}, u32[]{:S(2)}, u32[]{:S(2)}) async-start(bf16[16,336,128]{2,1,0:T(8,128)(2,1)} %bitcast.11), calls=%async_computation | async-start | bytes 2752512 | tf_op jit(solution)/shard_map/all_to_all | solution.py:699
  28.1 33.1 %all-to-all-start.1 = ((bf16[16,512,128]{2,1,0:T(8,128)(2,1)}), bf16[16,512,128]{2,1,0:T(8,128)(2,1)}, u32[]{:S(2)}, u32[]{:S(2)}) async-start(bf16[16,512,128]{2,1,0:T(8,128)(2,1)} %bitcast.10), calls=%async_computation.1 | async-start | bytes 4194304 | tf_op jit(solution)/shard_map/all_to_all | solution.py:699
  32.6 1.6 %collective-permute-start = (bf16[16,64,128]{2,1,0:T(8,128)(2,1)S(1)}, bf16[16,64,128]{2,1,0:T(8,128)(2,1)S(1)}, u32[]{:S(2)}, u32[]{:S(2)}) collective-permute-start(bf16[16,64,128]{2,1,0:T(8,128)(2,1)S(1)} %slice.4), channel_id=1, source_target_pairs={{0,2},{2,0},{4,6},{6,4},{8,10},{10,8},{12,14},{14,12},{1,3},{3,1},... | collective-permute-start | bytes 786440 | tf_op jit(solution)/shard_map/ppermute | solution.py:735
  38.7 22.6 %collective-permute-start.1 = (bf16[128,512]{1,0:T(8,128)(2,1)S(1)}, bf16[128,512]{1,0:T(8,128)(2,1)S(1)}, u32[]{:S(2)}, u32[]{:S(2)}) collective-permute-start(bf16[128,512]{1,0:T(8,128)(2,1)S(1)} %get-tuple-element.51), channel_id=1, source_target_pairs={{0,16},{1,17},{2,18},{3,19},{4,20},{5,21},{6,22},{7,23},{8,24},{9,... | collective-permute-start | bytes 393224 | tf_op jit(solution)/shard_map/ppermute | solution.py:641
  61.3 5.8 %copy-start = (f32[1024,128]{1,0:T(8,128)S(1)}, f32[1024,128]{1,0:T(8,128)}, u32[]{:S(2)}) copy-start(f32[1024,128]{1,0:T(8,128)} %get-tuple-element.46.refs_3_.refs_4_.refs_6_.refs_8_) | copy-start | bytes 1572868
  61.3 5.8 %copy-start.3 = (f32[8,8,512]{2,1,0:T(8,128)S(1)}, f32[8,8,512]{2,1,0:T(8,128)}, u32[]{:S(2)}) copy-start(f32[8,8,512]{2,1,0:T(8,128)} %get-tuple-element.52.refs_6_.refs_5_.refs_9_) | copy-start | bytes 393220
  65.8 1.3 collective-permute-start.2
  67.1 4.1 %copy-start.1 = (f32[64,1024]{1,0:T(8,128)S(1)}, f32[64,1024]{1,0:T(8,128)}, u32[]{:S(2)}) copy-start(f32[64,1024]{1,0:T(8,128)} %get-tuple-element.47.refs_4_.refs_7_.refs_9_) | copy-start | bytes 786436
  67.1 4.1 %copy-start.2 = (f32[8,128,512]{2,1,0:T(8,128)S(1)}, f32[8,128,512]{2,1,0:T(8,128)}, u32[]{:S(2)}) copy-start(f32[8,128,512]{2,1,0:T(8,128)} %get-tuple-element.59.refs_8_) | copy-start | bytes 6291460
  69.7 11.3 %collective-permute-start.3 = (bf16[128,512]{1,0:T(8,128)(2,1)S(1)}, bf16[128,512]{1,0:T(8,128)(2,1)S(1)}, u32[]{:S(2)}, u32[]{:S(2)}) collective-permute-start(bf16[128,512]{1,0:T(8,128)(2,1)S(1)} %get-tuple-element.65), channel_id=1, source_target_pairs={{16,0},{17,1},{18,2},{19,3},{20,4},{21,5},{22,6},{23,7},{24,8},{25... | collective-permute-start | bytes 393224 | tf_op jit(solution)/shard_map/ppermute | solution.py:641
  71.2 9.8 %copy-start.4 = (f32[8,8,512]{2,1,0:T(8,128)S(1)}, f32[8,8,512]{2,1,0:T(8,128)}, u32[]{:S(2)}) copy-start(f32[8,8,512]{2,1,0:T(8,128)} %get-tuple-element.49.refs_6_.refs_13_) | copy-start | bytes 393220
  124.1 5.0 %collective-permute-start.4 = (f32[40,128]{1,0:T(8,128)S(1)}, f32[40,128]{1,0:T(8,128)S(1)}, u32[]{:S(2)}, u32[]{:S(2)}) collective-permute-start(f32[40,128]{1,0:T(8,128)S(1)} %shard_map.178.own_ref), channel_id=1, source_target_pairs={{0,16},{16,0},{1,17},{17,1},{2,18},{18,2},{3,19},{19,3},{4,20},{20... | collective-permute-start | bytes 61448 | tf_op jit(solution)/shard_map/ppermute | solution.py:672
